TPU v7x, 32 devices: a whole 2x2x4 slice. The times are simulated.
32 devices in a mesh: member: 4 (over z), dp: 8 (over y, x, core).
Axes of the slice: x: 2, y: 2, z: 4, core: 2. Of those that a mesh axis runs over, the one named last changes fastest.
Arguments:
- teacher_feats: bfloat16 [4, 128, 1024], P('member', 'dp'), may hold values from -8 to 8
- teacher_gain: float32 [4, 1024], P('member'), may hold values from 0.1 to 1.9
- teacher_head: bfloat16 [4, 1024, 3072], P('member', None, 'dp'), may hold values from -1 to 1
- teacher_bias: float32 [4, 3072], P('member', 'dp'), may hold values from -1 to 4
- student_feats: bfloat16 [128, 1024], P('member'), may hold values from -6 to 6
- student_gain: float32 [1024], replicated, may hold values from 0.1 to 1.9
- student_head: bfloat16 [1024, 3072], P('member', 'dp'), may hold values from -0.1875 to 0.1875
- student_bias: float32 [3072], P('dp'), may hold values from -1 to 4
Outputs:
- loss: float32 [], replicated
- head_grad: float32 [1024, 3072], P('member', 'dp')
- bias_grad: float32 [3072], P('dp')
All inputs are finite; a program needn't handle non-finite values.
Results may differ from a plain program's by a relative error of at most 0.022.
Values may be sent and summed in bfloat16 or wider, within the bound.
No kernel may reach another device: no remote copies, remote signals or barrier semaphores. Data moves between devices by JAX's collectives and lax.ppermute only.
A program may use at most 64 MiB of HBM per device.

v0:
```python
import jax
import jax.numpy as jnp
from jax import lax
from jax.sharding import PartitionSpec as P


def joined(shard, axis, combine):
    everything = jax.tree.map(lambda part: lax.all_gather(part, axis), shard)
    initial = jax.tree.map(lambda part: part[0], everything)

    def step(k, so_far):
        return combine(so_far, jax.tree.map(lambda part: part[k], everything))

    return lax.fori_loop(1, lax.axis_size(axis), step, initial)


def norm_rows(values, gain_row):
    values = values.astype(jnp.float32)
    center = values - jnp.mean(values, axis=-1, keepdims=True)
    spread = jnp.mean(center * center, axis=-1, keepdims=True)
    return center * lax.rsqrt(spread + 1e-06) * gain_row


def combine_scores(earlier, later):
    maxima = jnp.maximum(earlier[0], later[0])
    totals = earlier[1] * jnp.exp(earlier[0] - maxima) + later[1] * jnp.exp(later[0] - maxima)
    return (maxima, totals)


def row_folder(source, portion):
    return jnp.dot(source, portion, preferred_element_type=jnp.float32)


def on_device(
    teacher_feats,
    teacher_gain,
    teacher_head,
    teacher_bias,
    student_feats,
    student_gain,
    student_head,
    student_bias,
):
    members = lax.axis_size("member")
    dp_count = lax.axis_size("dp")
    normed = norm_rows(teacher_feats[0], teacher_gain[0]).astype(jnp.bfloat16)
    weights = teacher_head[0]
    offsets = teacher_bias[0]
    logits = (
        jnp.dot(
            lax.all_gather(normed, "dp", axis=0, tiled=True),
            weights,
            preferred_element_type=jnp.float32,
        )
        + offsets
    )
    images = logits.shape[0]
    local_max = jnp.max(logits, axis=1)
    local_total = jnp.sum(jnp.exp(logits - local_max[:, None]), axis=1)
    maxima, totals = joined((local_max, local_total), "dp", combine_scores)
    log_norm = maxima + jnp.log(totals)
    log_prob = logits - log_norm[:, None]
    normed_s = norm_rows(student_feats, student_gain).astype(jnp.bfloat16)
    col_count = student_head.shape[1]
    classes = col_count * dp_count
    summed = lax.psum_scatter(
        log_prob.astype(jnp.bfloat16), "member", scatter_dimension=0, tiled=True
    ).astype(jnp.float32)
    target = summed / members
    student_logits = row_folder(
        normed_s, lax.all_gather(student_head, "member", axis=0, tiled=True)
    )
    alphas = jnp.exp(student_logits + student_bias)
    alpha_sum = lax.psum(jnp.sum(alphas, axis=1), "dp")
    partial_value = jnp.sum(-lax.lgamma(alpha_sum) / dp_count) + jnp.sum(
        lax.lgamma(alphas) - (alphas - 1.0) * target
    )
    term_signal = alphas * (lax.digamma(alphas) - lax.digamma(alpha_sum)[:, None] - target)
    loss_value = lax.psum(partial_value, ("member", "dp")) / (images * classes)
    columns = normed_s.astype(jnp.float32)
    head_grad = (
        lax.psum_scatter(
            lax.dot_general(
                columns,
                term_signal,
                (((0,), (0,)), ((), ())),
                precision=lax.Precision.HIGHEST,
                preferred_element_type=jnp.float32,
            ).astype(jnp.bfloat16),
            "member",
            scatter_dimension=0,
            tiled=True,
        ).astype(jnp.float32)
        / images
    )
    bias_grad = lax.psum(jnp.sum(term_signal, axis=0), "member") / images
    return (loss_value, head_grad, bias_grad)


def solution(mesh):
    placed = (
        P("member", "dp", None),
        P("member", None),
        P("member", None, "dp"),
        P("member", "dp"),
        P("member", None),
        P(),
        P("member", "dp"),
        P("dp"),
    )
    return jax.shard_map(
        on_device,
        mesh=mesh,
        in_specs=placed,
        out_specs=(P(), P("member", "dp"), P("dp")),
        check_vma=False,
    )
```

profile of v0, /device:TPU:0, one launch (start us, length us, event | category | flops | bytes accessed | tf_op | source)
XLA Modules:
  0.0 139.6 jit_solution(8779560553481564888)
XLA Ops:
  7.2 0.0 copy-start
  7.2 0.0 reduce-scatter.3.cloned.1.call-start
  7.2 0.9 convert_reduce_fusion.1
  8.2 0.9 fusion.12
  9.1 0.8 fusion.14
  10.0 10.8 %all_gather.19 = bf16[128,1024]{1,0:T(8,128)(2,1)S(1)} all-gather(bf16[16,1024]{1,0:T(8,128)(2,1)S(1)} %fusion.14), channel_id=1, replica_groups=mesh['member'=4,'dp'=8] {'dp'}, dimensions={0}, use_global_device_ids=true | all-gather | bytes 294912 | tf_op jit(solution)/shard_map/all_gather | solution.py:51
  20.7 0.7 reduce.1
  21.4 0.0 copy-done
  21.5 0.0 copy-start.1
  21.5 0.4 fusion.34
  21.8 0.0 copy-start.2
  21.9 0.2 exponential_reduce_fusion
  22.0 8.7 %all-gather.3 = f32[8,1,128]{2,1,0:T(1,128)S(1)} all-gather(f32[1,1,128]{2,1,0:T(1,128)S(1)} %bitcast.49), channel_id=3, replica_groups=mesh['member'=4,'dp'=8] {'dp'}, dimensions={0}, use_global_device_ids=true | all-gather | bytes 4608 | tf_op jit(solution)/shard_map/all_gather | solution.py:8
  30.8 7.8 %all-gather.2 = f32[8,1,128]{2,1,0:T(1,128)S(1)} all-gather(f32[1,1,128]{2,1,0:T(1,128)S(1)} %bitcast.47), channel_id=2, replica_groups=mesh['member'=4,'dp'=8] {'dp'}, dimensions={0}, use_global_device_ids=true | all-gather | bytes 4608 | tf_op jit(solution)/shard_map/all_gather | solution.py:8
  38.5 0.3 while.17
  38.8 0.0 copy-start.4
  38.8 0.0 copy-start.5
  38.9 0.7 subtract_convert_fusion
  39.6 0.0 reduce-scatter.3.cloned.1.call-update
  39.6 0.0 reduce-scatter.5.cloned.1.call-start
  39.7 0.0 copy-done.1
  39.7 0.1 convert_reduce_fusion
  39.8 0.2 fusion.6
  40.0 0.0 copy-done.2
  40.0 21.4 %all_gather.18 = bf16[1024,384]{1,0:T(8,128)(2,1)S(1)} all-gather(bf16[256,384]{1,0:T(8,128)(2,1)S(1)} %copy-done.2), channel_id=1, replica_groups=mesh['member'=4,'dp'=8] {'member'}, dimensions={0}, use_global_device_ids=true | all-gather | bytes 983040 | tf_op jit(solution)/shard_map/all_gather | solution.py:71
  61.4 0.0 reduce-scatter.3.cloned.1.call-done
  61.4 0.0 copy-done.4
  61.4 0.0 copy-done.5
  61.4 0.0 copy-start.3
  61.4 2.0 %subtract_reduce_fusion = (f32[]{:T(128)}, f32[32]{0:T(128)S(1)}, f32[32,384]{1,0:T(8,128)S(1)}) fusion(bf16[32,384]{1,0:T(8,128)(2,1)} %reduce-scatter.3.cloned.1.call-done, f32[384]{0:T(512)S(1)} %copy-done.5, bf16[1024,384]{1,0:T(8,128)(2,1)S(1)} %all_gather.18, bf16[32,1024]{1,0:T(8,128)(2,1)S(1)} %copy-done.1, f32[1024]{0:T(1024)S(1)} %copy-done.4, ...), kind=kOutput, calls=%fused_computation.39 | convolution fusion | flops 26042336 | bytes 931716 | tf_op jit(solution)/shard_map/dot_general | solution.py:31
  63.4 11.8 %psum.21 = f32[32]{0:T(128)S(1)} all-reduce(f32[32]{0:T(128)S(1)} %get-tuple-element.139), channel_id=1, replica_groups=mesh['member'=4,'dp'=8] {'dp'}, use_global_device_ids=true, to_apply=%region_3.0 | all-reduce | flops 32 | bytes 256 | tf_op jit(solution)/shard_map/psum | solution.py:74
  75.2 0.1 compare_select_fusion.2
  75.3 0.0 copy-done.3
  75.3 0.4 fusion.32
  75.6 1.8 %convolution_convert_fusion = bf16[1024,384]{1,0:T(8,128)(2,1)} fusion(f32[32,384]{1,0:T(8,128)S(1)} %get-tuple-element.153, bf16[32,1024]{1,0:T(8,128)(2,1)S(1)} %copy-done.1, f32[1024]{0:T(1024)S(1)} %copy-done.4, f32[32]{0:T(128)S(1)} %add_rsqrt_fusion.1, f32[32]{0:T(128)S(1)} %broadcast_multiply_fusion.2), kind=kOutput, calls=%fused_computation.6 | convolution fusion | flops 151552000 | bytes 905472 | tf_op jit(solution)/shard_map/dot_general | solution.py:83
  77.4 0.0 reduce-scatter.5.cloned.1.call-update
  77.4 0.7 multiply_reduce_fusion
  79.4 38.7 %psum.22 = f32[]{:T(128)} all-reduce(f32[]{:T(128)S(6)} %add.108), channel_id=1, replica_groups=mesh['member'=4,'dp'=8] {'member','dp'}, use_global_device_ids=true, to_apply=%region_13.0 | all-reduce | flops 1 | bytes 8 | tf_op jit(solution)/shard_map/psum | solution.py:79
  118.8 10.5 %psum.23 = f32[384]{0:T(512)S(1)} all-reduce(f32[384]{0:T(512)S(1)} %get-tuple-element.152), channel_id=1, replica_groups=mesh['member'=4,'dp'=8] {'member'}, use_global_device_ids=true, to_apply=%region_16.0 | all-reduce | flops 384 | bytes 3072 | tf_op jit(solution)/shard_map/psum | solution.py:96
  129.3 0.6 broadcast_multiply_fusion
  129.9 0.0 reduce-scatter.5.cloned.1.call-done
  129.9 1.7 %convert_multiply_fusion = f32[256,384]{1,0:T(8,128)} fusion(bf16[256,384]{1,0:T(8,128)(2,1)} %reduce-scatter.5.cloned.1.call-done), kind=kLoop, calls=%fused_computation.11 | loop fusion | flops 196608 | bytes 589824 | tf_op jit(solution)/shard_map/div | solution.py:82
  (14 shorter events, 0.2 us)
Async XLA Ops:
  7.2 14.3 %copy-start = (bf16[1,1024,384]{2,1,0:T(8,128)(2,1)S(1)}, bf16[1,1024,384]{2,1,0:T(8,128)(2,1)}, u32[]{:S(2)}) copy-start(bf16[1,1024,384]{2,1,0:T(8,128)(2,1)} %param.12) | copy-start | bytes 2359300
  7.2 54.2 %reduce-scatter.3.cloned.1.call-start = ((), (), s32[]{:S(2)}) async-start(), calls=%async_computation.2 | async-start | bytes 122880 | tf_op jit(solution)/shard_map/reduce_scatter | solution.py:66
  21.5 18.2 %copy-start.1 = (bf16[32,1024]{1,0:T(8,128)(2,1)S(1)}, bf16[32,1024]{1,0:T(8,128)(2,1)}, u32[]{:S(2)}) copy-start(bf16[32,1024]{1,0:T(8,128)(2,1)} %param.14) | copy-start | bytes 196612
  21.8 18.2 %copy-start.2 = (bf16[256,384]{1,0:T(8,128)(2,1)S(1)}, bf16[256,384]{1,0:T(8,128)(2,1)}, u32[]{:S(2)}) copy-start(bf16[256,384]{1,0:T(8,128)(2,1)} %param.16) | copy-start | bytes 589828
  38.8 22.6 %copy-start.4 = (f32[1024]{0:T(1024)S(1)}, f32[1024]{0:T(1024)}, u32[]{:S(2)}) copy-start(f32[1024]{0:T(1024)} %param.15) | copy-start | bytes 12292
  38.8 22.5 %copy-start.5 = (f32[384]{0:T(512)S(1)}, f32[384]{0:T(512)}, u32[]{:S(2)}) copy-start(f32[384]{0:T(512)} %param.17) | copy-start | bytes 4612
  39.6 90.3 %reduce-scatter.5.cloned.1.call-start = ((), (), s32[]{:S(2)}) async-start(), calls=%async_computation.3 | async-start | bytes 983040 | tf_op jit(solution)/shard_map/reduce_scatter | solution.py:82
  61.4 13.9 %copy-start.3 = (bf16[32,384]{1,0:T(8,128)(2,1)S(1)}, bf16[32,384]{1,0:T(8,128)(2,1)}, u32[]{:S(2)}) copy-start(bf16[32,384]{1,0:T(8,128)(2,1)} %reduce-scatter.3.cloned.1.call-done) | copy-start | bytes 73732
Sparse Core Ops, SparseCore 0:
  39.7 19.7 reduce-scatter.2
  77.6 22.4 reduce-scatter.4
where the time goes:
time: 140 us
  blocking collectives  110 us (79%)
  between operations  17.2 us (12%)
  other arithmetic  8.24 us (6%)
  matrix products  4.15 us (3%)
    psum x1, blocking collectives, on_device(): loss_value = lax.psum(partial_value, ('member', 'dp')) / (images * classes)  38.7 us
    all_gather x1, blocking collectives, on_device(): lax.all_gather(student_head, 'member', axis=0, tiled=True)  21.4 us
    all_gather x2, blocking collectives, joined(): everything = jax.tree.map(lambda part: lax.all_gather(part, axis), shard)  16.5 us
    psum x1, blocking collectives, on_device(): alpha_sum = lax.psum(jnp.sum(alphas, axis=1), 'dp')  11.8 us
    all_gather x1, blocking collectives, on_device(): lax.all_gather(normed, 'dp', axis=0, tiled=True)  10.8 us
    psum x1, blocking collectives, on_device(): bias_grad = lax.psum(jnp.sum(term_signal, axis=0), 'member') / images  10.5 us
  transfers between devices with their start and end apart: 2, of which 0 were waited for; matrix products, arithmetic and copies ran while one was open for 1% of the time, Pallas kernels for 0%

commit v1 on v0

v1 whole, which is shorter than its diff:
```python
import functools
import math

import jax
import jax.numpy as jnp
from jax import lax
from jax.experimental import pallas as pl
from jax.experimental.pallas import tpu as pltpu
from jax.sharding import PartitionSpec as P

BF16, F32 = jnp.bfloat16, jnp.float32
LANES = 128
PAD = 16
LANCZOS = (
    0.99999999999980993227684700473478,
    676.520368121885098567009190444019,
    -1259.13921672240287047156078755283,
    771.3234287776530788486528258894,
    -176.61502916214059906584551354,
    12.507343278686904814458936853,
    -0.13857109526572011689554707,
    9.984369578019570859563e-6,
    1.50563273514931155834e-7,
)


def partner(index, k, size):
    return index ^ k if size & (size - 1) == 0 else (index + k) % size


def sender(index, k, size):
    return index ^ k if size & (size - 1) == 0 else (index - k + size) % size


def mixed(index, k, size, of):
    if size & (size - 1) == 0:
        return lax.bitwise_xor(index, jnp.int32(k))
    step = k if of is partner else size - k
    return lax.rem(index + jnp.int32(step), jnp.int32(size))


def send(value, axis, k, scale=1, groups=1):
    size = lax.axis_size(axis) // scale
    pairs = [
        (outer * scale + inner, partner(outer, k, size) * scale + inner)
        for outer in range(size)
        for inner in range(scale)
    ]
    return lax.ppermute(value, axis, pairs)


def swap_cores(value, axis):
    return lax.ppermute(value, axis, [(i, i ^ 1) for i in range(lax.axis_size(axis))])


def normed(values, gain_row):
    values = values.astype(F32)
    center = values - jnp.mean(values, axis=-1, keepdims=True)
    spread = jnp.mean(center * center, axis=-1, keepdims=True)
    return (center * lax.rsqrt(spread + 1e-06) * gain_row).astype(BF16)


def split3(value):
    high = value.astype(BF16)
    rest = value - high.astype(F32)
    middle = rest.astype(BF16)
    return high, middle, (rest - middle.astype(F32)).astype(BF16)


def diagonal(rows, lanes):
    return lax.broadcasted_iota(jnp.int32, (rows, lanes), 0) == lax.broadcasted_iota(
        jnp.int32, (rows, lanes), 1
    )


def to_lanes(column, lanes):
    return jnp.sum(
        jnp.where(diagonal(column.shape[0], lanes), column, 0.0), axis=0, keepdims=True
    )


def to_column(row, rows):
    return jnp.sum(jnp.where(diagonal(rows, row.shape[1]), row, 0.0), axis=1, keepdims=True)


def series(x):
    total = jnp.full_like(x, LANCZOS[0])
    slope = jnp.zeros_like(x)
    for k in range(1, 9):
        inverse = 1.0 / (x + float(k))
        term = LANCZOS[k] * inverse
        total = total + term
        slope = slope - term * inverse
    log_t = math.log(7.5) + jnp.log1p(x / 7.5)
    return total, slope, log_t


def log_gamma(x, log_x):
    total, _, log_t = series(x)
    t = x + 7.5
    return (
        (x + 0.5 - t / log_t) * log_t
        + 0.5 * math.log(2.0 * math.pi)
        + jnp.log(total)
        - log_x
    )


def di_gamma(x):
    total, slope, log_t = series(x)
    return log_t + slope / total - 7.0 / (x + 7.5) - 1.0 / x


def student_rows(members, feats_ref, gain_ref, *refs):
    outs, held = refs[:members], refs[members]
    mine = lax.axis_index("member")
    held[...] = normed(feats_ref[...], gain_ref[...])
    width = outs[0].shape[1]
    for k in range(members):
        at = mixed(mine, k, members, partner)
        if width % LANES == 0:
            outs[k][...] = held[:, pl.ds(pl.multiple_of(at * width, LANES), width)]
            continue
        for j in range(members):

            @pl.when(at == j)
            def _(k=k, j=j):
                outs[k][...] = held[:, j * width : (j + 1) * width]


def logits_kernel(members, peers, *refs):
    feats, refs = refs[:peers], refs[peers:]
    gain_ref, head_ref, bias_ref, refs = refs[0], refs[1], refs[2], refs[3:]
    columns, refs = refs[:members], refs[members:]
    student_ref, refs = refs[0], refs[1:]
    payloads, refs = refs[:members], refs[members:]
    columns_ref, gathered, shifted_ref, lse_ref, partial_ref = refs
    mine, place = lax.axis_index("member"), lax.axis_index("dp")
    rows = feats[0].shape[0]
    for k in range(peers):
        chip = mixed(place // 2, k // 2, peers // 2, sender)
        core = lax.bitwise_xor(lax.rem(place, jnp.int32(2)), jnp.int32(k % 2))
        at = chip * 2 + core
        gathered[pl.ds(pl.multiple_of(at * rows, rows), rows), :] = feats[k][...]
    block = columns[0].shape[0]
    for k in range(members):
        at = mixed(mine, k, members, sender)
        columns_ref[pl.ds(pl.multiple_of(at * block, block), block), :] = columns[k][...]
    values = normed(gathered[...], gain_ref[...])
    logits = jnp.dot(values, head_ref[...], preferred_element_type=F32) + bias_ref[...]
    top = jnp.max(logits, axis=1, keepdims=True)
    lse = top + jnp.log(jnp.sum(jnp.exp(logits - top), axis=1, keepdims=True))
    shifted_ref[...] = (logits - lse).astype(BF16)
    lse_ref[...] = jnp.broadcast_to(lse, lse_ref.shape)
    partial_ref[...] = jnp.dot(columns_ref[...], student_ref[...], preferred_element_type=F32)
    classes = logits.shape[1]
    for k in range(members):
        at = pl.ds(pl.multiple_of(mixed(mine, k, members, partner) * block, block), block)
        out = payloads[k]
        out[0:block, :] = shifted_ref[at, :]
        high, middle, _ = split3(partial_ref[at, :])
        out[block : 2 * block, :] = high
        out[2 * block : 3 * block, :] = middle
        lse_row = to_lanes(lse_ref[at, 0:1], classes)
        line = lax.broadcasted_iota(jnp.int32, (PAD, classes), 0)
        high, middle, low = split3(lse_row)
        packed = jnp.where(
            line == 0,
            high.astype(F32),
            jnp.where(line == 1, middle.astype(F32), jnp.where(line == 2, low.astype(F32), 0.0)),
        )
        out[3 * block :, :] = packed.astype(BF16)


def alphas_kernel(members, block, *refs):
    payloads, refs = refs[:members], refs[members:]
    bias_ref, alphas_ref, inner_ref, small_ref = refs
    mine = lax.axis_index("member")
    classes = bias_ref.shape[1]
    target = jnp.zeros((block, classes), F32)
    logits = jnp.zeros((block, classes), F32)
    small_ref[...] = jnp.zeros_like(small_ref)
    lse_total = jnp.zeros((1, LANES), F32)
    for k in range(members):
        got = payloads[k]
        target += got[0:block, :].astype(F32)
        logits += got[block : 2 * block, :].astype(F32) + got[2 * block : 3 * block, :].astype(F32)
        tail = got[3 * block :, 0:LANES].astype(F32)
        lse = tail[0:1, :] + tail[1:2, :] + tail[2:3, :]
        lse_total += lse
        small_ref[pl.ds(mixed(mine, k, members, sender), 1), :] = lse
    target = target * (1.0 / members)
    logits = logits + bias_ref[...]
    alphas = jnp.exp(logits)
    alphas_ref[...] = alphas
    inner_ref[...] = target
    sums = to_lanes(jnp.sum(alphas, axis=1, keepdims=True), LANES)
    parts = to_lanes(
        jnp.sum(log_gamma(alphas, logits) - (alphas - 1.0) * target, axis=1, keepdims=True), LANES
    )
    small_ref[members : members + 1, :] = sums
    small_ref[members + 1 : members + 2, :] = parts - lse_total * (1.0 / members) * (
        sums - float(classes)
    )


def digamma_kernel(alphas_ref, target_ref, inner_ref):
    inner_ref[...] = di_gamma(alphas_ref[...]) - target_ref[...]


def signal_kernel(members, peers, block, *refs):
    smalls, refs = refs[:peers], refs[peers:]
    alphas_ref, inner_ref, signal_ref, held = refs
    place = lax.axis_index("dp")
    for k in range(peers):
        chip = mixed(place // 2, k // 2, peers // 2, sender)
        core = lax.bitwise_xor(lax.rem(place, jnp.int32(2)), jnp.int32(k % 2))
        held[chip * 2 + core] = smalls[k][...]
    everything = held[...]
    classes = alphas_ref.shape[1]
    lse = everything[:, 0:members, :]
    top = jnp.max(lse, axis=0)
    norms = top + jnp.log(jnp.sum(jnp.exp(lse - top[None]), axis=0))
    norm_total = jnp.sum(norms, axis=0, keepdims=True) * (1.0 / members)
    own = jnp.sum(smalls[0][0:members, :], axis=0, keepdims=True) * (1.0 / members)
    alpha_sum = jnp.sum(everything[:, members, :], axis=0, keepdims=True)
    parts = jnp.sum(everything[:, members + 1, :], axis=0, keepdims=True)
    used = lax.broadcasted_iota(jnp.int32, (1, LANES), 1) < block
    alpha_sum = jnp.where(used, alpha_sum, 1.0)
    own_part = (
        parts
        - log_gamma(alpha_sum, jnp.log(alpha_sum))
        + norm_total * (alpha_sum - float(classes * peers))
    )
    loss = jnp.sum(jnp.where(used, own_part, 0.0), axis=1, keepdims=True)
    shift = to_column(di_gamma(alpha_sum) + own - norm_total, block)
    signal_ref[0:block, :] = (alphas_ref[...] * (inner_ref[...] - shift)).astype(BF16)
    line = lax.broadcasted_iota(jnp.int32, (PAD, classes), 0)
    high, middle, low = split3(loss)
    packed = jnp.where(
        line == 0,
        high.astype(F32),
        jnp.where(line == 1, middle.astype(F32), jnp.where(line == 2, low.astype(F32), 0.0)),
    )
    signal_ref[block:, :] = packed.astype(BF16)


def gradient_kernel(members, peers, block, *refs):
    signals, refs = refs[:members], refs[members:]
    columns_ref, loss_ref, grad_ref, bias_ref, held, losses = refs
    mine = lax.axis_index("member")
    images = members * block
    classes = bias_ref.shape[1]
    for k in range(members):
        at = mixed(mine, k, members, sender)
        held[pl.ds(pl.multiple_of(at * block, block), block), :] = signals[k][0:block, :]
        tail = signals[k][block:, 0:LANES].astype(F32)
        losses[pl.ds(at, 1), :] = tail[0:1, :] + tail[1:2, :] + tail[2:3, :]
    signal = held[...]
    grad = lax.dot_general(
        columns_ref[...], signal, (((0,), (0,)), ((), ())), preferred_element_type=F32
    )
    grad_ref[...] = grad * (1.0 / images)
    bias_ref[...] = jnp.sum(signal.astype(F32), axis=0, keepdims=True) * (1.0 / images)
    loss_ref[0, 0] = jnp.sum(losses[:, 0:1]) * (1.0 / (images * classes * peers))


def call(kernel, out_shape, scratch=(), out_specs=None):
    extra = {} if out_specs is None else {"out_specs": out_specs}
    return pl.pallas_call(
        kernel,
        out_shape=out_shape,
        scratch_shapes=list(scratch),
        compiler_params=pltpu.CompilerParams(vmem_limit_bytes=48 * 1024 * 1024),
        **extra,
    )


def on_device(
    teacher_feats,
    teacher_gain,
    teacher_head,
    teacher_bias,
    student_feats,
    student_gain,
    student_head,
    student_bias,
):
    members, peers = lax.axis_size("member"), lax.axis_size("dp")
    shape = jax.ShapeDtypeStruct
    feats = teacher_feats[0]
    rows, depth = feats.shape
    block = student_feats.shape[0]
    images = rows * peers
    width, classes = student_head.shape
    small_rows = -(-(members + 2) // 8) * 8

    chips = [feats] + [send(feats, "dp", k, 2) for k in range(1, peers // 2)]
    pieces = call(
        functools.partial(student_rows, members),
        [shape((block, width), BF16)] * members,
        [pltpu.VMEM((block, depth), BF16)],
    )(student_feats, student_gain[None])
    columns = [pieces[0]] + [send(pieces[k], "member", k) for k in range(1, members)]
    gathered = [part for chip in chips for part in (chip, swap_cores(chip, "dp"))]
    outs = call(
        functools.partial(logits_kernel, members, peers),
        [shape((3 * block + PAD, classes), BF16)] * members + [shape((images, width), BF16)],
        [
            pltpu.VMEM((images, depth), BF16),
            pltpu.VMEM((images, classes), BF16),
            pltpu.VMEM((images, LANES), F32),
            pltpu.VMEM((images, classes), F32),
        ],
    )(*gathered, teacher_gain, teacher_head[0], teacher_bias, *columns, student_head)
    payloads, own_columns = outs[:members], outs[members]
    got = [payloads[0]] + [send(payloads[k], "member", k) for k in range(1, members)]
    alphas, target, small = call(
        functools.partial(alphas_kernel, members, block),
        [shape((block, classes), F32)] * 2 + [shape((small_rows, LANES), F32)],
    )(*got, student_bias[None])
    chips = [small] + [send(small, "dp", k, 2) for k in range(1, peers // 2)]
    inner = call(digamma_kernel, shape((block, classes), F32))(alphas, target)
    smalls = [part for chip in chips for part in (chip, swap_cores(chip, "dp"))]
    signal = call(
        functools.partial(signal_kernel, members, peers, block),
        shape((block + PAD, classes), BF16),
        [pltpu.VMEM((peers, small_rows, LANES), F32)],
    )(*smalls, alphas, inner)
    signals = [signal] + [send(signal, "member", k) for k in range(1, members)]
    loss, head_grad, bias_grad = call(
        functools.partial(gradient_kernel, members, peers, block),
        [shape((1, 1), F32), shape((width, classes), F32), shape((1, classes), F32)],
        [pltpu.VMEM((images, classes), BF16), pltpu.VMEM((members, LANES), F32)],
        [
            pl.BlockSpec(memory_space=pltpu.SMEM),
            pl.BlockSpec(memory_space=pltpu.VMEM),
            pl.BlockSpec(memory_space=pltpu.VMEM),
        ],
    )(*signals, own_columns)
    return (loss[0, 0], head_grad, bias_grad[0])


def solution(mesh):
    placed = (
        P("member", "dp", None),
        P("member", None),
        P("member", None, "dp"),
        P("member", "dp"),
        P("member", None),
        P(),
        P("member", "dp"),
        P("dp"),
    )
    return jax.shard_map(
        on_device,
        mesh=mesh,
        in_specs=placed,
        out_specs=(P(), P("member", "dp"), P("dp")),
        check_vma=False,
    )
```

time: 140 us -> 53.3 us (0.38)
  blocking collectives: 110 us -> 0 us
  starting transfers between devices: 0.08 us -> 27 us
  waiting for transfers between devices: 0.04 us -> 18.5 us
  between operations: 17.2 us -> 0.77 us
  other arithmetic: 8.24 us -> 0.6 us
  matrix products: 4.15 us -> 0 us
  local copies, waits for them, and re-layouts: 0.04 us -> 3.6 us
  Pallas kernels: 0 us -> 2.56 us
    psum x3 -> x0, blocking collectives: 61.1 us -> none  [the longest x1 38.7 us: on_device(): loss_value = lax.psum(partial_value, ('member', 'dp')) / (images * classes)]
    all_gather x4 -> x0, blocking collectives: 48.6 us -> none  [the longest x1 21.4 us: on_device(): lax.all_gather(student_head, 'member', axis=0, tiled=True)]
    ppermute x0 -> x23, starting transfers between devices: none -> 27 us  [the longest x15 26.1 us: send(): return lax.ppermute(value, axis, pairs)]
    ppermute x0 -> x23, waiting for transfers between devices: none -> 18.5 us  [the longest x15 17.4 us: send(): return lax.ppermute(value, axis, pairs)]
    dot_general x3 -> x0, matrix products: 4.15 us -> none  [the longest x1 1.99 us: row_folder(): return jnp.dot(source, portion, preferred_element_type=jnp.float32)]
    unnamed x12 -> x16, local copies, waits for them, and re-layouts: 0.04 us -> 3.6 us
    reduce_sum x7 -> x0, other arithmetic: 3.41 us -> none  [the longest x2 1.14 us: norm_rows(): spread = jnp.mean(center * center, axis=-1, keepdims=True)]
    pallas_call x0 -> x6, Pallas kernels: none -> 2.56 us  [the longest x1 1 us: on_device(): call(functools.partial(gradient_kernel, members, peers, block), [shape((1...]
  transfers between devices with their start and end apart: 2 -> 23, of which waited for: 0 -> 12; matrix products, arithmetic and copies ran while one was open for 1% -> 0% of each run, Pallas kernels for 0% -> 1%
where the time goes in v1:
time: 53.3 us; the launch traced here: 53 us
  starting transfers between devices  27 us (51%)
  waiting for transfers between devices  18.5 us (35%)
  local copies, waits for them, and re-layouts  3.6 us (7%)
  Pallas kernels  2.56 us (5%)
  between operations  0.77 us (1%)
  other arithmetic  0.6 us (1%)
    ppermute x15, starting transfers between devices, send(): return lax.ppermute(value, axis, pairs)  26.1 us
    ppermute x15, waiting for transfers between devices, send(): return lax.ppermute(value, axis, pairs)  17.4 us
    unnamed x16, local copies, waits for them, and re-layouts  3.6 us
  transfers between devices with their start and end apart: 23, of which 12 were waited for; matrix products, arithmetic and copies ran while one was open for 0% of the time, Pallas kernels for 1%

profile of v1, /device:TPU:0, one launch (start us, length us, event | category | flops | bytes accessed | tf_op | source)
XLA Modules:
  0.0 53.0 jit_solution(466920555692504834)
XLA Ops:
  0.6 3.0 %collective-permute-start.1 = (bf16[16,1024]{1,0:T(8,128)(2,1)}, bf16[16,1024]{1,0:T(8,128)(2,1)S(1)}, u32[]{:S(2)}, u32[]{:S(2)}) collective-permute-start(bf16[16,1024]{1,0:T(8,128)(2,1)} %bitcast.5), channel_id=1, source_target_pairs={{0,2},{1,3},{2,0},{3,1},{4,6},{5,7},{6,4},{7,5},{8,10},{9,11},{10,... | collective-permute-start | bytes 98312 | tf_op jit(solution)/shard_map/ppermute | solution.py:49
  3.6 1.5 %collective-permute-start.3 = (bf16[16,1024]{1,0:T(8,128)(2,1)}, bf16[16,1024]{1,0:T(8,128)(2,1)S(1)}, u32[]{:S(2)}, u32[]{:S(2)}) collective-permute-start(bf16[16,1024]{1,0:T(8,128)(2,1)} %bitcast.6), channel_id=1, source_target_pairs={{0,4},{1,5},{2,6},{3,7},{4,0},{5,1},{6,2},{7,3},{8,12},{9,13},{10,... | collective-permute-start | bytes 98312 | tf_op jit(solution)/shard_map/ppermute | solution.py:49
  5.2 0.0 collective-permute-start.5
  5.2 0.8 %copy-done.2 = bf16[32,1024]{1,0:T(8,128)(2,1)S(1)} copy-done((bf16[32,1024]{1,0:T(8,128)(2,1)S(1)}, bf16[32,1024]{1,0:T(8,128)(2,1)}, u32[]{:S(2)}) %copy-start.2) | copy-done | bytes 65560
  6.0 0.7 %copy-done.5 = f32[1024]{0:T(1024)S(1)} copy-done((f32[1024]{0:T(1024)S(1)}, f32[1024]{0:T(1024)}, u32[]{:S(2)}) %copy-start.5) | copy-done | bytes 4120
  6.7 0.2 shard_map.103
  6.9 0.0 copy-start.4
  6.9 2.1 %collective-permute-start.7 = (bf16[32,256]{1,0:T(8,128)(2,1)S(1)}, bf16[32,256]{1,0:T(8,128)(2,1)S(1)}, u32[]{:S(2)}, u32[]{:S(2)}) collective-permute-start(bf16[32,256]{1,0:T(8,128)(2,1)S(1)} %get-tuple-element.19), channel_id=1, source_target_pairs={{0,8},{8,0},{16,24},{24,16},{1,9},{9,1},{17,25},{25,17},{2,10},{10... | collective-permute-start | bytes 49160 | tf_op jit(solution)/shard_map/ppermute | solution.py:49
  9.0 0.0 collective-permute-start
  9.0 1.7 %collective-permute-done.7.refs_12_ = bf16[32,256]{1,0:T(8,128)(2,1)S(1)} collective-permute-done((bf16[32,256]{1,0:T(8,128)(2,1)S(1)}, bf16[32,256]{1,0:T(8,128)(2,1)S(1)}, u32[]{:S(2)}, u32[]{:S(2)}) %collective-permute-start.7) | collective-permute-done | bytes 16416 | tf_op jit(solution)/shard_map/ppermute | solution.py:49
  10.7 3.0 %collective-permute-start.8 = (bf16[32,256]{1,0:T(8,128)(2,1)S(1)}, bf16[32,256]{1,0:T(8,128)(2,1)S(1)}, u32[]{:S(2)}, u32[]{:S(2)}) collective-permute-start(bf16[32,256]{1,0:T(8,128)(2,1)S(1)} %get-tuple-element.20), channel_id=1, source_target_pairs={{0,16},{8,24},{16,0},{24,8},{1,17},{9,25},{17,1},{25,9},{2,18},{10... | collective-permute-start | bytes 49160 | tf_op jit(solution)/shard_map/ppermute | solution.py:49
  13.8 0.0 collective-permute-done.1.refs_2_
  13.8 0.0 collective-permute-start.2
  13.8 0.0 collective-permute-done.3.refs_4_
  13.8 0.5 collective-permute-start.4
  14.3 0.0 collective-permute-done.5.refs_6_
  14.3 0.1 collective-permute-start.6
  14.4 1.1 %collective-permute-done.8.refs_13_ = bf16[32,256]{1,0:T(8,128)(2,1)S(1)} collective-permute-done((bf16[32,256]{1,0:T(8,128)(2,1)S(1)}, bf16[32,256]{1,0:T(8,128)(2,1)S(1)}, u32[]{:S(2)}, u32[]{:S(2)}) %collective-permute-start.8) | collective-permute-done | bytes 16416 | tf_op jit(solution)/shard_map/ppermute | solution.py:49
  15.5 4.0 %collective-permute-start.9 = (bf16[32,256]{1,0:T(8,128)(2,1)S(1)}, bf16[32,256]{1,0:T(8,128)(2,1)S(1)}, u32[]{:S(2)}, u32[]{:S(2)}) collective-permute-start(bf16[32,256]{1,0:T(8,128)(2,1)S(1)} %get-tuple-element.21), channel_id=1, source_target_pairs={{0,24},{8,16},{16,8},{24,0},{1,25},{9,17},{17,9},{25,1},{2,26},{10... | collective-permute-start | bytes 49160 | tf_op jit(solution)/shard_map/ppermute | solution.py:49
  19.5 1.7 %collective-permute-done.9.refs_14_ = bf16[32,256]{1,0:T(8,128)(2,1)S(1)} collective-permute-done((bf16[32,256]{1,0:T(8,128)(2,1)S(1)}, bf16[32,256]{1,0:T(8,128)(2,1)S(1)}, u32[]{:S(2)}, u32[]{:S(2)}) %collective-permute-start.9) | collective-permute-done | bytes 16416 | tf_op jit(solution)/shard_map/ppermute | solution.py:49
  21.3 0.0 copy-start
  21.3 1.1 %copy-done = bf16[1,1024,384]{2,1,0:T(8,128)(2,1)S(1)} copy-done((bf16[1,1024,384]{2,1,0:T(8,128)(2,1)S(1)}, bf16[1,1024,384]{2,1,0:T(8,128)(2,1)}, u32[]{:S(2)}) %copy-start) | copy-done | bytes 786456
  22.4 0.9 %copy-done.1 = bf16[256,384]{1,0:T(8,128)(2,1)S(1)} copy-done((bf16[256,384]{1,0:T(8,128)(2,1)S(1)}, bf16[256,384]{1,0:T(8,128)(2,1)}, u32[]{:S(2)}) %copy-start.1) | copy-done | bytes 196632
  23.3 0.9 %shard_map.104 = (bf16[112,384]{1,0:T(8,128)(2,1)S(1)}, bf16[112,384]{1,0:T(8,128)(2,1)S(1)}, bf16[112,384]{1,0:T(8,128)(2,1)S(1)}, bf16[112,384]{1,0:T(8,128)(2,1)S(1)}, bf16[128,256]{1,0:T(8,128)(2,1)S(1)}) custom-call(bf16[16,1024]{1,0:T(8,128)(2,1)S(1)} %bitcast.9, bf16[16,1024]{1,0:T(8,128)(2,1)S(1)} %collective-permute-done.refs_1_, ...), custom_call_target="tpu_custom_call" | custom-call | tf_op jit(solution)/shard_map/pallas_call | solution.py:306
  24.2 0.0 copy-start.7
  24.2 0.1 collective-permute-start.10
  24.3 4.4 %collective-permute-start.11 = (bf16[112,384]{1,0:T(8,128)(2,1)S(1)}, bf16[112,384]{1,0:T(8,128)(2,1)S(1)}, u32[]{:S(2)}, u32[]{:S(2)}) collective-permute-start(bf16[112,384]{1,0:T(8,128)(2,1)S(1)} %get-tuple-element.24), channel_id=1, source_target_pairs={{0,16},{8,24},{16,0},{24,8},{1,17},{9,25},{17,1},{25,9},{2,18},{10... | collective-permute-start | bytes 258056 | tf_op jit(solution)/shard_map/ppermute | solution.py:49
  28.7 1.0 %collective-permute-done.10.refs_1_ = bf16[112,384]{1,0:T(8,128)(2,1)S(1)} collective-permute-done((bf16[112,384]{1,0:T(8,128)(2,1)S(1)}, bf16[112,384]{1,0:T(8,128)(2,1)S(1)}, u32[]{:S(2)}, u32[]{:S(2)}) %collective-permute-start.10) | collective-permute-done | bytes 86048 | tf_op jit(solution)/shard_map/ppermute | solution.py:49
  29.7 2.4 %collective-permute-done.11.refs_2_ = bf16[112,384]{1,0:T(8,128)(2,1)S(1)} collective-permute-done((bf16[112,384]{1,0:T(8,128)(2,1)S(1)}, bf16[112,384]{1,0:T(8,128)(2,1)S(1)}, u32[]{:S(2)}, u32[]{:S(2)}) %collective-permute-start.11) | collective-permute-done | bytes 86048 | tf_op jit(solution)/shard_map/ppermute | solution.py:49
  32.0 2.9 %collective-permute-done.12.refs_3_ = bf16[112,384]{1,0:T(8,128)(2,1)S(1)} collective-permute-done((bf16[112,384]{1,0:T(8,128)(2,1)S(1)}, bf16[112,384]{1,0:T(8,128)(2,1)S(1)}, u32[]{:S(2)}, u32[]{:S(2)}) %collective-permute-start.12) | collective-permute-done | bytes 86048 | tf_op jit(solution)/shard_map/ppermute | solution.py:49
  34.9 0.2 shard_map.105
  35.2 1.5 %collective-permute-start.14 = (f32[8,128]{1,0:T(8,128)S(1)}, f32[8,128]{1,0:T(8,128)S(1)}, u32[]{:S(2)}, u32[]{:S(2)}) collective-permute-start(f32[8,128]{1,0:T(8,128)S(1)} %get-tuple-element.26.refs_0_), channel_id=1, source_target_pairs={{0,2},{1,3},{2,0},{3,1},{4,6},{5,7},{6,4},{7,5},{8,10},{9,11},{10,... | collective-permute-start | bytes 12296 | tf_op jit(solution)/shard_map/ppermute | solution.py:49
  36.7 1.5 %collective-permute-start.16 = (f32[8,128]{1,0:T(8,128)S(1)}, f32[8,128]{1,0:T(8,128)S(1)}, u32[]{:S(2)}, u32[]{:S(2)}) collective-permute-start(f32[8,128]{1,0:T(8,128)S(1)} %get-tuple-element.26.refs_0_), channel_id=1, source_target_pairs={{0,4},{1,5},{2,6},{3,7},{4,0},{5,1},{6,2},{7,3},{8,12},{9,13},{10,... | collective-permute-start | bytes 12296 | tf_op jit(solution)/shard_map/ppermute | solution.py:49
  38.2 0.5 collective-permute-start.18
  38.7 0.1 collective-permute-done.14.refs_2_
  38.8 0.4 collective-permute-start.15
  39.2 1.1 %collective-permute-done.16.refs_4_ = f32[8,128]{1,0:T(8,128)S(1)} collective-permute-done((f32[8,128]{1,0:T(8,128)S(1)}, f32[8,128]{1,0:T(8,128)S(1)}, u32[]{:S(2)}, u32[]{:S(2)}) %collective-permute-start.16) | collective-permute-done | bytes 4128 | tf_op jit(solution)/shard_map/ppermute | solution.py:49
  40.3 2.4 %collective-permute-done.18.refs_6_ = f32[8,128]{1,0:T(8,128)S(1)} collective-permute-done((f32[8,128]{1,0:T(8,128)S(1)}, f32[8,128]{1,0:T(8,128)S(1)}, u32[]{:S(2)}, u32[]{:S(2)}) %collective-permute-start.18) | collective-permute-done | bytes 4128 | tf_op jit(solution)/shard_map/ppermute | solution.py:49
  42.7 0.1 shard_map.106.refs_9_
  42.8 1.0 %collective-permute-done.19.refs_7_ = f32[8,128]{1,0:T(8,128)S(1)} collective-permute-done((f32[8,128]{1,0:T(8,128)S(1)}, f32[8,128]{1,0:T(8,128)S(1)}, u32[]{:S(2)}, u32[]{:S(2)}) %collective-permute-start.19) | collective-permute-done | bytes 4128 | tf_op jit(solution)/shard_map/ppermute | solution.py:53
  43.9 0.1 shard_map.107.refs_0_
  44.0 0.1 collective-permute-start.20
  44.1 1.6 %collective-permute-start.21 = (bf16[48,384]{1,0:T(8,128)(2,1)S(1)}, bf16[48,384]{1,0:T(8,128)(2,1)S(1)}, u32[]{:S(2)}, u32[]{:S(2)}) collective-permute-start(bf16[48,384]{1,0:T(8,128)(2,1)S(1)} %shard_map.107.refs_0_), channel_id=1, source_target_pairs={{0,16},{8,24},{16,0},{24,8},{1,17},{9,25},{17,1},{25,9},{2,18},{10... | collective-permute-start | bytes 110600 | tf_op jit(solution)/shard_map/ppermute | solution.py:49
  45.7 2.8 %collective-permute-start.22 = (bf16[48,384]{1,0:T(8,128)(2,1)S(1)}, bf16[48,384]{1,0:T(8,128)(2,1)S(1)}, u32[]{:S(2)}, u32[]{:S(2)}) collective-permute-start(bf16[48,384]{1,0:T(8,128)(2,1)S(1)} %shard_map.107.refs_0_), channel_id=1, source_target_pairs={{0,24},{8,16},{16,8},{24,0},{1,25},{9,17},{17,9},{25,1},{2,26},{10... | collective-permute-start | bytes 110600 | tf_op jit(solution)/shard_map/ppermute | solution.py:49
  48.5 0.6 %collective-permute-done.21.refs_2_ = bf16[48,384]{1,0:T(8,128)(2,1)S(1)} collective-permute-done((bf16[48,384]{1,0:T(8,128)(2,1)S(1)}, bf16[48,384]{1,0:T(8,128)(2,1)S(1)}, u32[]{:S(2)}, u32[]{:S(2)}) %collective-permute-start.21) | collective-permute-done | bytes 36896 | tf_op jit(solution)/shard_map/ppermute | solution.py:49
  49.0 2.4 %collective-permute-done.22.refs_3_ = bf16[48,384]{1,0:T(8,128)(2,1)S(1)} collective-permute-done((bf16[48,384]{1,0:T(8,128)(2,1)S(1)}, bf16[48,384]{1,0:T(8,128)(2,1)S(1)}, u32[]{:S(2)}, u32[]{:S(2)}) %collective-permute-start.22) | collective-permute-done | bytes 36896 | tf_op jit(solution)/shard_map/ppermute | solution.py:49
  51.4 1.0 %shard_map.108 = (f32[1,1]{1,0:T(1,128)}, f32[256,384]{1,0:T(8,128)}, f32[1,384]{1,0:T(1,128)S(1)}) custom-call(bf16[48,384]{1,0:T(8,128)(2,1)S(1)} %shard_map.107.refs_0_, bf16[48,384]{1,0:T(8,128)(2,1)S(1)} %collective-permute-done.20.refs_1_, bf16[48,384]{1,0:T(8,128)(2,1)S(1)} %collective-permute-done.21.refs_2_, ...), custom_call_target="tpu_custom_call" | custom-call | tf_op jit(solution)/shard_map/pallas_call | solution.py:331
  52.4 0.6 %reduce = f32[384]{0:T(512)} reduce(f32[1,384]{1,0:T(1,128)S(1)} %get-tuple-element.32, f32[]{:T(128)} %constant.4), dimensions={0}, to_apply=%get-tuple-element.32.reduce_sub_computation | reduce | bytes 3076 | tf_op jit(solution)/shard_map/pallas_call | solution.py:331
  (22 shorter events, 0.1 us)
Async XLA Ops:
  0.6 13.2 %collective-permute-start.1 = (bf16[16,1024]{1,0:T(8,128)(2,1)}, bf16[16,1024]{1,0:T(8,128)(2,1)S(1)}, u32[]{:S(2)}, u32[]{:S(2)}) collective-permute-start(bf16[16,1024]{1,0:T(8,128)(2,1)} %bitcast.5), channel_id=1, source_target_pairs={{0,2},{1,3},{2,0},{3,1},{4,6},{5,7},{6,4},{7,5},{8,10},{9,11},{10,... | collective-permute-start | bytes 98312 | tf_op jit(solution)/shard_map/ppermute | solution.py:49
  3.6 10.2 %collective-permute-start.3 = (bf16[16,1024]{1,0:T(8,128)(2,1)}, bf16[16,1024]{1,0:T(8,128)(2,1)S(1)}, u32[]{:S(2)}, u32[]{:S(2)}) collective-permute-start(bf16[16,1024]{1,0:T(8,128)(2,1)} %bitcast.6), channel_id=1, source_target_pairs={{0,4},{1,5},{2,6},{3,7},{4,0},{5,1},{6,2},{7,3},{8,12},{9,13},{10,... | collective-permute-start | bytes 98312 | tf_op jit(solution)/shard_map/ppermute | solution.py:49
  5.2 9.1 %collective-permute-start.5 = (bf16[16,1024]{1,0:T(8,128)(2,1)}, bf16[16,1024]{1,0:T(8,128)(2,1)S(1)}, u32[]{:S(2)}, u32[]{:S(2)}) collective-permute-start(bf16[16,1024]{1,0:T(8,128)(2,1)} %bitcast.7), channel_id=1, source_target_pairs={{0,6},{1,7},{2,4},{3,5},{4,2},{5,3},{6,0},{7,1},{8,14},{9,15},{10,... | collective-permute-start | bytes 98312 | tf_op jit(solution)/shard_map/ppermute | solution.py:49
  5.2 0.8 %copy-start.2 = (bf16[32,1024]{1,0:T(8,128)(2,1)S(1)}, bf16[32,1024]{1,0:T(8,128)(2,1)}, u32[]{:S(2)}) copy-start(bf16[32,1024]{1,0:T(8,128)(2,1)} %feats_ref.1) | copy-start | bytes 196612
  6.0 0.7 %copy-start.5 = (f32[1024]{0:T(1024)S(1)}, f32[1024]{0:T(1024)}, u32[]{:S(2)}) copy-start(f32[1024]{0:T(1024)} %param.13) | copy-start | bytes 12292
  6.7 2.3 %copy-start.3 = (bf16[1,16,1024]{2,1,0:T(8,128)(2,1)S(1)}, bf16[1,16,1024]{2,1,0:T(8,128)(2,1)}, u32[]{:S(2)}) copy-start(bf16[1,16,1024]{2,1,0:T(8,128)(2,1)} %param.8) | copy-start | bytes 98308
  6.9 14.3 %copy-start.4 = (f32[1,1024]{1,0:T(1,128)S(1)}, f32[1,1024]{1,0:T(1,128)}, u32[]{:S(2)}) copy-start(f32[1,1024]{1,0:T(1,128)} %refs_8_.1) | copy-start | bytes 12292
  6.9 3.8 %collective-permute-start.7 = (bf16[32,256]{1,0:T(8,128)(2,1)S(1)}, bf16[32,256]{1,0:T(8,128)(2,1)S(1)}, u32[]{:S(2)}, u32[]{:S(2)}) collective-permute-start(bf16[32,256]{1,0:T(8,128)(2,1)S(1)} %get-tuple-element.19), channel_id=1, source_target_pairs={{0,8},{8,0},{16,24},{24,16},{1,9},{9,1},{17,25},{25,17},{2,10},{10... | collective-permute-start | bytes 49160 | tf_op jit(solution)/shard_map/ppermute | solution.py:49
  9.0 12.2 %collective-permute-start = (bf16[16,1024]{1,0:T(8,128)(2,1)S(1)}, bf16[16,1024]{1,0:T(8,128)(2,1)S(1)}, u32[]{:S(2)}, u32[]{:S(2)}) collective-permute-start(bf16[16,1024]{1,0:T(8,128)(2,1)S(1)} %bitcast.8), channel_id=1, source_target_pairs={{0,1},{1,0},{2,3},{3,2},{4,5},{5,4},{6,7},{7,6},{8,9},{9,8},{10,11... | collective-permute-start | bytes 98312 | tf_op jit(solution)/shard_map/ppermute | solution.py:53
  10.7 4.7 %collective-permute-start.8 = (bf16[32,256]{1,0:T(8,128)(2,1)S(1)}, bf16[32,256]{1,0:T(8,128)(2,1)S(1)}, u32[]{:S(2)}, u32[]{:S(2)}) collective-permute-start(bf16[32,256]{1,0:T(8,128)(2,1)S(1)} %get-tuple-element.20), channel_id=1, source_target_pairs={{0,16},{8,24},{16,0},{24,8},{1,17},{9,25},{17,1},{25,9},{2,18},{10... | collective-permute-start | bytes 49160 | tf_op jit(solution)/shard_map/ppermute | solution.py:49
  13.8 7.4 %collective-permute-start.2 = (bf16[16,1024]{1,0:T(8,128)(2,1)S(1)}, bf16[16,1024]{1,0:T(8,128)(2,1)S(1)}, u32[]{:S(2)}, u32[]{:S(2)}) collective-permute-start(bf16[16,1024]{1,0:T(8,128)(2,1)S(1)} %collective-permute-done.1.refs_2_), channel_id=1, source_target_pairs={{0,1},{1,0},{2,3},{3,2},{4,5},{5,4},{6,7},{7,6},{8,9},{9,8},{10,11... | collective-permute-start | bytes 98312 | tf_op jit(solution)/shard_map/ppermute | solution.py:53
  13.8 7.4 %collective-permute-start.4 = (bf16[16,1024]{1,0:T(8,128)(2,1)S(1)}, bf16[16,1024]{1,0:T(8,128)(2,1)S(1)}, u32[]{:S(2)}, u32[]{:S(2)}) collective-permute-start(bf16[16,1024]{1,0:T(8,128)(2,1)S(1)} %collective-permute-done.3.refs_4_), channel_id=1, source_target_pairs={{0,1},{1,0},{2,3},{3,2},{4,5},{5,4},{6,7},{7,6},{8,9},{9,8},{10,11... | collective-permute-start | bytes 98312 | tf_op jit(solution)/shard_map/ppermute | solution.py:53
  14.3 6.9 %collective-permute-start.6 = (bf16[16,1024]{1,0:T(8,128)(2,1)S(1)}, bf16[16,1024]{1,0:T(8,128)(2,1)S(1)}, u32[]{:S(2)}, u32[]{:S(2)}) collective-permute-start(bf16[16,1024]{1,0:T(8,128)(2,1)S(1)} %collective-permute-done.5.refs_6_), channel_id=1, source_target_pairs={{0,1},{1,0},{2,3},{3,2},{4,5},{5,4},{6,7},{7,6},{8,9},{9,8},{10,11... | collective-permute-start | bytes 98312 | tf_op jit(solution)/shard_map/ppermute | solution.py:53
  15.5 5.8 %copy-start.6 = (f32[1,384]{1,0:T(1,128)S(1)}, f32[1,384]{1,0:T(1,128)}, u32[]{:S(2)}) copy-start(f32[1,384]{1,0:T(1,128)} %refs_10_.1) | copy-start | bytes 4612
  15.5 5.7 %collective-permute-start.9 = (bf16[32,256]{1,0:T(8,128)(2,1)S(1)}, bf16[32,256]{1,0:T(8,128)(2,1)S(1)}, u32[]{:S(2)}, u32[]{:S(2)}) collective-permute-start(bf16[32,256]{1,0:T(8,128)(2,1)S(1)} %get-tuple-element.21), channel_id=1, source_target_pairs={{0,24},{8,16},{16,8},{24,0},{1,25},{9,17},{17,9},{25,1},{2,26},{10... | collective-permute-start | bytes 49160 | tf_op jit(solution)/shard_map/ppermute | solution.py:49
  21.3 1.1 %copy-start = (bf16[1,1024,384]{2,1,0:T(8,128)(2,1)S(1)}, bf16[1,1024,384]{2,1,0:T(8,128)(2,1)}, u32[]{:S(2)}) copy-start(bf16[1,1024,384]{2,1,0:T(8,128)(2,1)} %param.10) | copy-start | bytes 2359300
  22.4 0.9 %copy-start.1 = (bf16[256,384]{1,0:T(8,128)(2,1)S(1)}, bf16[256,384]{1,0:T(8,128)(2,1)}, u32[]{:S(2)}) copy-start(bf16[256,384]{1,0:T(8,128)(2,1)} %refs_15_.1) | copy-start | bytes 589828
  24.2 4.5 %copy-start.7 = (f32[384]{0:T(512)S(1)}, f32[384]{0:T(512)}, u32[]{:S(2)}) copy-start(f32[384]{0:T(512)} %param.15) | copy-start | bytes 4612
  24.2 5.5 %collective-permute-start.10 = (bf16[112,384]{1,0:T(8,128)(2,1)S(1)}, bf16[112,384]{1,0:T(8,128)(2,1)S(1)}, u32[]{:S(2)}, u32[]{:S(2)}) collective-permute-start(bf16[112,384]{1,0:T(8,128)(2,1)S(1)} %get-tuple-element.23), channel_id=1, source_target_pairs={{0,8},{8,0},{16,24},{24,16},{1,9},{9,1},{17,25},{25,17},{2,10},{10... | collective-permute-start | bytes 258056 | tf_op jit(solution)/shard_map/ppermute | solution.py:49
  24.3 7.8 %collective-permute-start.11 = (bf16[112,384]{1,0:T(8,128)(2,1)S(1)}, bf16[112,384]{1,0:T(8,128)(2,1)S(1)}, u32[]{:S(2)}, u32[]{:S(2)}) collective-permute-start(bf16[112,384]{1,0:T(8,128)(2,1)S(1)} %get-tuple-element.24), channel_id=1, source_target_pairs={{0,16},{8,24},{16,0},{24,8},{1,17},{9,25},{17,1},{25,9},{2,18},{10... | collective-permute-start | bytes 258056 | tf_op jit(solution)/shard_map/ppermute | solution.py:49
  28.6 6.3 %collective-permute-start.12 = (bf16[112,384]{1,0:T(8,128)(2,1)S(1)}, bf16[112,384]{1,0:T(8,128)(2,1)S(1)}, u32[]{:S(2)}, u32[]{:S(2)}) collective-permute-start(bf16[112,384]{1,0:T(8,128)(2,1)S(1)} %get-tuple-element.25), channel_id=1, source_target_pairs={{0,24},{8,16},{16,8},{24,0},{1,25},{9,17},{17,9},{25,1},{2,26},{10... | collective-permute-start | bytes 258056 | tf_op jit(solution)/shard_map/ppermute | solution.py:49
  35.2 3.6 %collective-permute-start.14 = (f32[8,128]{1,0:T(8,128)S(1)}, f32[8,128]{1,0:T(8,128)S(1)}, u32[]{:S(2)}, u32[]{:S(2)}) collective-permute-start(f32[8,128]{1,0:T(8,128)S(1)} %get-tuple-element.26.refs_0_), channel_id=1, source_target_pairs={{0,2},{1,3},{2,0},{3,1},{4,6},{5,7},{6,4},{7,5},{8,10},{9,11},{10,... | collective-permute-start | bytes 12296 | tf_op jit(solution)/shard_map/ppermute | solution.py:49
  36.7 3.6 %collective-permute-start.16 = (f32[8,128]{1,0:T(8,128)S(1)}, f32[8,128]{1,0:T(8,128)S(1)}, u32[]{:S(2)}, u32[]{:S(2)}) collective-permute-start(f32[8,128]{1,0:T(8,128)S(1)} %get-tuple-element.26.refs_0_), channel_id=1, source_target_pairs={{0,4},{1,5},{2,6},{3,7},{4,0},{5,1},{6,2},{7,3},{8,12},{9,13},{10,... | collective-permute-start | bytes 12296 | tf_op jit(solution)/shard_map/ppermute | solution.py:49
  38.2 4.5 %collective-permute-start.18 = (f32[8,128]{1,0:T(8,128)S(1)}, f32[8,128]{1,0:T(8,128)S(1)}, u32[]{:S(2)}, u32[]{:S(2)}) collective-permute-start(f32[8,128]{1,0:T(8,128)S(1)} %get-tuple-element.26.refs_0_), channel_id=1, source_target_pairs={{0,6},{1,7},{2,4},{3,5},{4,2},{5,3},{6,0},{7,1},{8,14},{9,15},{10,... | collective-permute-start | bytes 12296 | tf_op jit(solution)/shard_map/ppermute | solution.py:49
  38.7 4.2 %collective-permute-start.13 = (f32[8,128]{1,0:T(8,128)S(1)}, f32[8,128]{1,0:T(8,128)S(1)}, u32[]{:S(2)}, u32[]{:S(2)}) collective-permute-start(f32[8,128]{1,0:T(8,128)S(1)} %get-tuple-element.26.refs_0_), channel_id=1, source_target_pairs={{0,1},{1,0},{2,3},{3,2},{4,5},{5,4},{6,7},{7,6},{8,9},{9,8},{10,11... | collective-permute-start | bytes 12296 | tf_op jit(solution)/shard_map/ppermute | solution.py:53
  38.8 4.1 %collective-permute-start.15 = (f32[8,128]{1,0:T(8,128)S(1)}, f32[8,128]{1,0:T(8,128)S(1)}, u32[]{:S(2)}, u32[]{:S(2)}) collective-permute-start(f32[8,128]{1,0:T(8,128)S(1)} %collective-permute-done.14.refs_2_), channel_id=1, source_target_pairs={{0,1},{1,0},{2,3},{3,2},{4,5},{5,4},{6,7},{7,6},{8,9},{9,8},{10,11... | collective-permute-start | bytes 12296 | tf_op jit(solution)/shard_map/ppermute | solution.py:53
  40.3 2.6 %collective-permute-start.17 = (f32[8,128]{1,0:T(8,128)S(1)}, f32[8,128]{1,0:T(8,128)S(1)}, u32[]{:S(2)}, u32[]{:S(2)}) collective-permute-start(f32[8,128]{1,0:T(8,128)S(1)} %collective-permute-done.16.refs_4_), channel_id=1, source_target_pairs={{0,1},{1,0},{2,3},{3,2},{4,5},{5,4},{6,7},{7,6},{8,9},{9,8},{10,11... | collective-permute-start | bytes 12296 | tf_op jit(solution)/shard_map/ppermute | solution.py:53
  42.7 1.2 %collective-permute-start.19 = (f32[8,128]{1,0:T(8,128)S(1)}, f32[8,128]{1,0:T(8,128)S(1)}, u32[]{:S(2)}, u32[]{:S(2)}) collective-permute-start(f32[8,128]{1,0:T(8,128)S(1)} %collective-permute-done.18.refs_6_), channel_id=1, source_target_pairs={{0,1},{1,0},{2,3},{3,2},{4,5},{5,4},{6,7},{7,6},{8,9},{9,8},{10,11... | collective-permute-start | bytes 12296 | tf_op jit(solution)/shard_map/ppermute | solution.py:53
  44.0 4.5 %collective-permute-start.20 = (bf16[48,384]{1,0:T(8,128)(2,1)S(1)}, bf16[48,384]{1,0:T(8,128)(2,1)S(1)}, u32[]{:S(2)}, u32[]{:S(2)}) collective-permute-start(bf16[48,384]{1,0:T(8,128)(2,1)S(1)} %shard_map.107.refs_0_), channel_id=1, source_target_pairs={{0,8},{8,0},{16,24},{24,16},{1,9},{9,1},{17,25},{25,17},{2,10},{10... | collective-permute-start | bytes 110600 | tf_op jit(solution)/shard_map/ppermute | solution.py:49
  44.1 4.9 %collective-permute-start.21 = (bf16[48,384]{1,0:T(8,128)(2,1)S(1)}, bf16[48,384]{1,0:T(8,128)(2,1)S(1)}, u32[]{:S(2)}, u32[]{:S(2)}) collective-permute-start(bf16[48,384]{1,0:T(8,128)(2,1)S(1)} %shard_map.107.refs_0_), channel_id=1, source_target_pairs={{0,16},{8,24},{16,0},{24,8},{1,17},{9,25},{17,1},{25,9},{2,18},{10... | collective-permute-start | bytes 110600 | tf_op jit(solution)/shard_map/ppermute | solution.py:49
  45.7 5.8 %collective-permute-start.22 = (bf16[48,384]{1,0:T(8,128)(2,1)S(1)}, bf16[48,384]{1,0:T(8,128)(2,1)S(1)}, u32[]{:S(2)}, u32[]{:S(2)}) collective-permute-start(bf16[48,384]{1,0:T(8,128)(2,1)S(1)} %shard_map.107.refs_0_), channel_id=1, source_target_pairs={{0,24},{8,16},{16,8},{24,0},{1,25},{9,17},{17,9},{25,1},{2,26},{10... | collective-permute-start | bytes 110600 | tf_op jit(solution)/shard_map/ppermute | solution.py:49

commit v2 on v1

--- a/solution.py
+++ b/solution.py
@@ -111,30 +111,37 @@
     return log_t + slope / total - 7.0 / (x + 7.5) - 1.0 / x
 
 
-def student_rows(members, feats_ref, gain_ref, *refs):
-    outs, held = refs[:members], refs[members]
-    mine = lax.axis_index("member")
-    held[...] = normed(feats_ref[...], gain_ref[...])
-    width = outs[0].shape[1]
-    for k in range(members):
-        at = mixed(mine, k, members, partner)
-        if width % LANES == 0:
-            outs[k][...] = held[:, pl.ds(pl.multiple_of(at * width, LANES), width)]
-            continue
-        for j in range(members):
-
-            @pl.when(at == j)
-            def _(k=k, j=j):
-                outs[k][...] = held[:, j * width : (j + 1) * width]
+def fetch_kernel(*refs):
+    count = len(refs) // 2
+    sources, targets, sems = refs[:count], refs[count : 2 * count], refs[2 * count]
+    copies = [
+        pltpu.make_async_copy(source, target, sems.at[i])
+        for i, (source, target) in enumerate(zip(sources, targets))
+    ]
+    for copy in copies:
+        copy.start()
+    for copy in copies:
+        copy.wait()
+
+
+def fetch(*arrays):
+    return pl.pallas_call(
+        fetch_kernel,
+        out_shape=[jax.ShapeDtypeStruct(a.shape, a.dtype) for a in arrays],
+        in_specs=[pl.BlockSpec(memory_space=pl.ANY)] * len(arrays),
+        out_specs=[pl.BlockSpec(memory_space=pltpu.VMEM)] * len(arrays),
+        scratch_shapes=[pltpu.SemaphoreType.DMA((len(arrays),))],
+        cost_estimate=pl.CostEstimate(flops=0, bytes_accessed=1 << 22, transcendentals=0),
+    )(*arrays)
 
 
 def logits_kernel(members, peers, *refs):
     feats, refs = refs[:peers], refs[peers:]
     gain_ref, head_ref, bias_ref, refs = refs[0], refs[1], refs[2], refs[3:]
-    columns, refs = refs[:members], refs[members:]
-    student_ref, refs = refs[0], refs[1:]
+    students, refs = refs[:members], refs[members:]
+    student_gain_ref, student_ref, refs = refs[0], refs[1], refs[2:]
     payloads, refs = refs[:members], refs[members:]
-    columns_ref, gathered, shifted_ref, lse_ref, partial_ref = refs
+    columns_ref, gathered, held, shifted_ref, lse_ref, partial_ref = refs
     mine, place = lax.axis_index("member"), lax.axis_index("dp")
     rows = feats[0].shape[0]
     for k in range(peers):
@@ -142,10 +149,22 @@
         core = lax.bitwise_xor(lax.rem(place, jnp.int32(2)), jnp.int32(k % 2))
         at = chip * 2 + core
         gathered[pl.ds(pl.multiple_of(at * rows, rows), rows), :] = feats[k][...]
-    block = columns[0].shape[0]
+    block = students[0].shape[0]
+    width = columns_ref.shape[1]
     for k in range(members):
         at = mixed(mine, k, members, sender)
-        columns_ref[pl.ds(pl.multiple_of(at * block, block), block), :] = columns[k][...]
+        held[pl.ds(pl.multiple_of(at * block, block), block), :] = normed(
+            students[k][...], student_gain_ref[...]
+        )
+    if width % LANES == 0:
+        columns_ref[...] = held[:, pl.ds(pl.multiple_of(mine * width, LANES), width)]
+    else:
+        for j in range(members):
+
+            @pl.when(mine == j)
+            def _(j=j):
+                columns_ref[...] = held[:, j * width : (j + 1) * width]
+
     values = normed(gathered[...], gain_ref[...])
     logits = jnp.dot(values, head_ref[...], preferred_element_type=F32) + bias_ref[...]
     top = jnp.max(logits, axis=1, keepdims=True)
@@ -296,29 +315,31 @@
     small_rows = -(-(members + 2) // 8) * 8
 
     chips = [feats] + [send(feats, "dp", k, 2) for k in range(1, peers // 2)]
-    pieces = call(
-        functools.partial(student_rows, members),
-        [shape((block, width), BF16)] * members,
-        [pltpu.VMEM((block, depth), BF16)],
-    )(student_feats, student_gain[None])
-    columns = [pieces[0]] + [send(pieces[k], "member", k) for k in range(1, members)]
+    students = [student_feats] + [
+        send(student_feats, "member", k) for k in reversed(range(1, members))
+    ][::-1]
+    head, student_head, *rows_of = fetch(
+        teacher_head[0], student_head, teacher_gain, teacher_bias, student_gain[None], student_bias[None]
+    )
+    teacher_gain, teacher_bias, student_gain, student_bias = rows_of
     gathered = [part for chip in chips for part in (chip, swap_cores(chip, "dp"))]
     outs = call(
         functools.partial(logits_kernel, members, peers),
         [shape((3 * block + PAD, classes), BF16)] * members + [shape((images, width), BF16)],
         [
             pltpu.VMEM((images, depth), BF16),
+            pltpu.VMEM((images, depth), BF16),
             pltpu.VMEM((images, classes), BF16),
             pltpu.VMEM((images, LANES), F32),
             pltpu.VMEM((images, classes), F32),
         ],
-    )(*gathered, teacher_gain, teacher_head[0], teacher_bias, *columns, student_head)
+    )(*gathered, teacher_gain, head, teacher_bias, *students, student_gain, student_head)
     payloads, own_columns = outs[:members], outs[members]
     got = [payloads[0]] + [send(payloads[k], "member", k) for k in range(1, members)]
     alphas, target, small = call(
         functools.partial(alphas_kernel, members, block),
         [shape((block, classes), F32)] * 2 + [shape((small_rows, LANES), F32)],
-    )(*got, student_bias[None])
+    )(*got, student_bias)
     chips = [small] + [send(small, "dp", k, 2) for k in range(1, peers // 2)]
     inner = call(digamma_kernel, shape((block, classes), F32))(alphas, target)
     smalls = [part for chip in chips for part in (chip, swap_cores(chip, "dp"))]

time: 53.3 us -> 49.5 us (0.929)
  waiting for transfers between devices: 18.5 us -> 15 us
  starting transfers between devices: 27 us -> 23.6 us
  Pallas kernels: 2.56 us -> 4.54 us
  local copies, waits for them, and re-layouts: 3.6 us -> 4.67 us
    ppermute x15, waiting for transfers between devices: 17.4 us -> 13.9 us  [send(): return lax.ppermute(value, axis, pairs)]
    ppermute x15, starting transfers between devices: 26.1 us -> 23.1 us  [send(): return lax.ppermute(value, axis, pairs)]
    pallas_call x1, Pallas kernels: 0.21 us -> 2.23 us  [fetch(): pl.pallas_call(fetch_kernel, out_shape=[jax.ShapeDtypeStruct(a.shape, a.d...]
    broadcast_in_dim x1, local copies, waits for them, and re-layouts: 0.01 us -> 1.24 us  [on_device(): student_bias[None]]
  transfers between devices with their start and end apart: 23 -> 23, of which waited for: 12 -> 13; matrix products, arithmetic and copies ran while one was open for 0% -> 3% of each run, Pallas kernels for 1% -> 5%
where the time goes in v2:
time: 49.5 us; the launch traced here: 49.2 us
  starting transfers between devices  23.6 us (48%)
  waiting for transfers between devices  15 us (30%)
  local copies, waits for them, and re-layouts  4.67 us (9%)
  Pallas kernels  4.54 us (9%)
  between operations  0.74 us (1%)
  other arithmetic  0.6 us (1%)
    ppermute x15, starting transfers between devices, send(): return lax.ppermute(value, axis, pairs)  23.1 us
    ppermute x15, waiting for transfers between devices, send(): return lax.ppermute(value, axis, pairs)  13.9 us
    unnamed x16, local copies, waits for them, and re-layouts  3.42 us
    pallas_call x1, Pallas kernels, fetch(): pl.pallas_call(fetch_kernel, out_shape=[jax.ShapeDtypeStruct(a.shape, a.d...  2.23 us
    broadcast_in_dim x1, local copies, waits for them, and re-layouts, on_device(): student_bias[None]  1.24 us
    ppermute x8, waiting for transfers between devices, swap_cores(): lax.ppermute(value, axis, [(i, i ^ 1) for i in range(lax.axis_size(axis))])  1.03 us
    pallas_call x1, Pallas kernels, on_device(): call(functools.partial(gradient_kernel, members, peers, block), [shape((1...  1 us
  transfers between devices with their start and end apart: 23, of which 13 were waited for; matrix products, arithmetic and copies ran while one was open for 3% of the time, Pallas kernels for 5%

profile of v2, /device:TPU:0, one launch (start us, length us, event | category | flops | bytes accessed | tf_op | source)
XLA Modules:
  0.0 49.2 jit_solution(806088840129459834)
XLA Ops:
  0.6 4.0 %collective-permute-start.5 = (bf16[16,1024]{1,0:T(8,128)(2,1)}, bf16[16,1024]{1,0:T(8,128)(2,1)S(1)}, u32[]{:S(2)}, u32[]{:S(2)}) collective-permute-start(bf16[16,1024]{1,0:T(8,128)(2,1)} %bitcast.4), channel_id=1, source_target_pairs={{0,6},{1,7},{2,4},{3,5},{4,2},{5,3},{6,0},{7,1},{8,14},{9,15},{10,... | collective-permute-start | bytes 98312 | tf_op jit(solution)/shard_map/ppermute | solution.py:49
  4.6 0.5 %collective-permute-start.3 = (bf16[16,1024]{1,0:T(8,128)(2,1)}, bf16[16,1024]{1,0:T(8,128)(2,1)S(1)}, u32[]{:S(2)}, u32[]{:S(2)}) collective-permute-start(bf16[16,1024]{1,0:T(8,128)(2,1)} %bitcast.5), channel_id=1, source_target_pairs={{0,4},{1,5},{2,6},{3,7},{4,0},{5,1},{6,2},{7,3},{8,12},{9,13},{10,... | collective-permute-start | bytes 98312 | tf_op jit(solution)/shard_map/ppermute | solution.py:49
  5.1 0.1 collective-permute-start.1
  5.2 0.0 collective-permute-start
  5.2 1.5 %collective-permute-done.5.refs_6_ = bf16[16,1024]{1,0:T(8,128)(2,1)S(1)} collective-permute-done((bf16[16,1024]{1,0:T(8,128)(2,1)}, bf16[16,1024]{1,0:T(8,128)(2,1)S(1)}, u32[]{:S(2)}, u32[]{:S(2)}) %collective-permute-start.5) | collective-permute-done | bytes 32800 | tf_op jit(solution)/shard_map/ppermute | solution.py:49
  6.7 0.0 collective-permute-start.6
  6.7 3.1 %collective-permute-start.8 = (bf16[32,1024]{1,0:T(8,128)(2,1)}, bf16[32,1024]{1,0:T(8,128)(2,1)S(1)}, u32[]{:S(2)}, u32[]{:S(2)}) collective-permute-start(bf16[32,1024]{1,0:T(8,128)(2,1)} %refs_11_.1), channel_id=1, source_target_pairs={{0,16},{8,24},{16,0},{24,8},{1,17},{9,25},{17,1},{25,9},{2,18},{10... | collective-permute-start | bytes 196616 | tf_op jit(solution)/shard_map/ppermute | solution.py:49
  9.8 0.0 collective-permute-done.3.refs_4_
  9.8 1.6 %collective-permute-start.7 = (bf16[32,1024]{1,0:T(8,128)(2,1)}, bf16[32,1024]{1,0:T(8,128)(2,1)S(1)}, u32[]{:S(2)}, u32[]{:S(2)}) collective-permute-start(bf16[32,1024]{1,0:T(8,128)(2,1)} %refs_11_.1), channel_id=1, source_target_pairs={{0,8},{8,0},{16,24},{24,16},{1,9},{9,1},{17,25},{25,17},{2,10},{10... | collective-permute-start | bytes 196616 | tf_op jit(solution)/shard_map/ppermute | solution.py:49
  11.4 1.5 %collective-permute-start.9 = (bf16[32,1024]{1,0:T(8,128)(2,1)}, bf16[32,1024]{1,0:T(8,128)(2,1)S(1)}, u32[]{:S(2)}, u32[]{:S(2)}) collective-permute-start(bf16[32,1024]{1,0:T(8,128)(2,1)} %refs_11_.1), channel_id=1, source_target_pairs={{0,24},{8,16},{16,8},{24,0},{1,25},{9,17},{17,9},{25,1},{2,26},{10... | collective-permute-start | bytes 196616 | tf_op jit(solution)/shard_map/ppermute | solution.py:49
  12.8 0.5 %collective-permute-start.2 = (bf16[16,1024]{1,0:T(8,128)(2,1)S(1)}, bf16[16,1024]{1,0:T(8,128)(2,1)S(1)}, u32[]{:S(2)}, u32[]{:S(2)}) collective-permute-start(bf16[16,1024]{1,0:T(8,128)(2,1)S(1)} %collective-permute-done.1.refs_2_), channel_id=1, source_target_pairs={{0,1},{1,0},{2,3},{3,2},{4,5},{5,4},{6,7},{7,6},{8,9},{9,8},{10,11... | collective-permute-start | bytes 98312 | tf_op jit(solution)/shard_map/ppermute | solution.py:53
  13.3 1.2 %broadcast_in_dim.7.refs_5_ = f32[1,384]{1,0:T(1,128)} reshape(f32[384]{0:T(512)} %param.15) | data formatting | bytes 3072 | tf_op jit(solution)/shard_map/broadcast_in_dim | solution.py:322
  14.6 2.2 %shard_map.103 = (bf16[1024,384]{1,0:T(8,128)(2,1)}, bf16[256,384]{1,0:T(8,128)(2,1)}, f32[1,1024]{1,0:T(1,128)}, f32[1,384]{1,0:T(1,128)}, f32[1,1024]{1,0:T(1,128)}, /*index=5*/f32[1,384]{1,0:T(1,128)}) custom-call(bf16[1024,384]{1,0:T(8,128)(2,1)} %bitcast.9, bf16[256,384]{1,0:T(8,128)(2,1)} %refs_1_.1, f32[1,1024]{1,0:T(1,128)} %refs_2_.1, ...), custom_call_target="tpu_custom_call" | custom-call | bytes 4194304 | tf_op jit(solution)/shard_map/pallas_call | solution.py:128
  16.8 0.0 collective-permute-done.8.refs_13_
  16.9 0.0 collective-permute-done.7.refs_12_
  16.9 0.8 %collective-permute-done.9.refs_14_ = bf16[32,1024]{1,0:T(8,128)(2,1)S(1)} collective-permute-done((bf16[32,1024]{1,0:T(8,128)(2,1)}, bf16[32,1024]{1,0:T(8,128)(2,1)S(1)}, u32[]{:S(2)}, u32[]{:S(2)}) %collective-permute-start.9) | collective-permute-done | bytes 65568 | tf_op jit(solution)/shard_map/ppermute | solution.py:49
  17.7 0.7 %copy-done.5 = f32[1,1024]{1,0:T(1,128)S(1)} copy-done((f32[1,1024]{1,0:T(1,128)S(1)}, f32[1,1024]{1,0:T(1,128)}, u32[]{:S(2)}) %copy-start.5) | copy-done | bytes 4120
  18.3 0.0 copy-done.4
  18.3 1.1 %copy-done = bf16[1024,384]{1,0:T(8,128)(2,1)S(1)} copy-done((bf16[1024,384]{1,0:T(8,128)(2,1)S(1)}, bf16[1024,384]{1,0:T(8,128)(2,1)}, u32[]{:S(2)}) %copy-start) | copy-done | bytes 786456
  19.5 0.9 %copy-done.1 = bf16[256,384]{1,0:T(8,128)(2,1)S(1)} copy-done((bf16[256,384]{1,0:T(8,128)(2,1)S(1)}, bf16[256,384]{1,0:T(8,128)(2,1)}, u32[]{:S(2)}) %copy-start.1) | copy-done | bytes 196632
  20.4 0.7 %copy-done.7 = f32[1,384]{1,0:T(1,128)S(1)} copy-done((f32[1,384]{1,0:T(1,128)S(1)}, f32[1,384]{1,0:T(1,128)}, u32[]{:S(2)}) %copy-start.7) | copy-done | bytes 1560
  21.1 0.8 %shard_map.104 = (bf16[112,384]{1,0:T(8,128)(2,1)S(1)}, bf16[112,384]{1,0:T(8,128)(2,1)S(1)}, bf16[112,384]{1,0:T(8,128)(2,1)S(1)}, bf16[112,384]{1,0:T(8,128)(2,1)S(1)}, bf16[128,256]{1,0:T(8,128)(2,1)S(1)}) custom-call(bf16[16,1024]{1,0:T(8,128)(2,1)S(1)} %bitcast.8, bf16[16,1024]{1,0:T(8,128)(2,1)S(1)} %collective-permute-done.refs_1_, ...), custom_call_target="tpu_custom_call" | custom-call | tf_op jit(solution)/shard_map/pallas_call | solution.py:326
  21.9 0.3 collective-permute-start.10
  22.2 2.2 %collective-permute-start.11 = (bf16[112,384]{1,0:T(8,128)(2,1)S(1)}, bf16[112,384]{1,0:T(8,128)(2,1)S(1)}, u32[]{:S(2)}, u32[]{:S(2)}) collective-permute-start(bf16[112,384]{1,0:T(8,128)(2,1)S(1)} %get-tuple-element.27), channel_id=1, source_target_pairs={{0,16},{8,24},{16,0},{24,8},{1,17},{9,25},{17,1},{25,9},{2,18},{10... | collective-permute-start | bytes 258056 | tf_op jit(solution)/shard_map/ppermute | solution.py:49
  24.4 2.0 %collective-permute-start.12 = (bf16[112,384]{1,0:T(8,128)(2,1)S(1)}, bf16[112,384]{1,0:T(8,128)(2,1)S(1)}, u32[]{:S(2)}, u32[]{:S(2)}) collective-permute-start(bf16[112,384]{1,0:T(8,128)(2,1)S(1)} %get-tuple-element.28), channel_id=1, source_target_pairs={{0,24},{8,16},{16,8},{24,0},{1,25},{9,17},{17,9},{25,1},{2,26},{10... | collective-permute-start | bytes 258056 | tf_op jit(solution)/shard_map/ppermute | solution.py:49
  26.4 1.7 %collective-permute-done.10.refs_1_ = bf16[112,384]{1,0:T(8,128)(2,1)S(1)} collective-permute-done((bf16[112,384]{1,0:T(8,128)(2,1)S(1)}, bf16[112,384]{1,0:T(8,128)(2,1)S(1)}, u32[]{:S(2)}, u32[]{:S(2)}) %collective-permute-start.10) | collective-permute-done | bytes 86048 | tf_op jit(solution)/shard_map/ppermute | solution.py:49
  28.1 0.5 collective-permute-done.11.refs_2_
  28.6 3.1 %collective-permute-done.12.refs_3_ = bf16[112,384]{1,0:T(8,128)(2,1)S(1)} collective-permute-done((bf16[112,384]{1,0:T(8,128)(2,1)S(1)}, bf16[112,384]{1,0:T(8,128)(2,1)S(1)}, u32[]{:S(2)}, u32[]{:S(2)}) %collective-permute-start.12) | collective-permute-done | bytes 86048 | tf_op jit(solution)/shard_map/ppermute | solution.py:49
  31.7 0.2 shard_map.105
  32.0 2.4 %collective-permute-start.18 = (f32[8,128]{1,0:T(8,128)S(1)}, f32[8,128]{1,0:T(8,128)S(1)}, u32[]{:S(2)}, u32[]{:S(2)}) collective-permute-start(f32[8,128]{1,0:T(8,128)S(1)} %get-tuple-element.30.refs_0_), channel_id=1, source_target_pairs={{0,6},{1,7},{2,4},{3,5},{4,2},{5,3},{6,0},{7,1},{8,14},{9,15},{10,... | collective-permute-start | bytes 12296 | tf_op jit(solution)/shard_map/ppermute | solution.py:49
  34.3 0.5 %collective-permute-start.16 = (f32[8,128]{1,0:T(8,128)S(1)}, f32[8,128]{1,0:T(8,128)S(1)}, u32[]{:S(2)}, u32[]{:S(2)}) collective-permute-start(f32[8,128]{1,0:T(8,128)S(1)} %get-tuple-element.30.refs_0_), channel_id=1, source_target_pairs={{0,4},{1,5},{2,6},{3,7},{4,0},{5,1},{6,2},{7,3},{8,12},{9,13},{10,... | collective-permute-start | bytes 12296 | tf_op jit(solution)/shard_map/ppermute | solution.py:49
  34.8 0.6 %collective-permute-start.14 = (f32[8,128]{1,0:T(8,128)S(1)}, f32[8,128]{1,0:T(8,128)S(1)}, u32[]{:S(2)}, u32[]{:S(2)}) collective-permute-start(f32[8,128]{1,0:T(8,128)S(1)} %get-tuple-element.30.refs_0_), channel_id=1, source_target_pairs={{0,2},{1,3},{2,0},{3,1},{4,6},{5,7},{6,4},{7,5},{8,10},{9,11},{10,... | collective-permute-start | bytes 12296 | tf_op jit(solution)/shard_map/ppermute | solution.py:49
  35.5 1.0 %collective-permute-done.18.refs_6_ = f32[8,128]{1,0:T(8,128)S(1)} collective-permute-done((f32[8,128]{1,0:T(8,128)S(1)}, f32[8,128]{1,0:T(8,128)S(1)}, u32[]{:S(2)}, u32[]{:S(2)}) %collective-permute-start.18) | collective-permute-done | bytes 4128 | tf_op jit(solution)/shard_map/ppermute | solution.py:49
  36.5 1.5 %collective-permute-done.16.refs_4_ = f32[8,128]{1,0:T(8,128)S(1)} collective-permute-done((f32[8,128]{1,0:T(8,128)S(1)}, f32[8,128]{1,0:T(8,128)S(1)}, u32[]{:S(2)}, u32[]{:S(2)}) %collective-permute-start.16) | collective-permute-done | bytes 4128 | tf_op jit(solution)/shard_map/ppermute | solution.py:49
  38.0 0.5 %collective-permute-done.14.refs_2_ = f32[8,128]{1,0:T(8,128)S(1)} collective-permute-done((f32[8,128]{1,0:T(8,128)S(1)}, f32[8,128]{1,0:T(8,128)S(1)}, u32[]{:S(2)}, u32[]{:S(2)}) %collective-permute-start.14) | collective-permute-done | bytes 4128 | tf_op jit(solution)/shard_map/ppermute | solution.py:49
  38.5 0.0 collective-permute-start.15
  38.5 0.1 shard_map.106.refs_9_
  38.6 0.5 %collective-permute-done.17.refs_5_ = f32[8,128]{1,0:T(8,128)S(1)} collective-permute-done((f32[8,128]{1,0:T(8,128)S(1)}, f32[8,128]{1,0:T(8,128)S(1)}, u32[]{:S(2)}, u32[]{:S(2)}) %collective-permute-start.17) | collective-permute-done | bytes 4128 | tf_op jit(solution)/shard_map/ppermute | solution.py:53
  39.1 0.5 %collective-permute-done.15.refs_3_ = f32[8,128]{1,0:T(8,128)S(1)} collective-permute-done((f32[8,128]{1,0:T(8,128)S(1)}, f32[8,128]{1,0:T(8,128)S(1)}, u32[]{:S(2)}, u32[]{:S(2)}) %collective-permute-start.15) | collective-permute-done | bytes 4128 | tf_op jit(solution)/shard_map/ppermute | solution.py:53
  39.6 0.1 shard_map.107.refs_0_
  39.8 2.5 %collective-permute-start.22 = (bf16[48,384]{1,0:T(8,128)(2,1)S(1)}, bf16[48,384]{1,0:T(8,128)(2,1)S(1)}, u32[]{:S(2)}, u32[]{:S(2)}) collective-permute-start(bf16[48,384]{1,0:T(8,128)(2,1)S(1)} %shard_map.107.refs_0_), channel_id=1, source_target_pairs={{0,24},{8,16},{16,8},{24,0},{1,25},{9,17},{17,9},{25,1},{2,26},{10... | collective-permute-start | bytes 110600 | tf_op jit(solution)/shard_map/ppermute | solution.py:49
  42.3 0.9 %collective-permute-start.21 = (bf16[48,384]{1,0:T(8,128)(2,1)S(1)}, bf16[48,384]{1,0:T(8,128)(2,1)S(1)}, u32[]{:S(2)}, u32[]{:S(2)}) collective-permute-start(bf16[48,384]{1,0:T(8,128)(2,1)S(1)} %shard_map.107.refs_0_), channel_id=1, source_target_pairs={{0,16},{8,24},{16,0},{24,8},{1,17},{9,25},{17,1},{25,9},{2,18},{10... | collective-permute-start | bytes 110600 | tf_op jit(solution)/shard_map/ppermute | solution.py:49
  43.2 1.0 %collective-permute-start.20 = (bf16[48,384]{1,0:T(8,128)(2,1)S(1)}, bf16[48,384]{1,0:T(8,128)(2,1)S(1)}, u32[]{:S(2)}, u32[]{:S(2)}) collective-permute-start(bf16[48,384]{1,0:T(8,128)(2,1)S(1)} %shard_map.107.refs_0_), channel_id=1, source_target_pairs={{0,8},{8,0},{16,24},{24,16},{1,9},{9,1},{17,25},{25,17},{2,10},{10... | collective-permute-start | bytes 110600 | tf_op jit(solution)/shard_map/ppermute | solution.py:49
  44.2 1.4 %collective-permute-done.22.refs_3_ = bf16[48,384]{1,0:T(8,128)(2,1)S(1)} collective-permute-done((bf16[48,384]{1,0:T(8,128)(2,1)S(1)}, bf16[48,384]{1,0:T(8,128)(2,1)S(1)}, u32[]{:S(2)}, u32[]{:S(2)}) %collective-permute-start.22) | collective-permute-done | bytes 36896 | tf_op jit(solution)/shard_map/ppermute | solution.py:49
  45.6 1.8 %collective-permute-done.21.refs_2_ = bf16[48,384]{1,0:T(8,128)(2,1)S(1)} collective-permute-done((bf16[48,384]{1,0:T(8,128)(2,1)S(1)}, bf16[48,384]{1,0:T(8,128)(2,1)S(1)}, u32[]{:S(2)}, u32[]{:S(2)}) %collective-permute-start.21) | collective-permute-done | bytes 36896 | tf_op jit(solution)/shard_map/ppermute | solution.py:49
  47.4 0.2 collective-permute-done.20.refs_1_
  47.6 1.0 %shard_map.108 = (f32[1,1]{1,0:T(1,128)}, f32[256,384]{1,0:T(8,128)}, f32[1,384]{1,0:T(1,128)S(1)}) custom-call(bf16[48,384]{1,0:T(8,128)(2,1)S(1)} %shard_map.107.refs_0_, bf16[48,384]{1,0:T(8,128)(2,1)S(1)} %collective-permute-done.20.refs_1_, bf16[48,384]{1,0:T(8,128)(2,1)S(1)} %collective-permute-done.21.refs_2_, ...), custom_call_target="tpu_custom_call" | custom-call | tf_op jit(solution)/shard_map/pallas_call | solution.py:352
  48.6 0.6 %reduce = f32[384]{0:T(512)} reduce(f32[1,384]{1,0:T(1,128)S(1)} %get-tuple-element.36, f32[]{:T(128)} %constant.4), dimensions={0}, to_apply=%get-tuple-element.36.reduce_sub_computation | reduce | bytes 3076 | tf_op jit(solution)/shard_map/pallas_call | solution.py:352
  (22 shorter events, 0.0 us)
Async XLA Ops:
  0.6 6.1 %collective-permute-start.5 = (bf16[16,1024]{1,0:T(8,128)(2,1)}, bf16[16,1024]{1,0:T(8,128)(2,1)S(1)}, u32[]{:S(2)}, u32[]{:S(2)}) collective-permute-start(bf16[16,1024]{1,0:T(8,128)(2,1)} %bitcast.4), channel_id=1, source_target_pairs={{0,6},{1,7},{2,4},{3,5},{4,2},{5,3},{6,0},{7,1},{8,14},{9,15},{10,... | collective-permute-start | bytes 98312 | tf_op jit(solution)/shard_map/ppermute | solution.py:49
  4.6 5.2 %collective-permute-start.3 = (bf16[16,1024]{1,0:T(8,128)(2,1)}, bf16[16,1024]{1,0:T(8,128)(2,1)S(1)}, u32[]{:S(2)}, u32[]{:S(2)}) collective-permute-start(bf16[16,1024]{1,0:T(8,128)(2,1)} %bitcast.5), channel_id=1, source_target_pairs={{0,4},{1,5},{2,6},{3,7},{4,0},{5,1},{6,2},{7,3},{8,12},{9,13},{10,... | collective-permute-start | bytes 98312 | tf_op jit(solution)/shard_map/ppermute | solution.py:49
  5.1 6.3 %collective-permute-start.1 = (bf16[16,1024]{1,0:T(8,128)(2,1)}, bf16[16,1024]{1,0:T(8,128)(2,1)S(1)}, u32[]{:S(2)}, u32[]{:S(2)}) collective-permute-start(bf16[16,1024]{1,0:T(8,128)(2,1)} %bitcast.6), channel_id=1, source_target_pairs={{0,2},{1,3},{2,0},{3,1},{4,6},{5,7},{6,4},{7,5},{8,10},{9,11},{10,... | collective-permute-start | bytes 98312 | tf_op jit(solution)/shard_map/ppermute | solution.py:49
  5.2 7.6 %collective-permute-start = (bf16[16,1024]{1,0:T(8,128)(2,1)}, bf16[16,1024]{1,0:T(8,128)(2,1)S(1)}, u32[]{:S(2)}, u32[]{:S(2)}) collective-permute-start(bf16[16,1024]{1,0:T(8,128)(2,1)} %bitcast.7), channel_id=1, source_target_pairs={{0,1},{1,0},{2,3},{3,2},{4,5},{5,4},{6,7},{7,6},{8,9},{9,8},{10,11... | collective-permute-start | bytes 98312 | tf_op jit(solution)/shard_map/ppermute | solution.py:53
  6.7 6.1 %collective-permute-start.6 = (bf16[16,1024]{1,0:T(8,128)(2,1)S(1)}, bf16[16,1024]{1,0:T(8,128)(2,1)S(1)}, u32[]{:S(2)}, u32[]{:S(2)}) collective-permute-start(bf16[16,1024]{1,0:T(8,128)(2,1)S(1)} %collective-permute-done.5.refs_6_), channel_id=1, source_target_pairs={{0,1},{1,0},{2,3},{3,2},{4,5},{5,4},{6,7},{7,6},{8,9},{9,8},{10,11... | collective-permute-start | bytes 98312 | tf_op jit(solution)/shard_map/ppermute | solution.py:53
  6.7 10.1 %collective-permute-start.8 = (bf16[32,1024]{1,0:T(8,128)(2,1)}, bf16[32,1024]{1,0:T(8,128)(2,1)S(1)}, u32[]{:S(2)}, u32[]{:S(2)}) collective-permute-start(bf16[32,1024]{1,0:T(8,128)(2,1)} %refs_11_.1), channel_id=1, source_target_pairs={{0,16},{8,24},{16,0},{24,8},{1,17},{9,25},{17,1},{25,9},{2,18},{10... | collective-permute-start | bytes 196616 | tf_op jit(solution)/shard_map/ppermute | solution.py:49
  9.8 7.1 %collective-permute-start.7 = (bf16[32,1024]{1,0:T(8,128)(2,1)}, bf16[32,1024]{1,0:T(8,128)(2,1)S(1)}, u32[]{:S(2)}, u32[]{:S(2)}) collective-permute-start(bf16[32,1024]{1,0:T(8,128)(2,1)} %refs_11_.1), channel_id=1, source_target_pairs={{0,8},{8,0},{16,24},{24,16},{1,9},{9,1},{17,25},{25,17},{2,10},{10... | collective-permute-start | bytes 196616 | tf_op jit(solution)/shard_map/ppermute | solution.py:49
  11.4 6.3 %collective-permute-start.9 = (bf16[32,1024]{1,0:T(8,128)(2,1)}, bf16[32,1024]{1,0:T(8,128)(2,1)S(1)}, u32[]{:S(2)}, u32[]{:S(2)}) collective-permute-start(bf16[32,1024]{1,0:T(8,128)(2,1)} %refs_11_.1), channel_id=1, source_target_pairs={{0,24},{8,16},{16,8},{24,0},{1,25},{9,17},{17,9},{25,1},{2,26},{10... | collective-permute-start | bytes 196616 | tf_op jit(solution)/shard_map/ppermute | solution.py:49
  12.8 4.0 %collective-permute-start.4 = (bf16[16,1024]{1,0:T(8,128)(2,1)S(1)}, bf16[16,1024]{1,0:T(8,128)(2,1)S(1)}, u32[]{:S(2)}, u32[]{:S(2)}) collective-permute-start(bf16[16,1024]{1,0:T(8,128)(2,1)S(1)} %collective-permute-done.3.refs_4_), channel_id=1, source_target_pairs={{0,1},{1,0},{2,3},{3,2},{4,5},{5,4},{6,7},{7,6},{8,9},{9,8},{10,11... | collective-permute-start | bytes 98312 | tf_op jit(solution)/shard_map/ppermute | solution.py:53
  12.8 4.0 %collective-permute-start.2 = (bf16[16,1024]{1,0:T(8,128)(2,1)S(1)}, bf16[16,1024]{1,0:T(8,128)(2,1)S(1)}, u32[]{:S(2)}, u32[]{:S(2)}) collective-permute-start(bf16[16,1024]{1,0:T(8,128)(2,1)S(1)} %collective-permute-done.1.refs_2_), channel_id=1, source_target_pairs={{0,1},{1,0},{2,3},{3,2},{4,5},{5,4},{6,7},{7,6},{8,9},{9,8},{10,11... | collective-permute-start | bytes 98312 | tf_op jit(solution)/shard_map/ppermute | solution.py:53
  14.6 3.1 %copy-start.2 = (bf16[32,1024]{1,0:T(8,128)(2,1)S(1)}, bf16[32,1024]{1,0:T(8,128)(2,1)}, u32[]{:S(2)}) copy-start(bf16[32,1024]{1,0:T(8,128)(2,1)} %refs_11_.1) | copy-start | bytes 196612
  14.6 3.1 %copy-start.3 = (bf16[1,16,1024]{2,1,0:T(8,128)(2,1)S(1)}, bf16[1,16,1024]{2,1,0:T(8,128)(2,1)}, u32[]{:S(2)}) copy-start(bf16[1,16,1024]{2,1,0:T(8,128)(2,1)} %param.8) | copy-start | bytes 98308
  17.6 0.7 %copy-start.5 = (f32[1,1024]{1,0:T(1,128)S(1)}, f32[1,1024]{1,0:T(1,128)}, u32[]{:S(2)}) copy-start(f32[1,1024]{1,0:T(1,128)} %get-tuple-element.23.refs_15_) | copy-start | bytes 12292
  17.6 0.7 %copy-start.4 = (f32[1,1024]{1,0:T(1,128)S(1)}, f32[1,1024]{1,0:T(1,128)}, u32[]{:S(2)}) copy-start(f32[1,1024]{1,0:T(1,128)} %get-tuple-element.20.refs_8_) | copy-start | bytes 12292
  18.3 1.1 %copy-start = (bf16[1024,384]{1,0:T(8,128)(2,1)S(1)}, bf16[1024,384]{1,0:T(8,128)(2,1)}, u32[]{:S(2)}) copy-start(bf16[1024,384]{1,0:T(8,128)(2,1)} %get-tuple-element.21.refs_9_) | copy-start | bytes 2359300
  19.5 0.9 %copy-start.1 = (bf16[256,384]{1,0:T(8,128)(2,1)S(1)}, bf16[256,384]{1,0:T(8,128)(2,1)}, u32[]{:S(2)}) copy-start(bf16[256,384]{1,0:T(8,128)(2,1)} %get-tuple-element.24.refs_16_) | copy-start | bytes 589828
  20.4 0.7 %copy-start.7 = (f32[1,384]{1,0:T(1,128)S(1)}, f32[1,384]{1,0:T(1,128)}, u32[]{:S(2)}) copy-start(f32[1,384]{1,0:T(1,128)} %get-tuple-element.22.refs_10_) | copy-start | bytes 4612
  21.9 6.2 %collective-permute-start.10 = (bf16[112,384]{1,0:T(8,128)(2,1)S(1)}, bf16[112,384]{1,0:T(8,128)(2,1)S(1)}, u32[]{:S(2)}, u32[]{:S(2)}) collective-permute-start(bf16[112,384]{1,0:T(8,128)(2,1)S(1)} %get-tuple-element.26), channel_id=1, source_target_pairs={{0,8},{8,0},{16,24},{24,16},{1,9},{9,1},{17,25},{25,17},{2,10},{10... | collective-permute-start | bytes 258056 | tf_op jit(solution)/shard_map/ppermute | solution.py:49
  22.2 6.4 %collective-permute-start.11 = (bf16[112,384]{1,0:T(8,128)(2,1)S(1)}, bf16[112,384]{1,0:T(8,128)(2,1)S(1)}, u32[]{:S(2)}, u32[]{:S(2)}) collective-permute-start(bf16[112,384]{1,0:T(8,128)(2,1)S(1)} %get-tuple-element.27), channel_id=1, source_target_pairs={{0,16},{8,24},{16,0},{24,8},{1,17},{9,25},{17,1},{25,9},{2,18},{10... | collective-permute-start | bytes 258056 | tf_op jit(solution)/shard_map/ppermute | solution.py:49
  24.4 7.3 %copy-start.6 = (f32[1,384]{1,0:T(1,128)S(1)}, f32[1,384]{1,0:T(1,128)}, u32[]{:S(2)}) copy-start(f32[1,384]{1,0:T(1,128)} %get-tuple-element.29.refs_4_) | copy-start | bytes 4612
  24.4 7.3 %collective-permute-start.12 = (bf16[112,384]{1,0:T(8,128)(2,1)S(1)}, bf16[112,384]{1,0:T(8,128)(2,1)S(1)}, u32[]{:S(2)}, u32[]{:S(2)}) collective-permute-start(bf16[112,384]{1,0:T(8,128)(2,1)S(1)} %get-tuple-element.28), channel_id=1, source_target_pairs={{0,24},{8,16},{16,8},{24,0},{1,25},{9,17},{17,9},{25,1},{2,26},{10... | collective-permute-start | bytes 258056 | tf_op jit(solution)/shard_map/ppermute | solution.py:49
  32.0 4.5 %collective-permute-start.18 = (f32[8,128]{1,0:T(8,128)S(1)}, f32[8,128]{1,0:T(8,128)S(1)}, u32[]{:S(2)}, u32[]{:S(2)}) collective-permute-start(f32[8,128]{1,0:T(8,128)S(1)} %get-tuple-element.30.refs_0_), channel_id=1, source_target_pairs={{0,6},{1,7},{2,4},{3,5},{4,2},{5,3},{6,0},{7,1},{8,14},{9,15},{10,... | collective-permute-start | bytes 12296 | tf_op jit(solution)/shard_map/ppermute | solution.py:49
  34.3 3.6 %collective-permute-start.16 = (f32[8,128]{1,0:T(8,128)S(1)}, f32[8,128]{1,0:T(8,128)S(1)}, u32[]{:S(2)}, u32[]{:S(2)}) collective-permute-start(f32[8,128]{1,0:T(8,128)S(1)} %get-tuple-element.30.refs_0_), channel_id=1, source_target_pairs={{0,4},{1,5},{2,6},{3,7},{4,0},{5,1},{6,2},{7,3},{8,12},{9,13},{10,... | collective-permute-start | bytes 12296 | tf_op jit(solution)/shard_map/ppermute | solution.py:49
  34.8 3.6 %collective-permute-start.14 = (f32[8,128]{1,0:T(8,128)S(1)}, f32[8,128]{1,0:T(8,128)S(1)}, u32[]{:S(2)}, u32[]{:S(2)}) collective-permute-start(f32[8,128]{1,0:T(8,128)S(1)} %get-tuple-element.30.refs_0_), channel_id=1, source_target_pairs={{0,2},{1,3},{2,0},{3,1},{4,6},{5,7},{6,4},{7,5},{8,10},{9,11},{10,... | collective-permute-start | bytes 12296 | tf_op jit(solution)/shard_map/ppermute | solution.py:49
  35.5 3.1 %collective-permute-start.13 = (f32[8,128]{1,0:T(8,128)S(1)}, f32[8,128]{1,0:T(8,128)S(1)}, u32[]{:S(2)}, u32[]{:S(2)}) collective-permute-start(f32[8,128]{1,0:T(8,128)S(1)} %get-tuple-element.30.refs_0_), channel_id=1, source_target_pairs={{0,1},{1,0},{2,3},{3,2},{4,5},{5,4},{6,7},{7,6},{8,9},{9,8},{10,11... | collective-permute-start | bytes 12296 | tf_op jit(solution)/shard_map/ppermute | solution.py:53
  36.5 2.1 %collective-permute-start.19 = (f32[8,128]{1,0:T(8,128)S(1)}, f32[8,128]{1,0:T(8,128)S(1)}, u32[]{:S(2)}, u32[]{:S(2)}) collective-permute-start(f32[8,128]{1,0:T(8,128)S(1)} %collective-permute-done.18.refs_6_), channel_id=1, source_target_pairs={{0,1},{1,0},{2,3},{3,2},{4,5},{5,4},{6,7},{7,6},{8,9},{9,8},{10,11... | collective-permute-start | bytes 12296 | tf_op jit(solution)/shard_map/ppermute | solution.py:53
  38.0 1.2 %collective-permute-start.17 = (f32[8,128]{1,0:T(8,128)S(1)}, f32[8,128]{1,0:T(8,128)S(1)}, u32[]{:S(2)}, u32[]{:S(2)}) collective-permute-start(f32[8,128]{1,0:T(8,128)S(1)} %collective-permute-done.16.refs_4_), channel_id=1, source_target_pairs={{0,1},{1,0},{2,3},{3,2},{4,5},{5,4},{6,7},{7,6},{8,9},{9,8},{10,11... | collective-permute-start | bytes 12296 | tf_op jit(solution)/shard_map/ppermute | solution.py:53
  38.5 1.2 %collective-permute-start.15 = (f32[8,128]{1,0:T(8,128)S(1)}, f32[8,128]{1,0:T(8,128)S(1)}, u32[]{:S(2)}, u32[]{:S(2)}) collective-permute-start(f32[8,128]{1,0:T(8,128)S(1)} %collective-permute-done.14.refs_2_), channel_id=1, source_target_pairs={{0,1},{1,0},{2,3},{3,2},{4,5},{5,4},{6,7},{7,6},{8,9},{9,8},{10,11... | collective-permute-start | bytes 12296 | tf_op jit(solution)/shard_map/ppermute | solution.py:53
  39.8 5.9 %collective-permute-start.22 = (bf16[48,384]{1,0:T(8,128)(2,1)S(1)}, bf16[48,384]{1,0:T(8,128)(2,1)S(1)}, u32[]{:S(2)}, u32[]{:S(2)}) collective-permute-start(bf16[48,384]{1,0:T(8,128)(2,1)S(1)} %shard_map.107.refs_0_), channel_id=1, source_target_pairs={{0,24},{8,16},{16,8},{24,0},{1,25},{9,17},{17,9},{25,1},{2,26},{10... | collective-permute-start | bytes 110600 | tf_op jit(solution)/shard_map/ppermute | solution.py:49
  42.3 5.1 %collective-permute-start.21 = (bf16[48,384]{1,0:T(8,128)(2,1)S(1)}, bf16[48,384]{1,0:T(8,128)(2,1)S(1)}, u32[]{:S(2)}, u32[]{:S(2)}) collective-permute-start(bf16[48,384]{1,0:T(8,128)(2,1)S(1)} %shard_map.107.refs_0_), channel_id=1, source_target_pairs={{0,16},{8,24},{16,0},{24,8},{1,17},{9,25},{17,1},{25,9},{2,18},{10... | collective-permute-start | bytes 110600 | tf_op jit(solution)/shard_map/ppermute | solution.py:49
  43.2 4.4 %collective-permute-start.20 = (bf16[48,384]{1,0:T(8,128)(2,1)S(1)}, bf16[48,384]{1,0:T(8,128)(2,1)S(1)}, u32[]{:S(2)}, u32[]{:S(2)}) collective-permute-start(bf16[48,384]{1,0:T(8,128)(2,1)S(1)} %shard_map.107.refs_0_), channel_id=1, source_target_pairs={{0,8},{8,0},{16,24},{24,16},{1,9},{9,1},{17,25},{25,17},{2,10},{10... | collective-permute-start | bytes 110600 | tf_op jit(solution)/shard_map/ppermute | solution.py:49

commit v3 on v2

v3 whole, which is shorter than its diff:
```python
import functools
import math

import jax
import jax.numpy as jnp
from jax import lax
from jax.experimental import pallas as pl
from jax.experimental.pallas import tpu as pltpu
from jax.sharding import PartitionSpec as P

BF16, F32 = jnp.bfloat16, jnp.float32
LANES = 128
PAD = 16
LANCZOS = (
    0.99999999999980993227684700473478,
    676.520368121885098567009190444019,
    -1259.13921672240287047156078755283,
    771.3234287776530788486528258894,
    -176.61502916214059906584551354,
    12.507343278686904814458936853,
    -0.13857109526572011689554707,
    9.984369578019570859563e-6,
    1.50563273514931155834e-7,
)


def partner(index, k, size):
    return index ^ k if size & (size - 1) == 0 else (index + k) % size


def sender(index, k, size):
    return index ^ k if size & (size - 1) == 0 else (index - k + size) % size


def mixed(index, k, size, of):
    if size & (size - 1) == 0:
        return lax.bitwise_xor(index, jnp.int32(k))
    step = k if of is partner else size - k
    return lax.rem(index + jnp.int32(step), jnp.int32(size))


def send(value, axis, k, scale=1, groups=1):
    size = lax.axis_size(axis) // scale
    pairs = [
        (outer * scale + inner, partner(outer, k, size) * scale + inner)
        for outer in range(size)
        for inner in range(scale)
    ]
    return lax.ppermute(value, axis, pairs)


def swap_cores(value, axis):
    return lax.ppermute(value, axis, [(i, i ^ 1) for i in range(lax.axis_size(axis))])


def normed(values, gain_row):
    values = values.astype(F32)
    center = values - jnp.mean(values, axis=-1, keepdims=True)
    spread = jnp.mean(center * center, axis=-1, keepdims=True)
    return (center * lax.rsqrt(spread + 1e-06) * gain_row).astype(BF16)


def split3(value):
    high = value.astype(BF16)
    rest = value - high.astype(F32)
    middle = rest.astype(BF16)
    return high, middle, (rest - middle.astype(F32)).astype(BF16)


def diagonal(rows, lanes):
    return lax.broadcasted_iota(jnp.int32, (rows, lanes), 0) == lax.broadcasted_iota(
        jnp.int32, (rows, lanes), 1
    )


def to_lanes(column, lanes):
    return jnp.sum(
        jnp.where(diagonal(column.shape[0], lanes), column, 0.0), axis=0, keepdims=True
    )


def to_column(row, rows):
    return jnp.sum(jnp.where(diagonal(rows, row.shape[1]), row, 0.0), axis=1, keepdims=True)


def series(x):
    total = jnp.full_like(x, LANCZOS[0])
    slope = jnp.zeros_like(x)
    for k in range(1, 9):
        inverse = 1.0 / (x + float(k))
        term = LANCZOS[k] * inverse
        total = total + term
        slope = slope - term * inverse
    log_t = math.log(7.5) + jnp.log1p(x / 7.5)
    return total, slope, log_t


def log_gamma(x, log_x):
    total, _, log_t = series(x)
    t = x + 7.5
    return (
        (x + 0.5 - t / log_t) * log_t
        + 0.5 * math.log(2.0 * math.pi)
        + jnp.log(total)
        - log_x
    )


def di_gamma(x):
    total, slope, log_t = series(x)
    return log_t + slope / total - 7.0 / (x + 7.5) - 1.0 / x


def fetch(sources, targets, sems):
    copies = [
        pltpu.make_async_copy(source, target, sems.at[i])
        for i, (source, target) in enumerate(zip(sources, targets, strict=True))
    ]
    for copy in copies:
        copy.start()
    return copies


def slot(at, rows):
    return pl.ds(pl.multiple_of(at * rows, rows), rows)


def prepare_kernel(other_ref, *refs):
    sources, (pair_ref, own_ref, gain_ref, sems) = refs[:2], refs[2:]
    copies = fetch(sources, (own_ref, gain_ref), sems)
    core = lax.rem(lax.axis_index("dp"), jnp.int32(2))
    rows = other_ref.shape[0]
    for copy in copies:
        copy.wait()
    pair_ref[slot(core, rows), :] = normed(own_ref[...], gain_ref[...])
    pair_ref[slot(1 - core, rows), :] = normed(other_ref[...], gain_ref[...])


def packed3(row, rows, lanes):
    line = lax.broadcasted_iota(jnp.int32, (rows, lanes), 0)
    high, middle, low = (part.astype(F32) for part in split3(row))
    lower = jnp.where(line == 2, low, 0.0)
    return jnp.where(line == 0, high, jnp.where(line == 1, middle, lower)).astype(BF16)


def logits_kernel(members, chips, *refs):
    pairs, refs = refs[:chips], refs[chips:]
    students, refs = refs[: members - 1], refs[members - 1 :]
    sources, refs = refs[:6], refs[6:]
    payloads, refs = refs[:members], refs[members:]
    columns_ref, gathered, held, shifted_ref, lse_ref, partial_ref, *params = refs
    own_ref, gain_ref, head_ref, student_ref, bias_ref, student_bias_ref, sems = params
    copies = fetch(sources, params[:6], sems)
    mine, chip = lax.axis_index("member"), lax.axis_index("dp") // 2
    for k in range(chips):
        at = mixed(chip, k, chips, sender)
        gathered[slot(at, pairs[k].shape[0]), :] = pairs[k][...]
    for copy in copies:
        copy.wait()
    block = own_ref.shape[0]
    width = columns_ref.shape[1]
    for k in range(members):
        source = own_ref if k == 0 else students[k - 1]
        at = slot(mixed(mine, k, members, sender), block)
        held[at, :] = normed(source[...], gain_ref[...])
    if width % LANES == 0:
        columns_ref[...] = held[:, pl.ds(pl.multiple_of(mine * width, LANES), width)]
    else:
        for j in range(members):

            @pl.when(mine == j)
            def _(j=j):
                columns_ref[...] = held[:, j * width : (j + 1) * width]

    logits = jnp.dot(gathered[...], head_ref[...], preferred_element_type=F32) + bias_ref[...]
    top = jnp.max(logits, axis=1, keepdims=True)
    lse = top + jnp.log(jnp.sum(jnp.exp(logits - top), axis=1, keepdims=True))
    shifted_ref[...] = (logits - lse).astype(BF16)
    lse_ref[...] = jnp.broadcast_to(lse, lse_ref.shape)
    partial_ref[...] = jnp.dot(columns_ref[...], student_ref[...], preferred_element_type=F32)
    classes = logits.shape[1]
    for k in range(members):
        at = slot(mixed(mine, k, members, partner), block)
        out = payloads[k]
        out[0:block, :] = shifted_ref[at, :]
        partial = partial_ref[at, :]
        if k == 0:
            partial += student_bias_ref[...][None, :]
        high, middle, _ = split3(partial)
        out[block : 2 * block, :] = high
        out[2 * block : 3 * block, :] = middle
        out[3 * block :, :] = packed3(to_lanes(lse_ref[at, 0:1], classes), PAD, classes)


def alphas_kernel(members, *refs):
    payloads, refs = refs[:members], refs[members:]
    alphas_ref, target_ref, small_ref = refs
    mine = lax.axis_index("member")
    block, classes = alphas_ref.shape
    target = jnp.zeros((block, classes), F32)
    logits = jnp.zeros((block, classes), F32)
    lse_total = jnp.zeros((1, LANES), F32)
    small_ref[...] = jnp.zeros_like(small_ref)
    for k in range(members):
        got = payloads[k]
        target += got[0:block, :].astype(F32)
        logits += got[block : 2 * block, :].astype(F32) + got[2 * block : 3 * block, :].astype(F32)
        tail = got[3 * block :, 0:LANES].astype(F32)
        lse = tail[0:1, :] + tail[1:2, :] + tail[2:3, :]
        lse_total += lse
        small_ref[pl.ds(mixed(mine, k, members, sender), 1), :] = lse
    target = target * (1.0 / members)
    alphas = jnp.exp(logits)
    alphas_ref[...] = alphas
    target_ref[...] = target
    sums = to_lanes(jnp.sum(alphas, axis=1, keepdims=True), LANES)
    parts = to_lanes(
        jnp.sum(log_gamma(alphas, logits) - (alphas - 1.0) * target, axis=1, keepdims=True), LANES
    )
    small_ref[members : members + 1, :] = sums
    small_ref[members + 1 : members + 2, :] = parts - lse_total * (1.0 / members) * (
        sums - float(classes)
    )


def digamma_kernel(alphas_ref, target_ref, inner_ref):
    inner_ref[...] = di_gamma(alphas_ref[...]) - target_ref[...]


def joined(parts, members):
    top = functools.reduce(jnp.maximum, parts)
    logs = top + jnp.log(sum(jnp.exp(part - top) for part in parts))
    line = lax.broadcasted_iota(jnp.int32, top.shape, 0)
    return jnp.where(line < members, logs, sum(parts))


def combine_kernel(members, own_ref, other_ref, out_ref):
    out_ref[...] = joined([own_ref[...], other_ref[...]], members)


def signal_kernel(members, chips, images, classes, *refs):
    smalls, refs = refs[:chips], refs[chips:]
    own_ref, alphas_ref, inner_ref, signal_ref, held = refs
    chip = lax.axis_index("dp") // 2
    block = alphas_ref.shape[0]
    for k in range(chips):
        held[mixed(chip, k, chips, sender)] = smalls[k][...]
    everything = joined([held[k] for k in range(chips)], members)
    norm_total = jnp.sum(everything[0:members, :], axis=0, keepdims=True) * (1.0 / members)
    own = jnp.sum(own_ref[0:members, :], axis=0, keepdims=True) * (1.0 / members)
    used = lax.broadcasted_iota(jnp.int32, (1, LANES), 1) < block
    alpha_sum = jnp.where(used, everything[members : members + 1, :], 1.0)
    shift = to_column(di_gamma(alpha_sum) + own - norm_total, block)
    signal_ref[0:block, :] = (alphas_ref[...] * (inner_ref[...] - shift)).astype(BF16)
    terms = (
        everything[members + 1 : members + 2, :]
        - log_gamma(alpha_sum, jnp.log(alpha_sum))
        + norm_total * (alpha_sum - float(classes))
    )
    loss = jnp.sum(jnp.where(used, terms, 0.0), axis=1, keepdims=True)
    signal_ref[block:, :] = packed3(loss, PAD, alphas_ref.shape[1])


def gradient_kernel(members, images, classes, *refs):
    signals, refs = refs[:members], refs[members:]
    columns_ref, loss_ref, grad_ref, bias_ref, held, losses = refs
    mine = lax.axis_index("member")
    block = images // members
    for k in range(members):
        at = mixed(mine, k, members, sender)
        held[slot(at, block), :] = signals[k][0:block, :]
        tail = signals[k][block:, 0:LANES].astype(F32)
        losses[pl.ds(at, 1), :] = tail[0:1, :] + tail[1:2, :] + tail[2:3, :]
    signal = held[...]
    grad = lax.dot_general(
        columns_ref[...], signal, (((0,), (0,)), ((), ())), preferred_element_type=F32
    )
    grad_ref[...] = grad * (1.0 / images)
    bias_ref[...] = jnp.sum(signal.astype(F32), axis=0) * (1.0 / images)
    loss_ref[0, 0] = jnp.sum(losses[:, 0:1]) * (1.0 / (images * classes))


def call(kernel, out_shape, scratch=(), in_specs=None, out_specs=None):
    extra = {}
    if in_specs is not None:
        extra["in_specs"] = in_specs
    if out_specs is not None:
        extra["out_specs"] = out_specs
    return pl.pallas_call(
        kernel,
        out_shape=out_shape,
        scratch_shapes=list(scratch),
        compiler_params=pltpu.CompilerParams(vmem_limit_bytes=48 * 1024 * 1024),
        **extra,
    )


def on_device(
    teacher_feats,
    teacher_gain,
    teacher_head,
    teacher_bias,
    student_feats,
    student_gain,
    student_head,
    student_bias,
):
    members, peers = lax.axis_size("member"), lax.axis_size("dp")
    chips = peers // 2
    shape = jax.ShapeDtypeStruct
    here, far = pl.BlockSpec(memory_space=pltpu.VMEM), pl.BlockSpec(memory_space=pltpu.HBM)
    feats = teacher_feats[0]
    rows, depth = feats.shape
    block = student_feats.shape[0]
    images = rows * peers
    width, classes = student_head.shape
    small_rows = -(-(members + 2) // 8) * 8

    other = swap_cores(feats, "dp")
    students = [send(student_feats, "member", k) for k in range(1, members)]
    pair = call(
        prepare_kernel,
        shape((2 * rows, depth), BF16),
        [
            pltpu.VMEM((rows, depth), BF16),
            pltpu.VMEM((1, depth), F32),
            pltpu.SemaphoreType.DMA((2,)),
        ],
        [here] + [far] * 2,
    )(other, feats, teacher_gain)
    pairs = [pair] + [send(pair, "dp", k, 2) for k in range(1, chips)]
    *payloads, own_columns = call(
        functools.partial(logits_kernel, members, chips),
        [shape((3 * block + PAD, classes), BF16)] * members + [shape((images, width), BF16)],
        [
            pltpu.VMEM((images, depth), BF16),
            pltpu.VMEM((images, depth), BF16),
            pltpu.VMEM((images, classes), BF16),
            pltpu.VMEM((images, LANES), F32),
            pltpu.VMEM((images, classes), F32),
            pltpu.VMEM((block, depth), BF16),
            pltpu.VMEM((1, depth), F32),
            pltpu.VMEM((depth, classes), BF16),
            pltpu.VMEM((width, classes), BF16),
            pltpu.VMEM((1, classes), F32),
            pltpu.VMEM((classes,), F32),
            pltpu.SemaphoreType.DMA((6,)),
        ],
        [here] * (chips + members - 1) + [far] * 6,
    )(
        *pairs,
        *students,
        student_feats,
        student_gain[None],
        teacher_head[0],
        student_head,
        teacher_bias,
        student_bias,
    )
    got = [payloads[0]] + [send(payloads[k], "member", k) for k in range(1, members)]
    alphas, target, own = call(
        functools.partial(alphas_kernel, members),
        [shape((block, classes), F32)] * 2 + [shape((small_rows, LANES), F32)],
    )(*got)
    other = swap_cores(own, "dp")
    inner = call(digamma_kernel, shape((block, classes), F32))(alphas, target)
    small = call(functools.partial(combine_kernel, members), shape(own.shape, F32))(own, other)
    smalls = [small] + [send(small, "dp", k, 2) for k in range(1, chips)]
    signal = call(
        functools.partial(signal_kernel, members, chips, images, classes * peers),
        shape((block + PAD, classes), BF16),
        [pltpu.VMEM((chips, small_rows, LANES), F32)],
    )(*smalls, own, alphas, inner)
    signals = [signal] + [send(signal, "member", k) for k in range(1, members)]
    loss, head_grad, bias_grad = call(
        functools.partial(gradient_kernel, members, images, classes * peers),
        [shape((1, 1), F32), shape((width, classes), F32), shape((classes,), F32)],
        [pltpu.VMEM((images, classes), BF16), pltpu.VMEM((members, LANES), F32)],
        out_specs=[pl.BlockSpec(memory_space=pltpu.SMEM), here, here],
    )(*signals, own_columns)
    return (loss[0, 0], head_grad, bias_grad)


def solution(mesh):
    placed = (
        P("member", "dp", None),
        P("member", None),
        P("member", None, "dp"),
        P("member", "dp"),
        P("member", None),
        P(),
        P("member", "dp"),
        P("dp"),
    )
    return jax.shard_map(
        on_device,
        mesh=mesh,
        in_specs=placed,
        out_specs=(P(), P("member", "dp"), P("dp")),
        check_vma=False,
    )
```

time: 49.5 us -> 46 us (0.929)
  starting transfers between devices: 23.6 us -> 21.7 us
  waiting for transfers between devices: 15 us -> 16.8 us
  Pallas kernels: 4.54 us -> 2.87 us
  local copies, waits for them, and re-layouts: 4.67 us -> 3.52 us
  other arithmetic: 0.6 us -> 0 us
    ppermute x15, waiting for transfers between devices: 13.9 us -> 15.7 us  [send(): return lax.ppermute(value, axis, pairs)]
    pallas_call x5 -> x6, Pallas kernels: 4.42 us -> 2.75 us  [the longest x1 1.1 us: on_device(): call(functools.partial(logits_kernel, members, chips), [shape((3 * block...]
    ppermute x15, starting transfers between devices: 23.1 us -> 21.7 us  [send(): return lax.ppermute(value, axis, pairs)]
    broadcast_in_dim x1 -> x0, local copies, waits for them, and re-layouts: 1.24 us -> none  [on_device(): student_bias[None]]
    pallas_call x1 -> x0, other arithmetic: 0.6 us -> none  [on_device(): call(functools.partial(gradient_kernel, members, peers, block), [shape((1...]
    ppermute x8 -> x2, starting transfers between devices: 0.53 us -> 0.01 us  [swap_cores(): lax.ppermute(value, axis, [(i, i ^ 1) for i in range(lax.axis_size(axis))])]
    ppermute x8 -> x2, waiting for transfers between devices: 1.03 us -> 1.16 us  [swap_cores(): lax.ppermute(value, axis, [(i, i ^ 1) for i in range(lax.axis_size(axis))])]
  transfers between devices with their start and end apart: 23 -> 17, of which waited for: 13 -> 13; matrix products, arithmetic and copies ran while one was open for 3% -> 0% of each run, Pallas kernels for 5% -> 1%
where the time goes in v3:
time: 46 us; the launch traced here: 45.7 us
  starting transfers between devices  21.7 us (47%)
  waiting for transfers between devices  16.8 us (37%)
  local copies, waits for them, and re-layouts  3.52 us (8%)
  Pallas kernels  2.87 us (6%)
  between operations  0.72 us (2%)
    ppermute x15, starting transfers between devices, send(): return lax.ppermute(value, axis, pairs)  21.7 us
    ppermute x15, waiting for transfers between devices, send(): return lax.ppermute(value, axis, pairs)  15.7 us
    unnamed x16, local copies, waits for them, and re-layouts  3.52 us
    ppermute x2, waiting for transfers between devices, swap_cores(): lax.ppermute(value, axis, [(i, i ^ 1) for i in range(lax.axis_size(axis))])  1.16 us
    pallas_call x1, Pallas kernels, on_device(): call(functools.partial(logits_kernel, members, chips), [shape((3 * block...  1.1 us
    pallas_call x1, Pallas kernels, on_device(): call(functools.partial(gradient_kernel, members, images, classes * peers)...  1 us
  transfers between devices with their start and end apart: 17, of which 13 were waited for; matrix products, arithmetic and copies ran while one was open for 0% of the time, Pallas kernels for 1%

profile of v3, /device:TPU:0, one launch (start us, length us, event | category | flops | bytes accessed | tf_op | source)
XLA Modules:
  0.0 45.7 jit_solution(12620078352064856857)
XLA Ops:
  0.6 4.1 %collective-permute-start.5 = (bf16[32,1024]{1,0:T(8,128)(2,1)}, bf16[32,1024]{1,0:T(8,128)(2,1)S(1)}, u32[]{:S(2)}, u32[]{:S(2)}) collective-permute-start(bf16[32,1024]{1,0:T(8,128)(2,1)} %refs_7_.1), channel_id=1, source_target_pairs={{0,16},{8,24},{16,0},{24,8},{1,17},{9,25},{17,1},{25,9},{2,18},{10... | collective-permute-start | bytes 196616 | tf_op jit(solution)/shard_map/ppermute | solution.py:49
  4.7 0.0 collective-permute-start
  4.7 1.6 %collective-permute-start.4 = (bf16[32,1024]{1,0:T(8,128)(2,1)}, bf16[32,1024]{1,0:T(8,128)(2,1)S(1)}, u32[]{:S(2)}, u32[]{:S(2)}) collective-permute-start(bf16[32,1024]{1,0:T(8,128)(2,1)} %refs_7_.1), channel_id=1, source_target_pairs={{0,8},{8,0},{16,24},{24,16},{1,9},{9,1},{17,25},{25,17},{2,10},{10... | collective-permute-start | bytes 196616 | tf_op jit(solution)/shard_map/ppermute | solution.py:49
  6.3 0.0 collective-permute-start.6
  6.4 0.0 collective-permute-done.other_ref
  6.4 0.8 %copy-done.3 = bf16[1,16,1024]{2,1,0:T(8,128)(2,1)S(1)} copy-done((bf16[1,16,1024]{2,1,0:T(8,128)(2,1)S(1)}, bf16[1,16,1024]{2,1,0:T(8,128)(2,1)}, u32[]{:S(2)}) %copy-start.3) | copy-done | bytes 32792
  7.1 0.7 %copy-done.5 = f32[1,1024]{1,0:T(1,128)S(1)} copy-done((f32[1,1024]{1,0:T(1,128)S(1)}, f32[1,1024]{1,0:T(1,128)}, u32[]{:S(2)}) %copy-start.5) | copy-done | bytes 4120
  7.8 0.2 shard_map.103.refs_0_
  8.1 0.0 copy-start.6
  8.1 0.0 copy-start.7
  8.1 2.7 %collective-permute-start.3 = (bf16[32,1024]{1,0:T(8,128)(2,1)S(1)}, bf16[32,1024]{1,0:T(8,128)(2,1)S(1)}, u32[]{:S(2)}, u32[]{:S(2)}) collective-permute-start(bf16[32,1024]{1,0:T(8,128)(2,1)S(1)} %shard_map.103.refs_0_), channel_id=1, source_target_pairs={{0,6},{1,7},{2,4},{3,5},{4,2},{5,3},{6,0},{7,1},{8,14},{9,15},{10,... | collective-permute-start | bytes 196616 | tf_op jit(solution)/shard_map/ppermute | solution.py:49
  10.8 0.5 %collective-permute-start.2 = (bf16[32,1024]{1,0:T(8,128)(2,1)S(1)}, bf16[32,1024]{1,0:T(8,128)(2,1)S(1)}, u32[]{:S(2)}, u32[]{:S(2)}) collective-permute-start(bf16[32,1024]{1,0:T(8,128)(2,1)S(1)} %shard_map.103.refs_0_), channel_id=1, source_target_pairs={{0,4},{1,5},{2,6},{3,7},{4,0},{5,1},{6,2},{7,3},{8,12},{9,13},{10,... | collective-permute-start | bytes 196616 | tf_op jit(solution)/shard_map/ppermute | solution.py:49
  11.3 0.0 collective-permute-done.5.refs_5_
  11.3 0.4 collective-permute-start.1
  11.7 0.0 collective-permute-done.4.refs_4_
  11.7 0.9 %collective-permute-done.6.refs_6_ = bf16[32,1024]{1,0:T(8,128)(2,1)S(1)} collective-permute-done((bf16[32,1024]{1,0:T(8,128)(2,1)}, bf16[32,1024]{1,0:T(8,128)(2,1)S(1)}, u32[]{:S(2)}, u32[]{:S(2)}) %collective-permute-start.6) | collective-permute-done | bytes 65568 | tf_op jit(solution)/shard_map/ppermute | solution.py:49
  12.6 0.8 %collective-permute-done.3.refs_3_ = bf16[32,1024]{1,0:T(8,128)(2,1)S(1)} collective-permute-done((bf16[32,1024]{1,0:T(8,128)(2,1)S(1)}, bf16[32,1024]{1,0:T(8,128)(2,1)S(1)}, u32[]{:S(2)}, u32[]{:S(2)}) %collective-permute-start.3) | collective-permute-done | bytes 65568 | tf_op jit(solution)/shard_map/ppermute | solution.py:49
  13.3 1.7 %collective-permute-done.2.refs_2_ = bf16[32,1024]{1,0:T(8,128)(2,1)S(1)} collective-permute-done((bf16[32,1024]{1,0:T(8,128)(2,1)S(1)}, bf16[32,1024]{1,0:T(8,128)(2,1)S(1)}, u32[]{:S(2)}, u32[]{:S(2)}) %collective-permute-start.2) | collective-permute-done | bytes 65568 | tf_op jit(solution)/shard_map/ppermute | solution.py:49
  15.0 0.5 %collective-permute-done.1.refs_1_ = bf16[32,1024]{1,0:T(8,128)(2,1)S(1)} collective-permute-done((bf16[32,1024]{1,0:T(8,128)(2,1)S(1)}, bf16[32,1024]{1,0:T(8,128)(2,1)S(1)}, u32[]{:S(2)}, u32[]{:S(2)}) %collective-permute-start.1) | collective-permute-done | bytes 65568 | tf_op jit(solution)/shard_map/ppermute | solution.py:49
  15.6 0.0 copy-done.2
  15.6 0.0 copy-start
  15.6 1.1 %copy-done = bf16[1,1024,384]{2,1,0:T(8,128)(2,1)S(1)} copy-done((bf16[1,1024,384]{2,1,0:T(8,128)(2,1)S(1)}, bf16[1,1024,384]{2,1,0:T(8,128)(2,1)}, u32[]{:S(2)}) %copy-start) | copy-done | bytes 786456
  16.7 0.9 %copy-done.1 = bf16[256,384]{1,0:T(8,128)(2,1)S(1)} copy-done((bf16[256,384]{1,0:T(8,128)(2,1)S(1)}, bf16[256,384]{1,0:T(8,128)(2,1)}, u32[]{:S(2)}) %copy-start.1) | copy-done | bytes 196632
  17.6 1.1 %shard_map.104 = (bf16[112,384]{1,0:T(8,128)(2,1)S(1)}, bf16[112,384]{1,0:T(8,128)(2,1)S(1)}, bf16[112,384]{1,0:T(8,128)(2,1)S(1)}, bf16[112,384]{1,0:T(8,128)(2,1)S(1)}, bf16[128,256]{1,0:T(8,128)(2,1)S(1)}) custom-call(bf16[32,1024]{1,0:T(8,128)(2,1)S(1)} %shard_map.103.refs_0_, bf16[32,1024]{1,0:T(8,128)(2,1)S(1)} %collective-permute-done.1.refs_1_, ...), custom_call_target="tpu_custom_call" | custom-call | tf_op jit(solution)/shard_map/pallas_call | solution.py:332
  18.8 1.3 %collective-permute-start.7 = (bf16[112,384]{1,0:T(8,128)(2,1)S(1)}, bf16[112,384]{1,0:T(8,128)(2,1)S(1)}, u32[]{:S(2)}, u32[]{:S(2)}) collective-permute-start(bf16[112,384]{1,0:T(8,128)(2,1)S(1)} %get-tuple-element.15), channel_id=1, source_target_pairs={{0,8},{8,0},{16,24},{24,16},{1,9},{9,1},{17,25},{25,17},{2,10},{10... | collective-permute-start | bytes 258056 | tf_op jit(solution)/shard_map/ppermute | solution.py:49
  20.0 3.0 %collective-permute-start.8 = (bf16[112,384]{1,0:T(8,128)(2,1)S(1)}, bf16[112,384]{1,0:T(8,128)(2,1)S(1)}, u32[]{:S(2)}, u32[]{:S(2)}) collective-permute-start(bf16[112,384]{1,0:T(8,128)(2,1)S(1)} %get-tuple-element.16), channel_id=1, source_target_pairs={{0,16},{8,24},{16,0},{24,8},{1,17},{9,25},{17,1},{25,9},{2,18},{10... | collective-permute-start | bytes 258056 | tf_op jit(solution)/shard_map/ppermute | solution.py:49
  23.0 0.2 collective-permute-start.9
  23.2 0.5 %collective-permute-done.7.refs_1_ = bf16[112,384]{1,0:T(8,128)(2,1)S(1)} collective-permute-done((bf16[112,384]{1,0:T(8,128)(2,1)S(1)}, bf16[112,384]{1,0:T(8,128)(2,1)S(1)}, u32[]{:S(2)}, u32[]{:S(2)}) %collective-permute-start.7) | collective-permute-done | bytes 86048 | tf_op jit(solution)/shard_map/ppermute | solution.py:49
  23.8 3.9 %collective-permute-done.8.refs_2_ = bf16[112,384]{1,0:T(8,128)(2,1)S(1)} collective-permute-done((bf16[112,384]{1,0:T(8,128)(2,1)S(1)}, bf16[112,384]{1,0:T(8,128)(2,1)S(1)}, u32[]{:S(2)}, u32[]{:S(2)}) %collective-permute-start.8) | collective-permute-done | bytes 86048 | tf_op jit(solution)/shard_map/ppermute | solution.py:49
  27.6 1.8 %collective-permute-done.9.refs_3_ = bf16[112,384]{1,0:T(8,128)(2,1)S(1)} collective-permute-done((bf16[112,384]{1,0:T(8,128)(2,1)S(1)}, bf16[112,384]{1,0:T(8,128)(2,1)S(1)}, u32[]{:S(2)}, u32[]{:S(2)}) %collective-permute-start.9) | collective-permute-done | bytes 86048 | tf_op jit(solution)/shard_map/ppermute | solution.py:49
  29.4 0.2 shard_map.105
  29.6 0.0 collective-permute-start.10
  29.6 1.2 %collective-permute-done.10.other_ref = f32[8,128]{1,0:T(8,128)S(1)} collective-permute-done((f32[8,128]{1,0:T(8,128)S(1)}, f32[8,128]{1,0:T(8,128)S(1)}, u32[]{:S(2)}, u32[]{:S(2)}) %collective-permute-start.10) | collective-permute-done | bytes 4128 | tf_op jit(solution)/shard_map/ppermute | solution.py:53
  30.8 1.6 %collective-permute-start.13 = (f32[8,128]{1,0:T(8,128)S(1)}, f32[8,128]{1,0:T(8,128)S(1)}, u32[]{:S(2)}, u32[]{:S(2)}) collective-permute-start(f32[8,128]{1,0:T(8,128)S(1)} %shard_map.106.refs_0_), channel_id=1, source_target_pairs={{0,6},{1,7},{2,4},{3,5},{4,2},{5,3},{6,0},{7,1},{8,14},{9,15},{10,... | collective-permute-start | bytes 12296 | tf_op jit(solution)/shard_map/ppermute | solution.py:49
  32.4 0.9 %collective-permute-start.12 = (f32[8,128]{1,0:T(8,128)S(1)}, f32[8,128]{1,0:T(8,128)S(1)}, u32[]{:S(2)}, u32[]{:S(2)}) collective-permute-start(f32[8,128]{1,0:T(8,128)S(1)} %shard_map.106.refs_0_), channel_id=1, source_target_pairs={{0,4},{1,5},{2,6},{3,7},{4,0},{5,1},{6,2},{7,3},{8,12},{9,13},{10,... | collective-permute-start | bytes 12296 | tf_op jit(solution)/shard_map/ppermute | solution.py:49
  33.3 1.1 %collective-permute-start.11 = (f32[8,128]{1,0:T(8,128)S(1)}, f32[8,128]{1,0:T(8,128)S(1)}, u32[]{:S(2)}, u32[]{:S(2)}) collective-permute-start(f32[8,128]{1,0:T(8,128)S(1)} %shard_map.106.refs_0_), channel_id=1, source_target_pairs={{0,2},{1,3},{2,0},{3,1},{4,6},{5,7},{6,4},{7,5},{8,10},{9,11},{10,... | collective-permute-start | bytes 12296 | tf_op jit(solution)/shard_map/ppermute | solution.py:49
  34.4 0.1 shard_map.107.refs_6_
  34.5 0.9 %collective-permute-done.13.refs_3_ = f32[8,128]{1,0:T(8,128)S(1)} collective-permute-done((f32[8,128]{1,0:T(8,128)S(1)}, f32[8,128]{1,0:T(8,128)S(1)}, u32[]{:S(2)}, u32[]{:S(2)}) %collective-permute-start.13) | collective-permute-done | bytes 4128 | tf_op jit(solution)/shard_map/ppermute | solution.py:49
  35.4 0.6 %collective-permute-done.12.refs_2_ = f32[8,128]{1,0:T(8,128)S(1)} collective-permute-done((f32[8,128]{1,0:T(8,128)S(1)}, f32[8,128]{1,0:T(8,128)S(1)}, u32[]{:S(2)}, u32[]{:S(2)}) %collective-permute-start.12) | collective-permute-done | bytes 4128 | tf_op jit(solution)/shard_map/ppermute | solution.py:49
  36.0 0.9 %collective-permute-done.11.refs_1_ = f32[8,128]{1,0:T(8,128)S(1)} collective-permute-done((f32[8,128]{1,0:T(8,128)S(1)}, f32[8,128]{1,0:T(8,128)S(1)}, u32[]{:S(2)}, u32[]{:S(2)}) %collective-permute-start.11) | collective-permute-done | bytes 4128 | tf_op jit(solution)/shard_map/ppermute | solution.py:49
  36.9 0.1 shard_map.108.refs_0_
  37.0 2.4 %collective-permute-start.16 = (bf16[48,384]{1,0:T(8,128)(2,1)S(1)}, bf16[48,384]{1,0:T(8,128)(2,1)S(1)}, u32[]{:S(2)}, u32[]{:S(2)}) collective-permute-start(bf16[48,384]{1,0:T(8,128)(2,1)S(1)} %shard_map.108.refs_0_), channel_id=1, source_target_pairs={{0,24},{8,16},{16,8},{24,0},{1,25},{9,17},{17,9},{25,1},{2,26},{10... | collective-permute-start | bytes 110600 | tf_op jit(solution)/shard_map/ppermute | solution.py:49
  39.4 0.7 %collective-permute-start.15 = (bf16[48,384]{1,0:T(8,128)(2,1)S(1)}, bf16[48,384]{1,0:T(8,128)(2,1)S(1)}, u32[]{:S(2)}, u32[]{:S(2)}) collective-permute-start(bf16[48,384]{1,0:T(8,128)(2,1)S(1)} %shard_map.108.refs_0_), channel_id=1, source_target_pairs={{0,16},{8,24},{16,0},{24,8},{1,17},{9,25},{17,1},{25,9},{2,18},{10... | collective-permute-start | bytes 110600 | tf_op jit(solution)/shard_map/ppermute | solution.py:49
  40.1 1.4 %collective-permute-start.14 = (bf16[48,384]{1,0:T(8,128)(2,1)S(1)}, bf16[48,384]{1,0:T(8,128)(2,1)S(1)}, u32[]{:S(2)}, u32[]{:S(2)}) collective-permute-start(bf16[48,384]{1,0:T(8,128)(2,1)S(1)} %shard_map.108.refs_0_), channel_id=1, source_target_pairs={{0,8},{8,0},{16,24},{24,16},{1,9},{9,1},{17,25},{25,17},{2,10},{10... | collective-permute-start | bytes 110600 | tf_op jit(solution)/shard_map/ppermute | solution.py:49
  41.5 1.7 %collective-permute-done.16.refs_3_ = bf16[48,384]{1,0:T(8,128)(2,1)S(1)} collective-permute-done((bf16[48,384]{1,0:T(8,128)(2,1)S(1)}, bf16[48,384]{1,0:T(8,128)(2,1)S(1)}, u32[]{:S(2)}, u32[]{:S(2)}) %collective-permute-start.16) | collective-permute-done | bytes 36896 | tf_op jit(solution)/shard_map/ppermute | solution.py:49
  43.2 1.5 %collective-permute-done.15.refs_2_ = bf16[48,384]{1,0:T(8,128)(2,1)S(1)} collective-permute-done((bf16[48,384]{1,0:T(8,128)(2,1)S(1)}, bf16[48,384]{1,0:T(8,128)(2,1)S(1)}, u32[]{:S(2)}, u32[]{:S(2)}) %collective-permute-start.15) | collective-permute-done | bytes 36896 | tf_op jit(solution)/shard_map/ppermute | solution.py:49
  44.7 0.0 collective-permute-done.14.refs_1_
  44.7 1.0 %shard_map.109 = (f32[1,1]{1,0:T(1,128)}, f32[256,384]{1,0:T(8,128)}, f32[384]{0:T(512)}) custom-call(bf16[48,384]{1,0:T(8,128)(2,1)S(1)} %shard_map.108.refs_0_, bf16[48,384]{1,0:T(8,128)(2,1)S(1)} %collective-permute-done.14.refs_1_, bf16[48,384]{1,0:T(8,128)(2,1)S(1)} %collective-permute-done.15.refs_2_, ...), custom_call_target="tpu_custom_call" | custom-call | tf_op jit(solution)/shard_map/pallas_call | solution.py:375
  (9 shorter events, 0.0 us)
Async XLA Ops:
  0.6 10.7 %collective-permute-start.5 = (bf16[32,1024]{1,0:T(8,128)(2,1)}, bf16[32,1024]{1,0:T(8,128)(2,1)S(1)}, u32[]{:S(2)}, u32[]{:S(2)}) collective-permute-start(bf16[32,1024]{1,0:T(8,128)(2,1)} %refs_7_.1), channel_id=1, source_target_pairs={{0,16},{8,24},{16,0},{24,8},{1,17},{9,25},{17,1},{25,9},{2,18},{10... | collective-permute-start | bytes 196616 | tf_op jit(solution)/shard_map/ppermute | solution.py:49
  4.7 10.8 %copy-start.2 = (bf16[32,1024]{1,0:T(8,128)(2,1)S(1)}, bf16[32,1024]{1,0:T(8,128)(2,1)}, u32[]{:S(2)}) copy-start(bf16[32,1024]{1,0:T(8,128)(2,1)} %refs_7_.1) | copy-start | bytes 196612
  4.7 1.6 %collective-permute-start = (bf16[16,1024]{1,0:T(8,128)(2,1)}, bf16[16,1024]{1,0:T(8,128)(2,1)S(1)}, u32[]{:S(2)}, u32[]{:S(2)}) collective-permute-start(bf16[16,1024]{1,0:T(8,128)(2,1)} %bitcast.5), channel_id=1, source_target_pairs={{0,1},{1,0},{2,3},{3,2},{4,5},{5,4},{6,7},{7,6},{8,9},{9,8},{10,11... | collective-permute-start | bytes 98312 | tf_op jit(solution)/shard_map/ppermute | solution.py:53
  4.7 6.9 %collective-permute-start.4 = (bf16[32,1024]{1,0:T(8,128)(2,1)}, bf16[32,1024]{1,0:T(8,128)(2,1)S(1)}, u32[]{:S(2)}, u32[]{:S(2)}) collective-permute-start(bf16[32,1024]{1,0:T(8,128)(2,1)} %refs_7_.1), channel_id=1, source_target_pairs={{0,8},{8,0},{16,24},{24,16},{1,9},{9,1},{17,25},{25,17},{2,10},{10... | collective-permute-start | bytes 196616 | tf_op jit(solution)/shard_map/ppermute | solution.py:49
  6.3 6.3 %collective-permute-start.6 = (bf16[32,1024]{1,0:T(8,128)(2,1)}, bf16[32,1024]{1,0:T(8,128)(2,1)S(1)}, u32[]{:S(2)}, u32[]{:S(2)}) collective-permute-start(bf16[32,1024]{1,0:T(8,128)(2,1)} %refs_7_.1), channel_id=1, source_target_pairs={{0,24},{8,16},{16,8},{24,0},{1,25},{9,17},{17,9},{25,1},{2,26},{10... | collective-permute-start | bytes 196616 | tf_op jit(solution)/shard_map/ppermute | solution.py:49
  6.4 0.8 %copy-start.3 = (bf16[1,16,1024]{2,1,0:T(8,128)(2,1)S(1)}, bf16[1,16,1024]{2,1,0:T(8,128)(2,1)}, u32[]{:S(2)}) copy-start(bf16[1,16,1024]{2,1,0:T(8,128)(2,1)} %param.8) | copy-start | bytes 98308
  7.1 0.7 %copy-start.5 = (f32[1,1024]{1,0:T(1,128)S(1)}, f32[1,1024]{1,0:T(1,128)}, u32[]{:S(2)}) copy-start(f32[1,1024]{1,0:T(1,128)} %refs_1_.1) | copy-start | bytes 12292
  7.8 7.8 %copy-start.4 = (f32[1024]{0:T(1024)S(1)}, f32[1024]{0:T(1024)}, u32[]{:S(2)}) copy-start(f32[1024]{0:T(1024)} %param.13) | copy-start | bytes 12292
  8.1 7.5 %copy-start.6 = (f32[384]{0:T(512)S(1)}, f32[384]{0:T(512)}, u32[]{:S(2)}) copy-start(f32[384]{0:T(512)} %refs_12_.1) | copy-start | bytes 4612
  8.1 7.5 %copy-start.7 = (f32[1,384]{1,0:T(1,128)S(1)}, f32[1,384]{1,0:T(1,128)}, u32[]{:S(2)}) copy-start(f32[1,384]{1,0:T(1,128)} %refs_11_.1) | copy-start | bytes 4612
  8.1 5.3 %collective-permute-start.3 = (bf16[32,1024]{1,0:T(8,128)(2,1)S(1)}, bf16[32,1024]{1,0:T(8,128)(2,1)S(1)}, u32[]{:S(2)}, u32[]{:S(2)}) collective-permute-start(bf16[32,1024]{1,0:T(8,128)(2,1)S(1)} %shard_map.103.refs_0_), channel_id=1, source_target_pairs={{0,6},{1,7},{2,4},{3,5},{4,2},{5,3},{6,0},{7,1},{8,14},{9,15},{10,... | collective-permute-start | bytes 196616 | tf_op jit(solution)/shard_map/ppermute | solution.py:49
  10.8 4.3 %collective-permute-start.2 = (bf16[32,1024]{1,0:T(8,128)(2,1)S(1)}, bf16[32,1024]{1,0:T(8,128)(2,1)S(1)}, u32[]{:S(2)}, u32[]{:S(2)}) collective-permute-start(bf16[32,1024]{1,0:T(8,128)(2,1)S(1)} %shard_map.103.refs_0_), channel_id=1, source_target_pairs={{0,4},{1,5},{2,6},{3,7},{4,0},{5,1},{6,2},{7,3},{8,12},{9,13},{10,... | collective-permute-start | bytes 196616 | tf_op jit(solution)/shard_map/ppermute | solution.py:49
  11.3 4.3 %collective-permute-start.1 = (bf16[32,1024]{1,0:T(8,128)(2,1)S(1)}, bf16[32,1024]{1,0:T(8,128)(2,1)S(1)}, u32[]{:S(2)}, u32[]{:S(2)}) collective-permute-start(bf16[32,1024]{1,0:T(8,128)(2,1)S(1)} %shard_map.103.refs_0_), channel_id=1, source_target_pairs={{0,2},{1,3},{2,0},{3,1},{4,6},{5,7},{6,4},{7,5},{8,10},{9,11},{10,... | collective-permute-start | bytes 196616 | tf_op jit(solution)/shard_map/ppermute | solution.py:49
  15.6 1.1 %copy-start = (bf16[1,1024,384]{2,1,0:T(8,128)(2,1)S(1)}, bf16[1,1024,384]{2,1,0:T(8,128)(2,1)}, u32[]{:S(2)}) copy-start(bf16[1,1024,384]{2,1,0:T(8,128)(2,1)} %param.10) | copy-start | bytes 2359300
  16.7 0.9 %copy-start.1 = (bf16[256,384]{1,0:T(8,128)(2,1)S(1)}, bf16[256,384]{1,0:T(8,128)(2,1)}, u32[]{:S(2)}) copy-start(bf16[256,384]{1,0:T(8,128)(2,1)} %refs_10_.1) | copy-start | bytes 589828
  18.8 5.0 %collective-permute-start.7 = (bf16[112,384]{1,0:T(8,128)(2,1)S(1)}, bf16[112,384]{1,0:T(8,128)(2,1)S(1)}, u32[]{:S(2)}, u32[]{:S(2)}) collective-permute-start(bf16[112,384]{1,0:T(8,128)(2,1)S(1)} %get-tuple-element.15), channel_id=1, source_target_pairs={{0,8},{8,0},{16,24},{24,16},{1,9},{9,1},{17,25},{25,17},{2,10},{10... | collective-permute-start | bytes 258056 | tf_op jit(solution)/shard_map/ppermute | solution.py:49
  20.0 7.6 %collective-permute-start.8 = (bf16[112,384]{1,0:T(8,128)(2,1)S(1)}, bf16[112,384]{1,0:T(8,128)(2,1)S(1)}, u32[]{:S(2)}, u32[]{:S(2)}) collective-permute-start(bf16[112,384]{1,0:T(8,128)(2,1)S(1)} %get-tuple-element.16), channel_id=1, source_target_pairs={{0,16},{8,24},{16,0},{24,8},{1,17},{9,25},{17,1},{25,9},{2,18},{10... | collective-permute-start | bytes 258056 | tf_op jit(solution)/shard_map/ppermute | solution.py:49
  23.0 6.4 %collective-permute-start.9 = (bf16[112,384]{1,0:T(8,128)(2,1)S(1)}, bf16[112,384]{1,0:T(8,128)(2,1)S(1)}, u32[]{:S(2)}, u32[]{:S(2)}) collective-permute-start(bf16[112,384]{1,0:T(8,128)(2,1)S(1)} %get-tuple-element.17), channel_id=1, source_target_pairs={{0,24},{8,16},{16,8},{24,0},{1,25},{9,17},{17,9},{25,1},{2,26},{10... | collective-permute-start | bytes 258056 | tf_op jit(solution)/shard_map/ppermute | solution.py:49
  29.6 1.2 %collective-permute-start.10 = (f32[8,128]{1,0:T(8,128)S(1)}, f32[8,128]{1,0:T(8,128)S(1)}, u32[]{:S(2)}, u32[]{:S(2)}) collective-permute-start(f32[8,128]{1,0:T(8,128)S(1)} %get-tuple-element.18.own_ref.refs_4_), channel_id=1, source_target_pairs={{0,1},{1,0},{2,3},{3,2},{4,5},{5,4},{6,7},{7,6},{8,9},{9,8},{10,11... | collective-permute-start | bytes 12296 | tf_op jit(solution)/shard_map/ppermute | solution.py:53
  30.8 4.6 %collective-permute-start.13 = (f32[8,128]{1,0:T(8,128)S(1)}, f32[8,128]{1,0:T(8,128)S(1)}, u32[]{:S(2)}, u32[]{:S(2)}) collective-permute-start(f32[8,128]{1,0:T(8,128)S(1)} %shard_map.106.refs_0_), channel_id=1, source_target_pairs={{0,6},{1,7},{2,4},{3,5},{4,2},{5,3},{6,0},{7,1},{8,14},{9,15},{10,... | collective-permute-start | bytes 12296 | tf_op jit(solution)/shard_map/ppermute | solution.py:49
  32.4 3.6 %collective-permute-start.12 = (f32[8,128]{1,0:T(8,128)S(1)}, f32[8,128]{1,0:T(8,128)S(1)}, u32[]{:S(2)}, u32[]{:S(2)}) collective-permute-start(f32[8,128]{1,0:T(8,128)S(1)} %shard_map.106.refs_0_), channel_id=1, source_target_pairs={{0,4},{1,5},{2,6},{3,7},{4,0},{5,1},{6,2},{7,3},{8,12},{9,13},{10,... | collective-permute-start | bytes 12296 | tf_op jit(solution)/shard_map/ppermute | solution.py:49
  33.3 3.6 %collective-permute-start.11 = (f32[8,128]{1,0:T(8,128)S(1)}, f32[8,128]{1,0:T(8,128)S(1)}, u32[]{:S(2)}, u32[]{:S(2)}) collective-permute-start(f32[8,128]{1,0:T(8,128)S(1)} %shard_map.106.refs_0_), channel_id=1, source_target_pairs={{0,2},{1,3},{2,0},{3,1},{4,6},{5,7},{6,4},{7,5},{8,10},{9,11},{10,... | collective-permute-start | bytes 12296 | tf_op jit(solution)/shard_map/ppermute | solution.py:49
  37.0 6.1 %collective-permute-start.16 = (bf16[48,384]{1,0:T(8,128)(2,1)S(1)}, bf16[48,384]{1,0:T(8,128)(2,1)S(1)}, u32[]{:S(2)}, u32[]{:S(2)}) collective-permute-start(bf16[48,384]{1,0:T(8,128)(2,1)S(1)} %shard_map.108.refs_0_), channel_id=1, source_target_pairs={{0,24},{8,16},{16,8},{24,0},{1,25},{9,17},{17,9},{25,1},{2,26},{10... | collective-permute-start | bytes 110600 | tf_op jit(solution)/shard_map/ppermute | solution.py:49
  39.4 5.3 %collective-permute-start.15 = (bf16[48,384]{1,0:T(8,128)(2,1)S(1)}, bf16[48,384]{1,0:T(8,128)(2,1)S(1)}, u32[]{:S(2)}, u32[]{:S(2)}) collective-permute-start(bf16[48,384]{1,0:T(8,128)(2,1)S(1)} %shard_map.108.refs_0_), channel_id=1, source_target_pairs={{0,16},{8,24},{16,0},{24,8},{1,17},{9,25},{17,1},{25,9},{2,18},{10... | collective-permute-start | bytes 110600 | tf_op jit(solution)/shard_map/ppermute | solution.py:49
  40.1 4.6 %collective-permute-start.14 = (bf16[48,384]{1,0:T(8,128)(2,1)S(1)}, bf16[48,384]{1,0:T(8,128)(2,1)S(1)}, u32[]{:S(2)}, u32[]{:S(2)}) collective-permute-start(bf16[48,384]{1,0:T(8,128)(2,1)S(1)} %shard_map.108.refs_0_), channel_id=1, source_target_pairs={{0,8},{8,0},{16,24},{24,16},{1,9},{9,1},{17,25},{25,17},{2,10},{10... | collective-permute-start | bytes 110600 | tf_op jit(solution)/shard_map/ppermute | solution.py:49

commit v4 on v3

--- a/solution.py
+++ b/solution.py
@@ -125,15 +125,15 @@
     return pl.ds(pl.multiple_of(at * rows, rows), rows)
 
 
-def prepare_kernel(other_ref, *refs):
-    sources, (pair_ref, own_ref, gain_ref, sems) = refs[:2], refs[2:]
-    copies = fetch(sources, (own_ref, gain_ref), sems)
+def first_kernel(out_ref):
+    out_ref[...] = jnp.zeros_like(out_ref)
+
+
+def pair_kernel(own_ref, other_ref, _, pair_ref):
     core = lax.rem(lax.axis_index("dp"), jnp.int32(2))
-    rows = other_ref.shape[0]
-    for copy in copies:
-        copy.wait()
-    pair_ref[slot(core, rows), :] = normed(own_ref[...], gain_ref[...])
-    pair_ref[slot(1 - core, rows), :] = normed(other_ref[...], gain_ref[...])
+    rows = own_ref.shape[0]
+    pair_ref[slot(core, rows), :] = own_ref[...]
+    pair_ref[slot(1 - core, rows), :] = other_ref[...]
 
 
 def packed3(row, rows, lanes):
@@ -146,11 +146,11 @@
 def logits_kernel(members, chips, *refs):
     pairs, refs = refs[:chips], refs[chips:]
     students, refs = refs[: members - 1], refs[members - 1 :]
-    sources, refs = refs[:6], refs[6:]
+    sources, refs = refs[:7], refs[7:]
     payloads, refs = refs[:members], refs[members:]
     columns_ref, gathered, held, shifted_ref, lse_ref, partial_ref, *params = refs
-    own_ref, gain_ref, head_ref, student_ref, bias_ref, student_bias_ref, sems = params
-    copies = fetch(sources, params[:6], sems)
+    own_ref, student_gain_ref, gain_ref, head_ref, student_ref, bias_ref, student_bias_ref, sems = params
+    copies = fetch(sources, params[:7], sems)
     mine, chip = lax.axis_index("member"), lax.axis_index("dp") // 2
     for k in range(chips):
         at = mixed(chip, k, chips, sender)
@@ -162,7 +162,7 @@
     for k in range(members):
         source = own_ref if k == 0 else students[k - 1]
         at = slot(mixed(mine, k, members, sender), block)
-        held[at, :] = normed(source[...], gain_ref[...])
+        held[at, :] = normed(source[...], student_gain_ref[...])
     if width % LANES == 0:
         columns_ref[...] = held[:, pl.ds(pl.multiple_of(mine * width, LANES), width)]
     else:
@@ -172,7 +172,8 @@
             def _(j=j):
                 columns_ref[...] = held[:, j * width : (j + 1) * width]
 
-    logits = jnp.dot(gathered[...], head_ref[...], preferred_element_type=F32) + bias_ref[...]
+    values = normed(gathered[...], gain_ref[...])
+    logits = jnp.dot(values, head_ref[...], preferred_element_type=F32) + bias_ref[...]
     top = jnp.max(logits, axis=1, keepdims=True)
     lse = top + jnp.log(jnp.sum(jnp.exp(logits - top), axis=1, keepdims=True))
     shifted_ref[...] = (logits - lse).astype(BF16)
@@ -251,14 +252,15 @@
     used = lax.broadcasted_iota(jnp.int32, (1, LANES), 1) < block
     alpha_sum = jnp.where(used, everything[members : members + 1, :], 1.0)
     shift = to_column(di_gamma(alpha_sum) + own - norm_total, block)
-    signal_ref[0:block, :] = (alphas_ref[...] * (inner_ref[...] - shift)).astype(BF16)
+    width = alphas_ref.shape[1]
+    signal_ref[:, 0:width] = (alphas_ref[...] * (inner_ref[...] - shift)).astype(BF16)
     terms = (
         everything[members + 1 : members + 2, :]
         - log_gamma(alpha_sum, jnp.log(alpha_sum))
         + norm_total * (alpha_sum - float(classes))
     )
     loss = jnp.sum(jnp.where(used, terms, 0.0), axis=1, keepdims=True)
-    signal_ref[block:, :] = packed3(loss, PAD, alphas_ref.shape[1])
+    signal_ref[:, width:] = packed3(loss, block, LANES)
 
 
 def gradient_kernel(members, images, classes, *refs):
@@ -266,10 +268,11 @@
     columns_ref, loss_ref, grad_ref, bias_ref, held, losses = refs
     mine = lax.axis_index("member")
     block = images // members
+    width = held.shape[1]
     for k in range(members):
         at = mixed(mine, k, members, sender)
-        held[slot(at, block), :] = signals[k][0:block, :]
-        tail = signals[k][block:, 0:LANES].astype(F32)
+        held[slot(at, block), :] = signals[k][:, 0:width]
+        tail = signals[k][:, width:].astype(F32)
         losses[pl.ds(at, 1), :] = tail[0:1, :] + tail[1:2, :] + tail[2:3, :]
     signal = held[...]
     grad = lax.dot_general(
@@ -280,8 +283,10 @@
     loss_ref[0, 0] = jnp.sum(losses[:, 0:1]) * (1.0 / (images * classes))
 
 
-def call(kernel, out_shape, scratch=(), in_specs=None, out_specs=None):
+def call(kernel, out_shape, scratch=(), in_specs=None, out_specs=None, flops=0):
     extra = {}
+    if flops:
+        extra["cost_estimate"] = pl.CostEstimate(flops=flops, bytes_accessed=0, transcendentals=0)
     if in_specs is not None:
         extra["in_specs"] = in_specs
     if out_specs is not None:
@@ -318,16 +323,8 @@
 
     other = swap_cores(feats, "dp")
     students = [send(student_feats, "member", k) for k in range(1, members)]
-    pair = call(
-        prepare_kernel,
-        shape((2 * rows, depth), BF16),
-        [
-            pltpu.VMEM((rows, depth), BF16),
-            pltpu.VMEM((1, depth), F32),
-            pltpu.SemaphoreType.DMA((2,)),
-        ],
-        [here] + [far] * 2,
-    )(other, feats, teacher_gain)
+    first = call(first_kernel, shape((8, LANES), F32), flops=1 << 33)()
+    pair = call(pair_kernel, shape((2 * rows, depth), BF16), flops=1 << 33)(feats, other, first)
     pairs = [pair] + [send(pair, "dp", k, 2) for k in range(1, chips)]
     *payloads, own_columns = call(
         functools.partial(logits_kernel, members, chips),
@@ -340,18 +337,20 @@
             pltpu.VMEM((images, classes), F32),
             pltpu.VMEM((block, depth), BF16),
             pltpu.VMEM((1, depth), F32),
+            pltpu.VMEM((1, depth), F32),
             pltpu.VMEM((depth, classes), BF16),
             pltpu.VMEM((width, classes), BF16),
             pltpu.VMEM((1, classes), F32),
             pltpu.VMEM((classes,), F32),
-            pltpu.SemaphoreType.DMA((6,)),
+            pltpu.SemaphoreType.DMA((7,)),
         ],
-        [here] * (chips + members - 1) + [far] * 6,
+        [here] * (chips + members - 1) + [far] * 7,
     )(
         *pairs,
         *students,
         student_feats,
         student_gain[None],
+        teacher_gain,
         teacher_head[0],
         student_head,
         teacher_bias,
@@ -368,7 +367,7 @@
     smalls = [small] + [send(small, "dp", k, 2) for k in range(1, chips)]
     signal = call(
         functools.partial(signal_kernel, members, chips, images, classes * peers),
-        shape((block + PAD, classes), BF16),
+        shape((block, classes + LANES), BF16),
         [pltpu.VMEM((chips, small_rows, LANES), F32)],
     )(*smalls, own, alphas, inner)
     signals = [signal] + [send(signal, "member", k) for k in range(1, members)]

time: 46 us -> 44.2 us (0.961)
  local copies, waits for them, and re-layouts: 3.52 us -> 0.04 us
  waiting for transfers between devices: 16.8 us -> 18.6 us
    unnamed x16, local copies, waits for them, and re-layouts: 3.52 us -> 0.04 us
    ppermute x2, waiting for transfers between devices: 1.16 us -> 2.52 us  [swap_cores(): lax.ppermute(value, axis, [(i, i ^ 1) for i in range(lax.axis_size(axis))])]
    ppermute x15, waiting for transfers between devices: 15.7 us -> 16.1 us  [send(): return lax.ppermute(value, axis, pairs)]
  transfers between devices with their start and end apart: 17 -> 17, of which waited for: 13 -> 14; matrix products, arithmetic and copies ran while one was open for 0% -> 0% of each run, Pallas kernels for 1% -> 0%
where the time goes in v4:
time: 44.2 us; the launch traced here: 44 us
  starting transfers between devices  21.7 us (49%)
  waiting for transfers between devices  18.6 us (42%)
  Pallas kernels  2.85 us (6%)
  between operations  0.77 us (2%)
    ppermute x15, starting transfers between devices, send(): return lax.ppermute(value, axis, pairs)  21.7 us
    ppermute x15, waiting for transfers between devices, send(): return lax.ppermute(value, axis, pairs)  16.1 us
    ppermute x2, waiting for transfers between devices, swap_cores(): lax.ppermute(value, axis, [(i, i ^ 1) for i in range(lax.axis_size(axis))])  2.52 us
    pallas_call x1, Pallas kernels, on_device(): call(functools.partial(logits_kernel, members, chips), [shape((3 * block...  1.32 us
    pallas_call x1, Pallas kernels, on_device(): call(functools.partial(gradient_kernel, members, images, classes * peers)...  1 us
  transfers between devices with their start and end apart: 17, of which 14 were waited for; matrix products, arithmetic and copies ran while one was open for 0% of the time, Pallas kernels for 0%

profile of v4, /device:TPU:0, one launch (start us, length us, event | category | flops | bytes accessed | tf_op | source)
XLA Modules:
  0.0 44.0 jit_solution(10473396199421098549)
XLA Ops:
  0.6 4.1 %collective-permute-start.5 = (bf16[32,1024]{1,0:T(8,128)(2,1)}, bf16[32,1024]{1,0:T(8,128)(2,1)S(1)}, u32[]{:S(2)}, u32[]{:S(2)}) collective-permute-start(bf16[32,1024]{1,0:T(8,128)(2,1)} %refs_7_.1), channel_id=1, source_target_pairs={{0,16},{8,24},{16,0},{24,8},{1,17},{9,25},{17,1},{25,9},{2,18},{10... | collective-permute-start | bytes 196616 | tf_op jit(solution)/shard_map/ppermute | solution.py:49
  4.7 1.6 %collective-permute-start.4 = (bf16[32,1024]{1,0:T(8,128)(2,1)}, bf16[32,1024]{1,0:T(8,128)(2,1)S(1)}, u32[]{:S(2)}, u32[]{:S(2)}) collective-permute-start(bf16[32,1024]{1,0:T(8,128)(2,1)} %refs_7_.1), channel_id=1, source_target_pairs={{0,8},{8,0},{16,24},{24,16},{1,9},{9,1},{17,25},{25,17},{2,10},{10... | collective-permute-start | bytes 196616 | tf_op jit(solution)/shard_map/ppermute | solution.py:49
  6.3 0.0 collective-permute-start.6
  6.3 0.0 collective-permute-start
  6.3 0.0 copy-start
  6.3 0.0 copy-start.1
  6.4 0.0 copy-start.2
  6.4 1.4 %collective-permute-done.other_ref = bf16[16,1024]{1,0:T(8,128)(2,1)S(1)} collective-permute-done((bf16[16,1024]{1,0:T(8,128)(2,1)}, bf16[16,1024]{1,0:T(8,128)(2,1)S(1)}, u32[]{:S(2)}, u32[]{:S(2)}) %collective-permute-start) | collective-permute-done | bytes 32800 | tf_op jit(solution)/shard_map/ppermute | solution.py:53
  7.7 0.0 copy-done.7
  7.8 0.0 copy-start.5
  7.8 0.0 copy-start.6
  7.8 2.7 %collective-permute-start.3 = (bf16[32,1024]{1,0:T(8,128)(2,1)S(1)}, bf16[32,1024]{1,0:T(8,128)(2,1)S(1)}, u32[]{:S(2)}, u32[]{:S(2)}) collective-permute-start(bf16[32,1024]{1,0:T(8,128)(2,1)S(1)} %shard_map.104.refs_0_), channel_id=1, source_target_pairs={{0,6},{1,7},{2,4},{3,5},{4,2},{5,3},{6,0},{7,1},{8,14},{9,15},{10,... | collective-permute-start | bytes 196616 | tf_op jit(solution)/shard_map/ppermute | solution.py:49
  10.5 0.5 %collective-permute-start.2 = (bf16[32,1024]{1,0:T(8,128)(2,1)S(1)}, bf16[32,1024]{1,0:T(8,128)(2,1)S(1)}, u32[]{:S(2)}, u32[]{:S(2)}) collective-permute-start(bf16[32,1024]{1,0:T(8,128)(2,1)S(1)} %shard_map.104.refs_0_), channel_id=1, source_target_pairs={{0,4},{1,5},{2,6},{3,7},{4,0},{5,1},{6,2},{7,3},{8,12},{9,13},{10,... | collective-permute-start | bytes 196616 | tf_op jit(solution)/shard_map/ppermute | solution.py:49
  11.0 0.0 collective-permute-done.5.refs_5_
  11.0 0.3 collective-permute-start.1
  11.3 0.0 collective-permute-done.4.refs_4_
  11.3 1.2 %collective-permute-done.6.refs_6_ = bf16[32,1024]{1,0:T(8,128)(2,1)S(1)} collective-permute-done((bf16[32,1024]{1,0:T(8,128)(2,1)}, bf16[32,1024]{1,0:T(8,128)(2,1)S(1)}, u32[]{:S(2)}, u32[]{:S(2)}) %collective-permute-start.6) | collective-permute-done | bytes 65568 | tf_op jit(solution)/shard_map/ppermute | solution.py:49
  12.6 0.4 collective-permute-done.3.refs_3_
  13.0 1.8 %collective-permute-done.2.refs_2_ = bf16[32,1024]{1,0:T(8,128)(2,1)S(1)} collective-permute-done((bf16[32,1024]{1,0:T(8,128)(2,1)S(1)}, bf16[32,1024]{1,0:T(8,128)(2,1)S(1)}, u32[]{:S(2)}, u32[]{:S(2)}) %collective-permute-start.2) | collective-permute-done | bytes 65568 | tf_op jit(solution)/shard_map/ppermute | solution.py:49
  14.8 0.5 %collective-permute-done.1.refs_1_ = bf16[32,1024]{1,0:T(8,128)(2,1)S(1)} collective-permute-done((bf16[32,1024]{1,0:T(8,128)(2,1)S(1)}, bf16[32,1024]{1,0:T(8,128)(2,1)S(1)}, u32[]{:S(2)}, u32[]{:S(2)}) %collective-permute-start.1) | collective-permute-done | bytes 65568 | tf_op jit(solution)/shard_map/ppermute | solution.py:49
  15.3 0.0 copy-done
  15.3 0.0 copy-done.1
  15.3 0.0 copy-done.2
  15.3 1.3 %shard_map.105 = (bf16[112,384]{1,0:T(8,128)(2,1)S(1)}, bf16[112,384]{1,0:T(8,128)(2,1)S(1)}, bf16[112,384]{1,0:T(8,128)(2,1)S(1)}, bf16[112,384]{1,0:T(8,128)(2,1)S(1)}, bf16[128,256]{1,0:T(8,128)(2,1)S(1)}) custom-call(bf16[32,1024]{1,0:T(8,128)(2,1)S(1)} %shard_map.104.refs_0_, bf16[32,1024]{1,0:T(8,128)(2,1)S(1)} %collective-permute-done.1.refs_1_, ...), custom_call_target="tpu_custom_call" | custom-call | tf_op jit(solution)/shard_map/pallas_call | solution.py:329
  16.7 0.7 %collective-permute-start.7 = (bf16[112,384]{1,0:T(8,128)(2,1)S(1)}, bf16[112,384]{1,0:T(8,128)(2,1)S(1)}, u32[]{:S(2)}, u32[]{:S(2)}) collective-permute-start(bf16[112,384]{1,0:T(8,128)(2,1)S(1)} %get-tuple-element.15), channel_id=1, source_target_pairs={{0,8},{8,0},{16,24},{24,16},{1,9},{9,1},{17,25},{25,17},{2,10},{10... | collective-permute-start | bytes 258056 | tf_op jit(solution)/shard_map/ppermute | solution.py:49
  17.4 3.5 %collective-permute-start.8 = (bf16[112,384]{1,0:T(8,128)(2,1)S(1)}, bf16[112,384]{1,0:T(8,128)(2,1)S(1)}, u32[]{:S(2)}, u32[]{:S(2)}) collective-permute-start(bf16[112,384]{1,0:T(8,128)(2,1)S(1)} %get-tuple-element.16), channel_id=1, source_target_pairs={{0,16},{8,24},{16,0},{24,8},{1,17},{9,25},{17,1},{25,9},{2,18},{10... | collective-permute-start | bytes 258056 | tf_op jit(solution)/shard_map/ppermute | solution.py:49
  20.9 0.2 collective-permute-start.9
  21.1 0.5 %collective-permute-done.7.refs_1_ = bf16[112,384]{1,0:T(8,128)(2,1)S(1)} collective-permute-done((bf16[112,384]{1,0:T(8,128)(2,1)S(1)}, bf16[112,384]{1,0:T(8,128)(2,1)S(1)}, u32[]{:S(2)}, u32[]{:S(2)}) %collective-permute-start.7) | collective-permute-done | bytes 86048 | tf_op jit(solution)/shard_map/ppermute | solution.py:49
  21.7 3.9 %collective-permute-done.8.refs_2_ = bf16[112,384]{1,0:T(8,128)(2,1)S(1)} collective-permute-done((bf16[112,384]{1,0:T(8,128)(2,1)S(1)}, bf16[112,384]{1,0:T(8,128)(2,1)S(1)}, u32[]{:S(2)}, u32[]{:S(2)}) %collective-permute-start.8) | collective-permute-done | bytes 86048 | tf_op jit(solution)/shard_map/ppermute | solution.py:49
  25.5 1.8 %collective-permute-done.9.refs_3_ = bf16[112,384]{1,0:T(8,128)(2,1)S(1)} collective-permute-done((bf16[112,384]{1,0:T(8,128)(2,1)S(1)}, bf16[112,384]{1,0:T(8,128)(2,1)S(1)}, u32[]{:S(2)}, u32[]{:S(2)}) %collective-permute-start.9) | collective-permute-done | bytes 86048 | tf_op jit(solution)/shard_map/ppermute | solution.py:49
  27.3 0.2 shard_map.106
  27.5 0.0 collective-permute-start.10
  27.5 1.2 %collective-permute-done.10.other_ref = f32[8,128]{1,0:T(8,128)S(1)} collective-permute-done((f32[8,128]{1,0:T(8,128)S(1)}, f32[8,128]{1,0:T(8,128)S(1)}, u32[]{:S(2)}, u32[]{:S(2)}) %collective-permute-start.10) | collective-permute-done | bytes 4128 | tf_op jit(solution)/shard_map/ppermute | solution.py:53
  28.7 1.7 %collective-permute-start.13 = (f32[8,128]{1,0:T(8,128)S(1)}, f32[8,128]{1,0:T(8,128)S(1)}, u32[]{:S(2)}, u32[]{:S(2)}) collective-permute-start(f32[8,128]{1,0:T(8,128)S(1)} %shard_map.107.refs_0_), channel_id=1, source_target_pairs={{0,6},{1,7},{2,4},{3,5},{4,2},{5,3},{6,0},{7,1},{8,14},{9,15},{10,... | collective-permute-start | bytes 12296 | tf_op jit(solution)/shard_map/ppermute | solution.py:49
  30.4 1.1 %collective-permute-start.12 = (f32[8,128]{1,0:T(8,128)S(1)}, f32[8,128]{1,0:T(8,128)S(1)}, u32[]{:S(2)}, u32[]{:S(2)}) collective-permute-start(f32[8,128]{1,0:T(8,128)S(1)} %shard_map.107.refs_0_), channel_id=1, source_target_pairs={{0,4},{1,5},{2,6},{3,7},{4,0},{5,1},{6,2},{7,3},{8,12},{9,13},{10,... | collective-permute-start | bytes 12296 | tf_op jit(solution)/shard_map/ppermute | solution.py:49
  31.5 0.8 %collective-permute-start.11 = (f32[8,128]{1,0:T(8,128)S(1)}, f32[8,128]{1,0:T(8,128)S(1)}, u32[]{:S(2)}, u32[]{:S(2)}) collective-permute-start(f32[8,128]{1,0:T(8,128)S(1)} %shard_map.107.refs_0_), channel_id=1, source_target_pairs={{0,2},{1,3},{2,0},{3,1},{4,6},{5,7},{6,4},{7,5},{8,10},{9,11},{10,... | collective-permute-start | bytes 12296 | tf_op jit(solution)/shard_map/ppermute | solution.py:49
  32.3 0.1 shard_map.108.refs_6_
  32.4 0.9 %collective-permute-done.13.refs_3_ = f32[8,128]{1,0:T(8,128)S(1)} collective-permute-done((f32[8,128]{1,0:T(8,128)S(1)}, f32[8,128]{1,0:T(8,128)S(1)}, u32[]{:S(2)}, u32[]{:S(2)}) %collective-permute-start.13) | collective-permute-done | bytes 4128 | tf_op jit(solution)/shard_map/ppermute | solution.py:49
  33.3 0.7 %collective-permute-done.12.refs_2_ = f32[8,128]{1,0:T(8,128)S(1)} collective-permute-done((f32[8,128]{1,0:T(8,128)S(1)}, f32[8,128]{1,0:T(8,128)S(1)}, u32[]{:S(2)}, u32[]{:S(2)}) %collective-permute-start.12) | collective-permute-done | bytes 4128 | tf_op jit(solution)/shard_map/ppermute | solution.py:49
  34.0 1.1 %collective-permute-done.11.refs_1_ = f32[8,128]{1,0:T(8,128)S(1)} collective-permute-done((f32[8,128]{1,0:T(8,128)S(1)}, f32[8,128]{1,0:T(8,128)S(1)}, u32[]{:S(2)}, u32[]{:S(2)}) %collective-permute-start.11) | collective-permute-done | bytes 4128 | tf_op jit(solution)/shard_map/ppermute | solution.py:49
  35.1 0.1 shard_map.109.refs_0_
  35.3 2.6 %collective-permute-start.16 = (bf16[32,512]{1,0:T(8,128)(2,1)S(1)}, bf16[32,512]{1,0:T(8,128)(2,1)S(1)}, u32[]{:S(2)}, u32[]{:S(2)}) collective-permute-start(bf16[32,512]{1,0:T(8,128)(2,1)S(1)} %shard_map.109.refs_0_), channel_id=1, source_target_pairs={{0,24},{8,16},{16,8},{24,0},{1,25},{9,17},{17,9},{25,1},{2,26},{10... | collective-permute-start | bytes 98312 | tf_op jit(solution)/shard_map/ppermute | solution.py:49
  37.8 0.5 %collective-permute-start.15 = (bf16[32,512]{1,0:T(8,128)(2,1)S(1)}, bf16[32,512]{1,0:T(8,128)(2,1)S(1)}, u32[]{:S(2)}, u32[]{:S(2)}) collective-permute-start(bf16[32,512]{1,0:T(8,128)(2,1)S(1)} %shard_map.109.refs_0_), channel_id=1, source_target_pairs={{0,16},{8,24},{16,0},{24,8},{1,17},{9,25},{17,1},{25,9},{2,18},{10... | collective-permute-start | bytes 98312 | tf_op jit(solution)/shard_map/ppermute | solution.py:49
  38.4 1.3 %collective-permute-start.14 = (bf16[32,512]{1,0:T(8,128)(2,1)S(1)}, bf16[32,512]{1,0:T(8,128)(2,1)S(1)}, u32[]{:S(2)}, u32[]{:S(2)}) collective-permute-start(bf16[32,512]{1,0:T(8,128)(2,1)S(1)} %shard_map.109.refs_0_), channel_id=1, source_target_pairs={{0,8},{8,0},{16,24},{24,16},{1,9},{9,1},{17,25},{25,17},{2,10},{10... | collective-permute-start | bytes 98312 | tf_op jit(solution)/shard_map/ppermute | solution.py:49
  39.7 1.7 %collective-permute-done.16.refs_3_ = bf16[32,512]{1,0:T(8,128)(2,1)S(1)} collective-permute-done((bf16[32,512]{1,0:T(8,128)(2,1)S(1)}, bf16[32,512]{1,0:T(8,128)(2,1)S(1)}, u32[]{:S(2)}, u32[]{:S(2)}) %collective-permute-start.16) | collective-permute-done | bytes 32800 | tf_op jit(solution)/shard_map/ppermute | solution.py:49
  41.4 1.6 %collective-permute-done.15.refs_2_ = bf16[32,512]{1,0:T(8,128)(2,1)S(1)} collective-permute-done((bf16[32,512]{1,0:T(8,128)(2,1)S(1)}, bf16[32,512]{1,0:T(8,128)(2,1)S(1)}, u32[]{:S(2)}, u32[]{:S(2)}) %collective-permute-start.15) | collective-permute-done | bytes 32800 | tf_op jit(solution)/shard_map/ppermute | solution.py:49
  43.0 0.0 collective-permute-done.14.refs_1_
  43.0 1.0 %shard_map.110 = (f32[1,1]{1,0:T(1,128)}, f32[256,384]{1,0:T(8,128)}, f32[384]{0:T(512)}) custom-call(bf16[32,512]{1,0:T(8,128)(2,1)S(1)} %shard_map.109.refs_0_, bf16[32,512]{1,0:T(8,128)(2,1)S(1)} %collective-permute-done.14.refs_1_, bf16[32,512]{1,0:T(8,128)(2,1)S(1)} %collective-permute-done.15.refs_2_, ...), custom_call_target="tpu_custom_call" | custom-call | tf_op jit(solution)/shard_map/pallas_call | solution.py:374
  (10 shorter events, 0.0 us)
Async XLA Ops:
  0.6 10.4 %collective-permute-start.5 = (bf16[32,1024]{1,0:T(8,128)(2,1)}, bf16[32,1024]{1,0:T(8,128)(2,1)S(1)}, u32[]{:S(2)}, u32[]{:S(2)}) collective-permute-start(bf16[32,1024]{1,0:T(8,128)(2,1)} %refs_7_.1), channel_id=1, source_target_pairs={{0,16},{8,24},{16,0},{24,8},{1,17},{9,25},{17,1},{25,9},{2,18},{10... | collective-permute-start | bytes 196616 | tf_op jit(solution)/shard_map/ppermute | solution.py:49
  4.7 6.6 %collective-permute-start.4 = (bf16[32,1024]{1,0:T(8,128)(2,1)}, bf16[32,1024]{1,0:T(8,128)(2,1)S(1)}, u32[]{:S(2)}, u32[]{:S(2)}) collective-permute-start(bf16[32,1024]{1,0:T(8,128)(2,1)} %refs_7_.1), channel_id=1, source_target_pairs={{0,8},{8,0},{16,24},{24,16},{1,9},{9,1},{17,25},{25,17},{2,10},{10... | collective-permute-start | bytes 196616 | tf_op jit(solution)/shard_map/ppermute | solution.py:49
  6.3 6.3 %collective-permute-start.6 = (bf16[32,1024]{1,0:T(8,128)(2,1)}, bf16[32,1024]{1,0:T(8,128)(2,1)S(1)}, u32[]{:S(2)}, u32[]{:S(2)}) collective-permute-start(bf16[32,1024]{1,0:T(8,128)(2,1)} %refs_7_.1), channel_id=1, source_target_pairs={{0,24},{8,16},{16,8},{24,0},{1,25},{9,17},{17,9},{25,1},{2,26},{10... | collective-permute-start | bytes 196616 | tf_op jit(solution)/shard_map/ppermute | solution.py:49
  6.3 1.4 %copy-start.7 = (bf16[1,16,1024]{2,1,0:T(8,128)(2,1)S(1)}, bf16[1,16,1024]{2,1,0:T(8,128)(2,1)}, u32[]{:S(2)}) copy-start(bf16[1,16,1024]{2,1,0:T(8,128)(2,1)} %param.8) | copy-start | bytes 98308
  6.3 1.4 %collective-permute-start = (bf16[16,1024]{1,0:T(8,128)(2,1)}, bf16[16,1024]{1,0:T(8,128)(2,1)S(1)}, u32[]{:S(2)}, u32[]{:S(2)}) collective-permute-start(bf16[16,1024]{1,0:T(8,128)(2,1)} %bitcast.6), channel_id=1, source_target_pairs={{0,1},{1,0},{2,3},{3,2},{4,5},{5,4},{6,7},{7,6},{8,9},{9,8},{10,11... | collective-permute-start | bytes 98312 | tf_op jit(solution)/shard_map/ppermute | solution.py:53
  6.3 9.0 %copy-start = (bf16[1,1024,384]{2,1,0:T(8,128)(2,1)S(1)}, bf16[1,1024,384]{2,1,0:T(8,128)(2,1)}, u32[]{:S(2)}) copy-start(bf16[1,1024,384]{2,1,0:T(8,128)(2,1)} %param.10) | copy-start | bytes 2359300
  6.3 9.0 %copy-start.1 = (bf16[256,384]{1,0:T(8,128)(2,1)S(1)}, bf16[256,384]{1,0:T(8,128)(2,1)}, u32[]{:S(2)}) copy-start(bf16[256,384]{1,0:T(8,128)(2,1)} %refs_11_.1) | copy-start | bytes 589828
  6.4 8.9 %copy-start.2 = (bf16[32,1024]{1,0:T(8,128)(2,1)S(1)}, bf16[32,1024]{1,0:T(8,128)(2,1)}, u32[]{:S(2)}) copy-start(bf16[32,1024]{1,0:T(8,128)(2,1)} %refs_7_.1) | copy-start | bytes 196612
  7.7 7.6 %copy-start.3 = (f32[1024]{0:T(1024)S(1)}, f32[1024]{0:T(1024)}, u32[]{:S(2)}) copy-start(f32[1024]{0:T(1024)} %param.13) | copy-start | bytes 12292
  7.7 7.6 %copy-start.4 = (f32[1,1024]{1,0:T(1,128)S(1)}, f32[1,1024]{1,0:T(1,128)}, u32[]{:S(2)}) copy-start(f32[1,1024]{1,0:T(1,128)} %refs_9_.1) | copy-start | bytes 12292
  7.8 7.6 %copy-start.5 = (f32[384]{0:T(512)S(1)}, f32[384]{0:T(512)}, u32[]{:S(2)}) copy-start(f32[384]{0:T(512)} %refs_13_.1) | copy-start | bytes 4612
  7.8 7.6 %copy-start.6 = (f32[1,384]{1,0:T(1,128)S(1)}, f32[1,384]{1,0:T(1,128)}, u32[]{:S(2)}) copy-start(f32[1,384]{1,0:T(1,128)} %refs_12_.1) | copy-start | bytes 4612
  7.8 5.2 %collective-permute-start.3 = (bf16[32,1024]{1,0:T(8,128)(2,1)S(1)}, bf16[32,1024]{1,0:T(8,128)(2,1)S(1)}, u32[]{:S(2)}, u32[]{:S(2)}) collective-permute-start(bf16[32,1024]{1,0:T(8,128)(2,1)S(1)} %shard_map.104.refs_0_), channel_id=1, source_target_pairs={{0,6},{1,7},{2,4},{3,5},{4,2},{5,3},{6,0},{7,1},{8,14},{9,15},{10,... | collective-permute-start | bytes 196616 | tf_op jit(solution)/shard_map/ppermute | solution.py:49
  10.5 4.3 %collective-permute-start.2 = (bf16[32,1024]{1,0:T(8,128)(2,1)S(1)}, bf16[32,1024]{1,0:T(8,128)(2,1)S(1)}, u32[]{:S(2)}, u32[]{:S(2)}) collective-permute-start(bf16[32,1024]{1,0:T(8,128)(2,1)S(1)} %shard_map.104.refs_0_), channel_id=1, source_target_pairs={{0,4},{1,5},{2,6},{3,7},{4,0},{5,1},{6,2},{7,3},{8,12},{9,13},{10,... | collective-permute-start | bytes 196616 | tf_op jit(solution)/shard_map/ppermute | solution.py:49
  11.0 4.3 %collective-permute-start.1 = (bf16[32,1024]{1,0:T(8,128)(2,1)S(1)}, bf16[32,1024]{1,0:T(8,128)(2,1)S(1)}, u32[]{:S(2)}, u32[]{:S(2)}) collective-permute-start(bf16[32,1024]{1,0:T(8,128)(2,1)S(1)} %shard_map.104.refs_0_), channel_id=1, source_target_pairs={{0,2},{1,3},{2,0},{3,1},{4,6},{5,7},{6,4},{7,5},{8,10},{9,11},{10,... | collective-permute-start | bytes 196616 | tf_op jit(solution)/shard_map/ppermute | solution.py:49
  16.7 5.0 %collective-permute-start.7 = (bf16[112,384]{1,0:T(8,128)(2,1)S(1)}, bf16[112,384]{1,0:T(8,128)(2,1)S(1)}, u32[]{:S(2)}, u32[]{:S(2)}) collective-permute-start(bf16[112,384]{1,0:T(8,128)(2,1)S(1)} %get-tuple-element.15), channel_id=1, source_target_pairs={{0,8},{8,0},{16,24},{24,16},{1,9},{9,1},{17,25},{25,17},{2,10},{10... | collective-permute-start | bytes 258056 | tf_op jit(solution)/shard_map/ppermute | solution.py:49
  17.4 8.1 %collective-permute-start.8 = (bf16[112,384]{1,0:T(8,128)(2,1)S(1)}, bf16[112,384]{1,0:T(8,128)(2,1)S(1)}, u32[]{:S(2)}, u32[]{:S(2)}) collective-permute-start(bf16[112,384]{1,0:T(8,128)(2,1)S(1)} %get-tuple-element.16), channel_id=1, source_target_pairs={{0,16},{8,24},{16,0},{24,8},{1,17},{9,25},{17,1},{25,9},{2,18},{10... | collective-permute-start | bytes 258056 | tf_op jit(solution)/shard_map/ppermute | solution.py:49
  20.9 6.4 %collective-permute-start.9 = (bf16[112,384]{1,0:T(8,128)(2,1)S(1)}, bf16[112,384]{1,0:T(8,128)(2,1)S(1)}, u32[]{:S(2)}, u32[]{:S(2)}) collective-permute-start(bf16[112,384]{1,0:T(8,128)(2,1)S(1)} %get-tuple-element.17), channel_id=1, source_target_pairs={{0,24},{8,16},{16,8},{24,0},{1,25},{9,17},{17,9},{25,1},{2,26},{10... | collective-permute-start | bytes 258056 | tf_op jit(solution)/shard_map/ppermute | solution.py:49
  27.5 1.2 %collective-permute-start.10 = (f32[8,128]{1,0:T(8,128)S(1)}, f32[8,128]{1,0:T(8,128)S(1)}, u32[]{:S(2)}, u32[]{:S(2)}) collective-permute-start(f32[8,128]{1,0:T(8,128)S(1)} %get-tuple-element.18.own_ref.refs_4_), channel_id=1, source_target_pairs={{0,1},{1,0},{2,3},{3,2},{4,5},{5,4},{6,7},{7,6},{8,9},{9,8},{10,11... | collective-permute-start | bytes 12296 | tf_op jit(solution)/shard_map/ppermute | solution.py:53
  28.7 4.6 %collective-permute-start.13 = (f32[8,128]{1,0:T(8,128)S(1)}, f32[8,128]{1,0:T(8,128)S(1)}, u32[]{:S(2)}, u32[]{:S(2)}) collective-permute-start(f32[8,128]{1,0:T(8,128)S(1)} %shard_map.107.refs_0_), channel_id=1, source_target_pairs={{0,6},{1,7},{2,4},{3,5},{4,2},{5,3},{6,0},{7,1},{8,14},{9,15},{10,... | collective-permute-start | bytes 12296 | tf_op jit(solution)/shard_map/ppermute | solution.py:49
  30.4 3.6 %collective-permute-start.12 = (f32[8,128]{1,0:T(8,128)S(1)}, f32[8,128]{1,0:T(8,128)S(1)}, u32[]{:S(2)}, u32[]{:S(2)}) collective-permute-start(f32[8,128]{1,0:T(8,128)S(1)} %shard_map.107.refs_0_), channel_id=1, source_target_pairs={{0,4},{1,5},{2,6},{3,7},{4,0},{5,1},{6,2},{7,3},{8,12},{9,13},{10,... | collective-permute-start | bytes 12296 | tf_op jit(solution)/shard_map/ppermute | solution.py:49
  31.5 3.6 %collective-permute-start.11 = (f32[8,128]{1,0:T(8,128)S(1)}, f32[8,128]{1,0:T(8,128)S(1)}, u32[]{:S(2)}, u32[]{:S(2)}) collective-permute-start(f32[8,128]{1,0:T(8,128)S(1)} %shard_map.107.refs_0_), channel_id=1, source_target_pairs={{0,2},{1,3},{2,0},{3,1},{4,6},{5,7},{6,4},{7,5},{8,10},{9,11},{10,... | collective-permute-start | bytes 12296 | tf_op jit(solution)/shard_map/ppermute | solution.py:49
  35.3 6.1 %collective-permute-start.16 = (bf16[32,512]{1,0:T(8,128)(2,1)S(1)}, bf16[32,512]{1,0:T(8,128)(2,1)S(1)}, u32[]{:S(2)}, u32[]{:S(2)}) collective-permute-start(bf16[32,512]{1,0:T(8,128)(2,1)S(1)} %shard_map.109.refs_0_), channel_id=1, source_target_pairs={{0,24},{8,16},{16,8},{24,0},{1,25},{9,17},{17,9},{25,1},{2,26},{10... | collective-permute-start | bytes 98312 | tf_op jit(solution)/shard_map/ppermute | solution.py:49
  37.8 5.2 %collective-permute-start.15 = (bf16[32,512]{1,0:T(8,128)(2,1)S(1)}, bf16[32,512]{1,0:T(8,128)(2,1)S(1)}, u32[]{:S(2)}, u32[]{:S(2)}) collective-permute-start(bf16[32,512]{1,0:T(8,128)(2,1)S(1)} %shard_map.109.refs_0_), channel_id=1, source_target_pairs={{0,16},{8,24},{16,0},{24,8},{1,17},{9,25},{17,1},{25,9},{2,18},{10... | collective-permute-start | bytes 98312 | tf_op jit(solution)/shard_map/ppermute | solution.py:49
  38.4 4.6 %collective-permute-start.14 = (bf16[32,512]{1,0:T(8,128)(2,1)S(1)}, bf16[32,512]{1,0:T(8,128)(2,1)S(1)}, u32[]{:S(2)}, u32[]{:S(2)}) collective-permute-start(bf16[32,512]{1,0:T(8,128)(2,1)S(1)} %shard_map.109.refs_0_), channel_id=1, source_target_pairs={{0,8},{8,0},{16,24},{24,16},{1,9},{9,1},{17,25},{25,17},{2,10},{10... | collective-permute-start | bytes 98312 | tf_op jit(solution)/shard_map/ppermute | solution.py:49

commit v5 on v4

--- a/solution.py
+++ b/solution.py
@@ -34,9 +34,9 @@
 
 def mixed(index, k, size, of):
     if size & (size - 1) == 0:
-        return lax.bitwise_xor(index, jnp.int32(k))
+        return lax.bitwise_xor(index, jnp.int32(k) if isinstance(k, int) else k)
     step = k if of is partner else size - k
-    return lax.rem(index + jnp.int32(step), jnp.int32(size))
+    return lax.rem(index + step, jnp.int32(size))
 
 
 def send(value, axis, k, scale=1, groups=1):
@@ -47,6 +47,16 @@
         for inner in range(scale)
     ]
     return lax.ppermute(value, axis, pairs)
+
+
+def send_split(value, j):
+    members, peers = lax.axis_size("member"), lax.axis_size("dp")
+    pairs = [
+        (m * peers + d, partner(m, 2 * j + 1 + d % 2, members) * peers + d)
+        for m in range(members)
+        for d in range(peers)
+    ]
+    return lax.ppermute(value, ("member", "dp"), pairs)
 
 
 def swap_cores(value, axis):
@@ -129,11 +139,16 @@
     out_ref[...] = jnp.zeros_like(out_ref)
 
 
-def pair_kernel(own_ref, other_ref, _, pair_ref):
-    core = lax.rem(lax.axis_index("dp"), jnp.int32(2))
-    rows = own_ref.shape[0]
-    pair_ref[slot(core, rows), :] = own_ref[...]
-    pair_ref[slot(1 - core, rows), :] = other_ref[...]
+def join_kernel(chips, splits, *refs):
+    out_ref, parts = refs[-1], refs[: chips + splits]
+    chip = lax.axis_index("dp") // 2
+    rows = parts[0].shape[0]
+    for k in range(chips):
+        out_ref[slot(mixed(chip, k, chips, sender), rows), :] = parts[k][...]
+    start = chips * rows
+    for part in parts[chips:]:
+        out_ref[start : start + part.shape[0], :] = part[...]
+        start += part.shape[0]
 
 
 def packed3(row, rows, lanes):
@@ -143,26 +158,33 @@
     return jnp.where(line == 0, high, jnp.where(line == 1, middle, lower)).astype(BF16)
 
 
-def logits_kernel(members, chips, *refs):
-    pairs, refs = refs[:chips], refs[chips:]
-    students, refs = refs[: members - 1], refs[members - 1 :]
+def logits_kernel(members, rows, *refs):
+    own_ref, other_ref, refs = refs[0], refs[1], refs[2:]
+    shared, refs = refs[: (members - 1) % 2], refs[(members - 1) % 2 :]
     sources, refs = refs[:7], refs[7:]
     payloads, refs = refs[:members], refs[members:]
     columns_ref, gathered, held, shifted_ref, lse_ref, partial_ref, *params = refs
-    own_ref, student_gain_ref, gain_ref, head_ref, student_ref, bias_ref, student_bias_ref, sems = params
-    copies = fetch(sources, params[:7], sems)
-    mine, chip = lax.axis_index("member"), lax.axis_index("dp") // 2
-    for k in range(chips):
-        at = mixed(chip, k, chips, sender)
-        gathered[slot(at, pairs[k].shape[0]), :] = pairs[k][...]
+    feats_ref, student_gain_ref, gain_ref, head_ref, student_ref, bias_ref, student_bias_ref = params[:7]
+    copies = fetch(sources, params[:7], params[7])
+    mine, place = lax.axis_index("member"), lax.axis_index("dp")
+    core = lax.rem(place, jnp.int32(2))
+    chips = gathered.shape[0] // (2 * rows)
     for copy in copies:
         copy.wait()
-    block = own_ref.shape[0]
+    block = feats_ref.shape[0]
     width = columns_ref.shape[1]
-    for k in range(members):
-        source = own_ref if k == 0 else students[k - 1]
-        at = slot(mixed(mine, k, members, sender), block)
-        held[at, :] = normed(source[...], student_gain_ref[...])
+    held[slot(mine, block), :] = normed(feats_ref[...], student_gain_ref[...])
+    for source, side in ((own_ref, core), (other_ref, 1 - core)):
+        for chip in range(chips):
+            at = slot(2 * chip + side, rows)
+            gathered[at, :] = normed(source[chip * rows : (chip + 1) * rows, :], gain_ref[...])
+        for j in range((members - 1) // 2):
+            start = chips * rows + j * block
+            at = slot(mixed(mine, 2 * j + 1 + side, members, sender), block)
+            held[at, :] = normed(source[start : start + block, :], student_gain_ref[...])
+    for part in shared:
+        at = slot(mixed(mine, members - 1, members, sender), block)
+        held[at, :] = normed(part[...], student_gain_ref[...])
     if width % LANES == 0:
         columns_ref[...] = held[:, pl.ds(pl.multiple_of(mine * width, LANES), width)]
     else:
@@ -172,8 +194,7 @@
             def _(j=j):
                 columns_ref[...] = held[:, j * width : (j + 1) * width]
 
-    values = normed(gathered[...], gain_ref[...])
-    logits = jnp.dot(values, head_ref[...], preferred_element_type=F32) + bias_ref[...]
+    logits = jnp.dot(gathered[...], head_ref[...], preferred_element_type=F32) + bias_ref[...]
     top = jnp.max(logits, axis=1, keepdims=True)
     lse = top + jnp.log(jnp.sum(jnp.exp(logits - top), axis=1, keepdims=True))
     shifted_ref[...] = (logits - lse).astype(BF16)
@@ -321,13 +342,17 @@
     width, classes = student_head.shape
     small_rows = -(-(members + 2) // 8) * 8
 
-    other = swap_cores(feats, "dp")
-    students = [send(student_feats, "member", k) for k in range(1, members)]
+    parts = [feats] + [send(feats, "dp", k, 2) for k in range(1, chips)]
+    parts += [send_split(student_feats, j) for j in range((members - 1) // 2)]
+    shared = [send(student_feats, "member", members - 1)] * ((members - 1) % 2)
     first = call(first_kernel, shape((8, LANES), F32), flops=1 << 33)()
-    pair = call(pair_kernel, shape((2 * rows, depth), BF16), flops=1 << 33)(feats, other, first)
-    pairs = [pair] + [send(pair, "dp", k, 2) for k in range(1, chips)]
+    own = call(
+        functools.partial(join_kernel, chips, (members - 1) // 2),
+        shape((chips * rows + (members - 1) // 2 * block, depth), BF16),
+        flops=1 << 33,
+    )(*parts, *shared, first)
     *payloads, own_columns = call(
-        functools.partial(logits_kernel, members, chips),
+        functools.partial(logits_kernel, members, rows),
         [shape((3 * block + PAD, classes), BF16)] * members + [shape((images, width), BF16)],
         [
             pltpu.VMEM((images, depth), BF16),
@@ -344,10 +369,11 @@
             pltpu.VMEM((classes,), F32),
             pltpu.SemaphoreType.DMA((7,)),
         ],
-        [here] * (chips + members - 1) + [far] * 7,
+        [here] * (2 + len(shared)) + [far] * 7,
     )(
-        *pairs,
-        *students,
+        own,
+        swap_cores(own, "dp"),
+        *shared,
         student_feats,
         student_gain[None],
         teacher_gain,

time: 44.2 us -> 43.8 us (level)
    ppermute x15 -> x13, starting transfers between devices: 21.7 us -> 19.5 us  [send(): return lax.ppermute(value, axis, pairs)]
    ppermute x0 -> x1, starting transfers between devices: none -> 1.98 us  [send_split(): return lax.ppermute(value, ('member', 'dp'), pairs)]
    ppermute x15 -> x13, waiting for transfers between devices: 16.1 us -> 15.6 us  [send(): return lax.ppermute(value, axis, pairs)]
  transfers between devices with their start and end apart: 17 -> 16, of which waited for: 14 -> 11; matrix products, arithmetic and copies ran while one was open for 0% -> 0% of each run, Pallas kernels for 0% -> 0%
where the time goes in v5:
time: 43.8 us; the launch traced here: 43.7 us
  starting transfers between devices  21.6 us (49%)
  waiting for transfers between devices  18.3 us (42%)
  Pallas kernels  2.95 us (7%)
  between operations  0.77 us (2%)
    ppermute x13, starting transfers between devices, send(): return lax.ppermute(value, axis, pairs)  19.5 us
    ppermute x13, waiting for transfers between devices, send(): return lax.ppermute(value, axis, pairs)  15.6 us
    ppermute x2, waiting for transfers between devices, swap_cores(): lax.ppermute(value, axis, [(i, i ^ 1) for i in range(lax.axis_size(axis))])  2.58 us
    ppermute x1, starting transfers between devices, send_split(): return lax.ppermute(value, ('member', 'dp'), pairs)  1.98 us
    pallas_call x1, Pallas kernels, on_device(): call(functools.partial(logits_kernel, members, rows), [shape((3 * block +...  1.41 us
    pallas_call x1, Pallas kernels, on_device(): call(functools.partial(gradient_kernel, members, images, classes * peers)...  1 us
  transfers between devices with their start and end apart: 16, of which 11 were waited for; matrix products, arithmetic and copies ran while one was open for 0% of the time, Pallas kernels for 0%

profile of v5, /device:TPU:0, one launch (start us, length us, event | category | flops | bytes accessed | tf_op | source)
XLA Modules:
  0.0 43.7 jit_solution(5387723064158286390)
XLA Ops:
  0.6 0.0 copy-start.7
  0.6 4.0 %collective-permute-start.2 = (bf16[16,1024]{1,0:T(8,128)(2,1)}, bf16[16,1024]{1,0:T(8,128)(2,1)S(1)}, u32[]{:S(2)}, u32[]{:S(2)}) collective-permute-start(bf16[16,1024]{1,0:T(8,128)(2,1)} %bitcast.6), channel_id=1, source_target_pairs={{0,6},{1,7},{2,4},{3,5},{4,2},{5,3},{6,0},{7,1},{8,14},{9,15},{10,... | collective-permute-start | bytes 98312 | tf_op jit(solution)/shard_map/ppermute | solution.py:49
  4.6 0.5 %collective-permute-start.1 = (bf16[16,1024]{1,0:T(8,128)(2,1)}, bf16[16,1024]{1,0:T(8,128)(2,1)S(1)}, u32[]{:S(2)}, u32[]{:S(2)}) collective-permute-start(bf16[16,1024]{1,0:T(8,128)(2,1)} %bitcast.7), channel_id=1, source_target_pairs={{0,4},{1,5},{2,6},{3,7},{4,0},{5,1},{6,2},{7,3},{8,12},{9,13},{10,... | collective-permute-start | bytes 98312 | tf_op jit(solution)/shard_map/ppermute | solution.py:49
  5.1 0.1 collective-permute-start
  5.2 2.0 %collective-permute-start.3 = (bf16[32,1024]{1,0:T(8,128)(2,1)}, bf16[32,1024]{1,0:T(8,128)(2,1)S(1)}, u32[]{:S(2)}, u32[]{:S(2)}) collective-permute-start(bf16[32,1024]{1,0:T(8,128)(2,1)} %refs_3_.1), channel_id=1, source_target_pairs={{0,8},{1,17},{2,10},{3,19},{4,12},{5,21},{6,14},{7,23},{8,0},{9,25... | collective-permute-start | bytes 196616 | tf_op jit(solution)/shard_map/ppermute | solution.py:59
  7.2 2.5 %collective-permute-start.4 = (bf16[32,1024]{1,0:T(8,128)(2,1)}, bf16[32,1024]{1,0:T(8,128)(2,1)S(1)}, u32[]{:S(2)}, u32[]{:S(2)}) collective-permute-start(bf16[32,1024]{1,0:T(8,128)(2,1)} %refs_3_.1), channel_id=1, source_target_pairs={{0,24},{8,16},{16,8},{24,0},{1,25},{9,17},{17,9},{25,1},{2,26},{10... | collective-permute-start | bytes 196616 | tf_op jit(solution)/shard_map/ppermute | solution.py:49
  9.7 0.0 collective-permute-done.2.refs_3_
  9.7 0.0 collective-permute-done.1.refs_2_
  9.7 0.0 collective-permute-done.refs_1_
  9.7 0.2 collective-permute-done.3.refs_4_
  9.9 3.7 %collective-permute-done.4.refs_5_.refs_2_ = bf16[32,1024]{1,0:T(8,128)(2,1)S(1)} collective-permute-done((bf16[32,1024]{1,0:T(8,128)(2,1)}, bf16[32,1024]{1,0:T(8,128)(2,1)S(1)}, u32[]{:S(2)}, u32[]{:S(2)}) %collective-permute-start.4) | collective-permute-done | bytes 65568 | tf_op jit(solution)/shard_map/ppermute | solution.py:49
  13.7 0.0 copy-done.7
  13.7 0.0 copy-start.5
  13.7 0.0 copy-start.6
  13.7 0.1 collective-permute-start.5
  13.8 1.4 %collective-permute-done.5.refs_1_ = bf16[96,1024]{1,0:T(8,128)(2,1)S(1)} collective-permute-done((bf16[96,1024]{1,0:T(8,128)(2,1)S(1)}, bf16[96,1024]{1,0:T(8,128)(2,1)S(1)}, u32[]{:S(2)}, u32[]{:S(2)}) %collective-permute-start.5) | collective-permute-done | bytes 196640 | tf_op jit(solution)/shard_map/ppermute | solution.py:63
  15.2 0.0 copy-done
  15.2 0.0 copy-done.1
  15.2 0.0 copy-done.2
  15.2 0.0 copy-done.3
  15.2 0.0 copy-done.4
  15.3 0.0 copy-done.5
  15.3 0.0 copy-done.6
  15.3 1.4 %shard_map.105 = (bf16[112,384]{1,0:T(8,128)(2,1)S(1)}, bf16[112,384]{1,0:T(8,128)(2,1)S(1)}, bf16[112,384]{1,0:T(8,128)(2,1)S(1)}, bf16[112,384]{1,0:T(8,128)(2,1)S(1)}, bf16[128,256]{1,0:T(8,128)(2,1)S(1)}) custom-call(bf16[96,1024]{1,0:T(8,128)(2,1)S(1)} %shard_map.104.refs_0_, bf16[96,1024]{1,0:T(8,128)(2,1)S(1)} %collective-permute-done.5.refs_1_, ...), custom_call_target="tpu_custom_call" | custom-call | tf_op jit(solution)/shard_map/pallas_call | solution.py:354
  16.7 0.7 %collective-permute-start.6 = (bf16[112,384]{1,0:T(8,128)(2,1)S(1)}, bf16[112,384]{1,0:T(8,128)(2,1)S(1)}, u32[]{:S(2)}, u32[]{:S(2)}) collective-permute-start(bf16[112,384]{1,0:T(8,128)(2,1)S(1)} %get-tuple-element.15), channel_id=1, source_target_pairs={{0,8},{8,0},{16,24},{24,16},{1,9},{9,1},{17,25},{25,17},{2,10},{10... | collective-permute-start | bytes 258056 | tf_op jit(solution)/shard_map/ppermute | solution.py:49
  17.3 2.4 %collective-permute-start.7 = (bf16[112,384]{1,0:T(8,128)(2,1)S(1)}, bf16[112,384]{1,0:T(8,128)(2,1)S(1)}, u32[]{:S(2)}, u32[]{:S(2)}) collective-permute-start(bf16[112,384]{1,0:T(8,128)(2,1)S(1)} %get-tuple-element.16), channel_id=1, source_target_pairs={{0,16},{8,24},{16,0},{24,8},{1,17},{9,25},{17,1},{25,9},{2,18},{10... | collective-permute-start | bytes 258056 | tf_op jit(solution)/shard_map/ppermute | solution.py:49
  19.7 1.4 %collective-permute-start.8 = (bf16[112,384]{1,0:T(8,128)(2,1)S(1)}, bf16[112,384]{1,0:T(8,128)(2,1)S(1)}, u32[]{:S(2)}, u32[]{:S(2)}) collective-permute-start(bf16[112,384]{1,0:T(8,128)(2,1)S(1)} %get-tuple-element.17), channel_id=1, source_target_pairs={{0,24},{8,16},{16,8},{24,0},{1,25},{9,17},{17,9},{25,1},{2,26},{10... | collective-permute-start | bytes 258056 | tf_op jit(solution)/shard_map/ppermute | solution.py:49
  21.1 1.3 %collective-permute-done.6.refs_1_ = bf16[112,384]{1,0:T(8,128)(2,1)S(1)} collective-permute-done((bf16[112,384]{1,0:T(8,128)(2,1)S(1)}, bf16[112,384]{1,0:T(8,128)(2,1)S(1)}, u32[]{:S(2)}, u32[]{:S(2)}) %collective-permute-start.6) | collective-permute-done | bytes 86048 | tf_op jit(solution)/shard_map/ppermute | solution.py:49
  22.4 4.7 %collective-permute-done.7.refs_2_ = bf16[112,384]{1,0:T(8,128)(2,1)S(1)} collective-permute-done((bf16[112,384]{1,0:T(8,128)(2,1)S(1)}, bf16[112,384]{1,0:T(8,128)(2,1)S(1)}, u32[]{:S(2)}, u32[]{:S(2)}) %collective-permute-start.7) | collective-permute-done | bytes 86048 | tf_op jit(solution)/shard_map/ppermute | solution.py:49
  27.1 0.0 collective-permute-done.8.refs_3_
  27.1 0.2 shard_map.106
  27.4 0.0 collective-permute-start.9
  27.4 1.2 %collective-permute-done.9.other_ref = f32[8,128]{1,0:T(8,128)S(1)} collective-permute-done((f32[8,128]{1,0:T(8,128)S(1)}, f32[8,128]{1,0:T(8,128)S(1)}, u32[]{:S(2)}, u32[]{:S(2)}) %collective-permute-start.9) | collective-permute-done | bytes 4128 | tf_op jit(solution)/shard_map/ppermute | solution.py:63
  28.6 2.5 %collective-permute-start.12 = (f32[8,128]{1,0:T(8,128)S(1)}, f32[8,128]{1,0:T(8,128)S(1)}, u32[]{:S(2)}, u32[]{:S(2)}) collective-permute-start(f32[8,128]{1,0:T(8,128)S(1)} %shard_map.107.refs_0_), channel_id=1, source_target_pairs={{0,6},{1,7},{2,4},{3,5},{4,2},{5,3},{6,0},{7,1},{8,14},{9,15},{10,... | collective-permute-start | bytes 12296 | tf_op jit(solution)/shard_map/ppermute | solution.py:49
  31.1 0.5 %collective-permute-start.11 = (f32[8,128]{1,0:T(8,128)S(1)}, f32[8,128]{1,0:T(8,128)S(1)}, u32[]{:S(2)}, u32[]{:S(2)}) collective-permute-start(f32[8,128]{1,0:T(8,128)S(1)} %shard_map.107.refs_0_), channel_id=1, source_target_pairs={{0,4},{1,5},{2,6},{3,7},{4,0},{5,1},{6,2},{7,3},{8,12},{9,13},{10,... | collective-permute-start | bytes 12296 | tf_op jit(solution)/shard_map/ppermute | solution.py:49
  31.6 0.5 %collective-permute-start.10 = (f32[8,128]{1,0:T(8,128)S(1)}, f32[8,128]{1,0:T(8,128)S(1)}, u32[]{:S(2)}, u32[]{:S(2)}) collective-permute-start(f32[8,128]{1,0:T(8,128)S(1)} %shard_map.107.refs_0_), channel_id=1, source_target_pairs={{0,2},{1,3},{2,0},{3,1},{4,6},{5,7},{6,4},{7,5},{8,10},{9,11},{10,... | collective-permute-start | bytes 12296 | tf_op jit(solution)/shard_map/ppermute | solution.py:49
  32.1 0.1 shard_map.108.refs_6_
  32.2 0.9 %collective-permute-done.12.refs_3_ = f32[8,128]{1,0:T(8,128)S(1)} collective-permute-done((f32[8,128]{1,0:T(8,128)S(1)}, f32[8,128]{1,0:T(8,128)S(1)}, u32[]{:S(2)}, u32[]{:S(2)}) %collective-permute-start.12) | collective-permute-done | bytes 4128 | tf_op jit(solution)/shard_map/ppermute | solution.py:49
  33.1 1.5 %collective-permute-done.11.refs_2_ = f32[8,128]{1,0:T(8,128)S(1)} collective-permute-done((f32[8,128]{1,0:T(8,128)S(1)}, f32[8,128]{1,0:T(8,128)S(1)}, u32[]{:S(2)}, u32[]{:S(2)}) %collective-permute-start.11) | collective-permute-done | bytes 4128 | tf_op jit(solution)/shard_map/ppermute | solution.py:49
  34.7 0.5 %collective-permute-done.10.refs_1_ = f32[8,128]{1,0:T(8,128)S(1)} collective-permute-done((f32[8,128]{1,0:T(8,128)S(1)}, f32[8,128]{1,0:T(8,128)S(1)}, u32[]{:S(2)}, u32[]{:S(2)}) %collective-permute-start.10) | collective-permute-done | bytes 4128 | tf_op jit(solution)/shard_map/ppermute | solution.py:49
  35.2 0.1 shard_map.109.refs_0_
  35.3 2.2 %collective-permute-start.15 = (bf16[32,512]{1,0:T(8,128)(2,1)S(1)}, bf16[32,512]{1,0:T(8,128)(2,1)S(1)}, u32[]{:S(2)}, u32[]{:S(2)}) collective-permute-start(bf16[32,512]{1,0:T(8,128)(2,1)S(1)} %shard_map.109.refs_0_), channel_id=1, source_target_pairs={{0,24},{8,16},{16,8},{24,0},{1,25},{9,17},{17,9},{25,1},{2,26},{10... | collective-permute-start | bytes 98312 | tf_op jit(solution)/shard_map/ppermute | solution.py:49
  37.5 0.8 %collective-permute-start.14 = (bf16[32,512]{1,0:T(8,128)(2,1)S(1)}, bf16[32,512]{1,0:T(8,128)(2,1)S(1)}, u32[]{:S(2)}, u32[]{:S(2)}) collective-permute-start(bf16[32,512]{1,0:T(8,128)(2,1)S(1)} %shard_map.109.refs_0_), channel_id=1, source_target_pairs={{0,16},{8,24},{16,0},{24,8},{1,17},{9,25},{17,1},{25,9},{2,18},{10... | collective-permute-start | bytes 98312 | tf_op jit(solution)/shard_map/ppermute | solution.py:49
  38.4 1.4 %collective-permute-start.13 = (bf16[32,512]{1,0:T(8,128)(2,1)S(1)}, bf16[32,512]{1,0:T(8,128)(2,1)S(1)}, u32[]{:S(2)}, u32[]{:S(2)}) collective-permute-start(bf16[32,512]{1,0:T(8,128)(2,1)S(1)} %shard_map.109.refs_0_), channel_id=1, source_target_pairs={{0,8},{8,0},{16,24},{24,16},{1,9},{9,1},{17,25},{25,17},{2,10},{10... | collective-permute-start | bytes 98312 | tf_op jit(solution)/shard_map/ppermute | solution.py:49
  39.8 1.3 %collective-permute-done.15.refs_3_ = bf16[32,512]{1,0:T(8,128)(2,1)S(1)} collective-permute-done((bf16[32,512]{1,0:T(8,128)(2,1)S(1)}, bf16[32,512]{1,0:T(8,128)(2,1)S(1)}, u32[]{:S(2)}, u32[]{:S(2)}) %collective-permute-start.15) | collective-permute-done | bytes 32800 | tf_op jit(solution)/shard_map/ppermute | solution.py:49
  41.1 1.5 %collective-permute-done.14.refs_2_ = bf16[32,512]{1,0:T(8,128)(2,1)S(1)} collective-permute-done((bf16[32,512]{1,0:T(8,128)(2,1)S(1)}, bf16[32,512]{1,0:T(8,128)(2,1)S(1)}, u32[]{:S(2)}, u32[]{:S(2)}) %collective-permute-start.14) | collective-permute-done | bytes 32800 | tf_op jit(solution)/shard_map/ppermute | solution.py:49
  42.7 0.0 collective-permute-done.13.refs_1_
  42.7 1.0 %shard_map.110 = (f32[1,1]{1,0:T(1,128)}, f32[256,384]{1,0:T(8,128)}, f32[384]{0:T(512)}) custom-call(bf16[32,512]{1,0:T(8,128)(2,1)S(1)} %shard_map.109.refs_0_, bf16[32,512]{1,0:T(8,128)(2,1)S(1)} %collective-permute-done.13.refs_1_, bf16[32,512]{1,0:T(8,128)(2,1)S(1)} %collective-permute-done.14.refs_2_, ...), custom_call_target="tpu_custom_call" | custom-call | tf_op jit(solution)/shard_map/pallas_call | solution.py:400
  (8 shorter events, 0.0 us)
Async XLA Ops:
  0.6 13.0 %copy-start.7 = (bf16[1,16,1024]{2,1,0:T(8,128)(2,1)S(1)}, bf16[1,16,1024]{2,1,0:T(8,128)(2,1)}, u32[]{:S(2)}) copy-start(bf16[1,16,1024]{2,1,0:T(8,128)(2,1)} %param.8) | copy-start | bytes 98308
  0.6 9.1 %collective-permute-start.2 = (bf16[16,1024]{1,0:T(8,128)(2,1)}, bf16[16,1024]{1,0:T(8,128)(2,1)S(1)}, u32[]{:S(2)}, u32[]{:S(2)}) collective-permute-start(bf16[16,1024]{1,0:T(8,128)(2,1)} %bitcast.6), channel_id=1, source_target_pairs={{0,6},{1,7},{2,4},{3,5},{4,2},{5,3},{6,0},{7,1},{8,14},{9,15},{10,... | collective-permute-start | bytes 98312 | tf_op jit(solution)/shard_map/ppermute | solution.py:49
  4.6 5.1 %collective-permute-start.1 = (bf16[16,1024]{1,0:T(8,128)(2,1)}, bf16[16,1024]{1,0:T(8,128)(2,1)S(1)}, u32[]{:S(2)}, u32[]{:S(2)}) collective-permute-start(bf16[16,1024]{1,0:T(8,128)(2,1)} %bitcast.7), channel_id=1, source_target_pairs={{0,4},{1,5},{2,6},{3,7},{4,0},{5,1},{6,2},{7,3},{8,12},{9,13},{10,... | collective-permute-start | bytes 98312 | tf_op jit(solution)/shard_map/ppermute | solution.py:49
  5.1 4.6 %collective-permute-start = (bf16[16,1024]{1,0:T(8,128)(2,1)}, bf16[16,1024]{1,0:T(8,128)(2,1)S(1)}, u32[]{:S(2)}, u32[]{:S(2)}) collective-permute-start(bf16[16,1024]{1,0:T(8,128)(2,1)} %bitcast.8), channel_id=1, source_target_pairs={{0,2},{1,3},{2,0},{3,1},{4,6},{5,7},{6,4},{7,5},{8,10},{9,11},{10,... | collective-permute-start | bytes 98312 | tf_op jit(solution)/shard_map/ppermute | solution.py:49
  5.2 4.7 %collective-permute-start.3 = (bf16[32,1024]{1,0:T(8,128)(2,1)}, bf16[32,1024]{1,0:T(8,128)(2,1)S(1)}, u32[]{:S(2)}, u32[]{:S(2)}) collective-permute-start(bf16[32,1024]{1,0:T(8,128)(2,1)} %refs_3_.1), channel_id=1, source_target_pairs={{0,8},{1,17},{2,10},{3,19},{4,12},{5,21},{6,14},{7,23},{8,0},{9,25... | collective-permute-start | bytes 196616 | tf_op jit(solution)/shard_map/ppermute | solution.py:59
  7.2 6.4 %collective-permute-start.4 = (bf16[32,1024]{1,0:T(8,128)(2,1)}, bf16[32,1024]{1,0:T(8,128)(2,1)S(1)}, u32[]{:S(2)}, u32[]{:S(2)}) collective-permute-start(bf16[32,1024]{1,0:T(8,128)(2,1)} %refs_3_.1), channel_id=1, source_target_pairs={{0,24},{8,16},{16,8},{24,0},{1,25},{9,17},{17,9},{25,1},{2,26},{10... | collective-permute-start | bytes 196616 | tf_op jit(solution)/shard_map/ppermute | solution.py:49
  9.7 5.5 %copy-start = (bf16[1,1024,384]{2,1,0:T(8,128)(2,1)S(1)}, bf16[1,1024,384]{2,1,0:T(8,128)(2,1)}, u32[]{:S(2)}) copy-start(bf16[1,1024,384]{2,1,0:T(8,128)(2,1)} %param.10) | copy-start | bytes 2359300
  9.7 5.5 %copy-start.1 = (bf16[256,384]{1,0:T(8,128)(2,1)S(1)}, bf16[256,384]{1,0:T(8,128)(2,1)}, u32[]{:S(2)}) copy-start(bf16[256,384]{1,0:T(8,128)(2,1)} %refs_7_.1) | copy-start | bytes 589828
  9.7 5.5 %copy-start.2 = (bf16[32,1024]{1,0:T(8,128)(2,1)S(1)}, bf16[32,1024]{1,0:T(8,128)(2,1)}, u32[]{:S(2)}) copy-start(bf16[32,1024]{1,0:T(8,128)(2,1)} %refs_3_.1) | copy-start | bytes 196612
  13.7 1.6 %copy-start.3 = (f32[1024]{0:T(1024)S(1)}, f32[1024]{0:T(1024)}, u32[]{:S(2)}) copy-start(f32[1024]{0:T(1024)} %param.13) | copy-start | bytes 12292
  13.7 1.6 %copy-start.4 = (f32[1,1024]{1,0:T(1,128)S(1)}, f32[1,1024]{1,0:T(1,128)}, u32[]{:S(2)}) copy-start(f32[1,1024]{1,0:T(1,128)} %refs_5_.1) | copy-start | bytes 12292
  13.7 1.6 %copy-start.5 = (f32[384]{0:T(512)S(1)}, f32[384]{0:T(512)}, u32[]{:S(2)}) copy-start(f32[384]{0:T(512)} %refs_9_.1) | copy-start | bytes 4612
  13.7 1.6 %copy-start.6 = (f32[1,384]{1,0:T(1,128)S(1)}, f32[1,384]{1,0:T(1,128)}, u32[]{:S(2)}) copy-start(f32[1,384]{1,0:T(1,128)} %refs_8_.1) | copy-start | bytes 4612
  13.7 1.5 %collective-permute-start.5 = (bf16[96,1024]{1,0:T(8,128)(2,1)S(1)}, bf16[96,1024]{1,0:T(8,128)(2,1)S(1)}, u32[]{:S(2)}, u32[]{:S(2)}) collective-permute-start(bf16[96,1024]{1,0:T(8,128)(2,1)S(1)} %shard_map.104.refs_0_), channel_id=1, source_target_pairs={{0,1},{1,0},{2,3},{3,2},{4,5},{5,4},{6,7},{7,6},{8,9},{9,8},{10,11... | collective-permute-start | bytes 589832 | tf_op jit(solution)/shard_map/ppermute | solution.py:63
  16.7 5.7 %collective-permute-start.6 = (bf16[112,384]{1,0:T(8,128)(2,1)S(1)}, bf16[112,384]{1,0:T(8,128)(2,1)S(1)}, u32[]{:S(2)}, u32[]{:S(2)}) collective-permute-start(bf16[112,384]{1,0:T(8,128)(2,1)S(1)} %get-tuple-element.15), channel_id=1, source_target_pairs={{0,8},{8,0},{16,24},{24,16},{1,9},{9,1},{17,25},{25,17},{2,10},{10... | collective-permute-start | bytes 258056 | tf_op jit(solution)/shard_map/ppermute | solution.py:49
  17.3 9.8 %collective-permute-start.7 = (bf16[112,384]{1,0:T(8,128)(2,1)S(1)}, bf16[112,384]{1,0:T(8,128)(2,1)S(1)}, u32[]{:S(2)}, u32[]{:S(2)}) collective-permute-start(bf16[112,384]{1,0:T(8,128)(2,1)S(1)} %get-tuple-element.16), channel_id=1, source_target_pairs={{0,16},{8,24},{16,0},{24,8},{1,17},{9,25},{17,1},{25,9},{2,18},{10... | collective-permute-start | bytes 258056 | tf_op jit(solution)/shard_map/ppermute | solution.py:49
  19.7 7.4 %collective-permute-start.8 = (bf16[112,384]{1,0:T(8,128)(2,1)S(1)}, bf16[112,384]{1,0:T(8,128)(2,1)S(1)}, u32[]{:S(2)}, u32[]{:S(2)}) collective-permute-start(bf16[112,384]{1,0:T(8,128)(2,1)S(1)} %get-tuple-element.17), channel_id=1, source_target_pairs={{0,24},{8,16},{16,8},{24,0},{1,25},{9,17},{17,9},{25,1},{2,26},{10... | collective-permute-start | bytes 258056 | tf_op jit(solution)/shard_map/ppermute | solution.py:49
  27.4 1.2 %collective-permute-start.9 = (f32[8,128]{1,0:T(8,128)S(1)}, f32[8,128]{1,0:T(8,128)S(1)}, u32[]{:S(2)}, u32[]{:S(2)}) collective-permute-start(f32[8,128]{1,0:T(8,128)S(1)} %get-tuple-element.18.own_ref.refs_4_), channel_id=1, source_target_pairs={{0,1},{1,0},{2,3},{3,2},{4,5},{5,4},{6,7},{7,6},{8,9},{9,8},{10,11... | collective-permute-start | bytes 12296 | tf_op jit(solution)/shard_map/ppermute | solution.py:63
  28.6 4.6 %collective-permute-start.12 = (f32[8,128]{1,0:T(8,128)S(1)}, f32[8,128]{1,0:T(8,128)S(1)}, u32[]{:S(2)}, u32[]{:S(2)}) collective-permute-start(f32[8,128]{1,0:T(8,128)S(1)} %shard_map.107.refs_0_), channel_id=1, source_target_pairs={{0,6},{1,7},{2,4},{3,5},{4,2},{5,3},{6,0},{7,1},{8,14},{9,15},{10,... | collective-permute-start | bytes 12296 | tf_op jit(solution)/shard_map/ppermute | solution.py:49
  31.1 3.6 %collective-permute-start.11 = (f32[8,128]{1,0:T(8,128)S(1)}, f32[8,128]{1,0:T(8,128)S(1)}, u32[]{:S(2)}, u32[]{:S(2)}) collective-permute-start(f32[8,128]{1,0:T(8,128)S(1)} %shard_map.107.refs_0_), channel_id=1, source_target_pairs={{0,4},{1,5},{2,6},{3,7},{4,0},{5,1},{6,2},{7,3},{8,12},{9,13},{10,... | collective-permute-start | bytes 12296 | tf_op jit(solution)/shard_map/ppermute | solution.py:49
  31.6 3.6 %collective-permute-start.10 = (f32[8,128]{1,0:T(8,128)S(1)}, f32[8,128]{1,0:T(8,128)S(1)}, u32[]{:S(2)}, u32[]{:S(2)}) collective-permute-start(f32[8,128]{1,0:T(8,128)S(1)} %shard_map.107.refs_0_), channel_id=1, source_target_pairs={{0,2},{1,3},{2,0},{3,1},{4,6},{5,7},{6,4},{7,5},{8,10},{9,11},{10,... | collective-permute-start | bytes 12296 | tf_op jit(solution)/shard_map/ppermute | solution.py:49
  35.3 5.8 %collective-permute-start.15 = (bf16[32,512]{1,0:T(8,128)(2,1)S(1)}, bf16[32,512]{1,0:T(8,128)(2,1)S(1)}, u32[]{:S(2)}, u32[]{:S(2)}) collective-permute-start(bf16[32,512]{1,0:T(8,128)(2,1)S(1)} %shard_map.109.refs_0_), channel_id=1, source_target_pairs={{0,24},{8,16},{16,8},{24,0},{1,25},{9,17},{17,9},{25,1},{2,26},{10... | collective-permute-start | bytes 98312 | tf_op jit(solution)/shard_map/ppermute | solution.py:49
  37.5 5.2 %collective-permute-start.14 = (bf16[32,512]{1,0:T(8,128)(2,1)S(1)}, bf16[32,512]{1,0:T(8,128)(2,1)S(1)}, u32[]{:S(2)}, u32[]{:S(2)}) collective-permute-start(bf16[32,512]{1,0:T(8,128)(2,1)S(1)} %shard_map.109.refs_0_), channel_id=1, source_target_pairs={{0,16},{8,24},{16,0},{24,8},{1,17},{9,25},{17,1},{25,9},{2,18},{10... | collective-permute-start | bytes 98312 | tf_op jit(solution)/shard_map/ppermute | solution.py:49
  38.4 4.3 %collective-permute-start.13 = (bf16[32,512]{1,0:T(8,128)(2,1)S(1)}, bf16[32,512]{1,0:T(8,128)(2,1)S(1)}, u32[]{:S(2)}, u32[]{:S(2)}) collective-permute-start(bf16[32,512]{1,0:T(8,128)(2,1)S(1)} %shard_map.109.refs_0_), channel_id=1, source_target_pairs={{0,8},{8,0},{16,24},{24,16},{1,9},{9,1},{17,25},{25,17},{2,10},{10... | collective-permute-start | bytes 98312 | tf_op jit(solution)/shard_map/ppermute | solution.py:49

commit v6 on v5

--- a/solution.py
+++ b/solution.py
@@ -49,10 +49,15 @@
     return lax.ppermute(value, axis, pairs)
 
 
+def split_step(j, core, members):
+    return jnp.where(core == 0, 2 * j + 1, 2 * j + 2 if 2 * j + 2 < members else 1)
+
+
 def send_split(value, j):
     members, peers = lax.axis_size("member"), lax.axis_size("dp")
+    steps = 2 * j + 1, (2 * j + 2 if 2 * j + 2 < members else 1)
     pairs = [
-        (m * peers + d, partner(m, 2 * j + 1 + d % 2, members) * peers + d)
+        (m * peers + d, partner(m, steps[d % 2], members) * peers + d)
         for m in range(members)
         for d in range(peers)
     ]
@@ -139,16 +144,21 @@
     out_ref[...] = jnp.zeros_like(out_ref)
 
 
-def join_kernel(chips, splits, *refs):
-    out_ref, parts = refs[-1], refs[: chips + splits]
+def student_kernel(*refs):
+    *parts, gain_ref, _, out_ref = refs
+    rows = parts[0].shape[0]
+    for j, part in enumerate(parts):
+        out_ref[j * rows : (j + 1) * rows, :] = normed(part[...], gain_ref[...])
+
+
+def join_kernel(chips, *refs):
+    *parts, student_ref, out_ref = refs
     chip = lax.axis_index("dp") // 2
     rows = parts[0].shape[0]
     for k in range(chips):
         out_ref[slot(mixed(chip, k, chips, sender), rows), :] = parts[k][...]
     start = chips * rows
-    for part in parts[chips:]:
-        out_ref[start : start + part.shape[0], :] = part[...]
-        start += part.shape[0]
+    out_ref[start:, :] = student_ref[...]
 
 
 def packed3(row, rows, lanes):
@@ -160,7 +170,6 @@
 
 def logits_kernel(members, rows, *refs):
     own_ref, other_ref, refs = refs[0], refs[1], refs[2:]
-    shared, refs = refs[: (members - 1) % 2], refs[(members - 1) % 2 :]
     sources, refs = refs[:7], refs[7:]
     payloads, refs = refs[:members], refs[members:]
     columns_ref, gathered, held, shifted_ref, lse_ref, partial_ref, *params = refs
@@ -178,13 +187,10 @@
         for chip in range(chips):
             at = slot(2 * chip + side, rows)
             gathered[at, :] = normed(source[chip * rows : (chip + 1) * rows, :], gain_ref[...])
-        for j in range((members - 1) // 2):
+        for j in range(members // 2):
             start = chips * rows + j * block
-            at = slot(mixed(mine, 2 * j + 1 + side, members, sender), block)
-            held[at, :] = normed(source[start : start + block, :], student_gain_ref[...])
-    for part in shared:
-        at = slot(mixed(mine, members - 1, members, sender), block)
-        held[at, :] = normed(part[...], student_gain_ref[...])
+            at = slot(mixed(mine, split_step(j, side, members), members, sender), block)
+            held[at, :] = source[start : start + block, :]
     if width % LANES == 0:
         columns_ref[...] = held[:, pl.ds(pl.multiple_of(mine * width, LANES), width)]
     else:
@@ -342,15 +348,16 @@
     width, classes = student_head.shape
     small_rows = -(-(members + 2) // 8) * 8
 
+    first = call(first_kernel, shape((8, LANES), F32), flops=1 << 28)()
+    students = call(
+        student_kernel, shape((members // 2 * block, depth), BF16), flops=1 << 33
+    )(*[send_split(student_feats, j) for j in range(members // 2)], student_gain[None], first)
     parts = [feats] + [send(feats, "dp", k, 2) for k in range(1, chips)]
-    parts += [send_split(student_feats, j) for j in range((members - 1) // 2)]
-    shared = [send(student_feats, "member", members - 1)] * ((members - 1) % 2)
-    first = call(first_kernel, shape((8, LANES), F32), flops=1 << 33)()
     own = call(
-        functools.partial(join_kernel, chips, (members - 1) // 2),
-        shape((chips * rows + (members - 1) // 2 * block, depth), BF16),
+        functools.partial(join_kernel, chips),
+        shape((chips * rows + members // 2 * block, depth), BF16),
         flops=1 << 33,
-    )(*parts, *shared, first)
+    )(*parts, students)
     *payloads, own_columns = call(
         functools.partial(logits_kernel, members, rows),
         [shape((3 * block + PAD, classes), BF16)] * members + [shape((images, width), BF16)],
@@ -369,11 +376,10 @@
             pltpu.VMEM((classes,), F32),
             pltpu.SemaphoreType.DMA((7,)),
         ],
-        [here] * (2 + len(shared)) + [far] * 7,
+        [here] * 2 + [far] * 7,
     )(
         own,
         swap_cores(own, "dp"),
-        *shared,
         student_feats,
         student_gain[None],
         teacher_gain,

time: 43.8 us -> 42.2 us (0.963)
  waiting for transfers between devices: 18.3 us -> 16.6 us
    ppermute x1 -> x2, starting transfers between devices: 1.98 us -> 5.56 us  [send_split(): return lax.ppermute(value, ('member', 'dp'), pairs)]
    ppermute x13 -> x12, starting transfers between devices: 19.5 us -> 15.9 us  [send(): return lax.ppermute(value, axis, pairs)]
    ppermute x13 -> x12, waiting for transfers between devices: 15.6 us -> 13.6 us  [send(): return lax.ppermute(value, axis, pairs)]
  transfers between devices with their start and end apart: 16 -> 16, of which waited for: 11 -> 14; matrix products, arithmetic and copies ran while one was open for 0% -> 0% of each run, Pallas kernels for 0% -> 1%
where the time goes in v6:
time: 42.2 us; the launch traced here: 42.1 us
  starting transfers between devices  21.6 us (51%)
  waiting for transfers between devices  16.6 us (39%)
  Pallas kernels  3.12 us (7%)
  between operations  0.75 us (2%)
    ppermute x12, starting transfers between devices, send(): return lax.ppermute(value, axis, pairs)  15.9 us
    ppermute x12, waiting for transfers between devices, send(): return lax.ppermute(value, axis, pairs)  13.6 us
    ppermute x2, starting transfers between devices, send_split(): return lax.ppermute(value, ('member', 'dp'), pairs)  5.56 us
    ppermute x2, waiting for transfers between devices, swap_cores(): lax.ppermute(value, axis, [(i, i ^ 1) for i in range(lax.axis_size(axis))])  2.67 us
    pallas_call x1, Pallas kernels, on_device(): call(functools.partial(logits_kernel, members, rows), [shape((3 * block +...  1.36 us
    pallas_call x1, Pallas kernels, on_device(): call(functools.partial(gradient_kernel, members, images, classes * peers)...  1 us
  transfers between devices with their start and end apart: 16, of which 14 were waited for; matrix products, arithmetic and copies ran while one was open for 0% of the time, Pallas kernels for 1%

profile of v6, /device:TPU:0, one launch (start us, length us, event | category | flops | bytes accessed | tf_op | source)
XLA Modules:
  0.0 42.1 jit_solution(18417628995660553037)
XLA Ops:
  0.6 3.1 %collective-permute-start.3 = (bf16[32,1024]{1,0:T(8,128)(2,1)}, bf16[32,1024]{1,0:T(8,128)(2,1)S(1)}, u32[]{:S(2)}, u32[]{:S(2)}) collective-permute-start(bf16[32,1024]{1,0:T(8,128)(2,1)} %refs_2_.1), channel_id=1, source_target_pairs={{0,8},{1,17},{2,10},{3,19},{4,12},{5,21},{6,14},{7,23},{8,0},{9,25... | collective-permute-start | bytes 196616 | tf_op jit(solution)/shard_map/ppermute | solution.py:64
  3.7 2.5 %collective-permute-start.4 = (bf16[32,1024]{1,0:T(8,128)(2,1)}, bf16[32,1024]{1,0:T(8,128)(2,1)S(1)}, u32[]{:S(2)}, u32[]{:S(2)}) collective-permute-start(bf16[32,1024]{1,0:T(8,128)(2,1)} %refs_2_.1), channel_id=1, source_target_pairs={{0,24},{1,9},{2,26},{3,11},{4,28},{5,13},{6,30},{7,15},{8,16},{9,1... | collective-permute-start | bytes 196616 | tf_op jit(solution)/shard_map/ppermute | solution.py:64
  6.2 2.4 %collective-permute-start.2 = (bf16[16,1024]{1,0:T(8,128)(2,1)}, bf16[16,1024]{1,0:T(8,128)(2,1)S(1)}, u32[]{:S(2)}, u32[]{:S(2)}) collective-permute-start(bf16[16,1024]{1,0:T(8,128)(2,1)} %bitcast.7), channel_id=1, source_target_pairs={{0,6},{1,7},{2,4},{3,5},{4,2},{5,3},{6,0},{7,1},{8,14},{9,15},{10,... | collective-permute-start | bytes 98312 | tf_op jit(solution)/shard_map/ppermute | solution.py:49
  8.6 0.5 %collective-permute-start.1 = (bf16[16,1024]{1,0:T(8,128)(2,1)}, bf16[16,1024]{1,0:T(8,128)(2,1)S(1)}, u32[]{:S(2)}, u32[]{:S(2)}) collective-permute-start(bf16[16,1024]{1,0:T(8,128)(2,1)} %bitcast.8), channel_id=1, source_target_pairs={{0,4},{1,5},{2,6},{3,7},{4,0},{5,1},{6,2},{7,3},{8,12},{9,13},{10,... | collective-permute-start | bytes 98312 | tf_op jit(solution)/shard_map/ppermute | solution.py:49
  9.2 0.5 %collective-permute-start = (bf16[16,1024]{1,0:T(8,128)(2,1)}, bf16[16,1024]{1,0:T(8,128)(2,1)S(1)}, u32[]{:S(2)}, u32[]{:S(2)}) collective-permute-start(bf16[16,1024]{1,0:T(8,128)(2,1)} %bitcast.9), channel_id=1, source_target_pairs={{0,2},{1,3},{2,0},{3,1},{4,6},{5,7},{6,4},{7,5},{8,10},{9,11},{10,... | collective-permute-start | bytes 98312 | tf_op jit(solution)/shard_map/ppermute | solution.py:49
  9.7 0.0 collective-permute-done.3.refs_0_
  9.7 0.3 collective-permute-done.4.refs_1_
  10.0 0.0 copy-done.3
  10.0 0.2 shard_map.104.refs_4_
  10.2 0.0 copy-start
  10.2 0.0 copy-start.1
  10.2 0.0 copy-start.2
  10.3 1.0 %collective-permute-done.2.refs_3_ = bf16[16,1024]{1,0:T(8,128)(2,1)S(1)} collective-permute-done((bf16[16,1024]{1,0:T(8,128)(2,1)}, bf16[16,1024]{1,0:T(8,128)(2,1)S(1)}, u32[]{:S(2)}, u32[]{:S(2)}) %collective-permute-start.2) | collective-permute-done | bytes 32800 | tf_op jit(solution)/shard_map/ppermute | solution.py:49
  11.3 1.5 %collective-permute-done.1.refs_2_ = bf16[16,1024]{1,0:T(8,128)(2,1)S(1)} collective-permute-done((bf16[16,1024]{1,0:T(8,128)(2,1)}, bf16[16,1024]{1,0:T(8,128)(2,1)S(1)}, u32[]{:S(2)}, u32[]{:S(2)}) %collective-permute-start.1) | collective-permute-done | bytes 32800 | tf_op jit(solution)/shard_map/ppermute | solution.py:49
  12.8 0.5 %collective-permute-done.refs_1_ = bf16[16,1024]{1,0:T(8,128)(2,1)S(1)} collective-permute-done((bf16[16,1024]{1,0:T(8,128)(2,1)}, bf16[16,1024]{1,0:T(8,128)(2,1)S(1)}, u32[]{:S(2)}, u32[]{:S(2)}) %collective-permute-start) | collective-permute-done | bytes 32800 | tf_op jit(solution)/shard_map/ppermute | solution.py:49
  13.3 0.0 copy-done.7
  13.3 0.0 copy-start.6
  13.3 0.1 collective-permute-start.5
  13.4 1.5 %collective-permute-done.5.refs_1_ = bf16[128,1024]{1,0:T(8,128)(2,1)S(1)} collective-permute-done((bf16[128,1024]{1,0:T(8,128)(2,1)S(1)}, bf16[128,1024]{1,0:T(8,128)(2,1)S(1)}, u32[]{:S(2)}, u32[]{:S(2)}) %collective-permute-start.5) | collective-permute-done | bytes 262176 | tf_op jit(solution)/shard_map/ppermute | solution.py:68
  14.9 0.0 copy-done
  14.9 0.0 copy-done.1
  14.9 0.0 copy-done.2
  14.9 0.0 copy-done.4
  15.0 1.4 %shard_map.106 = (bf16[112,384]{1,0:T(8,128)(2,1)S(1)}, bf16[112,384]{1,0:T(8,128)(2,1)S(1)}, bf16[112,384]{1,0:T(8,128)(2,1)S(1)}, bf16[112,384]{1,0:T(8,128)(2,1)S(1)}, bf16[128,256]{1,0:T(8,128)(2,1)S(1)}) custom-call(bf16[128,1024]{1,0:T(8,128)(2,1)S(1)} %shard_map.105.refs_0_, bf16[128,1024]{1,0:T(8,128)(2,1)S(1)} %collective-permute-done.5.refs_1_, ...), custom_call_target="tpu_custom_call" | custom-call | tf_op jit(solution)/shard_map/pallas_call | solution.py:361
  16.3 0.7 %collective-permute-start.6 = (bf16[112,384]{1,0:T(8,128)(2,1)S(1)}, bf16[112,384]{1,0:T(8,128)(2,1)S(1)}, u32[]{:S(2)}, u32[]{:S(2)}) collective-permute-start(bf16[112,384]{1,0:T(8,128)(2,1)S(1)} %get-tuple-element.15), channel_id=1, source_target_pairs={{0,8},{8,0},{16,24},{24,16},{1,9},{9,1},{17,25},{25,17},{2,10},{10... | collective-permute-start | bytes 258056 | tf_op jit(solution)/shard_map/ppermute | solution.py:49
  17.1 1.2 %collective-permute-start.7 = (bf16[112,384]{1,0:T(8,128)(2,1)S(1)}, bf16[112,384]{1,0:T(8,128)(2,1)S(1)}, u32[]{:S(2)}, u32[]{:S(2)}) collective-permute-start(bf16[112,384]{1,0:T(8,128)(2,1)S(1)} %get-tuple-element.16), channel_id=1, source_target_pairs={{0,16},{8,24},{16,0},{24,8},{1,17},{9,25},{17,1},{25,9},{2,18},{10... | collective-permute-start | bytes 258056 | tf_op jit(solution)/shard_map/ppermute | solution.py:49
  18.3 2.5 %collective-permute-start.8 = (bf16[112,384]{1,0:T(8,128)(2,1)S(1)}, bf16[112,384]{1,0:T(8,128)(2,1)S(1)}, u32[]{:S(2)}, u32[]{:S(2)}) collective-permute-start(bf16[112,384]{1,0:T(8,128)(2,1)S(1)} %get-tuple-element.17), channel_id=1, source_target_pairs={{0,24},{8,16},{16,8},{24,0},{1,25},{9,17},{17,9},{25,1},{2,26},{10... | collective-permute-start | bytes 258056 | tf_op jit(solution)/shard_map/ppermute | solution.py:49
  20.8 1.1 %collective-permute-done.6.refs_1_ = bf16[112,384]{1,0:T(8,128)(2,1)S(1)} collective-permute-done((bf16[112,384]{1,0:T(8,128)(2,1)S(1)}, bf16[112,384]{1,0:T(8,128)(2,1)S(1)}, u32[]{:S(2)}, u32[]{:S(2)}) %collective-permute-start.6) | collective-permute-done | bytes 86048 | tf_op jit(solution)/shard_map/ppermute | solution.py:49
  21.9 5.0 %collective-permute-done.7.refs_2_ = bf16[112,384]{1,0:T(8,128)(2,1)S(1)} collective-permute-done((bf16[112,384]{1,0:T(8,128)(2,1)S(1)}, bf16[112,384]{1,0:T(8,128)(2,1)S(1)}, u32[]{:S(2)}, u32[]{:S(2)}) %collective-permute-start.7) | collective-permute-done | bytes 86048 | tf_op jit(solution)/shard_map/ppermute | solution.py:49
  26.9 0.0 collective-permute-done.8.refs_3_
  26.9 0.2 shard_map.107
  27.1 0.0 collective-permute-start.9
  27.1 1.2 %collective-permute-done.9.other_ref = f32[8,128]{1,0:T(8,128)S(1)} collective-permute-done((f32[8,128]{1,0:T(8,128)S(1)}, f32[8,128]{1,0:T(8,128)S(1)}, u32[]{:S(2)}, u32[]{:S(2)}) %collective-permute-start.9) | collective-permute-done | bytes 4128 | tf_op jit(solution)/shard_map/ppermute | solution.py:68
  28.3 1.6 %collective-permute-start.12 = (f32[8,128]{1,0:T(8,128)S(1)}, f32[8,128]{1,0:T(8,128)S(1)}, u32[]{:S(2)}, u32[]{:S(2)}) collective-permute-start(f32[8,128]{1,0:T(8,128)S(1)} %shard_map.108.refs_0_), channel_id=1, source_target_pairs={{0,6},{1,7},{2,4},{3,5},{4,2},{5,3},{6,0},{7,1},{8,14},{9,15},{10,... | collective-permute-start | bytes 12296 | tf_op jit(solution)/shard_map/ppermute | solution.py:49
  29.8 0.5 %collective-permute-start.11 = (f32[8,128]{1,0:T(8,128)S(1)}, f32[8,128]{1,0:T(8,128)S(1)}, u32[]{:S(2)}, u32[]{:S(2)}) collective-permute-start(f32[8,128]{1,0:T(8,128)S(1)} %shard_map.108.refs_0_), channel_id=1, source_target_pairs={{0,4},{1,5},{2,6},{3,7},{4,0},{5,1},{6,2},{7,3},{8,12},{9,13},{10,... | collective-permute-start | bytes 12296 | tf_op jit(solution)/shard_map/ppermute | solution.py:49
  30.3 1.5 %collective-permute-start.10 = (f32[8,128]{1,0:T(8,128)S(1)}, f32[8,128]{1,0:T(8,128)S(1)}, u32[]{:S(2)}, u32[]{:S(2)}) collective-permute-start(f32[8,128]{1,0:T(8,128)S(1)} %shard_map.108.refs_0_), channel_id=1, source_target_pairs={{0,2},{1,3},{2,0},{3,1},{4,6},{5,7},{6,4},{7,5},{8,10},{9,11},{10,... | collective-permute-start | bytes 12296 | tf_op jit(solution)/shard_map/ppermute | solution.py:49
  31.8 0.1 shard_map.109.refs_6_
  31.9 0.9 %collective-permute-done.12.refs_3_ = f32[8,128]{1,0:T(8,128)S(1)} collective-permute-done((f32[8,128]{1,0:T(8,128)S(1)}, f32[8,128]{1,0:T(8,128)S(1)}, u32[]{:S(2)}, u32[]{:S(2)}) %collective-permute-start.12) | collective-permute-done | bytes 4128 | tf_op jit(solution)/shard_map/ppermute | solution.py:49
  32.8 0.6 %collective-permute-done.11.refs_2_ = f32[8,128]{1,0:T(8,128)S(1)} collective-permute-done((f32[8,128]{1,0:T(8,128)S(1)}, f32[8,128]{1,0:T(8,128)S(1)}, u32[]{:S(2)}, u32[]{:S(2)}) %collective-permute-start.11) | collective-permute-done | bytes 4128 | tf_op jit(solution)/shard_map/ppermute | solution.py:49
  33.4 0.5 %collective-permute-done.10.refs_1_ = f32[8,128]{1,0:T(8,128)S(1)} collective-permute-done((f32[8,128]{1,0:T(8,128)S(1)}, f32[8,128]{1,0:T(8,128)S(1)}, u32[]{:S(2)}, u32[]{:S(2)}) %collective-permute-start.10) | collective-permute-done | bytes 4128 | tf_op jit(solution)/shard_map/ppermute | solution.py:49
  34.0 0.1 shard_map.110.refs_0_
  34.1 0.9 %collective-permute-start.15 = (bf16[32,512]{1,0:T(8,128)(2,1)S(1)}, bf16[32,512]{1,0:T(8,128)(2,1)S(1)}, u32[]{:S(2)}, u32[]{:S(2)}) collective-permute-start(bf16[32,512]{1,0:T(8,128)(2,1)S(1)} %shard_map.110.refs_0_), channel_id=1, source_target_pairs={{0,24},{8,16},{16,8},{24,0},{1,25},{9,17},{17,9},{25,1},{2,26},{10... | collective-permute-start | bytes 98312 | tf_op jit(solution)/shard_map/ppermute | solution.py:49
  35.0 2.2 %collective-permute-start.14 = (bf16[32,512]{1,0:T(8,128)(2,1)S(1)}, bf16[32,512]{1,0:T(8,128)(2,1)S(1)}, u32[]{:S(2)}, u32[]{:S(2)}) collective-permute-start(bf16[32,512]{1,0:T(8,128)(2,1)S(1)} %shard_map.110.refs_0_), channel_id=1, source_target_pairs={{0,16},{8,24},{16,0},{24,8},{1,17},{9,25},{17,1},{25,9},{2,18},{10... | collective-permute-start | bytes 98312 | tf_op jit(solution)/shard_map/ppermute | solution.py:49
  37.1 1.4 %collective-permute-start.13 = (bf16[32,512]{1,0:T(8,128)(2,1)S(1)}, bf16[32,512]{1,0:T(8,128)(2,1)S(1)}, u32[]{:S(2)}, u32[]{:S(2)}) collective-permute-start(bf16[32,512]{1,0:T(8,128)(2,1)S(1)} %shard_map.110.refs_0_), channel_id=1, source_target_pairs={{0,8},{8,0},{16,24},{24,16},{1,9},{9,1},{17,25},{25,17},{2,10},{10... | collective-permute-start | bytes 98312 | tf_op jit(solution)/shard_map/ppermute | solution.py:49
  38.6 1.4 %collective-permute-done.15.refs_3_ = bf16[32,512]{1,0:T(8,128)(2,1)S(1)} collective-permute-done((bf16[32,512]{1,0:T(8,128)(2,1)S(1)}, bf16[32,512]{1,0:T(8,128)(2,1)S(1)}, u32[]{:S(2)}, u32[]{:S(2)}) %collective-permute-start.15) | collective-permute-done | bytes 32800 | tf_op jit(solution)/shard_map/ppermute | solution.py:49
  40.0 0.5 %collective-permute-done.14.refs_2_ = bf16[32,512]{1,0:T(8,128)(2,1)S(1)} collective-permute-done((bf16[32,512]{1,0:T(8,128)(2,1)S(1)}, bf16[32,512]{1,0:T(8,128)(2,1)S(1)}, u32[]{:S(2)}, u32[]{:S(2)}) %collective-permute-start.14) | collective-permute-done | bytes 32800 | tf_op jit(solution)/shard_map/ppermute | solution.py:49
  40.5 0.6 %collective-permute-done.13.refs_1_ = bf16[32,512]{1,0:T(8,128)(2,1)S(1)} collective-permute-done((bf16[32,512]{1,0:T(8,128)(2,1)S(1)}, bf16[32,512]{1,0:T(8,128)(2,1)S(1)}, u32[]{:S(2)}, u32[]{:S(2)}) %collective-permute-start.13) | collective-permute-done | bytes 32800 | tf_op jit(solution)/shard_map/ppermute | solution.py:49
  41.1 1.0 %shard_map.111 = (f32[1,1]{1,0:T(1,128)}, f32[256,384]{1,0:T(8,128)}, f32[384]{0:T(512)}) custom-call(bf16[32,512]{1,0:T(8,128)(2,1)S(1)} %shard_map.110.refs_0_, bf16[32,512]{1,0:T(8,128)(2,1)S(1)} %collective-permute-done.13.refs_1_, bf16[32,512]{1,0:T(8,128)(2,1)S(1)} %collective-permute-done.14.refs_2_, ...), custom_call_target="tpu_custom_call" | custom-call | tf_op jit(solution)/shard_map/pallas_call | solution.py:406
  (9 shorter events, 0.1 us)
Async XLA Ops:
  0.6 9.1 %collective-permute-start.3 = (bf16[32,1024]{1,0:T(8,128)(2,1)}, bf16[32,1024]{1,0:T(8,128)(2,1)S(1)}, u32[]{:S(2)}, u32[]{:S(2)}) collective-permute-start(bf16[32,1024]{1,0:T(8,128)(2,1)} %refs_2_.1), channel_id=1, source_target_pairs={{0,8},{1,17},{2,10},{3,19},{4,12},{5,21},{6,14},{7,23},{8,0},{9,25... | collective-permute-start | bytes 196616 | tf_op jit(solution)/shard_map/ppermute | solution.py:64
  3.7 6.3 %collective-permute-start.4 = (bf16[32,1024]{1,0:T(8,128)(2,1)}, bf16[32,1024]{1,0:T(8,128)(2,1)S(1)}, u32[]{:S(2)}, u32[]{:S(2)}) collective-permute-start(bf16[32,1024]{1,0:T(8,128)(2,1)} %refs_2_.1), channel_id=1, source_target_pairs={{0,24},{1,9},{2,26},{3,11},{4,28},{5,13},{6,30},{7,15},{8,16},{9,1... | collective-permute-start | bytes 196616 | tf_op jit(solution)/shard_map/ppermute | solution.py:64
  6.2 3.8 %copy-start.3 = (f32[1024]{0:T(1024)S(1)}, f32[1024]{0:T(1024)}, u32[]{:S(2)}) copy-start(f32[1024]{0:T(1024)} %param.13) | copy-start | bytes 12292
  6.2 5.1 %collective-permute-start.2 = (bf16[16,1024]{1,0:T(8,128)(2,1)}, bf16[16,1024]{1,0:T(8,128)(2,1)S(1)}, u32[]{:S(2)}, u32[]{:S(2)}) collective-permute-start(bf16[16,1024]{1,0:T(8,128)(2,1)} %bitcast.7), channel_id=1, source_target_pairs={{0,6},{1,7},{2,4},{3,5},{4,2},{5,3},{6,0},{7,1},{8,14},{9,15},{10,... | collective-permute-start | bytes 98312 | tf_op jit(solution)/shard_map/ppermute | solution.py:49
  8.6 4.1 %collective-permute-start.1 = (bf16[16,1024]{1,0:T(8,128)(2,1)}, bf16[16,1024]{1,0:T(8,128)(2,1)S(1)}, u32[]{:S(2)}, u32[]{:S(2)}) collective-permute-start(bf16[16,1024]{1,0:T(8,128)(2,1)} %bitcast.8), channel_id=1, source_target_pairs={{0,4},{1,5},{2,6},{3,7},{4,0},{5,1},{6,2},{7,3},{8,12},{9,13},{10,... | collective-permute-start | bytes 98312 | tf_op jit(solution)/shard_map/ppermute | solution.py:49
  9.2 4.1 %collective-permute-start = (bf16[16,1024]{1,0:T(8,128)(2,1)}, bf16[16,1024]{1,0:T(8,128)(2,1)S(1)}, u32[]{:S(2)}, u32[]{:S(2)}) collective-permute-start(bf16[16,1024]{1,0:T(8,128)(2,1)} %bitcast.9), channel_id=1, source_target_pairs={{0,2},{1,3},{2,0},{3,1},{4,6},{5,7},{6,4},{7,5},{8,10},{9,11},{10,... | collective-permute-start | bytes 98312 | tf_op jit(solution)/shard_map/ppermute | solution.py:49
  10.0 3.3 %copy-start.7 = (bf16[1,16,1024]{2,1,0:T(8,128)(2,1)S(1)}, bf16[1,16,1024]{2,1,0:T(8,128)(2,1)}, u32[]{:S(2)}) copy-start(bf16[1,16,1024]{2,1,0:T(8,128)(2,1)} %param.8) | copy-start | bytes 98308
  10.2 4.7 %copy-start = (bf16[1,1024,384]{2,1,0:T(8,128)(2,1)S(1)}, bf16[1,1024,384]{2,1,0:T(8,128)(2,1)}, u32[]{:S(2)}) copy-start(bf16[1,1024,384]{2,1,0:T(8,128)(2,1)} %param.10) | copy-start | bytes 2359300
  10.2 4.7 %copy-start.1 = (bf16[256,384]{1,0:T(8,128)(2,1)S(1)}, bf16[256,384]{1,0:T(8,128)(2,1)}, u32[]{:S(2)}) copy-start(bf16[256,384]{1,0:T(8,128)(2,1)} %refs_6_.1) | copy-start | bytes 589828
  10.2 4.7 %copy-start.2 = (bf16[32,1024]{1,0:T(8,128)(2,1)S(1)}, bf16[32,1024]{1,0:T(8,128)(2,1)}, u32[]{:S(2)}) copy-start(bf16[32,1024]{1,0:T(8,128)(2,1)} %refs_2_.1) | copy-start | bytes 196612
  13.3 1.7 %copy-start.4 = (f32[1,1024]{1,0:T(1,128)S(1)}, f32[1,1024]{1,0:T(1,128)}, u32[]{:S(2)}) copy-start(f32[1,1024]{1,0:T(1,128)} %refs_4_.1) | copy-start | bytes 12292
  13.3 1.7 %copy-start.5 = (f32[384]{0:T(512)S(1)}, f32[384]{0:T(512)}, u32[]{:S(2)}) copy-start(f32[384]{0:T(512)} %refs_8_.1) | copy-start | bytes 4612
  13.3 1.6 %copy-start.6 = (f32[1,384]{1,0:T(1,128)S(1)}, f32[1,384]{1,0:T(1,128)}, u32[]{:S(2)}) copy-start(f32[1,384]{1,0:T(1,128)} %refs_7_.1) | copy-start | bytes 4612
  13.3 1.6 %collective-permute-start.5 = (bf16[128,1024]{1,0:T(8,128)(2,1)S(1)}, bf16[128,1024]{1,0:T(8,128)(2,1)S(1)}, u32[]{:S(2)}, u32[]{:S(2)}) collective-permute-start(bf16[128,1024]{1,0:T(8,128)(2,1)S(1)} %shard_map.105.refs_0_), channel_id=1, source_target_pairs={{0,1},{1,0},{2,3},{3,2},{4,5},{5,4},{6,7},{7,6},{8,9},{9,8},{10,11... | collective-permute-start | bytes 786440 | tf_op jit(solution)/shard_map/ppermute | solution.py:68
  16.3 5.5 %collective-permute-start.6 = (bf16[112,384]{1,0:T(8,128)(2,1)S(1)}, bf16[112,384]{1,0:T(8,128)(2,1)S(1)}, u32[]{:S(2)}, u32[]{:S(2)}) collective-permute-start(bf16[112,384]{1,0:T(8,128)(2,1)S(1)} %get-tuple-element.15), channel_id=1, source_target_pairs={{0,8},{8,0},{16,24},{24,16},{1,9},{9,1},{17,25},{25,17},{2,10},{10... | collective-permute-start | bytes 258056 | tf_op jit(solution)/shard_map/ppermute | solution.py:49
  17.1 9.8 %collective-permute-start.7 = (bf16[112,384]{1,0:T(8,128)(2,1)S(1)}, bf16[112,384]{1,0:T(8,128)(2,1)S(1)}, u32[]{:S(2)}, u32[]{:S(2)}) collective-permute-start(bf16[112,384]{1,0:T(8,128)(2,1)S(1)} %get-tuple-element.16), channel_id=1, source_target_pairs={{0,16},{8,24},{16,0},{24,8},{1,17},{9,25},{17,1},{25,9},{2,18},{10... | collective-permute-start | bytes 258056 | tf_op jit(solution)/shard_map/ppermute | solution.py:49
  18.3 8.5 %collective-permute-start.8 = (bf16[112,384]{1,0:T(8,128)(2,1)S(1)}, bf16[112,384]{1,0:T(8,128)(2,1)S(1)}, u32[]{:S(2)}, u32[]{:S(2)}) collective-permute-start(bf16[112,384]{1,0:T(8,128)(2,1)S(1)} %get-tuple-element.17), channel_id=1, source_target_pairs={{0,24},{8,16},{16,8},{24,0},{1,25},{9,17},{17,9},{25,1},{2,26},{10... | collective-permute-start | bytes 258056 | tf_op jit(solution)/shard_map/ppermute | solution.py:49
  27.1 1.2 %collective-permute-start.9 = (f32[8,128]{1,0:T(8,128)S(1)}, f32[8,128]{1,0:T(8,128)S(1)}, u32[]{:S(2)}, u32[]{:S(2)}) collective-permute-start(f32[8,128]{1,0:T(8,128)S(1)} %get-tuple-element.18.own_ref.refs_4_), channel_id=1, source_target_pairs={{0,1},{1,0},{2,3},{3,2},{4,5},{5,4},{6,7},{7,6},{8,9},{9,8},{10,11... | collective-permute-start | bytes 12296 | tf_op jit(solution)/shard_map/ppermute | solution.py:68
  28.3 4.6 %collective-permute-start.12 = (f32[8,128]{1,0:T(8,128)S(1)}, f32[8,128]{1,0:T(8,128)S(1)}, u32[]{:S(2)}, u32[]{:S(2)}) collective-permute-start(f32[8,128]{1,0:T(8,128)S(1)} %shard_map.108.refs_0_), channel_id=1, source_target_pairs={{0,6},{1,7},{2,4},{3,5},{4,2},{5,3},{6,0},{7,1},{8,14},{9,15},{10,... | collective-permute-start | bytes 12296 | tf_op jit(solution)/shard_map/ppermute | solution.py:49
  29.8 3.6 %collective-permute-start.11 = (f32[8,128]{1,0:T(8,128)S(1)}, f32[8,128]{1,0:T(8,128)S(1)}, u32[]{:S(2)}, u32[]{:S(2)}) collective-permute-start(f32[8,128]{1,0:T(8,128)S(1)} %shard_map.108.refs_0_), channel_id=1, source_target_pairs={{0,4},{1,5},{2,6},{3,7},{4,0},{5,1},{6,2},{7,3},{8,12},{9,13},{10,... | collective-permute-start | bytes 12296 | tf_op jit(solution)/shard_map/ppermute | solution.py:49
  30.3 3.6 %collective-permute-start.10 = (f32[8,128]{1,0:T(8,128)S(1)}, f32[8,128]{1,0:T(8,128)S(1)}, u32[]{:S(2)}, u32[]{:S(2)}) collective-permute-start(f32[8,128]{1,0:T(8,128)S(1)} %shard_map.108.refs_0_), channel_id=1, source_target_pairs={{0,2},{1,3},{2,0},{3,1},{4,6},{5,7},{6,4},{7,5},{8,10},{9,11},{10,... | collective-permute-start | bytes 12296 | tf_op jit(solution)/shard_map/ppermute | solution.py:49
  34.1 5.9 %collective-permute-start.15 = (bf16[32,512]{1,0:T(8,128)(2,1)S(1)}, bf16[32,512]{1,0:T(8,128)(2,1)S(1)}, u32[]{:S(2)}, u32[]{:S(2)}) collective-permute-start(bf16[32,512]{1,0:T(8,128)(2,1)S(1)} %shard_map.110.refs_0_), channel_id=1, source_target_pairs={{0,24},{8,16},{16,8},{24,0},{1,25},{9,17},{17,9},{25,1},{2,26},{10... | collective-permute-start | bytes 98312 | tf_op jit(solution)/shard_map/ppermute | solution.py:49
  35.0 5.5 %collective-permute-start.14 = (bf16[32,512]{1,0:T(8,128)(2,1)S(1)}, bf16[32,512]{1,0:T(8,128)(2,1)S(1)}, u32[]{:S(2)}, u32[]{:S(2)}) collective-permute-start(bf16[32,512]{1,0:T(8,128)(2,1)S(1)} %shard_map.110.refs_0_), channel_id=1, source_target_pairs={{0,16},{8,24},{16,0},{24,8},{1,17},{9,25},{17,1},{25,9},{2,18},{10... | collective-permute-start | bytes 98312 | tf_op jit(solution)/shard_map/ppermute | solution.py:49
  37.1 3.9 %collective-permute-start.13 = (bf16[32,512]{1,0:T(8,128)(2,1)S(1)}, bf16[32,512]{1,0:T(8,128)(2,1)S(1)}, u32[]{:S(2)}, u32[]{:S(2)}) collective-permute-start(bf16[32,512]{1,0:T(8,128)(2,1)S(1)} %shard_map.110.refs_0_), channel_id=1, source_target_pairs={{0,8},{8,0},{16,24},{24,16},{1,9},{9,1},{17,25},{25,17},{2,10},{10... | collective-permute-start | bytes 98312 | tf_op jit(solution)/shard_map/ppermute | solution.py:49

commit v7 on v6

--- a/solution.py
+++ b/solution.py
@@ -172,7 +172,7 @@
     own_ref, other_ref, refs = refs[0], refs[1], refs[2:]
     sources, refs = refs[:7], refs[7:]
     payloads, refs = refs[:members], refs[members:]
-    columns_ref, gathered, held, shifted_ref, lse_ref, partial_ref, *params = refs
+    own_logits_ref, columns_ref, gathered, held, shifted_ref, lse_ref, partial_ref, *params = refs
     feats_ref, student_gain_ref, gain_ref, head_ref, student_ref, bias_ref, student_bias_ref = params[:7]
     copies = fetch(sources, params[:7], params[7])
     mine, place = lax.axis_index("member"), lax.axis_index("dp")
@@ -211,29 +211,27 @@
         at = slot(mixed(mine, k, members, partner), block)
         out = payloads[k]
         out[0:block, :] = shifted_ref[at, :]
-        partial = partial_ref[at, :]
         if k == 0:
-            partial += student_bias_ref[...][None, :]
-        high, middle, _ = split3(partial)
-        out[block : 2 * block, :] = high
-        out[2 * block : 3 * block, :] = middle
-        out[3 * block :, :] = packed3(to_lanes(lse_ref[at, 0:1], classes), PAD, classes)
+            own_logits_ref[...] = partial_ref[at, :] + student_bias_ref[...][None, :]
+        out[block : 2 * block, :] = partial_ref[at, :].astype(BF16)
+        out[2 * block :, :] = packed3(to_lanes(lse_ref[at, 0:1], classes), PAD, classes)
 
 
 def alphas_kernel(members, *refs):
     payloads, refs = refs[:members], refs[members:]
-    alphas_ref, target_ref, small_ref = refs
+    own_logits_ref, alphas_ref, target_ref, small_ref = refs
     mine = lax.axis_index("member")
     block, classes = alphas_ref.shape
     target = jnp.zeros((block, classes), F32)
-    logits = jnp.zeros((block, classes), F32)
+    logits = own_logits_ref[...]
     lse_total = jnp.zeros((1, LANES), F32)
     small_ref[...] = jnp.zeros_like(small_ref)
     for k in range(members):
         got = payloads[k]
         target += got[0:block, :].astype(F32)
-        logits += got[block : 2 * block, :].astype(F32) + got[2 * block : 3 * block, :].astype(F32)
-        tail = got[3 * block :, 0:LANES].astype(F32)
+        if k > 0:
+            logits += got[block : 2 * block, :].astype(F32)
+        tail = got[2 * block :, 0:LANES].astype(F32)
         lse = tail[0:1, :] + tail[1:2, :] + tail[2:3, :]
         lse_total += lse
         small_ref[pl.ds(mixed(mine, k, members, sender), 1), :] = lse
@@ -358,9 +356,10 @@
         shape((chips * rows + members // 2 * block, depth), BF16),
         flops=1 << 33,
     )(*parts, students)
-    *payloads, own_columns = call(
+    *payloads, own_logits, own_columns = call(
         functools.partial(logits_kernel, members, rows),
-        [shape((3 * block + PAD, classes), BF16)] * members + [shape((images, width), BF16)],
+        [shape((2 * block + PAD, classes), BF16)] * members
+        + [shape((block, classes), F32), shape((images, width), BF16)],
         [
             pltpu.VMEM((images, depth), BF16),
             pltpu.VMEM((images, depth), BF16),
@@ -392,7 +391,7 @@
     alphas, target, own = call(
         functools.partial(alphas_kernel, members),
         [shape((block, classes), F32)] * 2 + [shape((small_rows, LANES), F32)],
-    )(*got)
+    )(*got, own_logits)
     other = swap_cores(own, "dp")
     inner = call(digamma_kernel, shape((block, classes), F32))(alphas, target)
     small = call(functools.partial(combine_kernel, members), shape(own.shape, F32))(own, other)

time: 42.2 us -> 40.5 us (0.960)
  waiting for transfers between devices: 16.6 us -> 14.8 us
    ppermute x12, waiting for transfers between devices: 13.6 us -> 11.8 us  [send(): return lax.ppermute(value, axis, pairs)]
where the time goes in v7:
time: 40.5 us; the launch traced here: 40.3 us
  starting transfers between devices  21.6 us (53%)
  waiting for transfers between devices  14.8 us (37%)
  Pallas kernels  3.13 us (8%)
  between operations  0.75 us (2%)
    ppermute x12, starting transfers between devices, send(): return lax.ppermute(value, axis, pairs)  15.9 us
    ppermute x12, waiting for transfers between devices, send(): return lax.ppermute(value, axis, pairs)  11.8 us
    ppermute x2, starting transfers between devices, send_split(): return lax.ppermute(value, ('member', 'dp'), pairs)  5.56 us
    ppermute x2, waiting for transfers between devices, swap_cores(): lax.ppermute(value, axis, [(i, i ^ 1) for i in range(lax.axis_size(axis))])  2.67 us
    pallas_call x1, Pallas kernels, on_device(): call(functools.partial(logits_kernel, members, rows), [shape((2 * block +...  1.38 us
    pallas_call x1, Pallas kernels, on_device(): call(functools.partial(gradient_kernel, members, images, classes * peers)...  1 us
  transfers between devices with their start and end apart: 16, of which 14 were waited for; matrix products, arithmetic and copies ran while one was open for 0% of the time, Pallas kernels for 1%

profile of v7, /device:TPU:0, one launch (start us, length us, event | category | flops | bytes accessed | tf_op | source)
XLA Modules:
  0.0 40.3 jit_solution(4094952450402403094)
XLA Ops:
  0.6 3.1 %collective-permute-start.3 = (bf16[32,1024]{1,0:T(8,128)(2,1)}, bf16[32,1024]{1,0:T(8,128)(2,1)S(1)}, u32[]{:S(2)}, u32[]{:S(2)}) collective-permute-start(bf16[32,1024]{1,0:T(8,128)(2,1)} %refs_2_.1), channel_id=1, source_target_pairs={{0,8},{1,17},{2,10},{3,19},{4,12},{5,21},{6,14},{7,23},{8,0},{9,25... | collective-permute-start | bytes 196616 | tf_op jit(solution)/shard_map/ppermute | solution.py:64
  3.7 2.5 %collective-permute-start.4 = (bf16[32,1024]{1,0:T(8,128)(2,1)}, bf16[32,1024]{1,0:T(8,128)(2,1)S(1)}, u32[]{:S(2)}, u32[]{:S(2)}) collective-permute-start(bf16[32,1024]{1,0:T(8,128)(2,1)} %refs_2_.1), channel_id=1, source_target_pairs={{0,24},{1,9},{2,26},{3,11},{4,28},{5,13},{6,30},{7,15},{8,16},{9,1... | collective-permute-start | bytes 196616 | tf_op jit(solution)/shard_map/ppermute | solution.py:64
  6.2 2.4 %collective-permute-start.2 = (bf16[16,1024]{1,0:T(8,128)(2,1)}, bf16[16,1024]{1,0:T(8,128)(2,1)S(1)}, u32[]{:S(2)}, u32[]{:S(2)}) collective-permute-start(bf16[16,1024]{1,0:T(8,128)(2,1)} %bitcast.7), channel_id=1, source_target_pairs={{0,6},{1,7},{2,4},{3,5},{4,2},{5,3},{6,0},{7,1},{8,14},{9,15},{10,... | collective-permute-start | bytes 98312 | tf_op jit(solution)/shard_map/ppermute | solution.py:49
  8.6 0.5 %collective-permute-start.1 = (bf16[16,1024]{1,0:T(8,128)(2,1)}, bf16[16,1024]{1,0:T(8,128)(2,1)S(1)}, u32[]{:S(2)}, u32[]{:S(2)}) collective-permute-start(bf16[16,1024]{1,0:T(8,128)(2,1)} %bitcast.8), channel_id=1, source_target_pairs={{0,4},{1,5},{2,6},{3,7},{4,0},{5,1},{6,2},{7,3},{8,12},{9,13},{10,... | collective-permute-start | bytes 98312 | tf_op jit(solution)/shard_map/ppermute | solution.py:49
  9.2 0.5 %collective-permute-start = (bf16[16,1024]{1,0:T(8,128)(2,1)}, bf16[16,1024]{1,0:T(8,128)(2,1)S(1)}, u32[]{:S(2)}, u32[]{:S(2)}) collective-permute-start(bf16[16,1024]{1,0:T(8,128)(2,1)} %bitcast.9), channel_id=1, source_target_pairs={{0,2},{1,3},{2,0},{3,1},{4,6},{5,7},{6,4},{7,5},{8,10},{9,11},{10,... | collective-permute-start | bytes 98312 | tf_op jit(solution)/shard_map/ppermute | solution.py:49
  9.7 0.0 collective-permute-done.3.refs_0_
  9.7 0.3 collective-permute-done.4.refs_1_
  10.0 0.0 copy-done.3
  10.0 0.2 shard_map.104.refs_4_
  10.2 0.0 copy-start
  10.2 0.0 copy-start.1
  10.2 0.0 copy-start.2
  10.3 1.0 %collective-permute-done.2.refs_3_ = bf16[16,1024]{1,0:T(8,128)(2,1)S(1)} collective-permute-done((bf16[16,1024]{1,0:T(8,128)(2,1)}, bf16[16,1024]{1,0:T(8,128)(2,1)S(1)}, u32[]{:S(2)}, u32[]{:S(2)}) %collective-permute-start.2) | collective-permute-done | bytes 32800 | tf_op jit(solution)/shard_map/ppermute | solution.py:49
  11.3 1.5 %collective-permute-done.1.refs_2_ = bf16[16,1024]{1,0:T(8,128)(2,1)S(1)} collective-permute-done((bf16[16,1024]{1,0:T(8,128)(2,1)}, bf16[16,1024]{1,0:T(8,128)(2,1)S(1)}, u32[]{:S(2)}, u32[]{:S(2)}) %collective-permute-start.1) | collective-permute-done | bytes 32800 | tf_op jit(solution)/shard_map/ppermute | solution.py:49
  12.8 0.5 %collective-permute-done.refs_1_ = bf16[16,1024]{1,0:T(8,128)(2,1)S(1)} collective-permute-done((bf16[16,1024]{1,0:T(8,128)(2,1)}, bf16[16,1024]{1,0:T(8,128)(2,1)S(1)}, u32[]{:S(2)}, u32[]{:S(2)}) %collective-permute-start) | collective-permute-done | bytes 32800 | tf_op jit(solution)/shard_map/ppermute | solution.py:49
  13.3 0.0 copy-done.7
  13.3 0.0 copy-start.6
  13.3 0.1 collective-permute-start.5
  13.4 1.5 %collective-permute-done.5.refs_1_ = bf16[128,1024]{1,0:T(8,128)(2,1)S(1)} collective-permute-done((bf16[128,1024]{1,0:T(8,128)(2,1)S(1)}, bf16[128,1024]{1,0:T(8,128)(2,1)S(1)}, u32[]{:S(2)}, u32[]{:S(2)}) %collective-permute-start.5) | collective-permute-done | bytes 262176 | tf_op jit(solution)/shard_map/ppermute | solution.py:68
  14.9 0.0 copy-done.2
  14.9 0.0 copy-done.4
  15.0 0.0 copy-done.5
  15.0 0.0 copy-done.6
  15.0 1.4 %shard_map.106 = (bf16[80,384]{1,0:T(8,128)(2,1)S(1)}, bf16[80,384]{1,0:T(8,128)(2,1)S(1)}, bf16[80,384]{1,0:T(8,128)(2,1)S(1)}, bf16[80,384]{1,0:T(8,128)(2,1)S...) custom-call(bf16[128,1024]{1,0:T(8,128)(2,1)S(1)} %shard_map.105.refs_0_, ...), custom_call_target="tpu_custom_call" | custom-call | tf_op jit(solution)/shard_map/pallas_call | solution.py:359
  16.4 0.8 %collective-permute-start.6 = (bf16[80,384]{1,0:T(8,128)(2,1)S(1)}, bf16[80,384]{1,0:T(8,128)(2,1)S(1)}, u32[]{:S(2)}, u32[]{:S(2)}) collective-permute-start(bf16[80,384]{1,0:T(8,128)(2,1)S(1)} %get-tuple-element.16), channel_id=1, source_target_pairs={{0,8},{8,0},{16,24},{24,16},{1,9},{9,1},{17,25},{25,17},{2,10},{10... | collective-permute-start | bytes 184328 | tf_op jit(solution)/shard_map/ppermute | solution.py:49
  17.1 1.2 %collective-permute-start.7 = (bf16[80,384]{1,0:T(8,128)(2,1)S(1)}, bf16[80,384]{1,0:T(8,128)(2,1)S(1)}, u32[]{:S(2)}, u32[]{:S(2)}) collective-permute-start(bf16[80,384]{1,0:T(8,128)(2,1)S(1)} %get-tuple-element.17), channel_id=1, source_target_pairs={{0,16},{8,24},{16,0},{24,8},{1,17},{9,25},{17,1},{25,9},{2,18},{10... | collective-permute-start | bytes 184328 | tf_op jit(solution)/shard_map/ppermute | solution.py:49
  18.3 2.5 %collective-permute-start.8 = (bf16[80,384]{1,0:T(8,128)(2,1)S(1)}, bf16[80,384]{1,0:T(8,128)(2,1)S(1)}, u32[]{:S(2)}, u32[]{:S(2)}) collective-permute-start(bf16[80,384]{1,0:T(8,128)(2,1)S(1)} %get-tuple-element.18), channel_id=1, source_target_pairs={{0,24},{8,16},{16,8},{24,0},{1,25},{9,17},{17,9},{25,1},{2,26},{10... | collective-permute-start | bytes 184328 | tf_op jit(solution)/shard_map/ppermute | solution.py:49
  20.8 0.5 %collective-permute-done.6.refs_1_ = bf16[80,384]{1,0:T(8,128)(2,1)S(1)} collective-permute-done((bf16[80,384]{1,0:T(8,128)(2,1)S(1)}, bf16[80,384]{1,0:T(8,128)(2,1)S(1)}, u32[]{:S(2)}, u32[]{:S(2)}) %collective-permute-start.6) | collective-permute-done | bytes 61472 | tf_op jit(solution)/shard_map/ppermute | solution.py:49
  21.3 3.7 %collective-permute-done.7.refs_2_ = bf16[80,384]{1,0:T(8,128)(2,1)S(1)} collective-permute-done((bf16[80,384]{1,0:T(8,128)(2,1)S(1)}, bf16[80,384]{1,0:T(8,128)(2,1)S(1)}, u32[]{:S(2)}, u32[]{:S(2)}) %collective-permute-start.7) | collective-permute-done | bytes 61472 | tf_op jit(solution)/shard_map/ppermute | solution.py:49
  25.1 0.0 collective-permute-done.8.refs_3_
  25.1 0.2 shard_map.107
  25.3 0.0 collective-permute-start.9
  25.3 1.2 %collective-permute-done.9.other_ref = f32[8,128]{1,0:T(8,128)S(1)} collective-permute-done((f32[8,128]{1,0:T(8,128)S(1)}, f32[8,128]{1,0:T(8,128)S(1)}, u32[]{:S(2)}, u32[]{:S(2)}) %collective-permute-start.9) | collective-permute-done | bytes 4128 | tf_op jit(solution)/shard_map/ppermute | solution.py:68
  26.5 1.6 %collective-permute-start.12 = (f32[8,128]{1,0:T(8,128)S(1)}, f32[8,128]{1,0:T(8,128)S(1)}, u32[]{:S(2)}, u32[]{:S(2)}) collective-permute-start(f32[8,128]{1,0:T(8,128)S(1)} %shard_map.108.refs_0_), channel_id=1, source_target_pairs={{0,6},{1,7},{2,4},{3,5},{4,2},{5,3},{6,0},{7,1},{8,14},{9,15},{10,... | collective-permute-start | bytes 12296 | tf_op jit(solution)/shard_map/ppermute | solution.py:49
  28.0 0.5 %collective-permute-start.11 = (f32[8,128]{1,0:T(8,128)S(1)}, f32[8,128]{1,0:T(8,128)S(1)}, u32[]{:S(2)}, u32[]{:S(2)}) collective-permute-start(f32[8,128]{1,0:T(8,128)S(1)} %shard_map.108.refs_0_), channel_id=1, source_target_pairs={{0,4},{1,5},{2,6},{3,7},{4,0},{5,1},{6,2},{7,3},{8,12},{9,13},{10,... | collective-permute-start | bytes 12296 | tf_op jit(solution)/shard_map/ppermute | solution.py:49
  28.5 1.5 %collective-permute-start.10 = (f32[8,128]{1,0:T(8,128)S(1)}, f32[8,128]{1,0:T(8,128)S(1)}, u32[]{:S(2)}, u32[]{:S(2)}) collective-permute-start(f32[8,128]{1,0:T(8,128)S(1)} %shard_map.108.refs_0_), channel_id=1, source_target_pairs={{0,2},{1,3},{2,0},{3,1},{4,6},{5,7},{6,4},{7,5},{8,10},{9,11},{10,... | collective-permute-start | bytes 12296 | tf_op jit(solution)/shard_map/ppermute | solution.py:49
  30.0 0.1 shard_map.109.refs_6_
  30.1 0.9 %collective-permute-done.12.refs_3_ = f32[8,128]{1,0:T(8,128)S(1)} collective-permute-done((f32[8,128]{1,0:T(8,128)S(1)}, f32[8,128]{1,0:T(8,128)S(1)}, u32[]{:S(2)}, u32[]{:S(2)}) %collective-permute-start.12) | collective-permute-done | bytes 4128 | tf_op jit(solution)/shard_map/ppermute | solution.py:49
  31.0 0.6 %collective-permute-done.11.refs_2_ = f32[8,128]{1,0:T(8,128)S(1)} collective-permute-done((f32[8,128]{1,0:T(8,128)S(1)}, f32[8,128]{1,0:T(8,128)S(1)}, u32[]{:S(2)}, u32[]{:S(2)}) %collective-permute-start.11) | collective-permute-done | bytes 4128 | tf_op jit(solution)/shard_map/ppermute | solution.py:49
  31.6 0.5 %collective-permute-done.10.refs_1_ = f32[8,128]{1,0:T(8,128)S(1)} collective-permute-done((f32[8,128]{1,0:T(8,128)S(1)}, f32[8,128]{1,0:T(8,128)S(1)}, u32[]{:S(2)}, u32[]{:S(2)}) %collective-permute-start.10) | collective-permute-done | bytes 4128 | tf_op jit(solution)/shard_map/ppermute | solution.py:49
  32.1 0.1 shard_map.110.refs_0_
  32.3 2.0 %collective-permute-start.15 = (bf16[32,512]{1,0:T(8,128)(2,1)S(1)}, bf16[32,512]{1,0:T(8,128)(2,1)S(1)}, u32[]{:S(2)}, u32[]{:S(2)}) collective-permute-start(bf16[32,512]{1,0:T(8,128)(2,1)S(1)} %shard_map.110.refs_0_), channel_id=1, source_target_pairs={{0,24},{8,16},{16,8},{24,0},{1,25},{9,17},{17,9},{25,1},{2,26},{10... | collective-permute-start | bytes 98312 | tf_op jit(solution)/shard_map/ppermute | solution.py:49
  34.2 0.8 %collective-permute-start.14 = (bf16[32,512]{1,0:T(8,128)(2,1)S(1)}, bf16[32,512]{1,0:T(8,128)(2,1)S(1)}, u32[]{:S(2)}, u32[]{:S(2)}) collective-permute-start(bf16[32,512]{1,0:T(8,128)(2,1)S(1)} %shard_map.110.refs_0_), channel_id=1, source_target_pairs={{0,16},{8,24},{16,0},{24,8},{1,17},{9,25},{17,1},{25,9},{2,18},{10... | collective-permute-start | bytes 98312 | tf_op jit(solution)/shard_map/ppermute | solution.py:49
  35.0 1.7 %collective-permute-start.13 = (bf16[32,512]{1,0:T(8,128)(2,1)S(1)}, bf16[32,512]{1,0:T(8,128)(2,1)S(1)}, u32[]{:S(2)}, u32[]{:S(2)}) collective-permute-start(bf16[32,512]{1,0:T(8,128)(2,1)S(1)} %shard_map.110.refs_0_), channel_id=1, source_target_pairs={{0,8},{8,0},{16,24},{24,16},{1,9},{9,1},{17,25},{25,17},{2,10},{10... | collective-permute-start | bytes 98312 | tf_op jit(solution)/shard_map/ppermute | solution.py:49
  36.8 1.3 %collective-permute-done.15.refs_3_ = bf16[32,512]{1,0:T(8,128)(2,1)S(1)} collective-permute-done((bf16[32,512]{1,0:T(8,128)(2,1)S(1)}, bf16[32,512]{1,0:T(8,128)(2,1)S(1)}, u32[]{:S(2)}, u32[]{:S(2)}) %collective-permute-start.15) | collective-permute-done | bytes 32800 | tf_op jit(solution)/shard_map/ppermute | solution.py:49
  38.1 1.1 %collective-permute-done.14.refs_2_ = bf16[32,512]{1,0:T(8,128)(2,1)S(1)} collective-permute-done((bf16[32,512]{1,0:T(8,128)(2,1)S(1)}, bf16[32,512]{1,0:T(8,128)(2,1)S(1)}, u32[]{:S(2)}, u32[]{:S(2)}) %collective-permute-start.14) | collective-permute-done | bytes 32800 | tf_op jit(solution)/shard_map/ppermute | solution.py:49
  39.2 0.1 collective-permute-done.13.refs_1_
  39.3 1.0 %shard_map.111 = (f32[1,1]{1,0:T(1,128)}, f32[256,384]{1,0:T(8,128)}, f32[384]{0:T(512)}) custom-call(bf16[32,512]{1,0:T(8,128)(2,1)S(1)} %shard_map.110.refs_0_, bf16[32,512]{1,0:T(8,128)(2,1)S(1)} %collective-permute-done.13.refs_1_, bf16[32,512]{1,0:T(8,128)(2,1)S(1)} %collective-permute-done.14.refs_2_, ...), custom_call_target="tpu_custom_call" | custom-call | tf_op jit(solution)/shard_map/pallas_call | solution.py:405
  (9 shorter events, 0.1 us)
Async XLA Ops:
  0.6 9.1 %collective-permute-start.3 = (bf16[32,1024]{1,0:T(8,128)(2,1)}, bf16[32,1024]{1,0:T(8,128)(2,1)S(1)}, u32[]{:S(2)}, u32[]{:S(2)}) collective-permute-start(bf16[32,1024]{1,0:T(8,128)(2,1)} %refs_2_.1), channel_id=1, source_target_pairs={{0,8},{1,17},{2,10},{3,19},{4,12},{5,21},{6,14},{7,23},{8,0},{9,25... | collective-permute-start | bytes 196616 | tf_op jit(solution)/shard_map/ppermute | solution.py:64
  3.7 6.3 %collective-permute-start.4 = (bf16[32,1024]{1,0:T(8,128)(2,1)}, bf16[32,1024]{1,0:T(8,128)(2,1)S(1)}, u32[]{:S(2)}, u32[]{:S(2)}) collective-permute-start(bf16[32,1024]{1,0:T(8,128)(2,1)} %refs_2_.1), channel_id=1, source_target_pairs={{0,24},{1,9},{2,26},{3,11},{4,28},{5,13},{6,30},{7,15},{8,16},{9,1... | collective-permute-start | bytes 196616 | tf_op jit(solution)/shard_map/ppermute | solution.py:64
  6.2 3.8 %copy-start.3 = (f32[1024]{0:T(1024)S(1)}, f32[1024]{0:T(1024)}, u32[]{:S(2)}) copy-start(f32[1024]{0:T(1024)} %param.13) | copy-start | bytes 12292
  6.2 5.1 %collective-permute-start.2 = (bf16[16,1024]{1,0:T(8,128)(2,1)}, bf16[16,1024]{1,0:T(8,128)(2,1)S(1)}, u32[]{:S(2)}, u32[]{:S(2)}) collective-permute-start(bf16[16,1024]{1,0:T(8,128)(2,1)} %bitcast.7), channel_id=1, source_target_pairs={{0,6},{1,7},{2,4},{3,5},{4,2},{5,3},{6,0},{7,1},{8,14},{9,15},{10,... | collective-permute-start | bytes 98312 | tf_op jit(solution)/shard_map/ppermute | solution.py:49
  8.6 4.1 %collective-permute-start.1 = (bf16[16,1024]{1,0:T(8,128)(2,1)}, bf16[16,1024]{1,0:T(8,128)(2,1)S(1)}, u32[]{:S(2)}, u32[]{:S(2)}) collective-permute-start(bf16[16,1024]{1,0:T(8,128)(2,1)} %bitcast.8), channel_id=1, source_target_pairs={{0,4},{1,5},{2,6},{3,7},{4,0},{5,1},{6,2},{7,3},{8,12},{9,13},{10,... | collective-permute-start | bytes 98312 | tf_op jit(solution)/shard_map/ppermute | solution.py:49
  9.2 4.1 %collective-permute-start = (bf16[16,1024]{1,0:T(8,128)(2,1)}, bf16[16,1024]{1,0:T(8,128)(2,1)S(1)}, u32[]{:S(2)}, u32[]{:S(2)}) collective-permute-start(bf16[16,1024]{1,0:T(8,128)(2,1)} %bitcast.9), channel_id=1, source_target_pairs={{0,2},{1,3},{2,0},{3,1},{4,6},{5,7},{6,4},{7,5},{8,10},{9,11},{10,... | collective-permute-start | bytes 98312 | tf_op jit(solution)/shard_map/ppermute | solution.py:49
  10.0 3.3 %copy-start.7 = (bf16[1,16,1024]{2,1,0:T(8,128)(2,1)S(1)}, bf16[1,16,1024]{2,1,0:T(8,128)(2,1)}, u32[]{:S(2)}) copy-start(bf16[1,16,1024]{2,1,0:T(8,128)(2,1)} %param.8) | copy-start | bytes 98308
  10.2 4.7 %copy-start = (bf16[1,1024,384]{2,1,0:T(8,128)(2,1)S(1)}, bf16[1,1024,384]{2,1,0:T(8,128)(2,1)}, u32[]{:S(2)}) copy-start(bf16[1,1024,384]{2,1,0:T(8,128)(2,1)} %param.10) | copy-start | bytes 2359300
  10.2 4.7 %copy-start.1 = (bf16[256,384]{1,0:T(8,128)(2,1)S(1)}, bf16[256,384]{1,0:T(8,128)(2,1)}, u32[]{:S(2)}) copy-start(bf16[256,384]{1,0:T(8,128)(2,1)} %refs_6_.1) | copy-start | bytes 589828
  10.2 4.7 %copy-start.2 = (bf16[32,1024]{1,0:T(8,128)(2,1)S(1)}, bf16[32,1024]{1,0:T(8,128)(2,1)}, u32[]{:S(2)}) copy-start(bf16[32,1024]{1,0:T(8,128)(2,1)} %refs_2_.1) | copy-start | bytes 196612
  13.3 1.7 %copy-start.4 = (f32[1,1024]{1,0:T(1,128)S(1)}, f32[1,1024]{1,0:T(1,128)}, u32[]{:S(2)}) copy-start(f32[1,1024]{1,0:T(1,128)} %refs_4_.1) | copy-start | bytes 12292
  13.3 1.7 %copy-start.5 = (f32[384]{0:T(512)S(1)}, f32[384]{0:T(512)}, u32[]{:S(2)}) copy-start(f32[384]{0:T(512)} %refs_8_.1) | copy-start | bytes 4612
  13.3 1.6 %copy-start.6 = (f32[1,384]{1,0:T(1,128)S(1)}, f32[1,384]{1,0:T(1,128)}, u32[]{:S(2)}) copy-start(f32[1,384]{1,0:T(1,128)} %refs_7_.1) | copy-start | bytes 4612
  13.3 1.6 %collective-permute-start.5 = (bf16[128,1024]{1,0:T(8,128)(2,1)S(1)}, bf16[128,1024]{1,0:T(8,128)(2,1)S(1)}, u32[]{:S(2)}, u32[]{:S(2)}) collective-permute-start(bf16[128,1024]{1,0:T(8,128)(2,1)S(1)} %shard_map.105.refs_0_), channel_id=1, source_target_pairs={{0,1},{1,0},{2,3},{3,2},{4,5},{5,4},{6,7},{7,6},{8,9},{9,8},{10,11... | collective-permute-start | bytes 786440 | tf_op jit(solution)/shard_map/ppermute | solution.py:68
  16.4 4.9 %collective-permute-start.6 = (bf16[80,384]{1,0:T(8,128)(2,1)S(1)}, bf16[80,384]{1,0:T(8,128)(2,1)S(1)}, u32[]{:S(2)}, u32[]{:S(2)}) collective-permute-start(bf16[80,384]{1,0:T(8,128)(2,1)S(1)} %get-tuple-element.16), channel_id=1, source_target_pairs={{0,8},{8,0},{16,24},{24,16},{1,9},{9,1},{17,25},{25,17},{2,10},{10... | collective-permute-start | bytes 184328 | tf_op jit(solution)/shard_map/ppermute | solution.py:49
  17.1 7.9 %collective-permute-start.7 = (bf16[80,384]{1,0:T(8,128)(2,1)S(1)}, bf16[80,384]{1,0:T(8,128)(2,1)S(1)}, u32[]{:S(2)}, u32[]{:S(2)}) collective-permute-start(bf16[80,384]{1,0:T(8,128)(2,1)S(1)} %get-tuple-element.17), channel_id=1, source_target_pairs={{0,16},{8,24},{16,0},{24,8},{1,17},{9,25},{17,1},{25,9},{2,18},{10... | collective-permute-start | bytes 184328 | tf_op jit(solution)/shard_map/ppermute | solution.py:49
  18.3 6.7 %collective-permute-start.8 = (bf16[80,384]{1,0:T(8,128)(2,1)S(1)}, bf16[80,384]{1,0:T(8,128)(2,1)S(1)}, u32[]{:S(2)}, u32[]{:S(2)}) collective-permute-start(bf16[80,384]{1,0:T(8,128)(2,1)S(1)} %get-tuple-element.18), channel_id=1, source_target_pairs={{0,24},{8,16},{16,8},{24,0},{1,25},{9,17},{17,9},{25,1},{2,26},{10... | collective-permute-start | bytes 184328 | tf_op jit(solution)/shard_map/ppermute | solution.py:49
  25.3 1.2 %collective-permute-start.9 = (f32[8,128]{1,0:T(8,128)S(1)}, f32[8,128]{1,0:T(8,128)S(1)}, u32[]{:S(2)}, u32[]{:S(2)}) collective-permute-start(f32[8,128]{1,0:T(8,128)S(1)} %get-tuple-element.20.own_ref.refs_4_), channel_id=1, source_target_pairs={{0,1},{1,0},{2,3},{3,2},{4,5},{5,4},{6,7},{7,6},{8,9},{9,8},{10,11... | collective-permute-start | bytes 12296 | tf_op jit(solution)/shard_map/ppermute | solution.py:68
  26.5 4.6 %collective-permute-start.12 = (f32[8,128]{1,0:T(8,128)S(1)}, f32[8,128]{1,0:T(8,128)S(1)}, u32[]{:S(2)}, u32[]{:S(2)}) collective-permute-start(f32[8,128]{1,0:T(8,128)S(1)} %shard_map.108.refs_0_), channel_id=1, source_target_pairs={{0,6},{1,7},{2,4},{3,5},{4,2},{5,3},{6,0},{7,1},{8,14},{9,15},{10,... | collective-permute-start | bytes 12296 | tf_op jit(solution)/shard_map/ppermute | solution.py:49
  28.0 3.6 %collective-permute-start.11 = (f32[8,128]{1,0:T(8,128)S(1)}, f32[8,128]{1,0:T(8,128)S(1)}, u32[]{:S(2)}, u32[]{:S(2)}) collective-permute-start(f32[8,128]{1,0:T(8,128)S(1)} %shard_map.108.refs_0_), channel_id=1, source_target_pairs={{0,4},{1,5},{2,6},{3,7},{4,0},{5,1},{6,2},{7,3},{8,12},{9,13},{10,... | collective-permute-start | bytes 12296 | tf_op jit(solution)/shard_map/ppermute | solution.py:49
  28.5 3.6 %collective-permute-start.10 = (f32[8,128]{1,0:T(8,128)S(1)}, f32[8,128]{1,0:T(8,128)S(1)}, u32[]{:S(2)}, u32[]{:S(2)}) collective-permute-start(f32[8,128]{1,0:T(8,128)S(1)} %shard_map.108.refs_0_), channel_id=1, source_target_pairs={{0,2},{1,3},{2,0},{3,1},{4,6},{5,7},{6,4},{7,5},{8,10},{9,11},{10,... | collective-permute-start | bytes 12296 | tf_op jit(solution)/shard_map/ppermute | solution.py:49
  32.3 5.8 %collective-permute-start.15 = (bf16[32,512]{1,0:T(8,128)(2,1)S(1)}, bf16[32,512]{1,0:T(8,128)(2,1)S(1)}, u32[]{:S(2)}, u32[]{:S(2)}) collective-permute-start(bf16[32,512]{1,0:T(8,128)(2,1)S(1)} %shard_map.110.refs_0_), channel_id=1, source_target_pairs={{0,24},{8,16},{16,8},{24,0},{1,25},{9,17},{17,9},{25,1},{2,26},{10... | collective-permute-start | bytes 98312 | tf_op jit(solution)/shard_map/ppermute | solution.py:49
  34.2 4.9 %collective-permute-start.14 = (bf16[32,512]{1,0:T(8,128)(2,1)S(1)}, bf16[32,512]{1,0:T(8,128)(2,1)S(1)}, u32[]{:S(2)}, u32[]{:S(2)}) collective-permute-start(bf16[32,512]{1,0:T(8,128)(2,1)S(1)} %shard_map.110.refs_0_), channel_id=1, source_target_pairs={{0,16},{8,24},{16,0},{24,8},{1,17},{9,25},{17,1},{25,9},{2,18},{10... | collective-permute-start | bytes 98312 | tf_op jit(solution)/shard_map/ppermute | solution.py:49
  35.0 4.3 %collective-permute-start.13 = (bf16[32,512]{1,0:T(8,128)(2,1)S(1)}, bf16[32,512]{1,0:T(8,128)(2,1)S(1)}, u32[]{:S(2)}, u32[]{:S(2)}) collective-permute-start(bf16[32,512]{1,0:T(8,128)(2,1)S(1)} %shard_map.110.refs_0_), channel_id=1, source_target_pairs={{0,8},{8,0},{16,24},{24,16},{1,9},{9,1},{17,25},{25,17},{2,10},{10... | collective-permute-start | bytes 98312 | tf_op jit(solution)/shard_map/ppermute | solution.py:49

commit v8 on v7

--- a/solution.py
+++ b/solution.py
@@ -126,16 +126,6 @@
     return log_t + slope / total - 7.0 / (x + 7.5) - 1.0 / x
 
 
-def fetch(sources, targets, sems):
-    copies = [
-        pltpu.make_async_copy(source, target, sems.at[i])
-        for i, (source, target) in enumerate(zip(sources, targets, strict=True))
-    ]
-    for copy in copies:
-        copy.start()
-    return copies
-
-
 def slot(at, rows):
     return pl.ds(pl.multiple_of(at * rows, rows), rows)
 
@@ -152,11 +142,11 @@
 
 
 def join_kernel(chips, *refs):
-    *parts, student_ref, out_ref = refs
+    *parts, gain_ref, student_ref, out_ref = refs
     chip = lax.axis_index("dp") // 2
     rows = parts[0].shape[0]
     for k in range(chips):
-        out_ref[slot(mixed(chip, k, chips, sender), rows), :] = parts[k][...]
+        out_ref[slot(mixed(chip, k, chips, sender), rows), :] = normed(parts[k][...], gain_ref[...])
     start = chips * rows
     out_ref[start:, :] = student_ref[...]
 
@@ -170,23 +160,20 @@
 
 def logits_kernel(members, rows, *refs):
     own_ref, other_ref, refs = refs[0], refs[1], refs[2:]
-    sources, refs = refs[:7], refs[7:]
+    feats_ref, student_gain_ref, head_ref, student_ref, bias_ref, student_bias_ref = refs[:6]
+    refs = refs[6:]
     payloads, refs = refs[:members], refs[members:]
-    own_logits_ref, columns_ref, gathered, held, shifted_ref, lse_ref, partial_ref, *params = refs
-    feats_ref, student_gain_ref, gain_ref, head_ref, student_ref, bias_ref, student_bias_ref = params[:7]
-    copies = fetch(sources, params[:7], params[7])
+    own_logits_ref, columns_ref, gathered, held, shifted_ref, lse_ref, partial_ref = refs
     mine, place = lax.axis_index("member"), lax.axis_index("dp")
     core = lax.rem(place, jnp.int32(2))
     chips = gathered.shape[0] // (2 * rows)
-    for copy in copies:
-        copy.wait()
     block = feats_ref.shape[0]
     width = columns_ref.shape[1]
     held[slot(mine, block), :] = normed(feats_ref[...], student_gain_ref[...])
     for source, side in ((own_ref, core), (other_ref, 1 - core)):
         for chip in range(chips):
             at = slot(2 * chip + side, rows)
-            gathered[at, :] = normed(source[chip * rows : (chip + 1) * rows, :], gain_ref[...])
+            gathered[at, :] = source[chip * rows : (chip + 1) * rows, :]
         for j in range(members // 2):
             start = chips * rows + j * block
             at = slot(mixed(mine, split_step(j, side, members), members, sender), block)
@@ -249,7 +236,8 @@
     )
 
 
-def digamma_kernel(alphas_ref, target_ref, inner_ref):
+def digamma_kernel(alphas_ref, target_ref, columns_ref, inner_ref, turned_ref):
+    turned_ref[...] = columns_ref[...].T
     inner_ref[...] = di_gamma(alphas_ref[...]) - target_ref[...]
 
 
@@ -290,7 +278,7 @@
 
 def gradient_kernel(members, images, classes, *refs):
     signals, refs = refs[:members], refs[members:]
-    columns_ref, loss_ref, grad_ref, bias_ref, held, losses = refs
+    turned_ref, loss_ref, grad_ref, bias_ref, held, losses = refs
     mine = lax.axis_index("member")
     block = images // members
     width = held.shape[1]
@@ -300,20 +288,16 @@
         tail = signals[k][:, width:].astype(F32)
         losses[pl.ds(at, 1), :] = tail[0:1, :] + tail[1:2, :] + tail[2:3, :]
     signal = held[...]
-    grad = lax.dot_general(
-        columns_ref[...], signal, (((0,), (0,)), ((), ())), preferred_element_type=F32
-    )
+    grad = jnp.dot(turned_ref[...], signal, preferred_element_type=F32)
     grad_ref[...] = grad * (1.0 / images)
     bias_ref[...] = jnp.sum(signal.astype(F32), axis=0) * (1.0 / images)
     loss_ref[0, 0] = jnp.sum(losses[:, 0:1]) * (1.0 / (images * classes))
 
 
-def call(kernel, out_shape, scratch=(), in_specs=None, out_specs=None, flops=0):
+def call(kernel, out_shape, scratch=(), out_specs=None, flops=0):
     extra = {}
     if flops:
         extra["cost_estimate"] = pl.CostEstimate(flops=flops, bytes_accessed=0, transcendentals=0)
-    if in_specs is not None:
-        extra["in_specs"] = in_specs
     if out_specs is not None:
         extra["out_specs"] = out_specs
     return pl.pallas_call(
@@ -338,7 +322,7 @@
     members, peers = lax.axis_size("member"), lax.axis_size("dp")
     chips = peers // 2
     shape = jax.ShapeDtypeStruct
-    here, far = pl.BlockSpec(memory_space=pltpu.VMEM), pl.BlockSpec(memory_space=pltpu.HBM)
+    here = pl.BlockSpec(memory_space=pltpu.VMEM)
     feats = teacher_feats[0]
     rows, depth = feats.shape
     block = student_feats.shape[0]
@@ -355,7 +339,7 @@
         functools.partial(join_kernel, chips),
         shape((chips * rows + members // 2 * block, depth), BF16),
         flops=1 << 33,
-    )(*parts, students)
+    )(*parts, teacher_gain, students)
     *payloads, own_logits, own_columns = call(
         functools.partial(logits_kernel, members, rows),
         [shape((2 * block + PAD, classes), BF16)] * members
@@ -366,22 +350,12 @@
             pltpu.VMEM((images, classes), BF16),
             pltpu.VMEM((images, LANES), F32),
             pltpu.VMEM((images, classes), F32),
-            pltpu.VMEM((block, depth), BF16),
-            pltpu.VMEM((1, depth), F32),
-            pltpu.VMEM((1, depth), F32),
-            pltpu.VMEM((depth, classes), BF16),
-            pltpu.VMEM((width, classes), BF16),
-            pltpu.VMEM((1, classes), F32),
-            pltpu.VMEM((classes,), F32),
-            pltpu.SemaphoreType.DMA((7,)),
         ],
-        [here] * 2 + [far] * 7,
     )(
         own,
         swap_cores(own, "dp"),
         student_feats,
         student_gain[None],
-        teacher_gain,
         teacher_head[0],
         student_head,
         teacher_bias,
@@ -393,7 +367,9 @@
         [shape((block, classes), F32)] * 2 + [shape((small_rows, LANES), F32)],
     )(*got, own_logits)
     other = swap_cores(own, "dp")
-    inner = call(digamma_kernel, shape((block, classes), F32))(alphas, target)
+    inner, turned = call(
+        digamma_kernel, [shape((block, classes), F32), shape((width, images), BF16)]
+    )(alphas, target, own_columns)
     small = call(functools.partial(combine_kernel, members), shape(own.shape, F32))(own, other)
     smalls = [small] + [send(small, "dp", k, 2) for k in range(1, chips)]
     signal = call(
@@ -407,7 +383,7 @@
         [shape((1, 1), F32), shape((width, classes), F32), shape((classes,), F32)],
         [pltpu.VMEM((images, classes), BF16), pltpu.VMEM((members, LANES), F32)],
         out_specs=[pl.BlockSpec(memory_space=pltpu.SMEM), here, here],
-    )(*signals, own_columns)
+    )(*signals, turned)
     return (loss[0, 0], head_grad, bias_grad)
 
 

time: 40.5 us -> 39.9 us (0.985)
  Pallas kernels: 3.13 us -> 2.55 us
    pallas_call x1, Pallas kernels: 1.38 us -> 0.62 us  [on_device(): call(functools.partial(logits_kernel, members, rows), [shape((2 * block +...]
where the time goes in v8:
time: 39.9 us; the launch traced here: 39.7 us
  starting transfers between devices  21.6 us (54%)
  waiting for transfers between devices  14.8 us (37%)
  Pallas kernels  2.55 us (6%)
  between operations  0.75 us (2%)
    ppermute x12, starting transfers between devices, send(): return lax.ppermute(value, axis, pairs)  15.9 us
    ppermute x12, waiting for transfers between devices, send(): return lax.ppermute(value, axis, pairs)  11.8 us
    ppermute x2, starting transfers between devices, send_split(): return lax.ppermute(value, ('member', 'dp'), pairs)  5.56 us
    ppermute x2, waiting for transfers between devices, swap_cores(): lax.ppermute(value, axis, [(i, i ^ 1) for i in range(lax.axis_size(axis))])  2.67 us
    pallas_call x1, Pallas kernels, on_device(): call(functools.partial(gradient_kernel, members, images, classes * peers)...  0.97 us
  transfers between devices with their start and end apart: 16, of which 14 were waited for; matrix products, arithmetic and copies ran while one was open for 0% of the time, Pallas kernels for 1%

profile of v8, /device:TPU:0, one launch (start us, length us, event | category | flops | bytes accessed | tf_op | source)
XLA Modules:
  0.0 39.7 jit_solution(13779083986826431740)
XLA Ops:
  0.6 3.1 %collective-permute-start.3 = (bf16[32,1024]{1,0:T(8,128)(2,1)}, bf16[32,1024]{1,0:T(8,128)(2,1)S(1)}, u32[]{:S(2)}, u32[]{:S(2)}) collective-permute-start(bf16[32,1024]{1,0:T(8,128)(2,1)} %refs_2_.1), channel_id=1, source_target_pairs={{0,8},{1,17},{2,10},{3,19},{4,12},{5,21},{6,14},{7,23},{8,0},{9,25... | collective-permute-start | bytes 196616 | tf_op jit(solution)/shard_map/ppermute | solution.py:64
  3.7 2.5 %collective-permute-start.4 = (bf16[32,1024]{1,0:T(8,128)(2,1)}, bf16[32,1024]{1,0:T(8,128)(2,1)S(1)}, u32[]{:S(2)}, u32[]{:S(2)}) collective-permute-start(bf16[32,1024]{1,0:T(8,128)(2,1)} %refs_2_.1), channel_id=1, source_target_pairs={{0,24},{1,9},{2,26},{3,11},{4,28},{5,13},{6,30},{7,15},{8,16},{9,1... | collective-permute-start | bytes 196616 | tf_op jit(solution)/shard_map/ppermute | solution.py:64
  6.2 2.4 %collective-permute-start.2 = (bf16[16,1024]{1,0:T(8,128)(2,1)}, bf16[16,1024]{1,0:T(8,128)(2,1)S(1)}, u32[]{:S(2)}, u32[]{:S(2)}) collective-permute-start(bf16[16,1024]{1,0:T(8,128)(2,1)} %bitcast.7), channel_id=1, source_target_pairs={{0,6},{1,7},{2,4},{3,5},{4,2},{5,3},{6,0},{7,1},{8,14},{9,15},{10,... | collective-permute-start | bytes 98312 | tf_op jit(solution)/shard_map/ppermute | solution.py:49
  8.6 0.5 %collective-permute-start.1 = (bf16[16,1024]{1,0:T(8,128)(2,1)}, bf16[16,1024]{1,0:T(8,128)(2,1)S(1)}, u32[]{:S(2)}, u32[]{:S(2)}) collective-permute-start(bf16[16,1024]{1,0:T(8,128)(2,1)} %bitcast.8), channel_id=1, source_target_pairs={{0,4},{1,5},{2,6},{3,7},{4,0},{5,1},{6,2},{7,3},{8,12},{9,13},{10,... | collective-permute-start | bytes 98312 | tf_op jit(solution)/shard_map/ppermute | solution.py:49
  9.2 0.5 %collective-permute-start = (bf16[16,1024]{1,0:T(8,128)(2,1)}, bf16[16,1024]{1,0:T(8,128)(2,1)S(1)}, u32[]{:S(2)}, u32[]{:S(2)}) collective-permute-start(bf16[16,1024]{1,0:T(8,128)(2,1)} %bitcast.9), channel_id=1, source_target_pairs={{0,2},{1,3},{2,0},{3,1},{4,6},{5,7},{6,4},{7,5},{8,10},{9,11},{10,... | collective-permute-start | bytes 98312 | tf_op jit(solution)/shard_map/ppermute | solution.py:49
  9.7 0.0 collective-permute-done.3.refs_0_
  9.7 0.3 collective-permute-done.4.refs_1_
  10.0 0.0 copy-done.3
  10.0 0.2 shard_map.104.refs_5_
  10.2 0.0 copy-start
  10.2 0.0 copy-start.1
  10.2 0.0 copy-start.2
  10.3 1.0 %collective-permute-done.2.refs_3_ = bf16[16,1024]{1,0:T(8,128)(2,1)S(1)} collective-permute-done((bf16[16,1024]{1,0:T(8,128)(2,1)}, bf16[16,1024]{1,0:T(8,128)(2,1)S(1)}, u32[]{:S(2)}, u32[]{:S(2)}) %collective-permute-start.2) | collective-permute-done | bytes 32800 | tf_op jit(solution)/shard_map/ppermute | solution.py:49
  11.3 1.5 %collective-permute-done.1.refs_2_ = bf16[16,1024]{1,0:T(8,128)(2,1)S(1)} collective-permute-done((bf16[16,1024]{1,0:T(8,128)(2,1)}, bf16[16,1024]{1,0:T(8,128)(2,1)S(1)}, u32[]{:S(2)}, u32[]{:S(2)}) %collective-permute-start.1) | collective-permute-done | bytes 32800 | tf_op jit(solution)/shard_map/ppermute | solution.py:49
  12.8 0.5 %collective-permute-done.refs_1_ = bf16[16,1024]{1,0:T(8,128)(2,1)S(1)} collective-permute-done((bf16[16,1024]{1,0:T(8,128)(2,1)}, bf16[16,1024]{1,0:T(8,128)(2,1)S(1)}, u32[]{:S(2)}, u32[]{:S(2)}) %collective-permute-start) | collective-permute-done | bytes 32800 | tf_op jit(solution)/shard_map/ppermute | solution.py:49
  13.3 0.0 copy-done.6
  13.3 0.0 copy-done.7
  13.3 0.2 shard_map.105.refs_0_
  13.5 0.0 copy-start.5
  13.5 0.1 collective-permute-start.5
  13.6 1.5 %collective-permute-done.5.refs_1_ = bf16[128,1024]{1,0:T(8,128)(2,1)S(1)} collective-permute-done((bf16[128,1024]{1,0:T(8,128)(2,1)S(1)}, bf16[128,1024]{1,0:T(8,128)(2,1)S(1)}, u32[]{:S(2)}, u32[]{:S(2)}) %collective-permute-start.5) | collective-permute-done | bytes 262176 | tf_op jit(solution)/shard_map/ppermute | solution.py:68
  15.1 0.0 copy-done
  15.1 0.0 copy-done.1
  15.2 0.6 %shard_map.106 = (bf16[80,384]{1,0:T(8,128)(2,1)S(1)}, bf16[80,384]{1,0:T(8,128)(2,1)S(1)}, bf16[80,384]{1,0:T(8,128)(2,1)S(1)}, bf16[80,384]{1,0:T(8,128)(2,1)S...) custom-call(bf16[128,1024]{1,0:T(8,128)(2,1)S(1)} %shard_map.105.refs_0_, ...), custom_call_target="tpu_custom_call" | custom-call | tf_op jit(solution)/shard_map/pallas_call | solution.py:343
  15.8 0.7 %collective-permute-start.6 = (bf16[80,384]{1,0:T(8,128)(2,1)S(1)}, bf16[80,384]{1,0:T(8,128)(2,1)S(1)}, u32[]{:S(2)}, u32[]{:S(2)}) collective-permute-start(bf16[80,384]{1,0:T(8,128)(2,1)S(1)} %get-tuple-element.18), channel_id=1, source_target_pairs={{0,8},{8,0},{16,24},{24,16},{1,9},{9,1},{17,25},{25,17},{2,10},{10... | collective-permute-start | bytes 184328 | tf_op jit(solution)/shard_map/ppermute | solution.py:49
  16.5 1.2 %collective-permute-start.7 = (bf16[80,384]{1,0:T(8,128)(2,1)S(1)}, bf16[80,384]{1,0:T(8,128)(2,1)S(1)}, u32[]{:S(2)}, u32[]{:S(2)}) collective-permute-start(bf16[80,384]{1,0:T(8,128)(2,1)S(1)} %get-tuple-element.19), channel_id=1, source_target_pairs={{0,16},{8,24},{16,0},{24,8},{1,17},{9,25},{17,1},{25,9},{2,18},{10... | collective-permute-start | bytes 184328 | tf_op jit(solution)/shard_map/ppermute | solution.py:49
  17.8 2.5 %collective-permute-start.8 = (bf16[80,384]{1,0:T(8,128)(2,1)S(1)}, bf16[80,384]{1,0:T(8,128)(2,1)S(1)}, u32[]{:S(2)}, u32[]{:S(2)}) collective-permute-start(bf16[80,384]{1,0:T(8,128)(2,1)S(1)} %get-tuple-element.20), channel_id=1, source_target_pairs={{0,24},{8,16},{16,8},{24,0},{1,25},{9,17},{17,9},{25,1},{2,26},{10... | collective-permute-start | bytes 184328 | tf_op jit(solution)/shard_map/ppermute | solution.py:49
  20.2 0.5 %collective-permute-done.6.refs_1_ = bf16[80,384]{1,0:T(8,128)(2,1)S(1)} collective-permute-done((bf16[80,384]{1,0:T(8,128)(2,1)S(1)}, bf16[80,384]{1,0:T(8,128)(2,1)S(1)}, u32[]{:S(2)}, u32[]{:S(2)}) %collective-permute-start.6) | collective-permute-done | bytes 61472 | tf_op jit(solution)/shard_map/ppermute | solution.py:49
  20.7 3.7 %collective-permute-done.7.refs_2_ = bf16[80,384]{1,0:T(8,128)(2,1)S(1)} collective-permute-done((bf16[80,384]{1,0:T(8,128)(2,1)S(1)}, bf16[80,384]{1,0:T(8,128)(2,1)S(1)}, u32[]{:S(2)}, u32[]{:S(2)}) %collective-permute-start.7) | collective-permute-done | bytes 61472 | tf_op jit(solution)/shard_map/ppermute | solution.py:49
  24.5 0.0 collective-permute-done.8.refs_3_
  24.5 0.2 shard_map.107
  24.7 0.0 collective-permute-start.9
  24.7 1.2 %collective-permute-done.9.other_ref = f32[8,128]{1,0:T(8,128)S(1)} collective-permute-done((f32[8,128]{1,0:T(8,128)S(1)}, f32[8,128]{1,0:T(8,128)S(1)}, u32[]{:S(2)}, u32[]{:S(2)}) %collective-permute-start.9) | collective-permute-done | bytes 4128 | tf_op jit(solution)/shard_map/ppermute | solution.py:68
  25.9 1.6 %collective-permute-start.12 = (f32[8,128]{1,0:T(8,128)S(1)}, f32[8,128]{1,0:T(8,128)S(1)}, u32[]{:S(2)}, u32[]{:S(2)}) collective-permute-start(f32[8,128]{1,0:T(8,128)S(1)} %shard_map.108.refs_0_), channel_id=1, source_target_pairs={{0,6},{1,7},{2,4},{3,5},{4,2},{5,3},{6,0},{7,1},{8,14},{9,15},{10,... | collective-permute-start | bytes 12296 | tf_op jit(solution)/shard_map/ppermute | solution.py:49
  27.4 0.5 %collective-permute-start.11 = (f32[8,128]{1,0:T(8,128)S(1)}, f32[8,128]{1,0:T(8,128)S(1)}, u32[]{:S(2)}, u32[]{:S(2)}) collective-permute-start(f32[8,128]{1,0:T(8,128)S(1)} %shard_map.108.refs_0_), channel_id=1, source_target_pairs={{0,4},{1,5},{2,6},{3,7},{4,0},{5,1},{6,2},{7,3},{8,12},{9,13},{10,... | collective-permute-start | bytes 12296 | tf_op jit(solution)/shard_map/ppermute | solution.py:49
  28.0 1.5 %collective-permute-start.10 = (f32[8,128]{1,0:T(8,128)S(1)}, f32[8,128]{1,0:T(8,128)S(1)}, u32[]{:S(2)}, u32[]{:S(2)}) collective-permute-start(f32[8,128]{1,0:T(8,128)S(1)} %shard_map.108.refs_0_), channel_id=1, source_target_pairs={{0,2},{1,3},{2,0},{3,1},{4,6},{5,7},{6,4},{7,5},{8,10},{9,11},{10,... | collective-permute-start | bytes 12296 | tf_op jit(solution)/shard_map/ppermute | solution.py:49
  29.4 0.1 shard_map.109
  29.6 0.9 %collective-permute-done.12.refs_3_ = f32[8,128]{1,0:T(8,128)S(1)} collective-permute-done((f32[8,128]{1,0:T(8,128)S(1)}, f32[8,128]{1,0:T(8,128)S(1)}, u32[]{:S(2)}, u32[]{:S(2)}) %collective-permute-start.12) | collective-permute-done | bytes 4128 | tf_op jit(solution)/shard_map/ppermute | solution.py:49
  30.5 0.6 %collective-permute-done.11.refs_2_ = f32[8,128]{1,0:T(8,128)S(1)} collective-permute-done((f32[8,128]{1,0:T(8,128)S(1)}, f32[8,128]{1,0:T(8,128)S(1)}, u32[]{:S(2)}, u32[]{:S(2)}) %collective-permute-start.11) | collective-permute-done | bytes 4128 | tf_op jit(solution)/shard_map/ppermute | solution.py:49
  31.1 0.5 %collective-permute-done.10.refs_1_ = f32[8,128]{1,0:T(8,128)S(1)} collective-permute-done((f32[8,128]{1,0:T(8,128)S(1)}, f32[8,128]{1,0:T(8,128)S(1)}, u32[]{:S(2)}, u32[]{:S(2)}) %collective-permute-start.10) | collective-permute-done | bytes 4128 | tf_op jit(solution)/shard_map/ppermute | solution.py:49
  31.6 0.1 shard_map.110.refs_0_
  31.7 1.9 %collective-permute-start.15 = (bf16[32,512]{1,0:T(8,128)(2,1)S(1)}, bf16[32,512]{1,0:T(8,128)(2,1)S(1)}, u32[]{:S(2)}, u32[]{:S(2)}) collective-permute-start(bf16[32,512]{1,0:T(8,128)(2,1)S(1)} %shard_map.110.refs_0_), channel_id=1, source_target_pairs={{0,24},{8,16},{16,8},{24,0},{1,25},{9,17},{17,9},{25,1},{2,26},{10... | collective-permute-start | bytes 98312 | tf_op jit(solution)/shard_map/ppermute | solution.py:49
  33.7 0.8 %collective-permute-start.14 = (bf16[32,512]{1,0:T(8,128)(2,1)S(1)}, bf16[32,512]{1,0:T(8,128)(2,1)S(1)}, u32[]{:S(2)}, u32[]{:S(2)}) collective-permute-start(bf16[32,512]{1,0:T(8,128)(2,1)S(1)} %shard_map.110.refs_0_), channel_id=1, source_target_pairs={{0,16},{8,24},{16,0},{24,8},{1,17},{9,25},{17,1},{25,9},{2,18},{10... | collective-permute-start | bytes 98312 | tf_op jit(solution)/shard_map/ppermute | solution.py:49
  34.5 1.7 %collective-permute-start.13 = (bf16[32,512]{1,0:T(8,128)(2,1)S(1)}, bf16[32,512]{1,0:T(8,128)(2,1)S(1)}, u32[]{:S(2)}, u32[]{:S(2)}) collective-permute-start(bf16[32,512]{1,0:T(8,128)(2,1)S(1)} %shard_map.110.refs_0_), channel_id=1, source_target_pairs={{0,8},{8,0},{16,24},{24,16},{1,9},{9,1},{17,25},{25,17},{2,10},{10... | collective-permute-start | bytes 98312 | tf_op jit(solution)/shard_map/ppermute | solution.py:49
  36.2 1.3 %collective-permute-done.15.refs_3_ = bf16[32,512]{1,0:T(8,128)(2,1)S(1)} collective-permute-done((bf16[32,512]{1,0:T(8,128)(2,1)S(1)}, bf16[32,512]{1,0:T(8,128)(2,1)S(1)}, u32[]{:S(2)}, u32[]{:S(2)}) %collective-permute-start.15) | collective-permute-done | bytes 32800 | tf_op jit(solution)/shard_map/ppermute | solution.py:49
  37.5 1.1 %collective-permute-done.14.refs_2_ = bf16[32,512]{1,0:T(8,128)(2,1)S(1)} collective-permute-done((bf16[32,512]{1,0:T(8,128)(2,1)S(1)}, bf16[32,512]{1,0:T(8,128)(2,1)S(1)}, u32[]{:S(2)}, u32[]{:S(2)}) %collective-permute-start.14) | collective-permute-done | bytes 32800 | tf_op jit(solution)/shard_map/ppermute | solution.py:49
  38.6 0.1 collective-permute-done.13.refs_1_
  38.7 1.0 %shard_map.111 = (f32[1,1]{1,0:T(1,128)}, f32[256,384]{1,0:T(8,128)}, f32[384]{0:T(512)}) custom-call(bf16[32,512]{1,0:T(8,128)(2,1)S(1)} %shard_map.110.refs_0_, bf16[32,512]{1,0:T(8,128)(2,1)S(1)} %collective-permute-done.13.refs_1_, bf16[32,512]{1,0:T(8,128)(2,1)S(1)} %collective-permute-done.14.refs_2_, ...), custom_call_target="tpu_custom_call" | custom-call | tf_op jit(solution)/shard_map/pallas_call | solution.py:381
  (9 shorter events, 0.0 us)
Async XLA Ops:
  0.6 9.1 %collective-permute-start.3 = (bf16[32,1024]{1,0:T(8,128)(2,1)}, bf16[32,1024]{1,0:T(8,128)(2,1)S(1)}, u32[]{:S(2)}, u32[]{:S(2)}) collective-permute-start(bf16[32,1024]{1,0:T(8,128)(2,1)} %refs_2_.1), channel_id=1, source_target_pairs={{0,8},{1,17},{2,10},{3,19},{4,12},{5,21},{6,14},{7,23},{8,0},{9,25... | collective-permute-start | bytes 196616 | tf_op jit(solution)/shard_map/ppermute | solution.py:64
  3.7 6.3 %collective-permute-start.4 = (bf16[32,1024]{1,0:T(8,128)(2,1)}, bf16[32,1024]{1,0:T(8,128)(2,1)S(1)}, u32[]{:S(2)}, u32[]{:S(2)}) collective-permute-start(bf16[32,1024]{1,0:T(8,128)(2,1)} %refs_2_.1), channel_id=1, source_target_pairs={{0,24},{1,9},{2,26},{3,11},{4,28},{5,13},{6,30},{7,15},{8,16},{9,1... | collective-permute-start | bytes 196616 | tf_op jit(solution)/shard_map/ppermute | solution.py:64
  6.2 3.8 %copy-start.3 = (f32[1024]{0:T(1024)S(1)}, f32[1024]{0:T(1024)}, u32[]{:S(2)}) copy-start(f32[1024]{0:T(1024)} %param.13) | copy-start | bytes 12292
  6.2 5.1 %collective-permute-start.2 = (bf16[16,1024]{1,0:T(8,128)(2,1)}, bf16[16,1024]{1,0:T(8,128)(2,1)S(1)}, u32[]{:S(2)}, u32[]{:S(2)}) collective-permute-start(bf16[16,1024]{1,0:T(8,128)(2,1)} %bitcast.7), channel_id=1, source_target_pairs={{0,6},{1,7},{2,4},{3,5},{4,2},{5,3},{6,0},{7,1},{8,14},{9,15},{10,... | collective-permute-start | bytes 98312 | tf_op jit(solution)/shard_map/ppermute | solution.py:49
  8.6 4.1 %collective-permute-start.1 = (bf16[16,1024]{1,0:T(8,128)(2,1)}, bf16[16,1024]{1,0:T(8,128)(2,1)S(1)}, u32[]{:S(2)}, u32[]{:S(2)}) collective-permute-start(bf16[16,1024]{1,0:T(8,128)(2,1)} %bitcast.8), channel_id=1, source_target_pairs={{0,4},{1,5},{2,6},{3,7},{4,0},{5,1},{6,2},{7,3},{8,12},{9,13},{10,... | collective-permute-start | bytes 98312 | tf_op jit(solution)/shard_map/ppermute | solution.py:49
  9.2 4.1 %collective-permute-start = (bf16[16,1024]{1,0:T(8,128)(2,1)}, bf16[16,1024]{1,0:T(8,128)(2,1)S(1)}, u32[]{:S(2)}, u32[]{:S(2)}) collective-permute-start(bf16[16,1024]{1,0:T(8,128)(2,1)} %bitcast.9), channel_id=1, source_target_pairs={{0,2},{1,3},{2,0},{3,1},{4,6},{5,7},{6,4},{7,5},{8,10},{9,11},{10,... | collective-permute-start | bytes 98312 | tf_op jit(solution)/shard_map/ppermute | solution.py:49
  10.0 3.3 %copy-start.6 = (bf16[1,16,1024]{2,1,0:T(8,128)(2,1)S(1)}, bf16[1,16,1024]{2,1,0:T(8,128)(2,1)}, u32[]{:S(2)}) copy-start(bf16[1,16,1024]{2,1,0:T(8,128)(2,1)} %param.8) | copy-start | bytes 98308
  10.0 3.3 %copy-start.7 = (f32[1,1024]{1,0:T(1,128)S(1)}, f32[1,1024]{1,0:T(1,128)}, u32[]{:S(2)}) copy-start(f32[1,1024]{1,0:T(1,128)} %refs_4_.1) | copy-start | bytes 12292
  10.2 4.9 %copy-start = (bf16[1,1024,384]{2,1,0:T(8,128)(2,1)S(1)}, bf16[1,1024,384]{2,1,0:T(8,128)(2,1)}, u32[]{:S(2)}) copy-start(bf16[1,1024,384]{2,1,0:T(8,128)(2,1)} %param.10) | copy-start | bytes 2359300
  10.2 4.9 %copy-start.1 = (bf16[256,384]{1,0:T(8,128)(2,1)S(1)}, bf16[256,384]{1,0:T(8,128)(2,1)}, u32[]{:S(2)}) copy-start(bf16[256,384]{1,0:T(8,128)(2,1)} %refs_5_.1) | copy-start | bytes 589828
  10.2 4.9 %copy-start.2 = (bf16[32,1024]{1,0:T(8,128)(2,1)S(1)}, bf16[32,1024]{1,0:T(8,128)(2,1)}, u32[]{:S(2)}) copy-start(bf16[32,1024]{1,0:T(8,128)(2,1)} %refs_2_.1) | copy-start | bytes 196612
  13.3 1.9 %copy-start.4 = (f32[384]{0:T(512)S(1)}, f32[384]{0:T(512)}, u32[]{:S(2)}) copy-start(f32[384]{0:T(512)} %refs_7_.1) | copy-start | bytes 4612
  13.5 1.6 %copy-start.5 = (f32[1,384]{1,0:T(1,128)S(1)}, f32[1,384]{1,0:T(1,128)}, u32[]{:S(2)}) copy-start(f32[1,384]{1,0:T(1,128)} %refs_6_.1) | copy-start | bytes 4612
  13.5 1.6 %collective-permute-start.5 = (bf16[128,1024]{1,0:T(8,128)(2,1)S(1)}, bf16[128,1024]{1,0:T(8,128)(2,1)S(1)}, u32[]{:S(2)}, u32[]{:S(2)}) collective-permute-start(bf16[128,1024]{1,0:T(8,128)(2,1)S(1)} %shard_map.105.refs_0_), channel_id=1, source_target_pairs={{0,1},{1,0},{2,3},{3,2},{4,5},{5,4},{6,7},{7,6},{8,9},{9,8},{10,11... | collective-permute-start | bytes 786440 | tf_op jit(solution)/shard_map/ppermute | solution.py:68
  15.8 4.9 %collective-permute-start.6 = (bf16[80,384]{1,0:T(8,128)(2,1)S(1)}, bf16[80,384]{1,0:T(8,128)(2,1)S(1)}, u32[]{:S(2)}, u32[]{:S(2)}) collective-permute-start(bf16[80,384]{1,0:T(8,128)(2,1)S(1)} %get-tuple-element.18), channel_id=1, source_target_pairs={{0,8},{8,0},{16,24},{24,16},{1,9},{9,1},{17,25},{25,17},{2,10},{10... | collective-permute-start | bytes 184328 | tf_op jit(solution)/shard_map/ppermute | solution.py:49
  16.5 8.0 %collective-permute-start.7 = (bf16[80,384]{1,0:T(8,128)(2,1)S(1)}, bf16[80,384]{1,0:T(8,128)(2,1)S(1)}, u32[]{:S(2)}, u32[]{:S(2)}) collective-permute-start(bf16[80,384]{1,0:T(8,128)(2,1)S(1)} %get-tuple-element.19), channel_id=1, source_target_pairs={{0,16},{8,24},{16,0},{24,8},{1,17},{9,25},{17,1},{25,9},{2,18},{10... | collective-permute-start | bytes 184328 | tf_op jit(solution)/shard_map/ppermute | solution.py:49
  17.8 6.7 %collective-permute-start.8 = (bf16[80,384]{1,0:T(8,128)(2,1)S(1)}, bf16[80,384]{1,0:T(8,128)(2,1)S(1)}, u32[]{:S(2)}, u32[]{:S(2)}) collective-permute-start(bf16[80,384]{1,0:T(8,128)(2,1)S(1)} %get-tuple-element.20), channel_id=1, source_target_pairs={{0,24},{8,16},{16,8},{24,0},{1,25},{9,17},{17,9},{25,1},{2,26},{10... | collective-permute-start | bytes 184328 | tf_op jit(solution)/shard_map/ppermute | solution.py:49
  24.7 1.2 %collective-permute-start.9 = (f32[8,128]{1,0:T(8,128)S(1)}, f32[8,128]{1,0:T(8,128)S(1)}, u32[]{:S(2)}, u32[]{:S(2)}) collective-permute-start(f32[8,128]{1,0:T(8,128)S(1)} %get-tuple-element.22.own_ref.refs_4_), channel_id=1, source_target_pairs={{0,1},{1,0},{2,3},{3,2},{4,5},{5,4},{6,7},{7,6},{8,9},{9,8},{10,11... | collective-permute-start | bytes 12296 | tf_op jit(solution)/shard_map/ppermute | solution.py:68
  25.9 4.6 %collective-permute-start.12 = (f32[8,128]{1,0:T(8,128)S(1)}, f32[8,128]{1,0:T(8,128)S(1)}, u32[]{:S(2)}, u32[]{:S(2)}) collective-permute-start(f32[8,128]{1,0:T(8,128)S(1)} %shard_map.108.refs_0_), channel_id=1, source_target_pairs={{0,6},{1,7},{2,4},{3,5},{4,2},{5,3},{6,0},{7,1},{8,14},{9,15},{10,... | collective-permute-start | bytes 12296 | tf_op jit(solution)/shard_map/ppermute | solution.py:49
  27.4 3.6 %collective-permute-start.11 = (f32[8,128]{1,0:T(8,128)S(1)}, f32[8,128]{1,0:T(8,128)S(1)}, u32[]{:S(2)}, u32[]{:S(2)}) collective-permute-start(f32[8,128]{1,0:T(8,128)S(1)} %shard_map.108.refs_0_), channel_id=1, source_target_pairs={{0,4},{1,5},{2,6},{3,7},{4,0},{5,1},{6,2},{7,3},{8,12},{9,13},{10,... | collective-permute-start | bytes 12296 | tf_op jit(solution)/shard_map/ppermute | solution.py:49
  28.0 3.6 %collective-permute-start.10 = (f32[8,128]{1,0:T(8,128)S(1)}, f32[8,128]{1,0:T(8,128)S(1)}, u32[]{:S(2)}, u32[]{:S(2)}) collective-permute-start(f32[8,128]{1,0:T(8,128)S(1)} %shard_map.108.refs_0_), channel_id=1, source_target_pairs={{0,2},{1,3},{2,0},{3,1},{4,6},{5,7},{6,4},{7,5},{8,10},{9,11},{10,... | collective-permute-start | bytes 12296 | tf_op jit(solution)/shard_map/ppermute | solution.py:49
  31.7 5.8 %collective-permute-start.15 = (bf16[32,512]{1,0:T(8,128)(2,1)S(1)}, bf16[32,512]{1,0:T(8,128)(2,1)S(1)}, u32[]{:S(2)}, u32[]{:S(2)}) collective-permute-start(bf16[32,512]{1,0:T(8,128)(2,1)S(1)} %shard_map.110.refs_0_), channel_id=1, source_target_pairs={{0,24},{8,16},{16,8},{24,0},{1,25},{9,17},{17,9},{25,1},{2,26},{10... | collective-permute-start | bytes 98312 | tf_op jit(solution)/shard_map/ppermute | solution.py:49
  33.7 4.9 %collective-permute-start.14 = (bf16[32,512]{1,0:T(8,128)(2,1)S(1)}, bf16[32,512]{1,0:T(8,128)(2,1)S(1)}, u32[]{:S(2)}, u32[]{:S(2)}) collective-permute-start(bf16[32,512]{1,0:T(8,128)(2,1)S(1)} %shard_map.110.refs_0_), channel_id=1, source_target_pairs={{0,16},{8,24},{16,0},{24,8},{1,17},{9,25},{17,1},{25,9},{2,18},{10... | collective-permute-start | bytes 98312 | tf_op jit(solution)/shard_map/ppermute | solution.py:49
  34.5 4.3 %collective-permute-start.13 = (bf16[32,512]{1,0:T(8,128)(2,1)S(1)}, bf16[32,512]{1,0:T(8,128)(2,1)S(1)}, u32[]{:S(2)}, u32[]{:S(2)}) collective-permute-start(bf16[32,512]{1,0:T(8,128)(2,1)S(1)} %shard_map.110.refs_0_), channel_id=1, source_target_pairs={{0,8},{8,0},{16,24},{24,16},{1,9},{9,1},{17,25},{25,17},{2,10},{10... | collective-permute-start | bytes 98312 | tf_op jit(solution)/shard_map/ppermute | solution.py:49

commit v9 on v8

--- a/solution.py
+++ b/solution.py
@@ -10,7 +10,7 @@
 
 BF16, F32 = jnp.bfloat16, jnp.float32
 LANES = 128
-PAD = 16
+PAD = 8
 LANCZOS = (
     0.99999999999980993227684700473478,
     676.520368121885098567009190444019,

time: 39.9 us -> 39.4 us (0.987)
  waiting for transfers between devices: 14.8 us -> 14.4 us
    ppermute x12, waiting for transfers between devices: 11.8 us -> 11.4 us  [send(): return lax.ppermute(value, axis, pairs)]
  transfers between devices with their start and end apart: 16 -> 16, of which waited for: 14 -> 13; matrix products, arithmetic and copies ran while one was open for 0% -> 0% of each run, Pallas kernels for 1% -> 1%
where the time goes in v9:
time: 39.4 us; the launch traced here: 39.3 us
  starting transfers between devices  21.6 us (55%)
  waiting for transfers between devices  14.4 us (37%)
  Pallas kernels  2.56 us (6%)
  between operations  0.75 us (2%)
    ppermute x12, starting transfers between devices, send(): return lax.ppermute(value, axis, pairs)  15.9 us
    ppermute x12, waiting for transfers between devices, send(): return lax.ppermute(value, axis, pairs)  11.4 us
    ppermute x2, starting transfers between devices, send_split(): return lax.ppermute(value, ('member', 'dp'), pairs)  5.56 us
    ppermute x2, waiting for transfers between devices, swap_cores(): lax.ppermute(value, axis, [(i, i ^ 1) for i in range(lax.axis_size(axis))])  2.67 us
    pallas_call x1, Pallas kernels, on_device(): call(functools.partial(gradient_kernel, members, images, classes * peers)...  0.97 us
  transfers between devices with their start and end apart: 16, of which 13 were waited for; matrix products, arithmetic and copies ran while one was open for 0% of the time, Pallas kernels for 1%

profile of v9, /device:TPU:0, one launch (start us, length us, event | category | flops | bytes accessed | tf_op | source)
XLA Modules:
  0.0 39.3 jit_solution(855962654675389780)
XLA Ops:
  0.6 3.1 %collective-permute-start.3 = (bf16[32,1024]{1,0:T(8,128)(2,1)}, bf16[32,1024]{1,0:T(8,128)(2,1)S(1)}, u32[]{:S(2)}, u32[]{:S(2)}) collective-permute-start(bf16[32,1024]{1,0:T(8,128)(2,1)} %refs_2_.1), channel_id=1, source_target_pairs={{0,8},{1,17},{2,10},{3,19},{4,12},{5,21},{6,14},{7,23},{8,0},{9,25... | collective-permute-start | bytes 196616 | tf_op jit(solution)/shard_map/ppermute | solution.py:64
  3.7 2.5 %collective-permute-start.4 = (bf16[32,1024]{1,0:T(8,128)(2,1)}, bf16[32,1024]{1,0:T(8,128)(2,1)S(1)}, u32[]{:S(2)}, u32[]{:S(2)}) collective-permute-start(bf16[32,1024]{1,0:T(8,128)(2,1)} %refs_2_.1), channel_id=1, source_target_pairs={{0,24},{1,9},{2,26},{3,11},{4,28},{5,13},{6,30},{7,15},{8,16},{9,1... | collective-permute-start | bytes 196616 | tf_op jit(solution)/shard_map/ppermute | solution.py:64
  6.2 2.4 %collective-permute-start.2 = (bf16[16,1024]{1,0:T(8,128)(2,1)}, bf16[16,1024]{1,0:T(8,128)(2,1)S(1)}, u32[]{:S(2)}, u32[]{:S(2)}) collective-permute-start(bf16[16,1024]{1,0:T(8,128)(2,1)} %bitcast.7), channel_id=1, source_target_pairs={{0,6},{1,7},{2,4},{3,5},{4,2},{5,3},{6,0},{7,1},{8,14},{9,15},{10,... | collective-permute-start | bytes 98312 | tf_op jit(solution)/shard_map/ppermute | solution.py:49
  8.6 0.5 %collective-permute-start.1 = (bf16[16,1024]{1,0:T(8,128)(2,1)}, bf16[16,1024]{1,0:T(8,128)(2,1)S(1)}, u32[]{:S(2)}, u32[]{:S(2)}) collective-permute-start(bf16[16,1024]{1,0:T(8,128)(2,1)} %bitcast.8), channel_id=1, source_target_pairs={{0,4},{1,5},{2,6},{3,7},{4,0},{5,1},{6,2},{7,3},{8,12},{9,13},{10,... | collective-permute-start | bytes 98312 | tf_op jit(solution)/shard_map/ppermute | solution.py:49
  9.2 0.5 %collective-permute-start = (bf16[16,1024]{1,0:T(8,128)(2,1)}, bf16[16,1024]{1,0:T(8,128)(2,1)S(1)}, u32[]{:S(2)}, u32[]{:S(2)}) collective-permute-start(bf16[16,1024]{1,0:T(8,128)(2,1)} %bitcast.9), channel_id=1, source_target_pairs={{0,2},{1,3},{2,0},{3,1},{4,6},{5,7},{6,4},{7,5},{8,10},{9,11},{10,... | collective-permute-start | bytes 98312 | tf_op jit(solution)/shard_map/ppermute | solution.py:49
  9.7 0.0 collective-permute-done.3.refs_0_
  9.7 0.3 collective-permute-done.4.refs_1_
  10.0 0.0 copy-done.3
  10.0 0.2 shard_map.104.refs_5_
  10.2 0.0 copy-start
  10.2 0.0 copy-start.1
  10.2 0.0 copy-start.2
  10.3 1.0 %collective-permute-done.2.refs_3_ = bf16[16,1024]{1,0:T(8,128)(2,1)S(1)} collective-permute-done((bf16[16,1024]{1,0:T(8,128)(2,1)}, bf16[16,1024]{1,0:T(8,128)(2,1)S(1)}, u32[]{:S(2)}, u32[]{:S(2)}) %collective-permute-start.2) | collective-permute-done | bytes 32800 | tf_op jit(solution)/shard_map/ppermute | solution.py:49
  11.3 1.5 %collective-permute-done.1.refs_2_ = bf16[16,1024]{1,0:T(8,128)(2,1)S(1)} collective-permute-done((bf16[16,1024]{1,0:T(8,128)(2,1)}, bf16[16,1024]{1,0:T(8,128)(2,1)S(1)}, u32[]{:S(2)}, u32[]{:S(2)}) %collective-permute-start.1) | collective-permute-done | bytes 32800 | tf_op jit(solution)/shard_map/ppermute | solution.py:49
  12.8 0.5 %collective-permute-done.refs_1_ = bf16[16,1024]{1,0:T(8,128)(2,1)S(1)} collective-permute-done((bf16[16,1024]{1,0:T(8,128)(2,1)}, bf16[16,1024]{1,0:T(8,128)(2,1)S(1)}, u32[]{:S(2)}, u32[]{:S(2)}) %collective-permute-start) | collective-permute-done | bytes 32800 | tf_op jit(solution)/shard_map/ppermute | solution.py:49
  13.3 0.0 copy-done.6
  13.3 0.0 copy-done.7
  13.3 0.2 shard_map.105.refs_0_
  13.5 0.0 copy-start.5
  13.5 0.1 collective-permute-start.5
  13.6 1.5 %collective-permute-done.5.refs_1_ = bf16[128,1024]{1,0:T(8,128)(2,1)S(1)} collective-permute-done((bf16[128,1024]{1,0:T(8,128)(2,1)S(1)}, bf16[128,1024]{1,0:T(8,128)(2,1)S(1)}, u32[]{:S(2)}, u32[]{:S(2)}) %collective-permute-start.5) | collective-permute-done | bytes 262176 | tf_op jit(solution)/shard_map/ppermute | solution.py:68
  15.1 0.0 copy-done
  15.1 0.0 copy-done.1
  15.2 0.6 %shard_map.106 = (bf16[72,384]{1,0:T(8,128)(2,1)S(1)}, bf16[72,384]{1,0:T(8,128)(2,1)S(1)}, bf16[72,384]{1,0:T(8,128)(2,1)S(1)}, bf16[72,384]{1,0:T(8,128)(2,1)S...) custom-call(bf16[128,1024]{1,0:T(8,128)(2,1)S(1)} %shard_map.105.refs_0_, ...), custom_call_target="tpu_custom_call" | custom-call | tf_op jit(solution)/shard_map/pallas_call | solution.py:343
  15.8 0.7 %collective-permute-start.6 = (bf16[72,384]{1,0:T(8,128)(2,1)S(1)}, bf16[72,384]{1,0:T(8,128)(2,1)S(1)}, u32[]{:S(2)}, u32[]{:S(2)}) collective-permute-start(bf16[72,384]{1,0:T(8,128)(2,1)S(1)} %get-tuple-element.18), channel_id=1, source_target_pairs={{0,8},{8,0},{16,24},{24,16},{1,9},{9,1},{17,25},{25,17},{2,10},{10... | collective-permute-start | bytes 165896 | tf_op jit(solution)/shard_map/ppermute | solution.py:49
  16.5 1.2 %collective-permute-start.7 = (bf16[72,384]{1,0:T(8,128)(2,1)S(1)}, bf16[72,384]{1,0:T(8,128)(2,1)S(1)}, u32[]{:S(2)}, u32[]{:S(2)}) collective-permute-start(bf16[72,384]{1,0:T(8,128)(2,1)S(1)} %get-tuple-element.19), channel_id=1, source_target_pairs={{0,16},{8,24},{16,0},{24,8},{1,17},{9,25},{17,1},{25,9},{2,18},{10... | collective-permute-start | bytes 165896 | tf_op jit(solution)/shard_map/ppermute | solution.py:49
  17.8 2.5 %collective-permute-start.8 = (bf16[72,384]{1,0:T(8,128)(2,1)S(1)}, bf16[72,384]{1,0:T(8,128)(2,1)S(1)}, u32[]{:S(2)}, u32[]{:S(2)}) collective-permute-start(bf16[72,384]{1,0:T(8,128)(2,1)S(1)} %get-tuple-element.20), channel_id=1, source_target_pairs={{0,24},{8,16},{16,8},{24,0},{1,25},{9,17},{17,9},{25,1},{2,26},{10... | collective-permute-start | bytes 165896 | tf_op jit(solution)/shard_map/ppermute | solution.py:49
  20.2 0.4 collective-permute-done.6.refs_1_
  20.6 3.4 %collective-permute-done.7.refs_2_ = bf16[72,384]{1,0:T(8,128)(2,1)S(1)} collective-permute-done((bf16[72,384]{1,0:T(8,128)(2,1)S(1)}, bf16[72,384]{1,0:T(8,128)(2,1)S(1)}, u32[]{:S(2)}, u32[]{:S(2)}) %collective-permute-start.7) | collective-permute-done | bytes 55328 | tf_op jit(solution)/shard_map/ppermute | solution.py:49
  24.0 0.0 collective-permute-done.8.refs_3_
  24.0 0.2 shard_map.107
  24.2 0.0 collective-permute-start.9
  24.3 1.2 %collective-permute-done.9.other_ref = f32[8,128]{1,0:T(8,128)S(1)} collective-permute-done((f32[8,128]{1,0:T(8,128)S(1)}, f32[8,128]{1,0:T(8,128)S(1)}, u32[]{:S(2)}, u32[]{:S(2)}) %collective-permute-start.9) | collective-permute-done | bytes 4128 | tf_op jit(solution)/shard_map/ppermute | solution.py:68
  25.4 1.6 %collective-permute-start.12 = (f32[8,128]{1,0:T(8,128)S(1)}, f32[8,128]{1,0:T(8,128)S(1)}, u32[]{:S(2)}, u32[]{:S(2)}) collective-permute-start(f32[8,128]{1,0:T(8,128)S(1)} %shard_map.108.refs_0_), channel_id=1, source_target_pairs={{0,6},{1,7},{2,4},{3,5},{4,2},{5,3},{6,0},{7,1},{8,14},{9,15},{10,... | collective-permute-start | bytes 12296 | tf_op jit(solution)/shard_map/ppermute | solution.py:49
  27.0 0.5 %collective-permute-start.11 = (f32[8,128]{1,0:T(8,128)S(1)}, f32[8,128]{1,0:T(8,128)S(1)}, u32[]{:S(2)}, u32[]{:S(2)}) collective-permute-start(f32[8,128]{1,0:T(8,128)S(1)} %shard_map.108.refs_0_), channel_id=1, source_target_pairs={{0,4},{1,5},{2,6},{3,7},{4,0},{5,1},{6,2},{7,3},{8,12},{9,13},{10,... | collective-permute-start | bytes 12296 | tf_op jit(solution)/shard_map/ppermute | solution.py:49
  27.5 1.5 %collective-permute-start.10 = (f32[8,128]{1,0:T(8,128)S(1)}, f32[8,128]{1,0:T(8,128)S(1)}, u32[]{:S(2)}, u32[]{:S(2)}) collective-permute-start(f32[8,128]{1,0:T(8,128)S(1)} %shard_map.108.refs_0_), channel_id=1, source_target_pairs={{0,2},{1,3},{2,0},{3,1},{4,6},{5,7},{6,4},{7,5},{8,10},{9,11},{10,... | collective-permute-start | bytes 12296 | tf_op jit(solution)/shard_map/ppermute | solution.py:49
  29.0 0.1 shard_map.109
  29.1 0.9 %collective-permute-done.12.refs_3_ = f32[8,128]{1,0:T(8,128)S(1)} collective-permute-done((f32[8,128]{1,0:T(8,128)S(1)}, f32[8,128]{1,0:T(8,128)S(1)}, u32[]{:S(2)}, u32[]{:S(2)}) %collective-permute-start.12) | collective-permute-done | bytes 4128 | tf_op jit(solution)/shard_map/ppermute | solution.py:49
  30.0 0.6 %collective-permute-done.11.refs_2_ = f32[8,128]{1,0:T(8,128)S(1)} collective-permute-done((f32[8,128]{1,0:T(8,128)S(1)}, f32[8,128]{1,0:T(8,128)S(1)}, u32[]{:S(2)}, u32[]{:S(2)}) %collective-permute-start.11) | collective-permute-done | bytes 4128 | tf_op jit(solution)/shard_map/ppermute | solution.py:49
  30.6 0.5 %collective-permute-done.10.refs_1_ = f32[8,128]{1,0:T(8,128)S(1)} collective-permute-done((f32[8,128]{1,0:T(8,128)S(1)}, f32[8,128]{1,0:T(8,128)S(1)}, u32[]{:S(2)}, u32[]{:S(2)}) %collective-permute-start.10) | collective-permute-done | bytes 4128 | tf_op jit(solution)/shard_map/ppermute | solution.py:49
  31.1 0.1 shard_map.110.refs_0_
  31.3 2.2 %collective-permute-start.15 = (bf16[32,512]{1,0:T(8,128)(2,1)S(1)}, bf16[32,512]{1,0:T(8,128)(2,1)S(1)}, u32[]{:S(2)}, u32[]{:S(2)}) collective-permute-start(bf16[32,512]{1,0:T(8,128)(2,1)S(1)} %shard_map.110.refs_0_), channel_id=1, source_target_pairs={{0,24},{8,16},{16,8},{24,0},{1,25},{9,17},{17,9},{25,1},{2,26},{10... | collective-permute-start | bytes 98312 | tf_op jit(solution)/shard_map/ppermute | solution.py:49
  33.5 0.4 %collective-permute-start.14 = (bf16[32,512]{1,0:T(8,128)(2,1)S(1)}, bf16[32,512]{1,0:T(8,128)(2,1)S(1)}, u32[]{:S(2)}, u32[]{:S(2)}) collective-permute-start(bf16[32,512]{1,0:T(8,128)(2,1)S(1)} %shard_map.110.refs_0_), channel_id=1, source_target_pairs={{0,16},{8,24},{16,0},{24,8},{1,17},{9,25},{17,1},{25,9},{2,18},{10... | collective-permute-start | bytes 98312 | tf_op jit(solution)/shard_map/ppermute | solution.py:49
  33.9 1.8 %collective-permute-start.13 = (bf16[32,512]{1,0:T(8,128)(2,1)S(1)}, bf16[32,512]{1,0:T(8,128)(2,1)S(1)}, u32[]{:S(2)}, u32[]{:S(2)}) collective-permute-start(bf16[32,512]{1,0:T(8,128)(2,1)S(1)} %shard_map.110.refs_0_), channel_id=1, source_target_pairs={{0,8},{8,0},{16,24},{24,16},{1,9},{9,1},{17,25},{25,17},{2,10},{10... | collective-permute-start | bytes 98312 | tf_op jit(solution)/shard_map/ppermute | solution.py:49
  35.7 1.6 %collective-permute-done.15.refs_3_ = bf16[32,512]{1,0:T(8,128)(2,1)S(1)} collective-permute-done((bf16[32,512]{1,0:T(8,128)(2,1)S(1)}, bf16[32,512]{1,0:T(8,128)(2,1)S(1)}, u32[]{:S(2)}, u32[]{:S(2)}) %collective-permute-start.15) | collective-permute-done | bytes 32800 | tf_op jit(solution)/shard_map/ppermute | solution.py:49
  37.3 1.0 %collective-permute-done.14.refs_2_ = bf16[32,512]{1,0:T(8,128)(2,1)S(1)} collective-permute-done((bf16[32,512]{1,0:T(8,128)(2,1)S(1)}, bf16[32,512]{1,0:T(8,128)(2,1)S(1)}, u32[]{:S(2)}, u32[]{:S(2)}) %collective-permute-start.14) | collective-permute-done | bytes 32800 | tf_op jit(solution)/shard_map/ppermute | solution.py:49
  38.3 0.0 collective-permute-done.13.refs_1_
  38.3 1.0 %shard_map.111 = (f32[1,1]{1,0:T(1,128)}, f32[256,384]{1,0:T(8,128)}, f32[384]{0:T(512)}) custom-call(bf16[32,512]{1,0:T(8,128)(2,1)S(1)} %shard_map.110.refs_0_, bf16[32,512]{1,0:T(8,128)(2,1)S(1)} %collective-permute-done.13.refs_1_, bf16[32,512]{1,0:T(8,128)(2,1)S(1)} %collective-permute-done.14.refs_2_, ...), custom_call_target="tpu_custom_call" | custom-call | tf_op jit(solution)/shard_map/pallas_call | solution.py:381
  (9 shorter events, 0.0 us)
Async XLA Ops:
  0.6 9.1 %collective-permute-start.3 = (bf16[32,1024]{1,0:T(8,128)(2,1)}, bf16[32,1024]{1,0:T(8,128)(2,1)S(1)}, u32[]{:S(2)}, u32[]{:S(2)}) collective-permute-start(bf16[32,1024]{1,0:T(8,128)(2,1)} %refs_2_.1), channel_id=1, source_target_pairs={{0,8},{1,17},{2,10},{3,19},{4,12},{5,21},{6,14},{7,23},{8,0},{9,25... | collective-permute-start | bytes 196616 | tf_op jit(solution)/shard_map/ppermute | solution.py:64
  3.7 6.3 %collective-permute-start.4 = (bf16[32,1024]{1,0:T(8,128)(2,1)}, bf16[32,1024]{1,0:T(8,128)(2,1)S(1)}, u32[]{:S(2)}, u32[]{:S(2)}) collective-permute-start(bf16[32,1024]{1,0:T(8,128)(2,1)} %refs_2_.1), channel_id=1, source_target_pairs={{0,24},{1,9},{2,26},{3,11},{4,28},{5,13},{6,30},{7,15},{8,16},{9,1... | collective-permute-start | bytes 196616 | tf_op jit(solution)/shard_map/ppermute | solution.py:64
  6.2 3.8 %copy-start.3 = (f32[1024]{0:T(1024)S(1)}, f32[1024]{0:T(1024)}, u32[]{:S(2)}) copy-start(f32[1024]{0:T(1024)} %param.13) | copy-start | bytes 12292
  6.2 5.1 %collective-permute-start.2 = (bf16[16,1024]{1,0:T(8,128)(2,1)}, bf16[16,1024]{1,0:T(8,128)(2,1)S(1)}, u32[]{:S(2)}, u32[]{:S(2)}) collective-permute-start(bf16[16,1024]{1,0:T(8,128)(2,1)} %bitcast.7), channel_id=1, source_target_pairs={{0,6},{1,7},{2,4},{3,5},{4,2},{5,3},{6,0},{7,1},{8,14},{9,15},{10,... | collective-permute-start | bytes 98312 | tf_op jit(solution)/shard_map/ppermute | solution.py:49
  8.6 4.1 %collective-permute-start.1 = (bf16[16,1024]{1,0:T(8,128)(2,1)}, bf16[16,1024]{1,0:T(8,128)(2,1)S(1)}, u32[]{:S(2)}, u32[]{:S(2)}) collective-permute-start(bf16[16,1024]{1,0:T(8,128)(2,1)} %bitcast.8), channel_id=1, source_target_pairs={{0,4},{1,5},{2,6},{3,7},{4,0},{5,1},{6,2},{7,3},{8,12},{9,13},{10,... | collective-permute-start | bytes 98312 | tf_op jit(solution)/shard_map/ppermute | solution.py:49
  9.2 4.1 %collective-permute-start = (bf16[16,1024]{1,0:T(8,128)(2,1)}, bf16[16,1024]{1,0:T(8,128)(2,1)S(1)}, u32[]{:S(2)}, u32[]{:S(2)}) collective-permute-start(bf16[16,1024]{1,0:T(8,128)(2,1)} %bitcast.9), channel_id=1, source_target_pairs={{0,2},{1,3},{2,0},{3,1},{4,6},{5,7},{6,4},{7,5},{8,10},{9,11},{10,... | collective-permute-start | bytes 98312 | tf_op jit(solution)/shard_map/ppermute | solution.py:49
  10.0 3.3 %copy-start.6 = (bf16[1,16,1024]{2,1,0:T(8,128)(2,1)S(1)}, bf16[1,16,1024]{2,1,0:T(8,128)(2,1)}, u32[]{:S(2)}) copy-start(bf16[1,16,1024]{2,1,0:T(8,128)(2,1)} %param.8) | copy-start | bytes 98308
  10.0 3.3 %copy-start.7 = (f32[1,1024]{1,0:T(1,128)S(1)}, f32[1,1024]{1,0:T(1,128)}, u32[]{:S(2)}) copy-start(f32[1,1024]{1,0:T(1,128)} %refs_4_.1) | copy-start | bytes 12292
  10.2 4.9 %copy-start = (bf16[1,1024,384]{2,1,0:T(8,128)(2,1)S(1)}, bf16[1,1024,384]{2,1,0:T(8,128)(2,1)}, u32[]{:S(2)}) copy-start(bf16[1,1024,384]{2,1,0:T(8,128)(2,1)} %param.10) | copy-start | bytes 2359300
  10.2 4.9 %copy-start.1 = (bf16[256,384]{1,0:T(8,128)(2,1)S(1)}, bf16[256,384]{1,0:T(8,128)(2,1)}, u32[]{:S(2)}) copy-start(bf16[256,384]{1,0:T(8,128)(2,1)} %refs_5_.1) | copy-start | bytes 589828
  10.2 4.9 %copy-start.2 = (bf16[32,1024]{1,0:T(8,128)(2,1)S(1)}, bf16[32,1024]{1,0:T(8,128)(2,1)}, u32[]{:S(2)}) copy-start(bf16[32,1024]{1,0:T(8,128)(2,1)} %refs_2_.1) | copy-start | bytes 196612
  13.3 1.9 %copy-start.4 = (f32[384]{0:T(512)S(1)}, f32[384]{0:T(512)}, u32[]{:S(2)}) copy-start(f32[384]{0:T(512)} %refs_7_.1) | copy-start | bytes 4612
  13.5 1.6 %copy-start.5 = (f32[1,384]{1,0:T(1,128)S(1)}, f32[1,384]{1,0:T(1,128)}, u32[]{:S(2)}) copy-start(f32[1,384]{1,0:T(1,128)} %refs_6_.1) | copy-start | bytes 4612
  13.5 1.6 %collective-permute-start.5 = (bf16[128,1024]{1,0:T(8,128)(2,1)S(1)}, bf16[128,1024]{1,0:T(8,128)(2,1)S(1)}, u32[]{:S(2)}, u32[]{:S(2)}) collective-permute-start(bf16[128,1024]{1,0:T(8,128)(2,1)S(1)} %shard_map.105.refs_0_), channel_id=1, source_target_pairs={{0,1},{1,0},{2,3},{3,2},{4,5},{5,4},{6,7},{7,6},{8,9},{9,8},{10,11... | collective-permute-start | bytes 786440 | tf_op jit(solution)/shard_map/ppermute | solution.py:68
  15.8 4.8 %collective-permute-start.6 = (bf16[72,384]{1,0:T(8,128)(2,1)S(1)}, bf16[72,384]{1,0:T(8,128)(2,1)S(1)}, u32[]{:S(2)}, u32[]{:S(2)}) collective-permute-start(bf16[72,384]{1,0:T(8,128)(2,1)S(1)} %get-tuple-element.18), channel_id=1, source_target_pairs={{0,8},{8,0},{16,24},{24,16},{1,9},{9,1},{17,25},{25,17},{2,10},{10... | collective-permute-start | bytes 165896 | tf_op jit(solution)/shard_map/ppermute | solution.py:49
  16.5 7.5 %collective-permute-start.7 = (bf16[72,384]{1,0:T(8,128)(2,1)S(1)}, bf16[72,384]{1,0:T(8,128)(2,1)S(1)}, u32[]{:S(2)}, u32[]{:S(2)}) collective-permute-start(bf16[72,384]{1,0:T(8,128)(2,1)S(1)} %get-tuple-element.19), channel_id=1, source_target_pairs={{0,16},{8,24},{16,0},{24,8},{1,17},{9,25},{17,1},{25,9},{2,18},{10... | collective-permute-start | bytes 165896 | tf_op jit(solution)/shard_map/ppermute | solution.py:49
  17.8 6.3 %collective-permute-start.8 = (bf16[72,384]{1,0:T(8,128)(2,1)S(1)}, bf16[72,384]{1,0:T(8,128)(2,1)S(1)}, u32[]{:S(2)}, u32[]{:S(2)}) collective-permute-start(bf16[72,384]{1,0:T(8,128)(2,1)S(1)} %get-tuple-element.20), channel_id=1, source_target_pairs={{0,24},{8,16},{16,8},{24,0},{1,25},{9,17},{17,9},{25,1},{2,26},{10... | collective-permute-start | bytes 165896 | tf_op jit(solution)/shard_map/ppermute | solution.py:49
  24.2 1.2 %collective-permute-start.9 = (f32[8,128]{1,0:T(8,128)S(1)}, f32[8,128]{1,0:T(8,128)S(1)}, u32[]{:S(2)}, u32[]{:S(2)}) collective-permute-start(f32[8,128]{1,0:T(8,128)S(1)} %get-tuple-element.22.own_ref.refs_4_), channel_id=1, source_target_pairs={{0,1},{1,0},{2,3},{3,2},{4,5},{5,4},{6,7},{7,6},{8,9},{9,8},{10,11... | collective-permute-start | bytes 12296 | tf_op jit(solution)/shard_map/ppermute | solution.py:68
  25.4 4.6 %collective-permute-start.12 = (f32[8,128]{1,0:T(8,128)S(1)}, f32[8,128]{1,0:T(8,128)S(1)}, u32[]{:S(2)}, u32[]{:S(2)}) collective-permute-start(f32[8,128]{1,0:T(8,128)S(1)} %shard_map.108.refs_0_), channel_id=1, source_target_pairs={{0,6},{1,7},{2,4},{3,5},{4,2},{5,3},{6,0},{7,1},{8,14},{9,15},{10,... | collective-permute-start | bytes 12296 | tf_op jit(solution)/shard_map/ppermute | solution.py:49
  27.0 3.6 %collective-permute-start.11 = (f32[8,128]{1,0:T(8,128)S(1)}, f32[8,128]{1,0:T(8,128)S(1)}, u32[]{:S(2)}, u32[]{:S(2)}) collective-permute-start(f32[8,128]{1,0:T(8,128)S(1)} %shard_map.108.refs_0_), channel_id=1, source_target_pairs={{0,4},{1,5},{2,6},{3,7},{4,0},{5,1},{6,2},{7,3},{8,12},{9,13},{10,... | collective-permute-start | bytes 12296 | tf_op jit(solution)/shard_map/ppermute | solution.py:49
  27.5 3.6 %collective-permute-start.10 = (f32[8,128]{1,0:T(8,128)S(1)}, f32[8,128]{1,0:T(8,128)S(1)}, u32[]{:S(2)}, u32[]{:S(2)}) collective-permute-start(f32[8,128]{1,0:T(8,128)S(1)} %shard_map.108.refs_0_), channel_id=1, source_target_pairs={{0,2},{1,3},{2,0},{3,1},{4,6},{5,7},{6,4},{7,5},{8,10},{9,11},{10,... | collective-permute-start | bytes 12296 | tf_op jit(solution)/shard_map/ppermute | solution.py:49
  31.3 6.1 %collective-permute-start.15 = (bf16[32,512]{1,0:T(8,128)(2,1)S(1)}, bf16[32,512]{1,0:T(8,128)(2,1)S(1)}, u32[]{:S(2)}, u32[]{:S(2)}) collective-permute-start(bf16[32,512]{1,0:T(8,128)(2,1)S(1)} %shard_map.110.refs_0_), channel_id=1, source_target_pairs={{0,24},{8,16},{16,8},{24,0},{1,25},{9,17},{17,9},{25,1},{2,26},{10... | collective-permute-start | bytes 98312 | tf_op jit(solution)/shard_map/ppermute | solution.py:49
  33.5 4.8 %collective-permute-start.14 = (bf16[32,512]{1,0:T(8,128)(2,1)S(1)}, bf16[32,512]{1,0:T(8,128)(2,1)S(1)}, u32[]{:S(2)}, u32[]{:S(2)}) collective-permute-start(bf16[32,512]{1,0:T(8,128)(2,1)S(1)} %shard_map.110.refs_0_), channel_id=1, source_target_pairs={{0,16},{8,24},{16,0},{24,8},{1,17},{9,25},{17,1},{25,9},{2,18},{10... | collective-permute-start | bytes 98312 | tf_op jit(solution)/shard_map/ppermute | solution.py:49
  33.9 4.4 %collective-permute-start.13 = (bf16[32,512]{1,0:T(8,128)(2,1)S(1)}, bf16[32,512]{1,0:T(8,128)(2,1)S(1)}, u32[]{:S(2)}, u32[]{:S(2)}) collective-permute-start(bf16[32,512]{1,0:T(8,128)(2,1)S(1)} %shard_map.110.refs_0_), channel_id=1, source_target_pairs={{0,8},{8,0},{16,24},{24,16},{1,9},{9,1},{17,25},{25,17},{2,10},{10... | collective-permute-start | bytes 98312 | tf_op jit(solution)/shard_map/ppermute | solution.py:49

commit v10 on v9

--- a/solution.py
+++ b/solution.py
@@ -205,7 +205,7 @@
 
 
 def alphas_kernel(members, *refs):
-    payloads, refs = refs[:members], refs[members:]
+    payloads, refs = refs[:1] + refs[1:members][::-1], refs[members:]
     own_logits_ref, alphas_ref, target_ref, small_ref = refs
     mine = lax.axis_index("member")
     block, classes = alphas_ref.shape
@@ -365,7 +365,7 @@
     alphas, target, own = call(
         functools.partial(alphas_kernel, members),
         [shape((block, classes), F32)] * 2 + [shape((small_rows, LANES), F32)],
-    )(*got, own_logits)
+    )(got[0], *got[1:][::-1], own_logits)
     other = swap_cores(own, "dp")
     inner, turned = call(
         digamma_kernel, [shape((block, classes), F32), shape((width, images), BF16)]

time: 39.4 us -> 39 us (0.990)
  waiting for transfers between devices: 14.4 us -> 13.9 us
    ppermute x12, waiting for transfers between devices: 11.4 us -> 10.9 us  [send(): return lax.ppermute(value, axis, pairs)]
  transfers between devices with their start and end apart: 16 -> 16, of which waited for: 13 -> 14; matrix products, arithmetic and copies ran while one was open for 0% -> 0% of each run, Pallas kernels for 1% -> 1%
where the time goes in v10:
time: 39 us; the launch traced here: 38.8 us
  starting transfers between devices  21.6 us (55%)
  waiting for transfers between devices  13.9 us (36%)
  Pallas kernels  2.56 us (7%)
  between operations  0.74 us (2%)
    ppermute x12, starting transfers between devices, send(): return lax.ppermute(value, axis, pairs)  15.9 us
    ppermute x12, waiting for transfers between devices, send(): return lax.ppermute(value, axis, pairs)  10.9 us
    ppermute x2, starting transfers between devices, send_split(): return lax.ppermute(value, ('member', 'dp'), pairs)  5.56 us
    ppermute x2, waiting for transfers between devices, swap_cores(): lax.ppermute(value, axis, [(i, i ^ 1) for i in range(lax.axis_size(axis))])  2.67 us
    pallas_call x1, Pallas kernels, on_device(): call(functools.partial(gradient_kernel, members, images, classes * peers)...  0.97 us
  transfers between devices with their start and end apart: 16, of which 14 were waited for; matrix products, arithmetic and copies ran while one was open for 0% of the time, Pallas kernels for 1%

profile of v10, /device:TPU:0, one launch (start us, length us, event | category | flops | bytes accessed | tf_op | source)
XLA Modules:
  0.0 38.8 jit_solution(10331734444319904264)
XLA Ops:
  0.6 3.1 %collective-permute-start.3 = (bf16[32,1024]{1,0:T(8,128)(2,1)}, bf16[32,1024]{1,0:T(8,128)(2,1)S(1)}, u32[]{:S(2)}, u32[]{:S(2)}) collective-permute-start(bf16[32,1024]{1,0:T(8,128)(2,1)} %refs_2_.1), channel_id=1, source_target_pairs={{0,8},{1,17},{2,10},{3,19},{4,12},{5,21},{6,14},{7,23},{8,0},{9,25... | collective-permute-start | bytes 196616 | tf_op jit(solution)/shard_map/ppermute | solution.py:64
  3.7 2.5 %collective-permute-start.4 = (bf16[32,1024]{1,0:T(8,128)(2,1)}, bf16[32,1024]{1,0:T(8,128)(2,1)S(1)}, u32[]{:S(2)}, u32[]{:S(2)}) collective-permute-start(bf16[32,1024]{1,0:T(8,128)(2,1)} %refs_2_.1), channel_id=1, source_target_pairs={{0,24},{1,9},{2,26},{3,11},{4,28},{5,13},{6,30},{7,15},{8,16},{9,1... | collective-permute-start | bytes 196616 | tf_op jit(solution)/shard_map/ppermute | solution.py:64
  6.2 2.4 %collective-permute-start.2 = (bf16[16,1024]{1,0:T(8,128)(2,1)}, bf16[16,1024]{1,0:T(8,128)(2,1)S(1)}, u32[]{:S(2)}, u32[]{:S(2)}) collective-permute-start(bf16[16,1024]{1,0:T(8,128)(2,1)} %bitcast.7), channel_id=1, source_target_pairs={{0,6},{1,7},{2,4},{3,5},{4,2},{5,3},{6,0},{7,1},{8,14},{9,15},{10,... | collective-permute-start | bytes 98312 | tf_op jit(solution)/shard_map/ppermute | solution.py:49
  8.6 0.5 %collective-permute-start.1 = (bf16[16,1024]{1,0:T(8,128)(2,1)}, bf16[16,1024]{1,0:T(8,128)(2,1)S(1)}, u32[]{:S(2)}, u32[]{:S(2)}) collective-permute-start(bf16[16,1024]{1,0:T(8,128)(2,1)} %bitcast.8), channel_id=1, source_target_pairs={{0,4},{1,5},{2,6},{3,7},{4,0},{5,1},{6,2},{7,3},{8,12},{9,13},{10,... | collective-permute-start | bytes 98312 | tf_op jit(solution)/shard_map/ppermute | solution.py:49
  9.2 0.5 %collective-permute-start = (bf16[16,1024]{1,0:T(8,128)(2,1)}, bf16[16,1024]{1,0:T(8,128)(2,1)S(1)}, u32[]{:S(2)}, u32[]{:S(2)}) collective-permute-start(bf16[16,1024]{1,0:T(8,128)(2,1)} %bitcast.9), channel_id=1, source_target_pairs={{0,2},{1,3},{2,0},{3,1},{4,6},{5,7},{6,4},{7,5},{8,10},{9,11},{10,... | collective-permute-start | bytes 98312 | tf_op jit(solution)/shard_map/ppermute | solution.py:49
  9.7 0.0 collective-permute-done.3.refs_0_
  9.7 0.3 collective-permute-done.4.refs_1_
  10.0 0.0 copy-done.3
  10.0 0.2 shard_map.104.refs_5_
  10.2 0.0 copy-start
  10.2 0.0 copy-start.1
  10.2 0.0 copy-start.2
  10.3 1.0 %collective-permute-done.2.refs_3_ = bf16[16,1024]{1,0:T(8,128)(2,1)S(1)} collective-permute-done((bf16[16,1024]{1,0:T(8,128)(2,1)}, bf16[16,1024]{1,0:T(8,128)(2,1)S(1)}, u32[]{:S(2)}, u32[]{:S(2)}) %collective-permute-start.2) | collective-permute-done | bytes 32800 | tf_op jit(solution)/shard_map/ppermute | solution.py:49
  11.3 1.5 %collective-permute-done.1.refs_2_ = bf16[16,1024]{1,0:T(8,128)(2,1)S(1)} collective-permute-done((bf16[16,1024]{1,0:T(8,128)(2,1)}, bf16[16,1024]{1,0:T(8,128)(2,1)S(1)}, u32[]{:S(2)}, u32[]{:S(2)}) %collective-permute-start.1) | collective-permute-done | bytes 32800 | tf_op jit(solution)/shard_map/ppermute | solution.py:49
  12.8 0.5 %collective-permute-done.refs_1_ = bf16[16,1024]{1,0:T(8,128)(2,1)S(1)} collective-permute-done((bf16[16,1024]{1,0:T(8,128)(2,1)}, bf16[16,1024]{1,0:T(8,128)(2,1)S(1)}, u32[]{:S(2)}, u32[]{:S(2)}) %collective-permute-start) | collective-permute-done | bytes 32800 | tf_op jit(solution)/shard_map/ppermute | solution.py:49
  13.3 0.0 copy-done.6
  13.3 0.0 copy-done.7
  13.3 0.2 shard_map.105.refs_0_
  13.5 0.0 copy-start.5
  13.5 0.1 collective-permute-start.5
  13.6 1.5 %collective-permute-done.5.refs_1_ = bf16[128,1024]{1,0:T(8,128)(2,1)S(1)} collective-permute-done((bf16[128,1024]{1,0:T(8,128)(2,1)S(1)}, bf16[128,1024]{1,0:T(8,128)(2,1)S(1)}, u32[]{:S(2)}, u32[]{:S(2)}) %collective-permute-start.5) | collective-permute-done | bytes 262176 | tf_op jit(solution)/shard_map/ppermute | solution.py:68
  15.1 0.0 copy-done
  15.1 0.0 copy-done.2
  15.2 0.6 %shard_map.106 = (bf16[72,384]{1,0:T(8,128)(2,1)S(1)}, bf16[72,384]{1,0:T(8,128)(2,1)S(1)}, bf16[72,384]{1,0:T(8,128)(2,1)S(1)}, bf16[72,384]{1,0:T(8,128)(2,1)S...) custom-call(bf16[128,1024]{1,0:T(8,128)(2,1)S(1)} %shard_map.105.refs_0_, ...), custom_call_target="tpu_custom_call" | custom-call | tf_op jit(solution)/shard_map/pallas_call | solution.py:343
  15.8 1.4 %collective-permute-start.6 = (bf16[72,384]{1,0:T(8,128)(2,1)S(1)}, bf16[72,384]{1,0:T(8,128)(2,1)S(1)}, u32[]{:S(2)}, u32[]{:S(2)}) collective-permute-start(bf16[72,384]{1,0:T(8,128)(2,1)S(1)} %get-tuple-element.18), channel_id=1, source_target_pairs={{0,24},{8,16},{16,8},{24,0},{1,25},{9,17},{17,9},{25,1},{2,26},{10... | collective-permute-start | bytes 165896 | tf_op jit(solution)/shard_map/ppermute | solution.py:49
  17.2 0.8 %collective-permute-start.7 = (bf16[72,384]{1,0:T(8,128)(2,1)S(1)}, bf16[72,384]{1,0:T(8,128)(2,1)S(1)}, u32[]{:S(2)}, u32[]{:S(2)}) collective-permute-start(bf16[72,384]{1,0:T(8,128)(2,1)S(1)} %get-tuple-element.19), channel_id=1, source_target_pairs={{0,16},{8,24},{16,0},{24,8},{1,17},{9,25},{17,1},{25,9},{2,18},{10... | collective-permute-start | bytes 165896 | tf_op jit(solution)/shard_map/ppermute | solution.py:49
  18.0 2.2 %collective-permute-start.8 = (bf16[72,384]{1,0:T(8,128)(2,1)S(1)}, bf16[72,384]{1,0:T(8,128)(2,1)S(1)}, u32[]{:S(2)}, u32[]{:S(2)}) collective-permute-start(bf16[72,384]{1,0:T(8,128)(2,1)S(1)} %get-tuple-element.20), channel_id=1, source_target_pairs={{0,8},{8,0},{16,24},{24,16},{1,9},{9,1},{17,25},{25,17},{2,10},{10... | collective-permute-start | bytes 165896 | tf_op jit(solution)/shard_map/ppermute | solution.py:49
  20.2 2.2 %collective-permute-done.6.refs_1_ = bf16[72,384]{1,0:T(8,128)(2,1)S(1)} collective-permute-done((bf16[72,384]{1,0:T(8,128)(2,1)S(1)}, bf16[72,384]{1,0:T(8,128)(2,1)S(1)}, u32[]{:S(2)}, u32[]{:S(2)}) %collective-permute-start.6) | collective-permute-done | bytes 55328 | tf_op jit(solution)/shard_map/ppermute | solution.py:49
  22.4 1.5 %collective-permute-done.7.refs_2_ = bf16[72,384]{1,0:T(8,128)(2,1)S(1)} collective-permute-done((bf16[72,384]{1,0:T(8,128)(2,1)S(1)}, bf16[72,384]{1,0:T(8,128)(2,1)S(1)}, u32[]{:S(2)}, u32[]{:S(2)}) %collective-permute-start.7) | collective-permute-done | bytes 55328 | tf_op jit(solution)/shard_map/ppermute | solution.py:49
  23.9 0.0 collective-permute-done.8.refs_3_
  23.9 0.2 shard_map.107
  24.2 0.0 collective-permute-start.9
  24.2 1.1 %collective-permute-done.9.other_ref = f32[8,128]{1,0:T(8,128)S(1)} collective-permute-done((f32[8,128]{1,0:T(8,128)S(1)}, f32[8,128]{1,0:T(8,128)S(1)}, u32[]{:S(2)}, u32[]{:S(2)}) %collective-permute-start.9) | collective-permute-done | bytes 4128 | tf_op jit(solution)/shard_map/ppermute | solution.py:68
  25.3 1.6 %collective-permute-start.12 = (f32[8,128]{1,0:T(8,128)S(1)}, f32[8,128]{1,0:T(8,128)S(1)}, u32[]{:S(2)}, u32[]{:S(2)}) collective-permute-start(f32[8,128]{1,0:T(8,128)S(1)} %shard_map.108.refs_0_), channel_id=1, source_target_pairs={{0,6},{1,7},{2,4},{3,5},{4,2},{5,3},{6,0},{7,1},{8,14},{9,15},{10,... | collective-permute-start | bytes 12296 | tf_op jit(solution)/shard_map/ppermute | solution.py:49
  26.9 0.5 %collective-permute-start.11 = (f32[8,128]{1,0:T(8,128)S(1)}, f32[8,128]{1,0:T(8,128)S(1)}, u32[]{:S(2)}, u32[]{:S(2)}) collective-permute-start(f32[8,128]{1,0:T(8,128)S(1)} %shard_map.108.refs_0_), channel_id=1, source_target_pairs={{0,4},{1,5},{2,6},{3,7},{4,0},{5,1},{6,2},{7,3},{8,12},{9,13},{10,... | collective-permute-start | bytes 12296 | tf_op jit(solution)/shard_map/ppermute | solution.py:49
  27.4 1.5 %collective-permute-start.10 = (f32[8,128]{1,0:T(8,128)S(1)}, f32[8,128]{1,0:T(8,128)S(1)}, u32[]{:S(2)}, u32[]{:S(2)}) collective-permute-start(f32[8,128]{1,0:T(8,128)S(1)} %shard_map.108.refs_0_), channel_id=1, source_target_pairs={{0,2},{1,3},{2,0},{3,1},{4,6},{5,7},{6,4},{7,5},{8,10},{9,11},{10,... | collective-permute-start | bytes 12296 | tf_op jit(solution)/shard_map/ppermute | solution.py:49
  28.9 0.1 shard_map.109
  29.0 0.9 %collective-permute-done.12.refs_3_ = f32[8,128]{1,0:T(8,128)S(1)} collective-permute-done((f32[8,128]{1,0:T(8,128)S(1)}, f32[8,128]{1,0:T(8,128)S(1)}, u32[]{:S(2)}, u32[]{:S(2)}) %collective-permute-start.12) | collective-permute-done | bytes 4128 | tf_op jit(solution)/shard_map/ppermute | solution.py:49
  29.9 0.6 %collective-permute-done.11.refs_2_ = f32[8,128]{1,0:T(8,128)S(1)} collective-permute-done((f32[8,128]{1,0:T(8,128)S(1)}, f32[8,128]{1,0:T(8,128)S(1)}, u32[]{:S(2)}, u32[]{:S(2)}) %collective-permute-start.11) | collective-permute-done | bytes 4128 | tf_op jit(solution)/shard_map/ppermute | solution.py:49
  30.5 0.5 %collective-permute-done.10.refs_1_ = f32[8,128]{1,0:T(8,128)S(1)} collective-permute-done((f32[8,128]{1,0:T(8,128)S(1)}, f32[8,128]{1,0:T(8,128)S(1)}, u32[]{:S(2)}, u32[]{:S(2)}) %collective-permute-start.10) | collective-permute-done | bytes 4128 | tf_op jit(solution)/shard_map/ppermute | solution.py:49
  31.0 0.1 shard_map.110.refs_0_
  31.2 1.4 %collective-permute-start.15 = (bf16[32,512]{1,0:T(8,128)(2,1)S(1)}, bf16[32,512]{1,0:T(8,128)(2,1)S(1)}, u32[]{:S(2)}, u32[]{:S(2)}) collective-permute-start(bf16[32,512]{1,0:T(8,128)(2,1)S(1)} %shard_map.110.refs_0_), channel_id=1, source_target_pairs={{0,24},{8,16},{16,8},{24,0},{1,25},{9,17},{17,9},{25,1},{2,26},{10... | collective-permute-start | bytes 98312 | tf_op jit(solution)/shard_map/ppermute | solution.py:49
  32.6 0.6 %collective-permute-start.14 = (bf16[32,512]{1,0:T(8,128)(2,1)S(1)}, bf16[32,512]{1,0:T(8,128)(2,1)S(1)}, u32[]{:S(2)}, u32[]{:S(2)}) collective-permute-start(bf16[32,512]{1,0:T(8,128)(2,1)S(1)} %shard_map.110.refs_0_), channel_id=1, source_target_pairs={{0,16},{8,24},{16,0},{24,8},{1,17},{9,25},{17,1},{25,9},{2,18},{10... | collective-permute-start | bytes 98312 | tf_op jit(solution)/shard_map/ppermute | solution.py:49
  33.2 2.5 %collective-permute-start.13 = (bf16[32,512]{1,0:T(8,128)(2,1)S(1)}, bf16[32,512]{1,0:T(8,128)(2,1)S(1)}, u32[]{:S(2)}, u32[]{:S(2)}) collective-permute-start(bf16[32,512]{1,0:T(8,128)(2,1)S(1)} %shard_map.110.refs_0_), channel_id=1, source_target_pairs={{0,8},{8,0},{16,24},{24,16},{1,9},{9,1},{17,25},{25,17},{2,10},{10... | collective-permute-start | bytes 98312 | tf_op jit(solution)/shard_map/ppermute | solution.py:49
  35.6 1.3 %collective-permute-done.15.refs_3_ = bf16[32,512]{1,0:T(8,128)(2,1)S(1)} collective-permute-done((bf16[32,512]{1,0:T(8,128)(2,1)S(1)}, bf16[32,512]{1,0:T(8,128)(2,1)S(1)}, u32[]{:S(2)}, u32[]{:S(2)}) %collective-permute-start.15) | collective-permute-done | bytes 32800 | tf_op jit(solution)/shard_map/ppermute | solution.py:49
  36.9 0.8 %collective-permute-done.14.refs_2_ = bf16[32,512]{1,0:T(8,128)(2,1)S(1)} collective-permute-done((bf16[32,512]{1,0:T(8,128)(2,1)S(1)}, bf16[32,512]{1,0:T(8,128)(2,1)S(1)}, u32[]{:S(2)}, u32[]{:S(2)}) %collective-permute-start.14) | collective-permute-done | bytes 32800 | tf_op jit(solution)/shard_map/ppermute | solution.py:49
  37.8 0.1 collective-permute-done.13.refs_1_
  37.9 1.0 %shard_map.111 = (f32[1,1]{1,0:T(1,128)}, f32[256,384]{1,0:T(8,128)}, f32[384]{0:T(512)}) custom-call(bf16[32,512]{1,0:T(8,128)(2,1)S(1)} %shard_map.110.refs_0_, bf16[32,512]{1,0:T(8,128)(2,1)S(1)} %collective-permute-done.13.refs_1_, bf16[32,512]{1,0:T(8,128)(2,1)S(1)} %collective-permute-done.14.refs_2_, ...), custom_call_target="tpu_custom_call" | custom-call | tf_op jit(solution)/shard_map/pallas_call | solution.py:381
  (9 shorter events, 0.0 us)
Async XLA Ops:
  0.6 9.1 %collective-permute-start.3 = (bf16[32,1024]{1,0:T(8,128)(2,1)}, bf16[32,1024]{1,0:T(8,128)(2,1)S(1)}, u32[]{:S(2)}, u32[]{:S(2)}) collective-permute-start(bf16[32,1024]{1,0:T(8,128)(2,1)} %refs_2_.1), channel_id=1, source_target_pairs={{0,8},{1,17},{2,10},{3,19},{4,12},{5,21},{6,14},{7,23},{8,0},{9,25... | collective-permute-start | bytes 196616 | tf_op jit(solution)/shard_map/ppermute | solution.py:64
  3.7 6.3 %collective-permute-start.4 = (bf16[32,1024]{1,0:T(8,128)(2,1)}, bf16[32,1024]{1,0:T(8,128)(2,1)S(1)}, u32[]{:S(2)}, u32[]{:S(2)}) collective-permute-start(bf16[32,1024]{1,0:T(8,128)(2,1)} %refs_2_.1), channel_id=1, source_target_pairs={{0,24},{1,9},{2,26},{3,11},{4,28},{5,13},{6,30},{7,15},{8,16},{9,1... | collective-permute-start | bytes 196616 | tf_op jit(solution)/shard_map/ppermute | solution.py:64
  6.2 3.8 %copy-start.3 = (f32[1024]{0:T(1024)S(1)}, f32[1024]{0:T(1024)}, u32[]{:S(2)}) copy-start(f32[1024]{0:T(1024)} %param.13) | copy-start | bytes 12292
  6.2 5.1 %collective-permute-start.2 = (bf16[16,1024]{1,0:T(8,128)(2,1)}, bf16[16,1024]{1,0:T(8,128)(2,1)S(1)}, u32[]{:S(2)}, u32[]{:S(2)}) collective-permute-start(bf16[16,1024]{1,0:T(8,128)(2,1)} %bitcast.7), channel_id=1, source_target_pairs={{0,6},{1,7},{2,4},{3,5},{4,2},{5,3},{6,0},{7,1},{8,14},{9,15},{10,... | collective-permute-start | bytes 98312 | tf_op jit(solution)/shard_map/ppermute | solution.py:49
  8.6 4.1 %collective-permute-start.1 = (bf16[16,1024]{1,0:T(8,128)(2,1)}, bf16[16,1024]{1,0:T(8,128)(2,1)S(1)}, u32[]{:S(2)}, u32[]{:S(2)}) collective-permute-start(bf16[16,1024]{1,0:T(8,128)(2,1)} %bitcast.8), channel_id=1, source_target_pairs={{0,4},{1,5},{2,6},{3,7},{4,0},{5,1},{6,2},{7,3},{8,12},{9,13},{10,... | collective-permute-start | bytes 98312 | tf_op jit(solution)/shard_map/ppermute | solution.py:49
  9.2 4.1 %collective-permute-start = (bf16[16,1024]{1,0:T(8,128)(2,1)}, bf16[16,1024]{1,0:T(8,128)(2,1)S(1)}, u32[]{:S(2)}, u32[]{:S(2)}) collective-permute-start(bf16[16,1024]{1,0:T(8,128)(2,1)} %bitcast.9), channel_id=1, source_target_pairs={{0,2},{1,3},{2,0},{3,1},{4,6},{5,7},{6,4},{7,5},{8,10},{9,11},{10,... | collective-permute-start | bytes 98312 | tf_op jit(solution)/shard_map/ppermute | solution.py:49
  10.0 3.3 %copy-start.6 = (bf16[1,16,1024]{2,1,0:T(8,128)(2,1)S(1)}, bf16[1,16,1024]{2,1,0:T(8,128)(2,1)}, u32[]{:S(2)}) copy-start(bf16[1,16,1024]{2,1,0:T(8,128)(2,1)} %param.8) | copy-start | bytes 98308
  10.0 3.3 %copy-start.7 = (f32[1,1024]{1,0:T(1,128)S(1)}, f32[1,1024]{1,0:T(1,128)}, u32[]{:S(2)}) copy-start(f32[1,1024]{1,0:T(1,128)} %refs_4_.1) | copy-start | bytes 12292
  10.2 4.9 %copy-start = (bf16[1,1024,384]{2,1,0:T(8,128)(2,1)S(1)}, bf16[1,1024,384]{2,1,0:T(8,128)(2,1)}, u32[]{:S(2)}) copy-start(bf16[1,1024,384]{2,1,0:T(8,128)(2,1)} %param.10) | copy-start | bytes 2359300
  10.2 4.9 %copy-start.1 = (bf16[256,384]{1,0:T(8,128)(2,1)S(1)}, bf16[256,384]{1,0:T(8,128)(2,1)}, u32[]{:S(2)}) copy-start(bf16[256,384]{1,0:T(8,128)(2,1)} %refs_5_.1) | copy-start | bytes 589828
  10.2 4.9 %copy-start.2 = (bf16[32,1024]{1,0:T(8,128)(2,1)S(1)}, bf16[32,1024]{1,0:T(8,128)(2,1)}, u32[]{:S(2)}) copy-start(bf16[32,1024]{1,0:T(8,128)(2,1)} %refs_2_.1) | copy-start | bytes 196612
  13.3 1.9 %copy-start.4 = (f32[384]{0:T(512)S(1)}, f32[384]{0:T(512)}, u32[]{:S(2)}) copy-start(f32[384]{0:T(512)} %refs_7_.1) | copy-start | bytes 4612
  13.5 1.6 %copy-start.5 = (f32[1,384]{1,0:T(1,128)S(1)}, f32[1,384]{1,0:T(1,128)}, u32[]{:S(2)}) copy-start(f32[1,384]{1,0:T(1,128)} %refs_6_.1) | copy-start | bytes 4612
  13.5 1.6 %collective-permute-start.5 = (bf16[128,1024]{1,0:T(8,128)(2,1)S(1)}, bf16[128,1024]{1,0:T(8,128)(2,1)S(1)}, u32[]{:S(2)}, u32[]{:S(2)}) collective-permute-start(bf16[128,1024]{1,0:T(8,128)(2,1)S(1)} %shard_map.105.refs_0_), channel_id=1, source_target_pairs={{0,1},{1,0},{2,3},{3,2},{4,5},{5,4},{6,7},{7,6},{8,9},{9,8},{10,11... | collective-permute-start | bytes 786440 | tf_op jit(solution)/shard_map/ppermute | solution.py:68
  15.8 6.6 %collective-permute-start.6 = (bf16[72,384]{1,0:T(8,128)(2,1)S(1)}, bf16[72,384]{1,0:T(8,128)(2,1)S(1)}, u32[]{:S(2)}, u32[]{:S(2)}) collective-permute-start(bf16[72,384]{1,0:T(8,128)(2,1)S(1)} %get-tuple-element.18), channel_id=1, source_target_pairs={{0,24},{8,16},{16,8},{24,0},{1,25},{9,17},{17,9},{25,1},{2,26},{10... | collective-permute-start | bytes 165896 | tf_op jit(solution)/shard_map/ppermute | solution.py:49
  17.2 6.7 %collective-permute-start.7 = (bf16[72,384]{1,0:T(8,128)(2,1)S(1)}, bf16[72,384]{1,0:T(8,128)(2,1)S(1)}, u32[]{:S(2)}, u32[]{:S(2)}) collective-permute-start(bf16[72,384]{1,0:T(8,128)(2,1)S(1)} %get-tuple-element.19), channel_id=1, source_target_pairs={{0,16},{8,24},{16,0},{24,8},{1,17},{9,25},{17,1},{25,9},{2,18},{10... | collective-permute-start | bytes 165896 | tf_op jit(solution)/shard_map/ppermute | solution.py:49
  18.0 5.9 %collective-permute-start.8 = (bf16[72,384]{1,0:T(8,128)(2,1)S(1)}, bf16[72,384]{1,0:T(8,128)(2,1)S(1)}, u32[]{:S(2)}, u32[]{:S(2)}) collective-permute-start(bf16[72,384]{1,0:T(8,128)(2,1)S(1)} %get-tuple-element.20), channel_id=1, source_target_pairs={{0,8},{8,0},{16,24},{24,16},{1,9},{9,1},{17,25},{25,17},{2,10},{10... | collective-permute-start | bytes 165896 | tf_op jit(solution)/shard_map/ppermute | solution.py:49
  24.2 1.2 %collective-permute-start.9 = (f32[8,128]{1,0:T(8,128)S(1)}, f32[8,128]{1,0:T(8,128)S(1)}, u32[]{:S(2)}, u32[]{:S(2)}) collective-permute-start(f32[8,128]{1,0:T(8,128)S(1)} %get-tuple-element.22.own_ref.refs_4_), channel_id=1, source_target_pairs={{0,1},{1,0},{2,3},{3,2},{4,5},{5,4},{6,7},{7,6},{8,9},{9,8},{10,11... | collective-permute-start | bytes 12296 | tf_op jit(solution)/shard_map/ppermute | solution.py:68
  25.3 4.6 %collective-permute-start.12 = (f32[8,128]{1,0:T(8,128)S(1)}, f32[8,128]{1,0:T(8,128)S(1)}, u32[]{:S(2)}, u32[]{:S(2)}) collective-permute-start(f32[8,128]{1,0:T(8,128)S(1)} %shard_map.108.refs_0_), channel_id=1, source_target_pairs={{0,6},{1,7},{2,4},{3,5},{4,2},{5,3},{6,0},{7,1},{8,14},{9,15},{10,... | collective-permute-start | bytes 12296 | tf_op jit(solution)/shard_map/ppermute | solution.py:49
  26.9 3.6 %collective-permute-start.11 = (f32[8,128]{1,0:T(8,128)S(1)}, f32[8,128]{1,0:T(8,128)S(1)}, u32[]{:S(2)}, u32[]{:S(2)}) collective-permute-start(f32[8,128]{1,0:T(8,128)S(1)} %shard_map.108.refs_0_), channel_id=1, source_target_pairs={{0,4},{1,5},{2,6},{3,7},{4,0},{5,1},{6,2},{7,3},{8,12},{9,13},{10,... | collective-permute-start | bytes 12296 | tf_op jit(solution)/shard_map/ppermute | solution.py:49
  27.4 3.6 %collective-permute-start.10 = (f32[8,128]{1,0:T(8,128)S(1)}, f32[8,128]{1,0:T(8,128)S(1)}, u32[]{:S(2)}, u32[]{:S(2)}) collective-permute-start(f32[8,128]{1,0:T(8,128)S(1)} %shard_map.108.refs_0_), channel_id=1, source_target_pairs={{0,2},{1,3},{2,0},{3,1},{4,6},{5,7},{6,4},{7,5},{8,10},{9,11},{10,... | collective-permute-start | bytes 12296 | tf_op jit(solution)/shard_map/ppermute | solution.py:49
  31.2 5.8 %collective-permute-start.15 = (bf16[32,512]{1,0:T(8,128)(2,1)S(1)}, bf16[32,512]{1,0:T(8,128)(2,1)S(1)}, u32[]{:S(2)}, u32[]{:S(2)}) collective-permute-start(bf16[32,512]{1,0:T(8,128)(2,1)S(1)} %shard_map.110.refs_0_), channel_id=1, source_target_pairs={{0,24},{8,16},{16,8},{24,0},{1,25},{9,17},{17,9},{25,1},{2,26},{10... | collective-permute-start | bytes 98312 | tf_op jit(solution)/shard_map/ppermute | solution.py:49
  32.6 5.2 %collective-permute-start.14 = (bf16[32,512]{1,0:T(8,128)(2,1)S(1)}, bf16[32,512]{1,0:T(8,128)(2,1)S(1)}, u32[]{:S(2)}, u32[]{:S(2)}) collective-permute-start(bf16[32,512]{1,0:T(8,128)(2,1)S(1)} %shard_map.110.refs_0_), channel_id=1, source_target_pairs={{0,16},{8,24},{16,0},{24,8},{1,17},{9,25},{17,1},{25,9},{2,18},{10... | collective-permute-start | bytes 98312 | tf_op jit(solution)/shard_map/ppermute | solution.py:49
  33.2 4.7 %collective-permute-start.13 = (bf16[32,512]{1,0:T(8,128)(2,1)S(1)}, bf16[32,512]{1,0:T(8,128)(2,1)S(1)}, u32[]{:S(2)}, u32[]{:S(2)}) collective-permute-start(bf16[32,512]{1,0:T(8,128)(2,1)S(1)} %shard_map.110.refs_0_), channel_id=1, source_target_pairs={{0,8},{8,0},{16,24},{24,16},{1,9},{9,1},{17,25},{25,17},{2,10},{10... | collective-permute-start | bytes 98312 | tf_op jit(solution)/shard_map/ppermute | solution.py:49

commit v11 on v10

--- a/solution.py
+++ b/solution.py
@@ -50,14 +50,14 @@
 
 
 def split_step(j, core, members):
-    return jnp.where(core == 0, 2 * j + 1, 2 * j + 2 if 2 * j + 2 < members else 1)
+    return jnp.where(core == 1, 2 * j + 1, 2 * j + 2 if 2 * j + 2 < members else 1)
 
 
 def send_split(value, j):
     members, peers = lax.axis_size("member"), lax.axis_size("dp")
     steps = 2 * j + 1, (2 * j + 2 if 2 * j + 2 < members else 1)
     pairs = [
-        (m * peers + d, partner(m, steps[d % 2], members) * peers + d)
+        (m * peers + d, partner(m, steps[1 - d % 2], members) * peers + d)
         for m in range(members)
         for d in range(peers)
     ]
@@ -134,11 +134,27 @@
     out_ref[...] = jnp.zeros_like(out_ref)
 
 
-def student_kernel(*refs):
-    *parts, gain_ref, _, out_ref = refs
-    rows = parts[0].shape[0]
-    for j, part in enumerate(parts):
-        out_ref[j * rows : (j + 1) * rows, :] = normed(part[...], gain_ref[...])
+def student_kernel(members, own_ref, *refs):
+    *parts, gain_ref, _, own_out, split_out, held, picked = refs
+    mine = lax.axis_index("member")
+    half, width = own_ref.shape[0] // 2, own_out.shape[1]
+    for j, part in enumerate([own_ref] + parts):
+        held[...] = normed(part[...], gain_ref[...])
+        if width % LANES == 0:
+            picked[...] = held[:, pl.ds(pl.multiple_of(mine * width, LANES), width)]
+        else:
+            for m in range(members):
+
+                @pl.when(mine == m)
+                def _(m=m):
+                    picked[...] = held[:, m * width : (m + 1) * width]
+
+        if j == 0:
+            own_out[...] = picked[...]
+            continue
+        for h in range(2):
+            at = (2 * (j - 1) + h) * width
+            split_out[:, at : at + width] = picked[h * half : (h + 1) * half, :]
 
 
 def join_kernel(chips, *refs):
@@ -160,33 +176,25 @@
 
 def logits_kernel(members, rows, *refs):
     own_ref, other_ref, refs = refs[0], refs[1], refs[2:]
-    feats_ref, student_gain_ref, head_ref, student_ref, bias_ref, student_bias_ref = refs[:6]
-    refs = refs[6:]
+    students_ref, head_ref, student_ref, bias_ref, student_bias_ref = refs[:5]
+    refs = refs[5:]
     payloads, refs = refs[:members], refs[members:]
-    own_logits_ref, columns_ref, gathered, held, shifted_ref, lse_ref, partial_ref = refs
+    own_logits_ref, columns_ref, gathered, shifted_ref, lse_ref, partial_ref = refs
     mine, place = lax.axis_index("member"), lax.axis_index("dp")
     core = lax.rem(place, jnp.int32(2))
     chips = gathered.shape[0] // (2 * rows)
-    block = feats_ref.shape[0]
-    width = columns_ref.shape[1]
-    held[slot(mine, block), :] = normed(feats_ref[...], student_gain_ref[...])
+    block, width = students_ref.shape
+    half = block // 2
+    columns_ref[slot(mine, block), :] = students_ref[...]
     for source, side in ((own_ref, core), (other_ref, 1 - core)):
         for chip in range(chips):
             at = slot(2 * chip + side, rows)
             gathered[at, :] = source[chip * rows : (chip + 1) * rows, :]
         for j in range(members // 2):
-            start = chips * rows + j * block
-            at = slot(mixed(mine, split_step(j, side, members), members, sender), block)
-            held[at, :] = source[start : start + block, :]
-    if width % LANES == 0:
-        columns_ref[...] = held[:, pl.ds(pl.multiple_of(mine * width, LANES), width)]
-    else:
-        for j in range(members):
-
-            @pl.when(mine == j)
-            def _(j=j):
-                columns_ref[...] = held[:, j * width : (j + 1) * width]
-
+            at = mixed(mine, split_step(j, side, members), members, sender)
+            for h in range(2):
+                piece = (2 * j + h) * width
+                columns_ref[slot(2 * at + h, half), :] = source[chips * rows :, piece : piece + width]
     logits = jnp.dot(gathered[...], head_ref[...], preferred_element_type=F32) + bias_ref[...]
     top = jnp.max(logits, axis=1, keepdims=True)
     lse = top + jnp.log(jnp.sum(jnp.exp(logits - top), axis=1, keepdims=True))
@@ -266,14 +274,14 @@
     alpha_sum = jnp.where(used, everything[members : members + 1, :], 1.0)
     shift = to_column(di_gamma(alpha_sum) + own - norm_total, block)
     width = alphas_ref.shape[1]
-    signal_ref[:, 0:width] = (alphas_ref[...] * (inner_ref[...] - shift)).astype(BF16)
+    signal_ref[0:block, :] = (alphas_ref[...] * (inner_ref[...] - shift)).astype(BF16)
     terms = (
         everything[members + 1 : members + 2, :]
         - log_gamma(alpha_sum, jnp.log(alpha_sum))
         + norm_total * (alpha_sum - float(classes))
     )
     loss = jnp.sum(jnp.where(used, terms, 0.0), axis=1, keepdims=True)
-    signal_ref[:, width:] = packed3(loss, block, LANES)
+    signal_ref[block:, :] = packed3(loss, PAD, width)
 
 
 def gradient_kernel(members, images, classes, *refs):
@@ -281,11 +289,10 @@
     turned_ref, loss_ref, grad_ref, bias_ref, held, losses = refs
     mine = lax.axis_index("member")
     block = images // members
-    width = held.shape[1]
     for k in range(members):
         at = mixed(mine, k, members, sender)
-        held[slot(at, block), :] = signals[k][:, 0:width]
-        tail = signals[k][:, width:].astype(F32)
+        held[slot(at, block), :] = signals[k][0:block, :]
+        tail = signals[k][block:, 0:LANES].astype(F32)
         losses[pl.ds(at, 1), :] = tail[0:1, :] + tail[1:2, :] + tail[2:3, :]
     signal = held[...]
     grad = jnp.dot(turned_ref[...], signal, preferred_element_type=F32)
@@ -331,13 +338,21 @@
     small_rows = -(-(members + 2) // 8) * 8
 
     first = call(first_kernel, shape((8, LANES), F32), flops=1 << 28)()
-    students = call(
-        student_kernel, shape((members // 2 * block, depth), BF16), flops=1 << 33
-    )(*[send_split(student_feats, j) for j in range(members // 2)], student_gain[None], first)
+    own_students, students = call(
+        functools.partial(student_kernel, members),
+        [shape((block, width), BF16), shape((block // 2, depth), BF16)],
+        [pltpu.VMEM((block, depth), BF16), pltpu.VMEM((block, width), BF16)],
+        flops=1 << 33,
+    )(
+        student_feats,
+        *[send_split(student_feats, j) for j in range(members // 2)],
+        student_gain[None],
+        first,
+    )
     parts = [feats] + [send(feats, "dp", k, 2) for k in range(1, chips)]
     own = call(
         functools.partial(join_kernel, chips),
-        shape((chips * rows + members // 2 * block, depth), BF16),
+        shape((chips * rows + block // 2, depth), BF16),
         flops=1 << 33,
     )(*parts, teacher_gain, students)
     *payloads, own_logits, own_columns = call(
@@ -346,7 +361,6 @@
         + [shape((block, classes), F32), shape((images, width), BF16)],
         [
             pltpu.VMEM((images, depth), BF16),
-            pltpu.VMEM((images, depth), BF16),
             pltpu.VMEM((images, classes), BF16),
             pltpu.VMEM((images, LANES), F32),
             pltpu.VMEM((images, classes), F32),
@@ -354,8 +368,7 @@
     )(
         own,
         swap_cores(own, "dp"),
-        student_feats,
-        student_gain[None],
+        own_students,
         teacher_head[0],
         student_head,
         teacher_bias,
@@ -374,7 +387,7 @@
     smalls = [small] + [send(small, "dp", k, 2) for k in range(1, chips)]
     signal = call(
         functools.partial(signal_kernel, members, chips, images, classes * peers),
-        shape((block, classes + LANES), BF16),
+        shape((block + PAD, classes), BF16),
         [pltpu.VMEM((chips, small_rows, LANES), F32)],
     )(*smalls, own, alphas, inner)
     signals = [signal] + [send(signal, "member", k) for k in range(1, members)]

time: 39 us -> 38.5 us (0.987)
  waiting for transfers between devices: 13.9 us -> 13.3 us
  transfers between devices with their start and end apart: 16 -> 16, of which waited for: 14 -> 13; matrix products, arithmetic and copies ran while one was open for 0% -> 0% of each run, Pallas kernels for 1% -> 1%
where the time goes in v11:
time: 38.5 us; the launch traced here: 38.3 us
  starting transfers between devices  21.7 us (56%)
  waiting for transfers between devices  13.3 us (35%)
  Pallas kernels  2.59 us (7%)
  between operations  0.75 us (2%)
    ppermute x12, starting transfers between devices, send(): return lax.ppermute(value, axis, pairs)  15.9 us
    ppermute x12, waiting for transfers between devices, send(): return lax.ppermute(value, axis, pairs)  10.7 us
    ppermute x2, starting transfers between devices, send_split(): return lax.ppermute(value, ('member', 'dp'), pairs)  5.68 us
    ppermute x2, waiting for transfers between devices, swap_cores(): lax.ppermute(value, axis, [(i, i ^ 1) for i in range(lax.axis_size(axis))])  2.53 us
    pallas_call x1, Pallas kernels, on_device(): call(functools.partial(gradient_kernel, members, images, classes * peers)...  0.97 us
  transfers between devices with their start and end apart: 16, of which 13 were waited for; matrix products, arithmetic and copies ran while one was open for 0% of the time, Pallas kernels for 1%

profile of v11, /device:TPU:0, one launch (start us, length us, event | category | flops | bytes accessed | tf_op | source)
XLA Modules:
  0.0 38.3 jit_solution(3280281920416520366)
XLA Ops:
  0.6 4.1 %collective-permute-start.3 = (bf16[32,1024]{1,0:T(8,128)(2,1)}, bf16[32,1024]{1,0:T(8,128)(2,1)S(1)}, u32[]{:S(2)}, u32[]{:S(2)}) collective-permute-start(bf16[32,1024]{1,0:T(8,128)(2,1)} %own_ref.1), channel_id=1, source_target_pairs={{0,16},{1,9},{2,18},{3,11},{4,20},{5,13},{6,22},{7,15},{8,24},{9,1... | collective-permute-start | bytes 196616 | tf_op jit(solution)/shard_map/ppermute | solution.py:64
  4.7 1.6 %collective-permute-start.4 = (bf16[32,1024]{1,0:T(8,128)(2,1)}, bf16[32,1024]{1,0:T(8,128)(2,1)S(1)}, u32[]{:S(2)}, u32[]{:S(2)}) collective-permute-start(bf16[32,1024]{1,0:T(8,128)(2,1)} %own_ref.1), channel_id=1, source_target_pairs={{0,8},{1,25},{2,10},{3,27},{4,12},{5,29},{6,14},{7,31},{8,0},{9,17... | collective-permute-start | bytes 196616 | tf_op jit(solution)/shard_map/ppermute | solution.py:64
  6.3 2.4 %collective-permute-start.2 = (bf16[16,1024]{1,0:T(8,128)(2,1)}, bf16[16,1024]{1,0:T(8,128)(2,1)S(1)}, u32[]{:S(2)}, u32[]{:S(2)}) collective-permute-start(bf16[16,1024]{1,0:T(8,128)(2,1)} %bitcast.5), channel_id=1, source_target_pairs={{0,6},{1,7},{2,4},{3,5},{4,2},{5,3},{6,0},{7,1},{8,14},{9,15},{10,... | collective-permute-start | bytes 98312 | tf_op jit(solution)/shard_map/ppermute | solution.py:49
  8.8 0.5 %collective-permute-start.1 = (bf16[16,1024]{1,0:T(8,128)(2,1)}, bf16[16,1024]{1,0:T(8,128)(2,1)S(1)}, u32[]{:S(2)}, u32[]{:S(2)}) collective-permute-start(bf16[16,1024]{1,0:T(8,128)(2,1)} %bitcast.6), channel_id=1, source_target_pairs={{0,4},{1,5},{2,6},{3,7},{4,0},{5,1},{6,2},{7,3},{8,12},{9,13},{10,... | collective-permute-start | bytes 98312 | tf_op jit(solution)/shard_map/ppermute | solution.py:49
  9.3 0.5 %collective-permute-start = (bf16[16,1024]{1,0:T(8,128)(2,1)}, bf16[16,1024]{1,0:T(8,128)(2,1)S(1)}, u32[]{:S(2)}, u32[]{:S(2)}) collective-permute-start(bf16[16,1024]{1,0:T(8,128)(2,1)} %bitcast.7), channel_id=1, source_target_pairs={{0,2},{1,3},{2,0},{3,1},{4,6},{5,7},{6,4},{7,5},{8,10},{9,11},{10,... | collective-permute-start | bytes 98312 | tf_op jit(solution)/shard_map/ppermute | solution.py:49
  9.8 0.0 collective-permute-done.3.refs_0_
  9.8 0.0 collective-permute-done.4.refs_1_
  9.8 0.0 copy-done.4
  9.8 0.0 copy-done.6
  9.8 0.0 copy-start.5
  9.8 0.0 copy-start.7
  9.9 0.2 shard_map.104
  10.1 1.2 %collective-permute-done.2.refs_3_ = bf16[16,1024]{1,0:T(8,128)(2,1)S(1)} collective-permute-done((bf16[16,1024]{1,0:T(8,128)(2,1)}, bf16[16,1024]{1,0:T(8,128)(2,1)S(1)}, u32[]{:S(2)}, u32[]{:S(2)}) %collective-permute-start.2) | collective-permute-done | bytes 32800 | tf_op jit(solution)/shard_map/ppermute | solution.py:49
  11.3 1.5 %collective-permute-done.1.refs_2_ = bf16[16,1024]{1,0:T(8,128)(2,1)S(1)} collective-permute-done((bf16[16,1024]{1,0:T(8,128)(2,1)}, bf16[16,1024]{1,0:T(8,128)(2,1)S(1)}, u32[]{:S(2)}, u32[]{:S(2)}) %collective-permute-start.1) | collective-permute-done | bytes 32800 | tf_op jit(solution)/shard_map/ppermute | solution.py:49
  12.9 0.5 %collective-permute-done.refs_1_ = bf16[16,1024]{1,0:T(8,128)(2,1)S(1)} collective-permute-done((bf16[16,1024]{1,0:T(8,128)(2,1)}, bf16[16,1024]{1,0:T(8,128)(2,1)S(1)}, u32[]{:S(2)}, u32[]{:S(2)}) %collective-permute-start) | collective-permute-done | bytes 32800 | tf_op jit(solution)/shard_map/ppermute | solution.py:49
  13.4 0.0 copy-done.5
  13.4 0.2 shard_map.105.refs_0_
  13.6 0.0 copy-start.2
  13.6 0.0 copy-start.3
  13.7 0.1 collective-permute-start.5
  13.7 1.4 %collective-permute-done.5.refs_1_ = bf16[80,1024]{1,0:T(8,128)(2,1)S(1)} collective-permute-done((bf16[80,1024]{1,0:T(8,128)(2,1)S(1)}, bf16[80,1024]{1,0:T(8,128)(2,1)S(1)}, u32[]{:S(2)}, u32[]{:S(2)}) %collective-permute-start.5) | collective-permute-done | bytes 163872 | tf_op jit(solution)/shard_map/ppermute | solution.py:68
  15.1 0.0 copy-done.2
  15.1 0.0 copy-done.3
  15.1 0.6 %shard_map.106 = (bf16[72,384]{1,0:T(8,128)(2,1)S(1)}, bf16[72,384]{1,0:T(8,128)(2,1)S(1)}, bf16[72,384]{1,0:T(8,128)(2,1)S(1)}, bf16[72,384]{1,0:T(8,128)(2,1)S...) custom-call(bf16[80,1024]{1,0:T(8,128)(2,1)S(1)} %shard_map.105.refs_0_, ...), custom_call_target="tpu_custom_call" | custom-call | tf_op jit(solution)/shard_map/pallas_call | solution.py:358
  15.8 0.3 collective-permute-start.6
  16.1 1.7 %collective-permute-start.7 = (bf16[72,384]{1,0:T(8,128)(2,1)S(1)}, bf16[72,384]{1,0:T(8,128)(2,1)S(1)}, u32[]{:S(2)}, u32[]{:S(2)}) collective-permute-start(bf16[72,384]{1,0:T(8,128)(2,1)S(1)} %get-tuple-element.23), channel_id=1, source_target_pairs={{0,16},{8,24},{16,0},{24,8},{1,17},{9,25},{17,1},{25,9},{2,18},{10... | collective-permute-start | bytes 165896 | tf_op jit(solution)/shard_map/ppermute | solution.py:49
  17.7 2.5 %collective-permute-start.8 = (bf16[72,384]{1,0:T(8,128)(2,1)S(1)}, bf16[72,384]{1,0:T(8,128)(2,1)S(1)}, u32[]{:S(2)}, u32[]{:S(2)}) collective-permute-start(bf16[72,384]{1,0:T(8,128)(2,1)S(1)} %get-tuple-element.24), channel_id=1, source_target_pairs={{0,8},{8,0},{16,24},{24,16},{1,9},{9,1},{17,25},{25,17},{2,10},{10... | collective-permute-start | bytes 165896 | tf_op jit(solution)/shard_map/ppermute | solution.py:49
  20.2 2.2 %collective-permute-done.6.refs_1_ = bf16[72,384]{1,0:T(8,128)(2,1)S(1)} collective-permute-done((bf16[72,384]{1,0:T(8,128)(2,1)S(1)}, bf16[72,384]{1,0:T(8,128)(2,1)S(1)}, u32[]{:S(2)}, u32[]{:S(2)}) %collective-permute-start.6) | collective-permute-done | bytes 55328 | tf_op jit(solution)/shard_map/ppermute | solution.py:49
  22.4 1.0 %collective-permute-done.7.refs_2_ = bf16[72,384]{1,0:T(8,128)(2,1)S(1)} collective-permute-done((bf16[72,384]{1,0:T(8,128)(2,1)S(1)}, bf16[72,384]{1,0:T(8,128)(2,1)S(1)}, u32[]{:S(2)}, u32[]{:S(2)}) %collective-permute-start.7) | collective-permute-done | bytes 55328 | tf_op jit(solution)/shard_map/ppermute | solution.py:49
  23.4 0.0 collective-permute-done.8.refs_3_
  23.4 0.2 shard_map.107
  23.7 0.0 collective-permute-start.9
  23.7 1.2 %collective-permute-done.9.other_ref = f32[8,128]{1,0:T(8,128)S(1)} collective-permute-done((f32[8,128]{1,0:T(8,128)S(1)}, f32[8,128]{1,0:T(8,128)S(1)}, u32[]{:S(2)}, u32[]{:S(2)}) %collective-permute-start.9) | collective-permute-done | bytes 4128 | tf_op jit(solution)/shard_map/ppermute | solution.py:68
  24.8 1.6 %collective-permute-start.12 = (f32[8,128]{1,0:T(8,128)S(1)}, f32[8,128]{1,0:T(8,128)S(1)}, u32[]{:S(2)}, u32[]{:S(2)}) collective-permute-start(f32[8,128]{1,0:T(8,128)S(1)} %shard_map.108.refs_0_), channel_id=1, source_target_pairs={{0,6},{1,7},{2,4},{3,5},{4,2},{5,3},{6,0},{7,1},{8,14},{9,15},{10,... | collective-permute-start | bytes 12296 | tf_op jit(solution)/shard_map/ppermute | solution.py:49
  26.4 0.5 %collective-permute-start.11 = (f32[8,128]{1,0:T(8,128)S(1)}, f32[8,128]{1,0:T(8,128)S(1)}, u32[]{:S(2)}, u32[]{:S(2)}) collective-permute-start(f32[8,128]{1,0:T(8,128)S(1)} %shard_map.108.refs_0_), channel_id=1, source_target_pairs={{0,4},{1,5},{2,6},{3,7},{4,0},{5,1},{6,2},{7,3},{8,12},{9,13},{10,... | collective-permute-start | bytes 12296 | tf_op jit(solution)/shard_map/ppermute | solution.py:49
  27.0 1.4 %collective-permute-start.10 = (f32[8,128]{1,0:T(8,128)S(1)}, f32[8,128]{1,0:T(8,128)S(1)}, u32[]{:S(2)}, u32[]{:S(2)}) collective-permute-start(f32[8,128]{1,0:T(8,128)S(1)} %shard_map.108.refs_0_), channel_id=1, source_target_pairs={{0,2},{1,3},{2,0},{3,1},{4,6},{5,7},{6,4},{7,5},{8,10},{9,11},{10,... | collective-permute-start | bytes 12296 | tf_op jit(solution)/shard_map/ppermute | solution.py:49
  28.4 0.1 shard_map.109
  28.5 0.9 %collective-permute-done.12.refs_3_ = f32[8,128]{1,0:T(8,128)S(1)} collective-permute-done((f32[8,128]{1,0:T(8,128)S(1)}, f32[8,128]{1,0:T(8,128)S(1)}, u32[]{:S(2)}, u32[]{:S(2)}) %collective-permute-start.12) | collective-permute-done | bytes 4128 | tf_op jit(solution)/shard_map/ppermute | solution.py:49
  29.4 0.6 %collective-permute-done.11.refs_2_ = f32[8,128]{1,0:T(8,128)S(1)} collective-permute-done((f32[8,128]{1,0:T(8,128)S(1)}, f32[8,128]{1,0:T(8,128)S(1)}, u32[]{:S(2)}, u32[]{:S(2)}) %collective-permute-start.11) | collective-permute-done | bytes 4128 | tf_op jit(solution)/shard_map/ppermute | solution.py:49
  30.1 0.5 %collective-permute-done.10.refs_1_ = f32[8,128]{1,0:T(8,128)S(1)} collective-permute-done((f32[8,128]{1,0:T(8,128)S(1)}, f32[8,128]{1,0:T(8,128)S(1)}, u32[]{:S(2)}, u32[]{:S(2)}) %collective-permute-start.10) | collective-permute-done | bytes 4128 | tf_op jit(solution)/shard_map/ppermute | solution.py:49
  30.6 0.1 shard_map.110.refs_0_
  30.7 1.6 %collective-permute-start.15 = (bf16[40,384]{1,0:T(8,128)(2,1)S(1)}, bf16[40,384]{1,0:T(8,128)(2,1)S(1)}, u32[]{:S(2)}, u32[]{:S(2)}) collective-permute-start(bf16[40,384]{1,0:T(8,128)(2,1)S(1)} %shard_map.110.refs_0_), channel_id=1, source_target_pairs={{0,24},{8,16},{16,8},{24,0},{1,25},{9,17},{17,9},{25,1},{2,26},{10... | collective-permute-start | bytes 92168 | tf_op jit(solution)/shard_map/ppermute | solution.py:49
  32.3 0.8 %collective-permute-start.14 = (bf16[40,384]{1,0:T(8,128)(2,1)S(1)}, bf16[40,384]{1,0:T(8,128)(2,1)S(1)}, u32[]{:S(2)}, u32[]{:S(2)}) collective-permute-start(bf16[40,384]{1,0:T(8,128)(2,1)S(1)} %shard_map.110.refs_0_), channel_id=1, source_target_pairs={{0,16},{8,24},{16,0},{24,8},{1,17},{9,25},{17,1},{25,9},{2,18},{10... | collective-permute-start | bytes 92168 | tf_op jit(solution)/shard_map/ppermute | solution.py:49
  33.1 2.0 %collective-permute-start.13 = (bf16[40,384]{1,0:T(8,128)(2,1)S(1)}, bf16[40,384]{1,0:T(8,128)(2,1)S(1)}, u32[]{:S(2)}, u32[]{:S(2)}) collective-permute-start(bf16[40,384]{1,0:T(8,128)(2,1)S(1)} %shard_map.110.refs_0_), channel_id=1, source_target_pairs={{0,8},{8,0},{16,24},{24,16},{1,9},{9,1},{17,25},{25,17},{2,10},{10... | collective-permute-start | bytes 92168 | tf_op jit(solution)/shard_map/ppermute | solution.py:49
  35.2 1.3 %collective-permute-done.15.refs_3_ = bf16[40,384]{1,0:T(8,128)(2,1)S(1)} collective-permute-done((bf16[40,384]{1,0:T(8,128)(2,1)S(1)}, bf16[40,384]{1,0:T(8,128)(2,1)S(1)}, u32[]{:S(2)}, u32[]{:S(2)}) %collective-permute-start.15) | collective-permute-done | bytes 30752 | tf_op jit(solution)/shard_map/ppermute | solution.py:49
  36.5 0.8 %collective-permute-done.14.refs_2_ = bf16[40,384]{1,0:T(8,128)(2,1)S(1)} collective-permute-done((bf16[40,384]{1,0:T(8,128)(2,1)S(1)}, bf16[40,384]{1,0:T(8,128)(2,1)S(1)}, u32[]{:S(2)}, u32[]{:S(2)}) %collective-permute-start.14) | collective-permute-done | bytes 30752 | tf_op jit(solution)/shard_map/ppermute | solution.py:49
  37.2 0.1 collective-permute-done.13.refs_1_
  37.4 1.0 %shard_map.111 = (f32[1,1]{1,0:T(1,128)}, f32[256,384]{1,0:T(8,128)}, f32[384]{0:T(512)}) custom-call(bf16[40,384]{1,0:T(8,128)(2,1)S(1)} %shard_map.110.refs_0_, bf16[40,384]{1,0:T(8,128)(2,1)S(1)} %collective-permute-done.13.refs_1_, bf16[40,384]{1,0:T(8,128)(2,1)S(1)} %collective-permute-done.14.refs_2_, ...), custom_call_target="tpu_custom_call" | custom-call | tf_op jit(solution)/shard_map/pallas_call | solution.py:394
  (9 shorter events, 0.0 us)
Async XLA Ops:
  0.6 9.2 %collective-permute-start.3 = (bf16[32,1024]{1,0:T(8,128)(2,1)}, bf16[32,1024]{1,0:T(8,128)(2,1)S(1)}, u32[]{:S(2)}, u32[]{:S(2)}) collective-permute-start(bf16[32,1024]{1,0:T(8,128)(2,1)} %own_ref.1), channel_id=1, source_target_pairs={{0,16},{1,9},{2,18},{3,11},{4,20},{5,13},{6,22},{7,15},{8,24},{9,1... | collective-permute-start | bytes 196616 | tf_op jit(solution)/shard_map/ppermute | solution.py:64
  4.7 5.1 %collective-permute-start.4 = (bf16[32,1024]{1,0:T(8,128)(2,1)}, bf16[32,1024]{1,0:T(8,128)(2,1)S(1)}, u32[]{:S(2)}, u32[]{:S(2)}) collective-permute-start(bf16[32,1024]{1,0:T(8,128)(2,1)} %own_ref.1), channel_id=1, source_target_pairs={{0,8},{1,25},{2,10},{3,27},{4,12},{5,29},{6,14},{7,31},{8,0},{9,17... | collective-permute-start | bytes 196616 | tf_op jit(solution)/shard_map/ppermute | solution.py:64
  6.3 3.5 %copy-start.4 = (bf16[32,1024]{1,0:T(8,128)(2,1)S(1)}, bf16[32,1024]{1,0:T(8,128)(2,1)}, u32[]{:S(2)}) copy-start(bf16[32,1024]{1,0:T(8,128)(2,1)} %own_ref.1) | copy-start | bytes 196612
  6.3 3.5 %copy-start.6 = (f32[1024]{0:T(1024)S(1)}, f32[1024]{0:T(1024)}, u32[]{:S(2)}) copy-start(f32[1024]{0:T(1024)} %param.13) | copy-start | bytes 12292
  6.3 5.0 %collective-permute-start.2 = (bf16[16,1024]{1,0:T(8,128)(2,1)}, bf16[16,1024]{1,0:T(8,128)(2,1)S(1)}, u32[]{:S(2)}, u32[]{:S(2)}) collective-permute-start(bf16[16,1024]{1,0:T(8,128)(2,1)} %bitcast.5), channel_id=1, source_target_pairs={{0,6},{1,7},{2,4},{3,5},{4,2},{5,3},{6,0},{7,1},{8,14},{9,15},{10,... | collective-permute-start | bytes 98312 | tf_op jit(solution)/shard_map/ppermute | solution.py:49
  8.8 4.1 %collective-permute-start.1 = (bf16[16,1024]{1,0:T(8,128)(2,1)}, bf16[16,1024]{1,0:T(8,128)(2,1)S(1)}, u32[]{:S(2)}, u32[]{:S(2)}) collective-permute-start(bf16[16,1024]{1,0:T(8,128)(2,1)} %bitcast.6), channel_id=1, source_target_pairs={{0,4},{1,5},{2,6},{3,7},{4,0},{5,1},{6,2},{7,3},{8,12},{9,13},{10,... | collective-permute-start | bytes 98312 | tf_op jit(solution)/shard_map/ppermute | solution.py:49
  9.3 4.1 %collective-permute-start = (bf16[16,1024]{1,0:T(8,128)(2,1)}, bf16[16,1024]{1,0:T(8,128)(2,1)S(1)}, u32[]{:S(2)}, u32[]{:S(2)}) collective-permute-start(bf16[16,1024]{1,0:T(8,128)(2,1)} %bitcast.7), channel_id=1, source_target_pairs={{0,2},{1,3},{2,0},{3,1},{4,6},{5,7},{6,4},{7,5},{8,10},{9,11},{10,... | collective-permute-start | bytes 98312 | tf_op jit(solution)/shard_map/ppermute | solution.py:49
  9.8 3.6 %copy-start.5 = (bf16[1,16,1024]{2,1,0:T(8,128)(2,1)S(1)}, bf16[1,16,1024]{2,1,0:T(8,128)(2,1)}, u32[]{:S(2)}) copy-start(bf16[1,16,1024]{2,1,0:T(8,128)(2,1)} %param.8) | copy-start | bytes 98308
  9.8 3.6 %copy-start.7 = (f32[1,1024]{1,0:T(1,128)S(1)}, f32[1,1024]{1,0:T(1,128)}, u32[]{:S(2)}) copy-start(f32[1,1024]{1,0:T(1,128)} %refs_4_.2) | copy-start | bytes 12292
  13.4 1.7 %copy-start = (bf16[1,1024,384]{2,1,0:T(8,128)(2,1)S(1)}, bf16[1,1024,384]{2,1,0:T(8,128)(2,1)}, u32[]{:S(2)}) copy-start(bf16[1,1024,384]{2,1,0:T(8,128)(2,1)} %param.10) | copy-start | bytes 2359300
  13.4 1.7 %copy-start.1 = (bf16[256,384]{1,0:T(8,128)(2,1)S(1)}, bf16[256,384]{1,0:T(8,128)(2,1)}, u32[]{:S(2)}) copy-start(bf16[256,384]{1,0:T(8,128)(2,1)} %refs_4_.3) | copy-start | bytes 589828
  13.6 1.5 %copy-start.2 = (f32[384]{0:T(512)S(1)}, f32[384]{0:T(512)}, u32[]{:S(2)}) copy-start(f32[384]{0:T(512)} %refs_6_.1) | copy-start | bytes 4612
  13.6 1.5 %copy-start.3 = (f32[1,384]{1,0:T(1,128)S(1)}, f32[1,384]{1,0:T(1,128)}, u32[]{:S(2)}) copy-start(f32[1,384]{1,0:T(1,128)} %refs_5_.1) | copy-start | bytes 4612
  13.7 1.5 %collective-permute-start.5 = (bf16[80,1024]{1,0:T(8,128)(2,1)S(1)}, bf16[80,1024]{1,0:T(8,128)(2,1)S(1)}, u32[]{:S(2)}, u32[]{:S(2)}) collective-permute-start(bf16[80,1024]{1,0:T(8,128)(2,1)S(1)} %shard_map.105.refs_0_), channel_id=1, source_target_pairs={{0,1},{1,0},{2,3},{3,2},{4,5},{5,4},{6,7},{7,6},{8,9},{9,8},{10,11... | collective-permute-start | bytes 491528 | tf_op jit(solution)/shard_map/ppermute | solution.py:68
  15.8 6.7 %collective-permute-start.6 = (bf16[72,384]{1,0:T(8,128)(2,1)S(1)}, bf16[72,384]{1,0:T(8,128)(2,1)S(1)}, u32[]{:S(2)}, u32[]{:S(2)}) collective-permute-start(bf16[72,384]{1,0:T(8,128)(2,1)S(1)} %get-tuple-element.22), channel_id=1, source_target_pairs={{0,24},{8,16},{16,8},{24,0},{1,25},{9,17},{17,9},{25,1},{2,26},{10... | collective-permute-start | bytes 165896 | tf_op jit(solution)/shard_map/ppermute | solution.py:49
  16.1 7.4 %collective-permute-start.7 = (bf16[72,384]{1,0:T(8,128)(2,1)S(1)}, bf16[72,384]{1,0:T(8,128)(2,1)S(1)}, u32[]{:S(2)}, u32[]{:S(2)}) collective-permute-start(bf16[72,384]{1,0:T(8,128)(2,1)S(1)} %get-tuple-element.23), channel_id=1, source_target_pairs={{0,16},{8,24},{16,0},{24,8},{1,17},{9,25},{17,1},{25,9},{2,18},{10... | collective-permute-start | bytes 165896 | tf_op jit(solution)/shard_map/ppermute | solution.py:49
  17.7 5.7 %collective-permute-start.8 = (bf16[72,384]{1,0:T(8,128)(2,1)S(1)}, bf16[72,384]{1,0:T(8,128)(2,1)S(1)}, u32[]{:S(2)}, u32[]{:S(2)}) collective-permute-start(bf16[72,384]{1,0:T(8,128)(2,1)S(1)} %get-tuple-element.24), channel_id=1, source_target_pairs={{0,8},{8,0},{16,24},{24,16},{1,9},{9,1},{17,25},{25,17},{2,10},{10... | collective-permute-start | bytes 165896 | tf_op jit(solution)/shard_map/ppermute | solution.py:49
  23.7 1.2 %collective-permute-start.9 = (f32[8,128]{1,0:T(8,128)S(1)}, f32[8,128]{1,0:T(8,128)S(1)}, u32[]{:S(2)}, u32[]{:S(2)}) collective-permute-start(f32[8,128]{1,0:T(8,128)S(1)} %get-tuple-element.26.own_ref.refs_4_), channel_id=1, source_target_pairs={{0,1},{1,0},{2,3},{3,2},{4,5},{5,4},{6,7},{7,6},{8,9},{9,8},{10,11... | collective-permute-start | bytes 12296 | tf_op jit(solution)/shard_map/ppermute | solution.py:68
  24.8 4.6 %collective-permute-start.12 = (f32[8,128]{1,0:T(8,128)S(1)}, f32[8,128]{1,0:T(8,128)S(1)}, u32[]{:S(2)}, u32[]{:S(2)}) collective-permute-start(f32[8,128]{1,0:T(8,128)S(1)} %shard_map.108.refs_0_), channel_id=1, source_target_pairs={{0,6},{1,7},{2,4},{3,5},{4,2},{5,3},{6,0},{7,1},{8,14},{9,15},{10,... | collective-permute-start | bytes 12296 | tf_op jit(solution)/shard_map/ppermute | solution.py:49
  26.4 3.6 %collective-permute-start.11 = (f32[8,128]{1,0:T(8,128)S(1)}, f32[8,128]{1,0:T(8,128)S(1)}, u32[]{:S(2)}, u32[]{:S(2)}) collective-permute-start(f32[8,128]{1,0:T(8,128)S(1)} %shard_map.108.refs_0_), channel_id=1, source_target_pairs={{0,4},{1,5},{2,6},{3,7},{4,0},{5,1},{6,2},{7,3},{8,12},{9,13},{10,... | collective-permute-start | bytes 12296 | tf_op jit(solution)/shard_map/ppermute | solution.py:49
  27.0 3.6 %collective-permute-start.10 = (f32[8,128]{1,0:T(8,128)S(1)}, f32[8,128]{1,0:T(8,128)S(1)}, u32[]{:S(2)}, u32[]{:S(2)}) collective-permute-start(f32[8,128]{1,0:T(8,128)S(1)} %shard_map.108.refs_0_), channel_id=1, source_target_pairs={{0,2},{1,3},{2,0},{3,1},{4,6},{5,7},{6,4},{7,5},{8,10},{9,11},{10,... | collective-permute-start | bytes 12296 | tf_op jit(solution)/shard_map/ppermute | solution.py:49
  30.7 5.8 %collective-permute-start.15 = (bf16[40,384]{1,0:T(8,128)(2,1)S(1)}, bf16[40,384]{1,0:T(8,128)(2,1)S(1)}, u32[]{:S(2)}, u32[]{:S(2)}) collective-permute-start(bf16[40,384]{1,0:T(8,128)(2,1)S(1)} %shard_map.110.refs_0_), channel_id=1, source_target_pairs={{0,24},{8,16},{16,8},{24,0},{1,25},{9,17},{17,9},{25,1},{2,26},{10... | collective-permute-start | bytes 92168 | tf_op jit(solution)/shard_map/ppermute | solution.py:49
  32.3 4.9 %collective-permute-start.14 = (bf16[40,384]{1,0:T(8,128)(2,1)S(1)}, bf16[40,384]{1,0:T(8,128)(2,1)S(1)}, u32[]{:S(2)}, u32[]{:S(2)}) collective-permute-start(bf16[40,384]{1,0:T(8,128)(2,1)S(1)} %shard_map.110.refs_0_), channel_id=1, source_target_pairs={{0,16},{8,24},{16,0},{24,8},{1,17},{9,25},{17,1},{25,9},{2,18},{10... | collective-permute-start | bytes 92168 | tf_op jit(solution)/shard_map/ppermute | solution.py:49
  33.1 4.2 %collective-permute-start.13 = (bf16[40,384]{1,0:T(8,128)(2,1)S(1)}, bf16[40,384]{1,0:T(8,128)(2,1)S(1)}, u32[]{:S(2)}, u32[]{:S(2)}) collective-permute-start(bf16[40,384]{1,0:T(8,128)(2,1)S(1)} %shard_map.110.refs_0_), channel_id=1, source_target_pairs={{0,8},{8,0},{16,24},{24,16},{1,9},{9,1},{17,25},{25,17},{2,10},{10... | collective-permute-start | bytes 92168 | tf_op jit(solution)/shard_map/ppermute | solution.py:49

commit v12 on v11

--- a/solution.py
+++ b/solution.py
@@ -49,15 +49,20 @@
     return lax.ppermute(value, axis, pairs)
 
 
+def split_steps(j, members):
+    return max(members - 2 - 2 * j, 1), members - 1 - 2 * j
+
+
 def split_step(j, core, members):
-    return jnp.where(core == 1, 2 * j + 1, 2 * j + 2 if 2 * j + 2 < members else 1)
+    steps = split_steps(j, members)
+    return jnp.where(core == 0, steps[0], steps[1])
 
 
 def send_split(value, j):
     members, peers = lax.axis_size("member"), lax.axis_size("dp")
-    steps = 2 * j + 1, (2 * j + 2 if 2 * j + 2 < members else 1)
+    steps = split_steps(j, members)
     pairs = [
-        (m * peers + d, partner(m, steps[1 - d % 2], members) * peers + d)
+        (m * peers + d, partner(m, steps[d % 2], members) * peers + d)
         for m in range(members)
         for d in range(peers)
     ]

time: 38.5 us -> 38.5 us (level)
  no operation moved by 1% of the time
where the time goes in v12:
time: 38.5 us; the launch traced here: 38.3 us
  starting transfers between devices  21.7 us (56%)
  waiting for transfers between devices  13.3 us (35%)
  Pallas kernels  2.58 us (7%)
  between operations  0.76 us (2%)
    ppermute x12, starting transfers between devices, send(): return lax.ppermute(value, axis, pairs)  15.9 us
    ppermute x12, waiting for transfers between devices, send(): return lax.ppermute(value, axis, pairs)  10.7 us
    ppermute x2, starting transfers between devices, send_split(): return lax.ppermute(value, ('member', 'dp'), pairs)  5.68 us
    ppermute x2, waiting for transfers between devices, swap_cores(): lax.ppermute(value, axis, [(i, i ^ 1) for i in range(lax.axis_size(axis))])  2.53 us
    pallas_call x1, Pallas kernels, on_device(): call(functools.partial(gradient_kernel, members, images, classes * peers)...  0.97 us
  transfers between devices with their start and end apart: 16, of which 13 were waited for; matrix products, arithmetic and copies ran while one was open for 0% of the time, Pallas kernels for 1%

profile of v12, /device:TPU:0, one launch (start us, length us, event | category | flops | bytes accessed | tf_op | source)
XLA Modules:
  0.0 38.3 jit_solution(7280121632799079208)
XLA Ops:
  0.6 4.1 %collective-permute-start.3 = (bf16[32,1024]{1,0:T(8,128)(2,1)}, bf16[32,1024]{1,0:T(8,128)(2,1)S(1)}, u32[]{:S(2)}, u32[]{:S(2)}) collective-permute-start(bf16[32,1024]{1,0:T(8,128)(2,1)} %own_ref.1), channel_id=1, source_target_pairs={{0,16},{1,25},{2,18},{3,27},{4,20},{5,29},{6,22},{7,31},{8,24},{9,... | collective-permute-start | bytes 196616 | tf_op jit(solution)/shard_map/ppermute | solution.py:69
  4.7 1.6 %collective-permute-start.4 = (bf16[32,1024]{1,0:T(8,128)(2,1)}, bf16[32,1024]{1,0:T(8,128)(2,1)S(1)}, u32[]{:S(2)}, u32[]{:S(2)}) collective-permute-start(bf16[32,1024]{1,0:T(8,128)(2,1)} %own_ref.1), channel_id=1, source_target_pairs={{0,8},{1,9},{2,10},{3,11},{4,12},{5,13},{6,14},{7,15},{8,0},{9,1},... | collective-permute-start | bytes 196616 | tf_op jit(solution)/shard_map/ppermute | solution.py:69
  6.3 2.4 %collective-permute-start.2 = (bf16[16,1024]{1,0:T(8,128)(2,1)}, bf16[16,1024]{1,0:T(8,128)(2,1)S(1)}, u32[]{:S(2)}, u32[]{:S(2)}) collective-permute-start(bf16[16,1024]{1,0:T(8,128)(2,1)} %bitcast.5), channel_id=1, source_target_pairs={{0,6},{1,7},{2,4},{3,5},{4,2},{5,3},{6,0},{7,1},{8,14},{9,15},{10,... | collective-permute-start | bytes 98312 | tf_op jit(solution)/shard_map/ppermute | solution.py:49
  8.8 0.5 %collective-permute-start.1 = (bf16[16,1024]{1,0:T(8,128)(2,1)}, bf16[16,1024]{1,0:T(8,128)(2,1)S(1)}, u32[]{:S(2)}, u32[]{:S(2)}) collective-permute-start(bf16[16,1024]{1,0:T(8,128)(2,1)} %bitcast.6), channel_id=1, source_target_pairs={{0,4},{1,5},{2,6},{3,7},{4,0},{5,1},{6,2},{7,3},{8,12},{9,13},{10,... | collective-permute-start | bytes 98312 | tf_op jit(solution)/shard_map/ppermute | solution.py:49
  9.3 0.5 %collective-permute-start = (bf16[16,1024]{1,0:T(8,128)(2,1)}, bf16[16,1024]{1,0:T(8,128)(2,1)S(1)}, u32[]{:S(2)}, u32[]{:S(2)}) collective-permute-start(bf16[16,1024]{1,0:T(8,128)(2,1)} %bitcast.7), channel_id=1, source_target_pairs={{0,2},{1,3},{2,0},{3,1},{4,6},{5,7},{6,4},{7,5},{8,10},{9,11},{10,... | collective-permute-start | bytes 98312 | tf_op jit(solution)/shard_map/ppermute | solution.py:49
  9.8 0.0 collective-permute-done.3.refs_0_
  9.8 0.0 collective-permute-done.4.refs_1_
  9.8 0.0 copy-done.4
  9.8 0.0 copy-done.6
  9.8 0.0 copy-start.5
  9.8 0.0 copy-start.7
  9.9 0.2 shard_map.104
  10.1 1.2 %collective-permute-done.2.refs_3_ = bf16[16,1024]{1,0:T(8,128)(2,1)S(1)} collective-permute-done((bf16[16,1024]{1,0:T(8,128)(2,1)}, bf16[16,1024]{1,0:T(8,128)(2,1)S(1)}, u32[]{:S(2)}, u32[]{:S(2)}) %collective-permute-start.2) | collective-permute-done | bytes 32800 | tf_op jit(solution)/shard_map/ppermute | solution.py:49
  11.3 1.5 %collective-permute-done.1.refs_2_ = bf16[16,1024]{1,0:T(8,128)(2,1)S(1)} collective-permute-done((bf16[16,1024]{1,0:T(8,128)(2,1)}, bf16[16,1024]{1,0:T(8,128)(2,1)S(1)}, u32[]{:S(2)}, u32[]{:S(2)}) %collective-permute-start.1) | collective-permute-done | bytes 32800 | tf_op jit(solution)/shard_map/ppermute | solution.py:49
  12.9 0.5 %collective-permute-done.refs_1_ = bf16[16,1024]{1,0:T(8,128)(2,1)S(1)} collective-permute-done((bf16[16,1024]{1,0:T(8,128)(2,1)}, bf16[16,1024]{1,0:T(8,128)(2,1)S(1)}, u32[]{:S(2)}, u32[]{:S(2)}) %collective-permute-start) | collective-permute-done | bytes 32800 | tf_op jit(solution)/shard_map/ppermute | solution.py:49
  13.4 0.0 copy-done.5
  13.4 0.0 copy-done.7
  13.4 0.2 shard_map.105.refs_0_
  13.6 0.0 copy-start.2
  13.6 0.0 copy-start.3
  13.7 0.1 collective-permute-start.5
  13.7 1.4 %collective-permute-done.5.refs_1_ = bf16[80,1024]{1,0:T(8,128)(2,1)S(1)} collective-permute-done((bf16[80,1024]{1,0:T(8,128)(2,1)S(1)}, bf16[80,1024]{1,0:T(8,128)(2,1)S(1)}, u32[]{:S(2)}, u32[]{:S(2)}) %collective-permute-start.5) | collective-permute-done | bytes 163872 | tf_op jit(solution)/shard_map/ppermute | solution.py:73
  15.1 0.0 copy-done.3
  15.1 0.6 %shard_map.106 = (bf16[72,384]{1,0:T(8,128)(2,1)S(1)}, bf16[72,384]{1,0:T(8,128)(2,1)S(1)}, bf16[72,384]{1,0:T(8,128)(2,1)S(1)}, bf16[72,384]{1,0:T(8,128)(2,1)S...) custom-call(bf16[80,1024]{1,0:T(8,128)(2,1)S(1)} %shard_map.105.refs_0_, ...), custom_call_target="tpu_custom_call" | custom-call | tf_op jit(solution)/shard_map/pallas_call | solution.py:363
  15.8 0.3 collective-permute-start.6
  16.1 1.7 %collective-permute-start.7 = (bf16[72,384]{1,0:T(8,128)(2,1)S(1)}, bf16[72,384]{1,0:T(8,128)(2,1)S(1)}, u32[]{:S(2)}, u32[]{:S(2)}) collective-permute-start(bf16[72,384]{1,0:T(8,128)(2,1)S(1)} %get-tuple-element.23), channel_id=1, source_target_pairs={{0,16},{8,24},{16,0},{24,8},{1,17},{9,25},{17,1},{25,9},{2,18},{10... | collective-permute-start | bytes 165896 | tf_op jit(solution)/shard_map/ppermute | solution.py:49
  17.7 2.5 %collective-permute-start.8 = (bf16[72,384]{1,0:T(8,128)(2,1)S(1)}, bf16[72,384]{1,0:T(8,128)(2,1)S(1)}, u32[]{:S(2)}, u32[]{:S(2)}) collective-permute-start(bf16[72,384]{1,0:T(8,128)(2,1)S(1)} %get-tuple-element.24), channel_id=1, source_target_pairs={{0,8},{8,0},{16,24},{24,16},{1,9},{9,1},{17,25},{25,17},{2,10},{10... | collective-permute-start | bytes 165896 | tf_op jit(solution)/shard_map/ppermute | solution.py:49
  20.2 2.2 %collective-permute-done.6.refs_1_ = bf16[72,384]{1,0:T(8,128)(2,1)S(1)} collective-permute-done((bf16[72,384]{1,0:T(8,128)(2,1)S(1)}, bf16[72,384]{1,0:T(8,128)(2,1)S(1)}, u32[]{:S(2)}, u32[]{:S(2)}) %collective-permute-start.6) | collective-permute-done | bytes 55328 | tf_op jit(solution)/shard_map/ppermute | solution.py:49
  22.4 1.0 %collective-permute-done.7.refs_2_ = bf16[72,384]{1,0:T(8,128)(2,1)S(1)} collective-permute-done((bf16[72,384]{1,0:T(8,128)(2,1)S(1)}, bf16[72,384]{1,0:T(8,128)(2,1)S(1)}, u32[]{:S(2)}, u32[]{:S(2)}) %collective-permute-start.7) | collective-permute-done | bytes 55328 | tf_op jit(solution)/shard_map/ppermute | solution.py:49
  23.4 0.0 collective-permute-done.8.refs_3_
  23.4 0.2 shard_map.107
  23.7 0.0 collective-permute-start.9
  23.7 1.2 %collective-permute-done.9.other_ref = f32[8,128]{1,0:T(8,128)S(1)} collective-permute-done((f32[8,128]{1,0:T(8,128)S(1)}, f32[8,128]{1,0:T(8,128)S(1)}, u32[]{:S(2)}, u32[]{:S(2)}) %collective-permute-start.9) | collective-permute-done | bytes 4128 | tf_op jit(solution)/shard_map/ppermute | solution.py:73
  24.8 1.6 %collective-permute-start.12 = (f32[8,128]{1,0:T(8,128)S(1)}, f32[8,128]{1,0:T(8,128)S(1)}, u32[]{:S(2)}, u32[]{:S(2)}) collective-permute-start(f32[8,128]{1,0:T(8,128)S(1)} %shard_map.108.refs_0_), channel_id=1, source_target_pairs={{0,6},{1,7},{2,4},{3,5},{4,2},{5,3},{6,0},{7,1},{8,14},{9,15},{10,... | collective-permute-start | bytes 12296 | tf_op jit(solution)/shard_map/ppermute | solution.py:49
  26.4 0.5 %collective-permute-start.11 = (f32[8,128]{1,0:T(8,128)S(1)}, f32[8,128]{1,0:T(8,128)S(1)}, u32[]{:S(2)}, u32[]{:S(2)}) collective-permute-start(f32[8,128]{1,0:T(8,128)S(1)} %shard_map.108.refs_0_), channel_id=1, source_target_pairs={{0,4},{1,5},{2,6},{3,7},{4,0},{5,1},{6,2},{7,3},{8,12},{9,13},{10,... | collective-permute-start | bytes 12296 | tf_op jit(solution)/shard_map/ppermute | solution.py:49
  26.9 1.5 %collective-permute-start.10 = (f32[8,128]{1,0:T(8,128)S(1)}, f32[8,128]{1,0:T(8,128)S(1)}, u32[]{:S(2)}, u32[]{:S(2)}) collective-permute-start(f32[8,128]{1,0:T(8,128)S(1)} %shard_map.108.refs_0_), channel_id=1, source_target_pairs={{0,2},{1,3},{2,0},{3,1},{4,6},{5,7},{6,4},{7,5},{8,10},{9,11},{10,... | collective-permute-start | bytes 12296 | tf_op jit(solution)/shard_map/ppermute | solution.py:49
  28.4 0.1 shard_map.109
  28.5 0.9 %collective-permute-done.12.refs_3_ = f32[8,128]{1,0:T(8,128)S(1)} collective-permute-done((f32[8,128]{1,0:T(8,128)S(1)}, f32[8,128]{1,0:T(8,128)S(1)}, u32[]{:S(2)}, u32[]{:S(2)}) %collective-permute-start.12) | collective-permute-done | bytes 4128 | tf_op jit(solution)/shard_map/ppermute | solution.py:49
  29.4 0.6 %collective-permute-done.11.refs_2_ = f32[8,128]{1,0:T(8,128)S(1)} collective-permute-done((f32[8,128]{1,0:T(8,128)S(1)}, f32[8,128]{1,0:T(8,128)S(1)}, u32[]{:S(2)}, u32[]{:S(2)}) %collective-permute-start.11) | collective-permute-done | bytes 4128 | tf_op jit(solution)/shard_map/ppermute | solution.py:49
  30.0 0.5 %collective-permute-done.10.refs_1_ = f32[8,128]{1,0:T(8,128)S(1)} collective-permute-done((f32[8,128]{1,0:T(8,128)S(1)}, f32[8,128]{1,0:T(8,128)S(1)}, u32[]{:S(2)}, u32[]{:S(2)}) %collective-permute-start.10) | collective-permute-done | bytes 4128 | tf_op jit(solution)/shard_map/ppermute | solution.py:49
  30.5 0.1 shard_map.110.refs_0_
  30.7 1.5 %collective-permute-start.15 = (bf16[40,384]{1,0:T(8,128)(2,1)S(1)}, bf16[40,384]{1,0:T(8,128)(2,1)S(1)}, u32[]{:S(2)}, u32[]{:S(2)}) collective-permute-start(bf16[40,384]{1,0:T(8,128)(2,1)S(1)} %shard_map.110.refs_0_), channel_id=1, source_target_pairs={{0,24},{8,16},{16,8},{24,0},{1,25},{9,17},{17,9},{25,1},{2,26},{10... | collective-permute-start | bytes 92168 | tf_op jit(solution)/shard_map/ppermute | solution.py:49
  32.2 0.9 %collective-permute-start.14 = (bf16[40,384]{1,0:T(8,128)(2,1)S(1)}, bf16[40,384]{1,0:T(8,128)(2,1)S(1)}, u32[]{:S(2)}, u32[]{:S(2)}) collective-permute-start(bf16[40,384]{1,0:T(8,128)(2,1)S(1)} %shard_map.110.refs_0_), channel_id=1, source_target_pairs={{0,16},{8,24},{16,0},{24,8},{1,17},{9,25},{17,1},{25,9},{2,18},{10... | collective-permute-start | bytes 92168 | tf_op jit(solution)/shard_map/ppermute | solution.py:49
  33.1 2.0 %collective-permute-start.13 = (bf16[40,384]{1,0:T(8,128)(2,1)S(1)}, bf16[40,384]{1,0:T(8,128)(2,1)S(1)}, u32[]{:S(2)}, u32[]{:S(2)}) collective-permute-start(bf16[40,384]{1,0:T(8,128)(2,1)S(1)} %shard_map.110.refs_0_), channel_id=1, source_target_pairs={{0,8},{8,0},{16,24},{24,16},{1,9},{9,1},{17,25},{25,17},{2,10},{10... | collective-permute-start | bytes 92168 | tf_op jit(solution)/shard_map/ppermute | solution.py:49
  35.1 1.3 %collective-permute-done.15.refs_3_ = bf16[40,384]{1,0:T(8,128)(2,1)S(1)} collective-permute-done((bf16[40,384]{1,0:T(8,128)(2,1)S(1)}, bf16[40,384]{1,0:T(8,128)(2,1)S(1)}, u32[]{:S(2)}, u32[]{:S(2)}) %collective-permute-start.15) | collective-permute-done | bytes 30752 | tf_op jit(solution)/shard_map/ppermute | solution.py:49
  36.4 0.8 %collective-permute-done.14.refs_2_ = bf16[40,384]{1,0:T(8,128)(2,1)S(1)} collective-permute-done((bf16[40,384]{1,0:T(8,128)(2,1)S(1)}, bf16[40,384]{1,0:T(8,128)(2,1)S(1)}, u32[]{:S(2)}, u32[]{:S(2)}) %collective-permute-start.14) | collective-permute-done | bytes 30752 | tf_op jit(solution)/shard_map/ppermute | solution.py:49
  37.2 0.2 collective-permute-done.13.refs_1_
  37.4 1.0 %shard_map.111 = (f32[1,1]{1,0:T(1,128)}, f32[256,384]{1,0:T(8,128)}, f32[384]{0:T(512)}) custom-call(bf16[40,384]{1,0:T(8,128)(2,1)S(1)} %shard_map.110.refs_0_, bf16[40,384]{1,0:T(8,128)(2,1)S(1)} %collective-permute-done.13.refs_1_, bf16[40,384]{1,0:T(8,128)(2,1)S(1)} %collective-permute-done.14.refs_2_, ...), custom_call_target="tpu_custom_call" | custom-call | tf_op jit(solution)/shard_map/pallas_call | solution.py:399
  (9 shorter events, 0.0 us)
Async XLA Ops:
  0.6 9.2 %collective-permute-start.3 = (bf16[32,1024]{1,0:T(8,128)(2,1)}, bf16[32,1024]{1,0:T(8,128)(2,1)S(1)}, u32[]{:S(2)}, u32[]{:S(2)}) collective-permute-start(bf16[32,1024]{1,0:T(8,128)(2,1)} %own_ref.1), channel_id=1, source_target_pairs={{0,16},{1,25},{2,18},{3,27},{4,20},{5,29},{6,22},{7,31},{8,24},{9,... | collective-permute-start | bytes 196616 | tf_op jit(solution)/shard_map/ppermute | solution.py:69
  4.7 5.1 %collective-permute-start.4 = (bf16[32,1024]{1,0:T(8,128)(2,1)}, bf16[32,1024]{1,0:T(8,128)(2,1)S(1)}, u32[]{:S(2)}, u32[]{:S(2)}) collective-permute-start(bf16[32,1024]{1,0:T(8,128)(2,1)} %own_ref.1), channel_id=1, source_target_pairs={{0,8},{1,9},{2,10},{3,11},{4,12},{5,13},{6,14},{7,15},{8,0},{9,1},... | collective-permute-start | bytes 196616 | tf_op jit(solution)/shard_map/ppermute | solution.py:69
  6.3 3.5 %copy-start.4 = (bf16[32,1024]{1,0:T(8,128)(2,1)S(1)}, bf16[32,1024]{1,0:T(8,128)(2,1)}, u32[]{:S(2)}) copy-start(bf16[32,1024]{1,0:T(8,128)(2,1)} %own_ref.1) | copy-start | bytes 196612
  6.3 3.5 %copy-start.6 = (f32[1024]{0:T(1024)S(1)}, f32[1024]{0:T(1024)}, u32[]{:S(2)}) copy-start(f32[1024]{0:T(1024)} %param.13) | copy-start | bytes 12292
  6.3 5.0 %collective-permute-start.2 = (bf16[16,1024]{1,0:T(8,128)(2,1)}, bf16[16,1024]{1,0:T(8,128)(2,1)S(1)}, u32[]{:S(2)}, u32[]{:S(2)}) collective-permute-start(bf16[16,1024]{1,0:T(8,128)(2,1)} %bitcast.5), channel_id=1, source_target_pairs={{0,6},{1,7},{2,4},{3,5},{4,2},{5,3},{6,0},{7,1},{8,14},{9,15},{10,... | collective-permute-start | bytes 98312 | tf_op jit(solution)/shard_map/ppermute | solution.py:49
  8.8 4.1 %collective-permute-start.1 = (bf16[16,1024]{1,0:T(8,128)(2,1)}, bf16[16,1024]{1,0:T(8,128)(2,1)S(1)}, u32[]{:S(2)}, u32[]{:S(2)}) collective-permute-start(bf16[16,1024]{1,0:T(8,128)(2,1)} %bitcast.6), channel_id=1, source_target_pairs={{0,4},{1,5},{2,6},{3,7},{4,0},{5,1},{6,2},{7,3},{8,12},{9,13},{10,... | collective-permute-start | bytes 98312 | tf_op jit(solution)/shard_map/ppermute | solution.py:49
  9.3 4.1 %collective-permute-start = (bf16[16,1024]{1,0:T(8,128)(2,1)}, bf16[16,1024]{1,0:T(8,128)(2,1)S(1)}, u32[]{:S(2)}, u32[]{:S(2)}) collective-permute-start(bf16[16,1024]{1,0:T(8,128)(2,1)} %bitcast.7), channel_id=1, source_target_pairs={{0,2},{1,3},{2,0},{3,1},{4,6},{5,7},{6,4},{7,5},{8,10},{9,11},{10,... | collective-permute-start | bytes 98312 | tf_op jit(solution)/shard_map/ppermute | solution.py:49
  9.8 3.6 %copy-start.5 = (bf16[1,16,1024]{2,1,0:T(8,128)(2,1)S(1)}, bf16[1,16,1024]{2,1,0:T(8,128)(2,1)}, u32[]{:S(2)}) copy-start(bf16[1,16,1024]{2,1,0:T(8,128)(2,1)} %param.8) | copy-start | bytes 98308
  9.8 3.6 %copy-start.7 = (f32[1,1024]{1,0:T(1,128)S(1)}, f32[1,1024]{1,0:T(1,128)}, u32[]{:S(2)}) copy-start(f32[1,1024]{1,0:T(1,128)} %refs_4_.2) | copy-start | bytes 12292
  13.4 1.7 %copy-start = (bf16[1,1024,384]{2,1,0:T(8,128)(2,1)S(1)}, bf16[1,1024,384]{2,1,0:T(8,128)(2,1)}, u32[]{:S(2)}) copy-start(bf16[1,1024,384]{2,1,0:T(8,128)(2,1)} %param.10) | copy-start | bytes 2359300
  13.4 1.7 %copy-start.1 = (bf16[256,384]{1,0:T(8,128)(2,1)S(1)}, bf16[256,384]{1,0:T(8,128)(2,1)}, u32[]{:S(2)}) copy-start(bf16[256,384]{1,0:T(8,128)(2,1)} %refs_4_.3) | copy-start | bytes 589828
  13.6 1.5 %copy-start.2 = (f32[384]{0:T(512)S(1)}, f32[384]{0:T(512)}, u32[]{:S(2)}) copy-start(f32[384]{0:T(512)} %refs_6_.1) | copy-start | bytes 4612
  13.6 1.5 %copy-start.3 = (f32[1,384]{1,0:T(1,128)S(1)}, f32[1,384]{1,0:T(1,128)}, u32[]{:S(2)}) copy-start(f32[1,384]{1,0:T(1,128)} %refs_5_.1) | copy-start | bytes 4612
  13.7 1.5 %collective-permute-start.5 = (bf16[80,1024]{1,0:T(8,128)(2,1)S(1)}, bf16[80,1024]{1,0:T(8,128)(2,1)S(1)}, u32[]{:S(2)}, u32[]{:S(2)}) collective-permute-start(bf16[80,1024]{1,0:T(8,128)(2,1)S(1)} %shard_map.105.refs_0_), channel_id=1, source_target_pairs={{0,1},{1,0},{2,3},{3,2},{4,5},{5,4},{6,7},{7,6},{8,9},{9,8},{10,11... | collective-permute-start | bytes 491528 | tf_op jit(solution)/shard_map/ppermute | solution.py:73
  15.8 6.7 %collective-permute-start.6 = (bf16[72,384]{1,0:T(8,128)(2,1)S(1)}, bf16[72,384]{1,0:T(8,128)(2,1)S(1)}, u32[]{:S(2)}, u32[]{:S(2)}) collective-permute-start(bf16[72,384]{1,0:T(8,128)(2,1)S(1)} %get-tuple-element.22), channel_id=1, source_target_pairs={{0,24},{8,16},{16,8},{24,0},{1,25},{9,17},{17,9},{25,1},{2,26},{10... | collective-permute-start | bytes 165896 | tf_op jit(solution)/shard_map/ppermute | solution.py:49
  16.1 7.4 %collective-permute-start.7 = (bf16[72,384]{1,0:T(8,128)(2,1)S(1)}, bf16[72,384]{1,0:T(8,128)(2,1)S(1)}, u32[]{:S(2)}, u32[]{:S(2)}) collective-permute-start(bf16[72,384]{1,0:T(8,128)(2,1)S(1)} %get-tuple-element.23), channel_id=1, source_target_pairs={{0,16},{8,24},{16,0},{24,8},{1,17},{9,25},{17,1},{25,9},{2,18},{10... | collective-permute-start | bytes 165896 | tf_op jit(solution)/shard_map/ppermute | solution.py:49
  17.7 5.7 %collective-permute-start.8 = (bf16[72,384]{1,0:T(8,128)(2,1)S(1)}, bf16[72,384]{1,0:T(8,128)(2,1)S(1)}, u32[]{:S(2)}, u32[]{:S(2)}) collective-permute-start(bf16[72,384]{1,0:T(8,128)(2,1)S(1)} %get-tuple-element.24), channel_id=1, source_target_pairs={{0,8},{8,0},{16,24},{24,16},{1,9},{9,1},{17,25},{25,17},{2,10},{10... | collective-permute-start | bytes 165896 | tf_op jit(solution)/shard_map/ppermute | solution.py:49
  23.7 1.2 %collective-permute-start.9 = (f32[8,128]{1,0:T(8,128)S(1)}, f32[8,128]{1,0:T(8,128)S(1)}, u32[]{:S(2)}, u32[]{:S(2)}) collective-permute-start(f32[8,128]{1,0:T(8,128)S(1)} %get-tuple-element.26.own_ref.refs_4_), channel_id=1, source_target_pairs={{0,1},{1,0},{2,3},{3,2},{4,5},{5,4},{6,7},{7,6},{8,9},{9,8},{10,11... | collective-permute-start | bytes 12296 | tf_op jit(solution)/shard_map/ppermute | solution.py:73
  24.8 4.6 %collective-permute-start.12 = (f32[8,128]{1,0:T(8,128)S(1)}, f32[8,128]{1,0:T(8,128)S(1)}, u32[]{:S(2)}, u32[]{:S(2)}) collective-permute-start(f32[8,128]{1,0:T(8,128)S(1)} %shard_map.108.refs_0_), channel_id=1, source_target_pairs={{0,6},{1,7},{2,4},{3,5},{4,2},{5,3},{6,0},{7,1},{8,14},{9,15},{10,... | collective-permute-start | bytes 12296 | tf_op jit(solution)/shard_map/ppermute | solution.py:49
  26.4 3.6 %collective-permute-start.11 = (f32[8,128]{1,0:T(8,128)S(1)}, f32[8,128]{1,0:T(8,128)S(1)}, u32[]{:S(2)}, u32[]{:S(2)}) collective-permute-start(f32[8,128]{1,0:T(8,128)S(1)} %shard_map.108.refs_0_), channel_id=1, source_target_pairs={{0,4},{1,5},{2,6},{3,7},{4,0},{5,1},{6,2},{7,3},{8,12},{9,13},{10,... | collective-permute-start | bytes 12296 | tf_op jit(solution)/shard_map/ppermute | solution.py:49
  26.9 3.6 %collective-permute-start.10 = (f32[8,128]{1,0:T(8,128)S(1)}, f32[8,128]{1,0:T(8,128)S(1)}, u32[]{:S(2)}, u32[]{:S(2)}) collective-permute-start(f32[8,128]{1,0:T(8,128)S(1)} %shard_map.108.refs_0_), channel_id=1, source_target_pairs={{0,2},{1,3},{2,0},{3,1},{4,6},{5,7},{6,4},{7,5},{8,10},{9,11},{10,... | collective-permute-start | bytes 12296 | tf_op jit(solution)/shard_map/ppermute | solution.py:49
  30.7 5.8 %collective-permute-start.15 = (bf16[40,384]{1,0:T(8,128)(2,1)S(1)}, bf16[40,384]{1,0:T(8,128)(2,1)S(1)}, u32[]{:S(2)}, u32[]{:S(2)}) collective-permute-start(bf16[40,384]{1,0:T(8,128)(2,1)S(1)} %shard_map.110.refs_0_), channel_id=1, source_target_pairs={{0,24},{8,16},{16,8},{24,0},{1,25},{9,17},{17,9},{25,1},{2,26},{10... | collective-permute-start | bytes 92168 | tf_op jit(solution)/shard_map/ppermute | solution.py:49
  32.2 5.0 %collective-permute-start.14 = (bf16[40,384]{1,0:T(8,128)(2,1)S(1)}, bf16[40,384]{1,0:T(8,128)(2,1)S(1)}, u32[]{:S(2)}, u32[]{:S(2)}) collective-permute-start(bf16[40,384]{1,0:T(8,128)(2,1)S(1)} %shard_map.110.refs_0_), channel_id=1, source_target_pairs={{0,16},{8,24},{16,0},{24,8},{1,17},{9,25},{17,1},{25,9},{2,18},{10... | collective-permute-start | bytes 92168 | tf_op jit(solution)/shard_map/ppermute | solution.py:49
  33.1 4.2 %collective-permute-start.13 = (bf16[40,384]{1,0:T(8,128)(2,1)S(1)}, bf16[40,384]{1,0:T(8,128)(2,1)S(1)}, u32[]{:S(2)}, u32[]{:S(2)}) collective-permute-start(bf16[40,384]{1,0:T(8,128)(2,1)S(1)} %shard_map.110.refs_0_), channel_id=1, source_target_pairs={{0,8},{8,0},{16,24},{24,16},{1,9},{9,1},{17,25},{25,17},{2,10},{10... | collective-permute-start | bytes 92168 | tf_op jit(solution)/shard_map/ppermute | solution.py:49
